TPU v7x, 32 devices: a whole 2x2x4 slice. The times are simulated.
32 devices in a mesh: dp: 8 (over z, x), expert: 4 (over y, core).
Axes of the slice: x: 2, y: 2, z: 4, core: 2. Of those that a mesh axis runs over, the one named last changes fastest.
Arguments:
- activations: bfloat16 [4096, 6144], P(('dp', 'expert')), may hold values from -6 to 6
- gate_gradient: bfloat16 [4096, 2, 8192], P(('dp', 'expert')), may hold values from -0.1796875 to 0.1796875
- routes: int32 [4096, 2], P(('dp', 'expert')), may hold values from 0 to 3, as said below
- sequence_ids: int32 [32, 128], P(('dp', 'expert')), may hold values from 0 to 3, never falling along the last dimension, each value on 1 to 64 neighbouring positions
- input_basis: bfloat16 [4, 6144, 6144], P('expert', None, 'dp'), may hold values from -0.109375 to 0.109375
- output_basis: bfloat16 [4, 8192, 8192], P('expert', None, 'dp'), may hold values from -0.09375 to 0.09375
- input_query: bfloat16 [4, 6144, 128], P('expert', 'dp'), may hold values from -0.078125 to 0.078125
- output_query: bfloat16 [4, 8192, 128], P('expert', 'dp'), may hold values from -0.0625 to 0.0625
Outputs:
- scores: float32 [128, 4], P(('dp', 'expert'))
Inputs may be any that keep to these rules, and one draw needn't show every extreme that they name: `routes`: each token names 2 different experts. Among the 128 tokens of one aligned block (the rows of one device) no expert is named more than 128 times, and in every block one expert is named exactly 128 times, the same expert in all blocks of an aligned group of 4 consecutive blocks.
All inputs are finite; a program needn't handle non-finite values.
Results may differ from a plain program's by a relative error of at most 0.004.
Values may be sent and summed in bfloat16 or wider, within the bound.
No kernel may reach another device: no remote copies, remote signals or barrier semaphores. Data moves between devices by JAX's collectives and lax.ppermute only.
A program may use at most 128 MiB of HBM per device.

v0:
```python
import jax
import jax.numpy as jnp
from jax import lax
from jax.sharding import PartitionSpec as P

RANK = 32
SEG_DEV = 4


def per_device(
    activations,
    gate_gradient,
    routes,
    sequence_ids,
    input_basis,
    output_basis,
    input_query,
    output_query,
):
    token_count = activations.shape[0]
    top_count = routes.shape[1]
    width = activations.shape[1]
    hidden = gate_gradient.shape[2]
    experts = lax.axis_size("expert")
    capacity = 2 * token_count * top_count // experts
    route_count = token_count * top_count
    local_input = input_basis[0]
    local_output = output_basis[0]
    query_rows_input = input_query[0]
    query_rows_output = output_query[0]
    columns = query_rows_input.shape[1]
    queries = columns // RANK
    flat_routes = routes.reshape(route_count)
    expert_hot = (flat_routes[:, None] == jnp.arange(experts, dtype=jnp.int32)[None, :]).astype(
        jnp.int32
    )
    before = jnp.cumsum(expert_hot, axis=0) - expert_hot
    slot_index = jnp.sum(before * expert_hot, axis=1)
    target = flat_routes * capacity + slot_index
    source_row = (
        jnp.zeros((experts * capacity,), jnp.int32)
        .at[target]
        .set(jnp.arange(route_count, dtype=jnp.int32) + 1)
    )
    filled = (source_row > 0)[:, None]
    route_index = jnp.maximum(source_row - 1, 0)
    nothing = jnp.zeros((), jnp.bfloat16)
    send_inputs = jnp.where(filled, activations[route_index // top_count], nothing).reshape(
        experts, capacity, width
    )
    send_gradient = jnp.where(
        filled, gate_gradient.reshape(route_count, hidden)[route_index], nothing
    ).reshape(experts, capacity, hidden)
    block = local_input
    shard_input = lax.psum_scatter(
        jnp.dot(block, query_rows_input, preferred_element_type=jnp.float32),
        "dp",
        scatter_dimension=0,
        tiled=True,
    ).astype(jnp.bfloat16)
    block = local_output
    shard_output = lax.psum_scatter(
        jnp.dot(block, query_rows_output, preferred_element_type=jnp.float32),
        "dp",
        scatter_dimension=0,
        tiled=True,
    ).astype(jnp.bfloat16)
    landed_inputs, landed_gradient = (
        lax.all_to_all(send_inputs, "expert", split_axis=0, concat_axis=0, tiled=True),
        lax.all_to_all(send_gradient, "expert", split_axis=0, concat_axis=0, tiled=True),
    )
    slot_landed_inputs = landed_inputs.reshape(experts * capacity, width)
    slot_landed_gradient = landed_gradient.reshape(experts * capacity, hidden)
    block = slot_landed_inputs
    input_terms = jnp.dot(
        block,
        lax.all_gather(shard_input, "dp", axis=0, tiled=True),
        preferred_element_type=jnp.float32,
    )
    block = slot_landed_gradient
    output_terms = jnp.dot(
        block,
        lax.all_gather(shard_output, "dp", axis=0, tiled=True),
        preferred_element_type=jnp.float32,
    )
    slot_scores = (
        (input_terms * output_terms)
        .reshape(slot_landed_inputs.shape[0], queries, RANK)
        .sum(axis=-1)
    )
    slot_scores = slot_scores.reshape(experts, capacity, queries)
    returned = lax.all_to_all(
        slot_scores.reshape(experts, capacity * queries),
        "expert",
        split_axis=0,
        concat_axis=0,
        tiled=True,
    )
    route_scores = returned.reshape(experts * capacity, queries)[target]
    token_scores = route_scores.reshape(token_count, top_count, queries).sum(axis=1)
    membership = (sequence_ids[0][:, None] == jnp.arange(SEG_DEV, dtype=jnp.int32)[None, :]).astype(
        jnp.float32
    )
    return jnp.dot(
        membership.T,
        token_scores,
        precision=lax.Precision.HIGHEST,
        preferred_element_type=jnp.float32,
    )


def solution(mesh):
    return jax.shard_map(
        per_device,
        mesh=mesh,
        in_specs=(
            P(("dp", "expert"), None),
            P(("dp", "expert"), None, None),
            P(("dp", "expert"), None),
            P(("dp", "expert"), None),
            P("expert", None, "dp"),
            P("expert", None, "dp"),
            P("expert", "dp", None),
            P("expert", "dp", None),
        ),
        out_specs=P(("dp", "expert"), None),
        check_vma=False,
    )
```

profile of v0, /device:TPU:0, one launch (start us, length us, event | category | flops | bytes accessed | tf_op | source)
XLA Modules:
  0.0 303.4 jit_solution(7198582446141692074)
XLA Ops:
  6.5 0.0 copy-start
  6.5 8.1 %fusion.2 = f32[6144,128]{1,0:T(8,128)} fusion(bf16[1,6144,768]{2,1,0:T(8,128)(2,1)} %param.12, bf16[1,768,128]{2,1,0:T(8,128)(2,1)} %param.14), kind=kOutput, calls=%fused_computation.6 | convolution fusion | flops 1207959552 | bytes 12779520 | tf_op jit(solution)/shard_map/dot_general | solution.py:56
  14.6 0.0 reduce-scatter.3.cloned.1.call-update
  14.6 0.0 copy-start.3
  14.6 0.0 reduce-scatter.5.cloned.1.call-start
  14.7 10.3 %fusion = f32[8192,128]{1,0:T(8,128)} fusion(bf16[1,8192,1024]{2,1,0:T(8,128)(2,1)} %param.13, bf16[1,1024,128]{2,1,0:T(8,128)(2,1)S(1)} %copy-done.2), kind=kOutput, calls=%fused_computation.4 | convolution fusion | flops 2147483648 | bytes 21233664 | tf_op jit(solution)/shard_map/dot_general | solution.py:63
  25.0 0.0 reduce-scatter.5.cloned.1.call-update
  25.0 0.1 copy.17
  25.1 0.1 eq.48
  25.3 0.1 eq.44
  25.4 0.1 copy.16
  25.5 0.1 mul.24
  25.7 1.2 reduce-window.6
  26.9 0.1 slice.14
  27.0 0.1 copy.19
  27.1 0.1 copy.20
  27.2 0.1 add_bitcast_fusion
  27.3 1.4 scatter_custom_fusion
  28.8 6.1 %gather_fusion = bf16[512,6144]{1,0:T(8,128)(2,1)} fusion(bf16[128,6144]{1,0:T(8,128)(2,1)S(1)} %copy-done, s32[1024]{0:T(1024)S(1)} %get-tuple-element.8), kind=kCustom, calls=%fused_computation | custom fusion | bytes 12584960 | tf_op jit(solution)/shard_map/gather | solution.py:48
  34.9 5.9 %broadcast_select_fusion.1 = bf16[4,128,6144]{2,1,0:T(8,128)(2,1)} fusion(bf16[4,128,6144]{2,1,0:T(8,128)(2,1)} %bitcast.49, pred[4,128]{1,0:T(4,128)(4,1)S(1)} %compare_bitcast_fusion), kind=kLoop, calls=%fused_computation.9 | loop fusion | flops 3145728 | bytes 12583424 | tf_op jit(solution)/shard_map/jit(_where)/select_n | solution.py:48
  40.8 5.3 %all-to-all-start = ((bf16[4,128,6144]{2,1,0:T(8,128)(2,1)}), bf16[4,128,6144]{2,1,0:T(8,128)(2,1)}, u32[]{:S(2)}, u32[]{:S(2)}) async-start(bf16[4,128,6144]{2,1,0:T(8,128)(2,1)} %broadcast_select_fusion.1), calls=%async_computation | async-start | bytes 12582912 | tf_op jit(solution)/shard_map/all_to_all | solution.py:69
  46.1 0.2 all-gather.3.cloned.1.call-start
  46.3 7.3 %reshape.85 = bf16[256,8192]{1,0:T(8,128)(2,1)} reshape(bf16[128,2,8192]{2,1,0:T(2,128)(2,1)} %param.9) | data formatting | bytes 8388608 | tf_op jit(solution)/shard_map/reshape | solution.py:52
  53.6 18.3 %gather_fusion.1 = bf16[512,8192]{1,0:T(8,128)(2,1)} fusion(bf16[256,8192]{1,0:T(8,128)(2,1)} %reshape.85, s32[1024]{0:T(1024)S(1)} %get-tuple-element.7), kind=kCustom, calls=%fused_computation.1 | custom fusion | bytes 16779264 | tf_op jit(solution)/shard_map/gather | solution.py:52
  71.9 20.1 %reduce-scatter.3.cloned.1.call-done = f32[768,128]{1,0:T(8,128)} async-done(((f32[6144,128]{1,0:T(8,128)}), f32[768,128]{1,0:T(8,128)}) %reduce-scatter.3.cloned.1.call-update) | async-done | bytes 393232 | tf_op jit(solution)/shard_map/reduce_scatter | solution.py:55
  91.9 1.7 convert_element_type.16
  93.6 0.0 all-gather.3.cloned.1.call-update
  93.7 7.3 %broadcast_select_fusion = bf16[4,128,8192]{2,1,0:T(8,128)(2,1)} fusion(bf16[4,128,8192]{2,1,0:T(8,128)(2,1)} %bitcast.48, pred[4,128]{1,0:T(4,128)(4,1)S(1)} %compare_bitcast_fusion), kind=kLoop, calls=%fused_computation.8 | loop fusion | flops 4194304 | bytes 16777728 | tf_op jit(solution)/shard_map/jit(_where)/select_n | solution.py:51
  100.9 16.6 %all-to-all-done = bf16[4,128,6144]{2,1,0:T(8,128)(2,1)} async-done(((bf16[4,128,6144]{2,1,0:T(8,128)(2,1)}), bf16[4,128,6144]{2,1,0:T(8,128)(2,1)}, u32[]{:S(2)}, u32[]{:S(2)}) %all-to-all-start) | async-done | bytes 6291488 | tf_op jit(solution)/shard_map/all_to_all | solution.py:69
  117.5 5.7 %all-to-all-start.1 = ((bf16[4,128,8192]{2,1,0:T(8,128)(2,1)}), bf16[4,128,8192]{2,1,0:T(8,128)(2,1)}, u32[]{:S(2)}, u32[]{:S(2)}) async-start(bf16[4,128,8192]{2,1,0:T(8,128)(2,1)} %broadcast_select_fusion), calls=%async_computation.2 | async-start | bytes 16777216 | tf_op jit(solution)/shard_map/all_to_all | solution.py:70
  123.2 0.3 all-gather.5.cloned.1.call-start
  123.5 59.9 %reduce-scatter.5.cloned.1.call-done = f32[1024,128]{1,0:T(8,128)} async-done(((f32[8192,128]{1,0:T(8,128)}), f32[1024,128]{1,0:T(8,128)}) %reduce-scatter.5.cloned.1.call-update) | async-done | bytes 524304 | tf_op jit(solution)/shard_map/reduce_scatter | solution.py:62
  183.4 1.8 convert_element_type.17
  185.2 0.0 all-gather.5.cloned.1.call-update
  185.2 44.2 %all-gather.3.cloned.1.call-done = bf16[6144,128]{1,0:T(8,128)(2,1)} async-done(((bf16[768,128]{1,0:T(8,128)(2,1)}), bf16[6144,128]{1,0:T(8,128)(2,1)}) %all-gather.3.cloned.1.call-update) | async-done | bytes 1572880 | tf_op jit(solution)/shard_map/all_gather | solution.py:77
  229.5 5.4 %fusion.14 = f32[512,128]{0,1:T(8,128)S(1)} fusion(bf16[512,6144]{1,0:T(8,128)(2,1)} %bitcast.7, bf16[6144,128]{1,0:T(8,128)(2,1)} %all-gather.3.cloned.1.call-done), kind=kOutput, calls=%fused_computation.39 | convolution fusion | flops 805306368 | bytes 8126464 | tf_op jit(solution)/shard_map/dot_general | solution.py:75
  234.9 0.0 all-to-all-done.1
  234.9 44.9 %all-gather.5.cloned.1.call-done = bf16[8192,128]{1,0:T(8,128)(2,1)} async-done(((bf16[1024,128]{1,0:T(8,128)(2,1)}), bf16[8192,128]{1,0:T(8,128)(2,1)}) %all-gather.5.cloned.1.call-update) | async-done | bytes 2097168 | tf_op jit(solution)/shard_map/all_gather | solution.py:83
  279.8 7.0 %bitcast_reduce_fusion = f32[512,4]{0,1:T(4,128)S(1)} fusion(f32[512,128]{0,1:T(8,128)S(1)} %fusion.14, bf16[512,8192]{1,0:T(8,128)(2,1)} %bitcast.11, bf16[8192,128]{1,0:T(8,128)(2,1)} %all-gather.5.cloned.1.call-done), kind=kOutput, calls=%fused_computation.11 | convolution fusion | flops 1073870848 | bytes 10756096 | tf_op jit(solution)/shard_map/dot_general | solution.py:81
  286.8 0.1 copy.21
  287.0 0.8 all_to_all.16
  287.7 3.2 %all-to-all-start.2 = ((f32[4,1,512]{2,1,0:T(1,128)}), f32[4,1,512]{2,1,0:T(1,128)S(1)}, u32[]{:S(2)}, u32[]{:S(2)}) async-start(f32[4,1,512]{2,1,0:T(1,128)} %all_to_all.16), calls=%async_computation.4 | async-start | bytes 16384 | tf_op jit(solution)/shard_map/all_to_all | solution.py:92
  291.0 3.8 %all-to-all-done.2 = f32[4,1,512]{2,1,0:T(1,128)S(1)} async-done(((f32[4,1,512]{2,1,0:T(1,128)}), f32[4,1,512]{2,1,0:T(1,128)S(1)}, u32[]{:S(2)}, u32[]{:S(2)}) %all-to-all-start.2) | async-done | bytes 8224 | tf_op jit(solution)/shard_map/all_to_all | solution.py:92
  294.8 0.3 reshape.88
  295.1 0.7 gather_fusion.2
  295.8 0.2 reduce_sum.32
  296.0 0.9 fusion.6
  296.9 0.0 copy-done.1
  (20 shorter events, 0.2 us)
Async XLA Ops:
  6.5 22.2 %copy-start = (bf16[128,6144]{1,0:T(8,128)(2,1)S(1)}, bf16[128,6144]{1,0:T(8,128)(2,1)}, u32[]{:S(2)}) copy-start(bf16[128,6144]{1,0:T(8,128)(2,1)} %param.8) | copy-start | bytes 4718596
  6.5 8.2 %copy-start.2 = (bf16[1,1024,128]{2,1,0:T(8,128)(2,1)S(1)}, bf16[1,1024,128]{2,1,0:T(8,128)(2,1)}, u32[]{:S(2)}) copy-start(bf16[1,1024,128]{2,1,0:T(8,128)(2,1)} %param.15) | copy-start | bytes 786436
  6.5 85.4 %reduce-scatter.3.cloned.1.call-start = ((), (), s32[]{:S(2)}) async-start(), calls=%async_computation.5 | async-start | bytes 3538944 | tf_op jit(solution)/shard_map/reduce_scatter | solution.py:55
  14.6 10.4 %copy-start.3 = (s32[128,2]{0,1:T(2,128)S(1)}, s32[128,2]{0,1:T(2,128)}, u32[]{:S(2)}) copy-start(s32[128,2]{0,1:T(2,128)} %param.10) | copy-start | bytes 3076
  14.6 168.8 %reduce-scatter.5.cloned.1.call-start = ((), (), s32[]{:S(2)}) async-start(), calls=%async_computation.7 | async-start | bytes 4718592 | tf_op jit(solution)/shard_map/reduce_scatter | solution.py:62
  40.8 76.7 %all-to-all-start = ((bf16[4,128,6144]{2,1,0:T(8,128)(2,1)}), bf16[4,128,6144]{2,1,0:T(8,128)(2,1)}, u32[]{:S(2)}, u32[]{:S(2)}) async-start(bf16[4,128,6144]{2,1,0:T(8,128)(2,1)} %broadcast_select_fusion.1), calls=%async_computation | async-start | bytes 12582912 | tf_op jit(solution)/shard_map/all_to_all | solution.py:69
  46.1 183.4 %all-gather.3.cloned.1.call-start = ((), (), s32[]{:S(2)}) async-start(), calls=%async_computation.6 | async-start | bytes 1769472 | tf_op jit(solution)/shard_map/all_gather | solution.py:77
  117.5 117.4 %all-to-all-start.1 = ((bf16[4,128,8192]{2,1,0:T(8,128)(2,1)}), bf16[4,128,8192]{2,1,0:T(8,128)(2,1)}, u32[]{:S(2)}, u32[]{:S(2)}) async-start(bf16[4,128,8192]{2,1,0:T(8,128)(2,1)} %broadcast_select_fusion), calls=%async_computation.2 | async-start | bytes 16777216 | tf_op jit(solution)/shard_map/all_to_all | solution.py:70
  123.2 156.6 %all-gather.5.cloned.1.call-start = ((), (), s32[]{:S(2)}) async-start(), calls=%async_computation.8 | async-start | bytes 2359296 | tf_op jit(solution)/shard_map/all_gather | solution.py:83
  279.8 17.1 %copy-start.1 = (bf16[128,6144]{1,0:T(8,128)(2,1)S(1)}, bf16[128,6144]{1,0:T(8,128)(2,1)}, u32[]{:S(2)}) copy-start(bf16[128,6144]{1,0:T(8,128)(2,1)} %param.8) | copy-start | bytes 4718596
  279.8 16.2 %copy-start.4 = (s32[1,128]{1,0:T(1,128)S(1)}, s32[1,128]{1,0:T(1,128)}, u32[]{:S(2)}) copy-start(s32[1,128]{1,0:T(1,128)} %param.11) | copy-start | bytes 1540
  287.7 7.0 %all-to-all-start.2 = ((f32[4,1,512]{2,1,0:T(1,128)}), f32[4,1,512]{2,1,0:T(1,128)S(1)}, u32[]{:S(2)}, u32[]{:S(2)}) async-start(f32[4,1,512]{2,1,0:T(1,128)} %all_to_all.16), calls=%async_computation.4 | async-start | bytes 16384 | tf_op jit(solution)/shard_map/all_to_all | solution.py:92
Sparse Core Ops, SparseCore 0:
  14.8 77.1 reduce-scatter.2
  95.6 87.8 reduce-scatter.4
  185.8 43.5 all-gather.2
  231.7 48.0 all-gather.4
where the time goes:
time: 304 us; the launch traced here: 303 us
  waiting for transfers between devices  190 us (62%)
  local copies, waits for them, and re-layouts  35.9 us (12%)
  matrix products  31.6 us (10%)
  other arithmetic  18.3 us (6%)
  starting transfers between devices  14.8 us (5%)
  between operations  13.3 us (4%)
    reduce_scatter x1, waiting for transfers between devices, per_device(): lax.psum_scatter(jnp.dot(block, query_rows_output, preferred_element_type...  59.9 us
    all_gather x1, waiting for transfers between devices, per_device(): lax.all_gather(shard_output, 'dp', axis=0, tiled=True)  44.9 us
    all_gather x1, waiting for transfers between devices, per_device(): lax.all_gather(shard_input, 'dp', axis=0, tiled=True)  44.2 us
    reduce_scatter x1, waiting for transfers between devices, per_device(): lax.psum_scatter(jnp.dot(block, query_rows_input, preferred_element_type=...  20.1 us
    gather x1, local copies, waits for them, and re-layouts, per_device(): gate_gradient.reshape(route_count, hidden)[route_index]  18.3 us
    all_to_all x1, waiting for transfers between devices, per_device(): lax.all_to_all(send_inputs, 'expert', split_axis=0, concat_axis=0, tiled=...  16.6 us
    dot_general x1, matrix products, per_device(): jnp.dot(block, query_rows_output, preferred_element_type=jnp.float32)  10.3 us
    dot_general x1, matrix products, per_device(): jnp.dot(block, query_rows_input, preferred_element_type=jnp.float32)  8.07 us
  transfers between devices with their start and end apart: 7, of which 6 were waited for; matrix products, arithmetic and copies ran while one was open for 22% of the time, Pallas kernels for 0%

commit v1 on v0

v1 whole, which is shorter than its diff:
```python
import jax
import jax.numpy as jnp
from jax import lax
from jax.experimental import pallas as pl
from jax.experimental.pallas import tpu as pltpu
from jax.sharding import PartitionSpec as P

RANK = 32
SEG_DEV = 4
CORES = 2
TOP_EXPONENT = 15.0
TAIL = 16


def bits_of(count):
    return (count - 1).bit_length()


def slot_order(order):
    width = len(order)
    return [
        sum(((slot >> (width - 1 - i)) & 1) << bit for i, bit in enumerate(order))
        for slot in range(1 << width)
    ]


def fold_kernel(table_ref, basis_ref, query_ref, out_ref):
    out_ref[...] = jnp.dot(
        basis_ref[...], query_ref[...], preferred_element_type=jnp.float32
    )


def fold_part(basis, query, table, rows):
    depth, columns = query.shape
    blocks = table.shape[0]
    return pl.pallas_call(
        fold_kernel,
        grid_spec=pltpu.PrefetchScalarGridSpec(
            num_scalar_prefetch=1,
            grid=(blocks,),
            in_specs=[
                pl.BlockSpec((rows, depth), lambda i, t: (t[i], 0)),
                pl.BlockSpec((depth, columns), lambda i, t: (0, 0)),
            ],
            out_specs=pl.BlockSpec((rows, columns), lambda i, t: (i, 0)),
        ),
        out_shape=jax.ShapeDtypeStruct((blocks * rows, columns), jnp.float32),
        compiler_params=pltpu.CompilerParams(vmem_limit_bytes=24 * 1024 * 1024),
        cost_estimate=pl.CostEstimate(
            flops=2 * blocks * rows * depth * columns,
            bytes_accessed=blocks * rows * (depth * 2 + columns * 4),
            transcendentals=0,
        ),
    )(table, basis, query)


def column_exponent(query):
    peak = jnp.max(jnp.abs(query), axis=0, keepdims=True).astype(jnp.float32)
    bound = jnp.maximum(peak * (0.25 * query.shape[0]), 1e-28)
    return jnp.floor(jnp.log2(bound)) + 1.0


def pack(values, exponent):
    scaled = values * jnp.exp2(TOP_EXPONENT - exponent)
    tail = jnp.broadcast_to(exponent, (TAIL, values.shape[1]))
    return jnp.concatenate([scaled, tail], axis=0).astype(jnp.float16)


def unpack(packed):
    rows = packed.shape[0] - TAIL
    exponent = packed[rows : rows + 1].astype(jnp.float32)
    return packed[:rows].astype(jnp.float32) * jnp.exp2(exponent - TOP_EXPONENT), exponent


def flip(size, mask):
    return [(i, i ^ mask) for i in range(size)]


def reduce_parts(keep, send, exponent, order, blocks):
    for stage, bit in enumerate(order):
        landed = lax.ppermute(pack(send, exponent), "dp", flip(blocks, 1 << bit))
        values, other = unpack(landed)
        total = keep + values
        exponent = jnp.maximum(exponent, other) + 1.0
        if stage + 1 < len(order):
            half = total.shape[0] // 2
            keep, send = total[:half], total[half:]
    return total


def per_device(
    activations,
    gate_gradient,
    routes,
    sequence_ids,
    input_basis,
    output_basis,
    input_query,
    output_query,
):
    blocks = lax.axis_size("dp")
    group = lax.axis_size("expert")
    halves = group // CORES
    place = lax.axis_index("dp")
    member = lax.axis_index("expert")
    half = member // CORES
    core = member % CORES
    tokens, top = routes.shape
    columns = input_query.shape[2]
    queries = columns // RANK
    count = bits_of(blocks)

    def folded(basis, query, order):
        rows = basis.shape[0] // (blocks * halves)
        slots = jnp.array(slot_order(order), jnp.int32) ^ place
        parts = jnp.arange(halves, dtype=jnp.int32) ^ half
        table = (parts[None, :] * blocks + slots[:, None]).reshape(-1)
        middle = table.shape[0] // 2
        exponent = column_exponent(query)
        send = fold_part(basis, query, table[middle:], rows)
        keep = fold_part(basis, query, table[:middle], rows)
        total = reduce_parts(keep, send, exponent, order, blocks)
        shard = total.astype(jnp.bfloat16).reshape(halves, rows, columns)
        pieces = [shard[0]] + [
            lax.ppermute(shard[d], "expert", flip(group, d * CORES))
            for d in range(1, halves)
        ]
        return lax.all_gather(jnp.concatenate(pieces, axis=1), "dp", axis=0, tiled=True)

    def gathered(array):
        parts = array.reshape(array.shape[0], halves, -1)
        mine = [
            lax.dynamic_index_in_dim(parts, half ^ d, axis=1, keepdims=False)
            for d in range(halves)
        ]
        mine = [
            block if d == 0 else lax.ppermute(block, "expert", flip(group, d * CORES))
            for d, block in enumerate(mine)
        ]
        landed = []
        for block in mine:
            landed.append(block)
            landed.append(lax.ppermute(block, "expert", flip(group, 1)))
        return jnp.concatenate(landed, axis=0)

    fold_input = folded(input_basis[0], input_query[0], list(range(count)))
    fold_output = folded(
        output_basis[0], output_query[0], [(i + 1) % count for i in range(count)]
    )
    group_inputs = gathered(activations)
    group_gradient = [gathered(gate_gradient[:, k]) for k in range(top)]

    small = jnp.concatenate([routes.T, sequence_ids], axis=0)
    small = lax.all_gather(small, "expert", axis=0)
    small = small[member ^ jnp.arange(group, dtype=jnp.int32)]
    group_routes = [small[:, k].reshape(-1) for k in range(top)]
    group_sequences = small[:, top]

    expert_of = [(half ^ d) * CORES + core for d in range(halves)]

    def chosen(terms, route):
        out = jnp.zeros((terms.shape[0], columns), jnp.float32)
        for d in range(halves):
            hit = (route == expert_of[d])[:, None]
            out = out + jnp.where(hit, terms[:, d * columns : (d + 1) * columns], 0.0)
        return out

    input_terms = jnp.dot(group_inputs, fold_input, preferred_element_type=jnp.float32)
    input_chosen = jnp.stack([chosen(input_terms, route) for route in group_routes])
    for bit in range(bits_of(halves)):
        landed = lax.ppermute(
            input_chosen, "expert", flip(group, CORES << bit)
        ).reshape(top, halves, CORES * tokens, columns)
        order = [d ^ (1 << bit) for d in range(halves)]
        landed = jnp.concatenate([landed[:, d : d + 1] for d in order], axis=1)
        input_chosen = input_chosen + landed.reshape(input_chosen.shape)

    token_products = jnp.zeros((group * tokens, columns), jnp.float32)
    for k in range(top):
        output_terms = jnp.dot(
            group_gradient[k], fold_output, preferred_element_type=jnp.float32
        )
        token_products = token_products + input_chosen[k] * chosen(output_terms, group_routes[k])
    token_scores = token_products.reshape(group, tokens, queries, RANK).sum(axis=-1)
    membership = (
        group_sequences[:, :, None] == jnp.arange(SEG_DEV, dtype=jnp.int32)[None, None, :]
    ).astype(jnp.float32)
    partial = jnp.einsum(
        "gts,gtq->gsq",
        membership,
        token_scores,
        precision=lax.Precision.HIGHEST,
        preferred_element_type=jnp.float32,
    )
    scores = partial[0]
    for d in range(1, group):
        scores = scores + lax.ppermute(partial[d], "expert", flip(group, d))
    return scores


def solution(mesh):
    return jax.shard_map(
        per_device,
        mesh=mesh,
        in_specs=(
            P(("dp", "expert"), None),
            P(("dp", "expert"), None, None),
            P(("dp", "expert"), None),
            P(("dp", "expert"), None),
            P("expert", None, "dp"),
            P("expert", None, "dp"),
            P("expert", "dp", None),
            P("expert", "dp", None),
        ),
        out_specs=P(("dp", "expert"), None),
        check_vma=False,
    )
```

time: 304 us -> 248 us (0.82)
  waiting for transfers between devices: 190 us -> 59.8 us
  blocking collectives: 0 us -> 45.9 us
  local copies, waits for them, and re-layouts: 35.9 us -> 70 us
  matrix products: 31.6 us -> 11.9 us
  Pallas kernels: 0 us -> 14.3 us
  other arithmetic: 18.3 us -> 11.6 us
  starting transfers between devices: 14.8 us -> 19.4 us
    all_gather x2, waiting for transfers between devices: 89.1 us -> 0.04 us  [folded(): lax.all_gather(jnp.concatenate(pieces, axis=1), 'dp', axis=0, tiled=True)]
    reduce_scatter x2 -> x0, waiting for transfers between devices: 80 us -> none  [the longest x1 59.9 us: per_device(): lax.psum_scatter(jnp.dot(block, query_rows_output, preferred_element_type...]
    ppermute x0 -> x21, waiting for transfers between devices: none -> 59.7 us  [the longest x6 43.2 us: reduce_parts(): landed = lax.ppermute(pack(send, exponent), 'dp', flip(blocks, 1 << bit))]
    all_gather x0 -> x1, blocking collectives: none -> 45.9 us  [per_device(): small = lax.all_gather(small, 'expert', axis=0)]
    unnamed x11 -> x31, local copies, waits for them, and re-layouts: 0.13 us -> 40.5 us
    gather x3 -> x1, local copies, waits for them, and re-layouts: 25.1 us -> 0.57 us  [per_device(): small = small[member ^ jnp.arange(group, dtype=jnp.int32)]]
    all_to_all x3 -> x0, waiting for transfers between devices: 20.3 us -> none  [the longest x1 16.6 us: per_device(): lax.all_to_all(send_inputs, 'expert', split_axis=0, concat_axis=0, tiled=...]
    dot_general x5 -> x4, matrix products: 31.6 us -> 11.9 us  [the longest x2 8.43 us: per_device(): jnp.dot(group_gradient[k], fold_output, preferred_element_type=jnp.float32)]
  transfers between devices with their start and end apart: 7 -> 23, of which waited for: 6 -> 10; matrix products, arithmetic and copies ran while one was open for 22% -> 26% of each run, Pallas kernels for 0% -> 5%
where the time goes in v1:
time: 248 us; the launch traced here: 247 us
  local copies, waits for them, and re-layouts  70 us (28%)
  waiting for transfers between devices  59.8 us (24%)
  blocking collectives  45.9 us (19%)
  starting transfers between devices  19.4 us (8%)
  Pallas kernels  14.3 us (6%)
  between operations  13.9 us (6%)
  matrix products  11.9 us (5%)
  other arithmetic  11.6 us (5%)
    all_gather x1, blocking collectives, per_device(): small = lax.all_gather(small, 'expert', axis=0)  45.9 us
    ppermute x6, waiting for transfers between devices, reduce_parts(): landed = lax.ppermute(pack(send, exponent), 'dp', flip(blocks, 1 << bit))  43.2 us
    unnamed x31, local copies, waits for them, and re-layouts  40.5 us
    slice x1, local copies, waits for them, and re-layouts, per_device(): group_gradient = [gathered(gate_gradient[:, k]) for k in range(top)]  15 us
    pallas_call x4, Pallas kernels, fold_part(): pl.pallas_call(fold_kernel, grid_spec=pltpu.PrefetchScalarGridSpec(num_sc...  14.3 us
    dynamic_slice x8, local copies, waits for them, and re-layouts, gathered(): lax.dynamic_index_in_dim(parts, half ^ d, axis=1, keepdims=False)  12.1 us
    ppermute x1, waiting for transfers between devices, per_device(): lax.ppermute(input_chosen, 'expert', flip(group, CORES << bit))  8.91 us
    ppermute x6, starting transfers between devices, reduce_parts(): landed = lax.ppermute(pack(send, exponent), 'dp', flip(blocks, 1 << bit))  8.88 us
  transfers between devices with their start and end apart: 23, of which 10 were waited for; matrix products, arithmetic and copies ran while one was open for 26% of the time, Pallas kernels for 5%

profile of v1, /device:TPU:0, one launch (start us, length us, event | category | flops | bytes accessed | tf_op | source)
XLA Modules:
  0.0 246.8 jit_solution(2183341437871287684)
XLA Ops:
  7.4 1.0 abs_reduce_fusion.1
  8.4 3.7 %copy-done.2 = bf16[1,6144,768]{2,1,0:T(8,128)(2,1)S(1)} copy-done((bf16[1,6144,768]{2,1,0:T(8,128)(2,1)S(1)}, bf16[1,6144,768]{2,1,0:T(8,128)(2,1)}, u32[]{:S(2)}) %copy-start.2) | copy-done | bytes 9437208
  12.1 0.9 copy-done.5
  13.0 3.1 %shard_map.101 = f32[3072,128]{1,0:T(8,128)S(1)} custom-call(s32[8]{0:T(128)S(1)} %slice.164.table_ref, bf16[6144,768]{1,0:T(8,128)(2,1)S(1)} %bitcast.99, bf16[768,128]{1,0:T(8,128)(2,1)S(1)} %bitcast.103), custom_call_target="tpu_custom_call" | custom-call | flops 603979776 | bytes 6291456 | tf_op jit(solution)/shard_map/pallas_call | solution.py:36
  16.3 1.1 pad_maximum_fusion.1
  17.4 2.9 %collective-permute-start.3 = (f16[3088,128]{1,0:T(8,128)(2,1)}, f16[3088,128]{1,0:T(8,128)(2,1)}, u32[]{:S(2)}, u32[]{:S(2)}) collective-permute-start(f16[3088,128]{1,0:T(8,128)(2,1)} %pad_maximum_fusion.1), channel_id=1, source_target_pairs={{0,4},{4,0},{8,12},{12,8},{16,20},{20,16},{24,28},{28,24},{1,5},{5... | collective-permute-start | bytes 2371592 | tf_op jit(solution)/shard_map/ppermute | solution.py:81
  20.5 5.8 %copy-done = bf16[1,8192,1024]{2,1,0:T(8,128)(2,1)S(1)} copy-done((bf16[1,8192,1024]{2,1,0:T(8,128)(2,1)S(1)}, bf16[1,8192,1024]{2,1,0:T(8,128)(2,1)}, u32[]{:S(2)}) %copy-start) | copy-done | bytes 16777240
  26.3 4.1 %shard_map.103 = f32[4096,128]{1,0:T(8,128)S(1)} custom-call(s32[8]{0:T(128)S(1)} %slice.187.table_ref, bf16[8192,1024]{1,0:T(8,128)(2,1)S(1)} %bitcast.97, bf16[1024,128]{1,0:T(8,128)(2,1)S(1)} %bitcast.101), custom_call_target="tpu_custom_call" | custom-call | flops 1073741824 | bytes 10485760 | tf_op jit(solution)/shard_map/pallas_call | solution.py:36
  30.9 1.6 collective-permute-start.11
  32.7 3.7 %copy-done.3 = bf16[1,6144,768]{2,1,0:T(8,128)(2,1)S(1)} copy-done((bf16[1,6144,768]{2,1,0:T(8,128)(2,1)S(1)}, bf16[1,6144,768]{2,1,0:T(8,128)(2,1)}, u32[]{:S(2)}) %copy-start.3) | copy-done | bytes 9437208
  36.4 3.1 %shard_map.100 = f32[3072,128]{1,0:T(8,128)S(1)} custom-call(s32[8]{0:T(128)S(1)} %slice.162.table_ref, bf16[6144,768]{1,0:T(8,128)(2,1)S(1)} %bitcast.100, bf16[768,128]{1,0:T(8,128)(2,1)S(1)} %bitcast.104), custom_call_target="tpu_custom_call" | custom-call | flops 603979776 | bytes 6291456 | tf_op jit(solution)/shard_map/pallas_call | solution.py:36
  39.5 5.8 %copy-done.1 = bf16[1,8192,1024]{2,1,0:T(8,128)(2,1)S(1)} copy-done((bf16[1,8192,1024]{2,1,0:T(8,128)(2,1)S(1)}, bf16[1,8192,1024]{2,1,0:T(8,128)(2,1)}, u32[]{:S(2)}) %copy-start.1) | copy-done | bytes 16777240
  45.3 4.1 %shard_map.102 = f32[4096,128]{1,0:T(8,128)S(1)} custom-call(s32[8]{0:T(128)S(1)} %slice.185.table_ref, bf16[8192,1024]{1,0:T(8,128)(2,1)S(1)} %bitcast.98, bf16[1024,128]{1,0:T(8,128)(2,1)S(1)} %bitcast.102), custom_call_target="tpu_custom_call" | custom-call | flops 1073741824 | bytes 10485760 | tf_op jit(solution)/shard_map/pallas_call | solution.py:36
  50.0 1.3 multiply_add_fusion.1
  52.1 5.0 %collective-permute-done.11 = f16[4112,128]{1,0:T(8,128)(2,1)S(1)} collective-permute-done((f16[4112,128]{1,0:T(8,128)(2,1)S(1)}, f16[4112,128]{1,0:T(8,128)(2,1)S(1)}, u32[]{:S(2)}, u32[]{:S(2)}) %collective-permute-start.11) | collective-permute-done | bytes 1052704 | tf_op jit(solution)/shard_map/ppermute | solution.py:81
  57.5 6.7 %collective-permute-done.4 = f16[1552,128]{1,0:T(8,128)(2,1)S(1)} collective-permute-done((f16[1552,128]{1,0:T(8,128)(2,1)S(1)}, f16[1552,128]{1,0:T(8,128)(2,1)S(1)}, u32[]{:S(2)}, u32[]{:S(2)}) %collective-permute-start.4) | collective-permute-done | bytes 397344 | tf_op jit(solution)/shard_map/ppermute | solution.py:81
  64.4 2.7 %collective-permute-start.5 = (f16[784,128]{1,0:T(8,128)(2,1)S(1)}, f16[784,128]{1,0:T(8,128)(2,1)S(1)}, u32[]{:S(2)}, u32[]{:S(2)}) collective-permute-start(f16[784,128]{1,0:T(8,128)(2,1)S(1)} %pad_maximum_fusion.8), channel_id=1, source_target_pairs={{0,16},{4,20},{8,24},{12,28},{16,0},{20,4},{24,8},{28,12},{1,17},{... | collective-permute-start | bytes 602120 | tf_op jit(solution)/shard_map/ppermute | solution.py:81
  67.6 20.1 %collective-permute-done.5 = f16[784,128]{1,0:T(8,128)(2,1)S(1)} collective-permute-done((f16[784,128]{1,0:T(8,128)(2,1)S(1)}, f16[784,128]{1,0:T(8,128)(2,1)S(1)}, u32[]{:S(2)}, u32[]{:S(2)}) %collective-permute-start.5) | collective-permute-done | bytes 200736 | tf_op jit(solution)/shard_map/ppermute | solution.py:81
  87.8 1.6 collective-permute-start.6
  89.4 3.1 %collective-permute-done.6 = bf16[384,128]{1,0:T(8,128)(2,1)S(1)} collective-permute-done((bf16[384,128]{1,0:T(8,128)(2,1)S(1)}, bf16[384,128]{1,0:T(8,128)(2,1)S(1)}, u32[]{:S(2)}, u32[]{:S(2)}) %collective-permute-start.6) | collective-permute-done | bytes 98336 | tf_op jit(solution)/shard_map/ppermute | solution.py:125
  93.3 4.6 %collective-permute-done.12 = f16[2064,128]{1,0:T(8,128)(2,1)S(1)} collective-permute-done((f16[2064,128]{1,0:T(8,128)(2,1)S(1)}, f16[2064,128]{1,0:T(8,128)(2,1)S(1)}, u32[]{:S(2)}, u32[]{:S(2)}) %collective-permute-start.12) | collective-permute-done | bytes 528416 | tf_op jit(solution)/shard_map/ppermute | solution.py:81
  98.7 1.2 slice_add_fusion
  100.7 1.9 copy.28
  102.7 6.7 %collective-permute-done.13 = f16[1040,128]{1,0:T(8,128)(2,1)S(1)} collective-permute-done((f16[1040,128]{1,0:T(8,128)(2,1)S(1)}, f16[1040,128]{1,0:T(8,128)(2,1)S(1)}, u32[]{:S(2)}, u32[]{:S(2)}) %collective-permute-start.13) | collective-permute-done | bytes 266272 | tf_op jit(solution)/shard_map/ppermute | solution.py:81
  109.5 1.6 collective-permute-start.14
  111.2 1.2 copy.30
  112.9 1.2 copy.29
  114.0 1.6 collective-permute-done.14
  116.4 15.0 %fusion.57 = (bf16[128,1,8192]{2,1,0:T(2,128)(2,1)}, bf16[128,1,8192]{2,1,0:T(2,128)(2,1)}) fusion(bf16[128,2,8192]{2,1,0:T(2,128)(2,1)} %param.11), kind=kLoop, calls=%fused_computation.138 | loop fusion | bytes 8388608 | tf_op jit(solution)/shard_map/slice | solution.py:151
  131.4 8.8 %copy.39 = bf16[128,1,8192]{0,2,1:T(8,128)(2,1)S(1)} copy(bf16[128,1,8192]{2,1,0:T(2,128)(2,1)} %get-tuple-element.17) | data formatting | bytes 4194304
  140.2 9.2 %copy.40 = bf16[128,1,8192]{0,2,1:T(8,128)(2,1)} copy(bf16[128,1,8192]{2,1,0:T(2,128)(2,1)} %get-tuple-element.18) | data formatting | bytes 4194304
  149.4 3.3 %constant_dynamic-slice_fusion.1 = (bf16[128,1,4096]{0,2,1:T(8,128)(2,1)S(1)}, bf16[128,1,4096]{0,2,1:T(8,128)(2,1)}, bf16[128,1,4096]{0,2,1:T(8,128)(2,1)}, bf16[128,1,4096]{0,2,1:T(8,128)(2,1)}) fusion(bf16[128,2,4096]{0,2,1:T(8,128)(2,1)} %bitcast.106, s32[]{:T(128)S(6)} %select_n.61, s32[]{:T(128)S(6)} %select_n.62, bf16[128,2,4096]{0,2,1:T(8,128)(2,1)S(1)} %bitcast.105), kind=kLoop, calls=%fused_computation.90 | loop fusion | bytes 8388616 | tf_op jit(solution)/shard_map/jit(dynamic_index_in_dim)/dynamic_slice | solution.py:133
  152.7 2.4 copy.33
  155.1 1.8 collective-permute-start.9
  156.8 1.3 copy.36
  158.4 45.9 %all-gather.1 = s32[4,3,128]{2,1,0:T(4,128)S(1)} all-gather(s32[1,3,128]{2,1,0:T(4,128)S(1)} %add_bitcast_fusion.2), channel_id=2, replica_groups=mesh['dp'=8,'expert'=4] {'expert'}, dimensions={0}, use_global_device_ids=true | all-gather | bytes 7680 | tf_op jit(solution)/shard_map/all_gather | solution.py:154
  205.0 3.3 %fusion.16 = f32[512,256]{1,0:T(8,128)S(1)} fusion(bf16[3072,256]{1,0:T(8,128)(2,1)} %all-gather.5.cloned.1.call-done, bf16[128,3072]{1,0:T(8,128)(2,1)} %collective-permute-done.2, bf16[128,3072]{1,0:T(8,128)(2,1)} %collective-permute-done.1, bf16[128,3072]{1,0:T(8,128)(2,1)} %collective-permute-done, bf16[128,3072]{1,0:T(8,128)(2,1)} %bitcast.5), kind=kOutput, calls=%fused_computation.17 | convolution fusion | flops 817889280 | bytes 5242880 | tf_op jit(solution)/shard_map/dot_general | solution.py:168
  208.7 0.8 pad_maximum_fusion.3
  209.5 1.7 collective-permute-start.7
  211.3 1.4 copy.32
  213.2 1.3 copy.35
  215.1 8.9 %collective-permute-done.7 = f32[2,512,128]{2,1,0:T(8,128)} collective-permute-done((f32[2,512,128]{2,1,0:T(8,128)}, f32[2,512,128]{2,1,0:T(8,128)}, u32[]{:S(2)}, u32[]{:S(2)}) %collective-permute-start.7) | collective-permute-done | bytes 524320 | tf_op jit(solution)/shard_map/ppermute | solution.py:171
  224.0 1.1 fusion.58
  225.3 5.4 %fusion = f32[512,256]{1,0:T(8,128)S(1)} fusion(bf16[4096,256]{1,0:T(8,128)(2,1)} %all-gather.7.cloned.1.call-done, bf16[128,4096]{1,0:T(8,128)(2,1)} %collective-permute-done.10, bf16[128,4096]{1,0:T(8,128)(2,1)} %collective-permute-done.9, bf16[128,4096]{1,0:T(8,128)(2,1)} %collective-permute-done.8, bf16[128,4096]{1,0:T(8,128)(2,1)S(1)} %bitcast.109), kind=kOutput, calls=%fused_computation.1 | convolution fusion | flops 1090519040 | bytes 6815744 | tf_op jit(solution)/shard_map/dot_general | solution.py:180
  230.8 3.0 %fusion.8 = f32[512,256]{1,0:T(8,128)S(1)} fusion(bf16[4096,256]{1,0:T(8,128)(2,1)S(1)} %copy-done.13, bf16[128,4096]{1,0:T(8,128)(2,1)} %collective-permute-done.17, bf16[128,4096]{1,0:T(8,128)(2,1)} %collective-permute-done.16, bf16[128,4096]{1,0:T(8,128)(2,1)} %collective-permute-done.15, bf16[128,4096]{1,0:T(8,128)(2,1)} %bitcast.37), kind=kOutput, calls=%fused_computation.9 | convolution fusion | flops 1090519040 | bytes 6815744 | tf_op jit(solution)/shard_map/dot_general | solution.py:180
  234.6 1.8 collective-permute-start.19
  236.4 1.8 collective-permute-done.19
  238.2 1.2 collective-permute-done.20
  (117 shorter events, 12.3 us)
Async XLA Ops:
  6.5 198.5 %all-gather.5.cloned.1.call-start = ((), (), s32[]{:S(2)}) async-start(), calls=%async_computation | async-start | bytes 1769472 | tf_op jit(solution)/shard_map/all_gather | solution.py:128
  8.4 3.7 %copy-start.2 = (bf16[1,6144,768]{2,1,0:T(8,128)(2,1)S(1)}, bf16[1,6144,768]{2,1,0:T(8,128)(2,1)}, u32[]{:S(2)}) copy-start(bf16[1,6144,768]{2,1,0:T(8,128)(2,1)} %param.14) | copy-start | bytes 28311556
  12.1 0.9 copy-start.5
  16.1 4.3 %copy-start.4 = (bf16[1,1024,128]{2,1,0:T(8,128)(2,1)S(1)}, bf16[1,1024,128]{2,1,0:T(8,128)(2,1)}, u32[]{:S(2)}) copy-start(bf16[1,1024,128]{2,1,0:T(8,128)(2,1)} %param.17) | copy-start | bytes 786436
  17.4 32.0 %collective-permute-start.3 = (f16[3088,128]{1,0:T(8,128)(2,1)}, f16[3088,128]{1,0:T(8,128)(2,1)}, u32[]{:S(2)}, u32[]{:S(2)}) collective-permute-start(f16[3088,128]{1,0:T(8,128)(2,1)} %pad_maximum_fusion.1), channel_id=1, source_target_pairs={{0,4},{4,0},{8,12},{12,8},{16,20},{20,16},{24,28},{28,24},{1,5},{5... | collective-permute-start | bytes 2371592 | tf_op jit(solution)/shard_map/ppermute | solution.py:81
  20.5 5.8 %copy-start = (bf16[1,8192,1024]{2,1,0:T(8,128)(2,1)S(1)}, bf16[1,8192,1024]{2,1,0:T(8,128)(2,1)}, u32[]{:S(2)}) copy-start(bf16[1,8192,1024]{2,1,0:T(8,128)(2,1)} %param.15) | copy-start | bytes 50331652
  30.4 2.3 copy-start.6
  30.9 26.2 %collective-permute-start.11 = (f16[4112,128]{1,0:T(8,128)(2,1)S(1)}, f16[4112,128]{1,0:T(8,128)(2,1)S(1)}, u32[]{:S(2)}, u32[]{:S(2)}) collective-permute-start(f16[4112,128]{1,0:T(8,128)(2,1)S(1)} %pad_maximum_fusion), channel_id=1, source_target_pairs={{0,8},{4,12},{8,0},{12,4},{16,24},{20,28},{24,16},{28,20},{1,9},{5... | collective-permute-start | bytes 3158024 | tf_op jit(solution)/shard_map/ppermute | solution.py:81
  32.7 3.7 %copy-start.3 = (bf16[1,6144,768]{2,1,0:T(8,128)(2,1)S(1)}, bf16[1,6144,768]{2,1,0:T(8,128)(2,1)}, u32[]{:S(2)}) copy-start(bf16[1,6144,768]{2,1,0:T(8,128)(2,1)} %param.14) | copy-start | bytes 28311556
  39.5 5.8 %copy-start.1 = (bf16[1,8192,1024]{2,1,0:T(8,128)(2,1)S(1)}, bf16[1,8192,1024]{2,1,0:T(8,128)(2,1)}, u32[]{:S(2)}) copy-start(bf16[1,8192,1024]{2,1,0:T(8,128)(2,1)} %param.15) | copy-start | bytes 50331652
  51.6 12.6 %collective-permute-start.4 = (f16[1552,128]{1,0:T(8,128)(2,1)S(1)}, f16[1552,128]{1,0:T(8,128)(2,1)S(1)}, u32[]{:S(2)}, u32[]{:S(2)}) collective-permute-start(f16[1552,128]{1,0:T(8,128)(2,1)S(1)} %pad_maximum_fusion.5), channel_id=1, source_target_pairs={{0,8},{4,12},{8,0},{12,4},{16,24},{20,28},{24,16},{28,20},{1,9},{5... | collective-permute-start | bytes 1191944 | tf_op jit(solution)/shard_map/ppermute | solution.py:81
  64.4 23.3 %collective-permute-start.5 = (f16[784,128]{1,0:T(8,128)(2,1)S(1)}, f16[784,128]{1,0:T(8,128)(2,1)S(1)}, u32[]{:S(2)}, u32[]{:S(2)}) collective-permute-start(f16[784,128]{1,0:T(8,128)(2,1)S(1)} %pad_maximum_fusion.8), channel_id=1, source_target_pairs={{0,16},{4,20},{8,24},{12,28},{16,0},{20,4},{24,8},{28,12},{1,17},{... | collective-permute-start | bytes 602120 | tf_op jit(solution)/shard_map/ppermute | solution.py:81
  67.2 30.6 %collective-permute-start.12 = (f16[2064,128]{1,0:T(8,128)(2,1)S(1)}, f16[2064,128]{1,0:T(8,128)(2,1)S(1)}, u32[]{:S(2)}, u32[]{:S(2)}) collective-permute-start(f16[2064,128]{1,0:T(8,128)(2,1)S(1)} %pad_maximum_fusion.2), channel_id=1, source_target_pairs={{0,16},{4,20},{8,24},{12,28},{16,0},{20,4},{24,8},{28,12},{1,17},{... | collective-permute-start | bytes 1585160 | tf_op jit(solution)/shard_map/ppermute | solution.py:81
  87.8 4.7 %collective-permute-start.6 = (bf16[384,128]{1,0:T(8,128)(2,1)S(1)}, bf16[384,128]{1,0:T(8,128)(2,1)S(1)}, u32[]{:S(2)}, u32[]{:S(2)}) collective-permute-start(bf16[384,128]{1,0:T(8,128)(2,1)S(1)} %get-tuple-element.40), channel_id=1, source_target_pairs={{0,2},{1,3},{2,0},{3,1},{4,6},{5,7},{6,4},{7,5},{8,10},{9,11},{10,... | collective-permute-start | bytes 294920 | tf_op jit(solution)/shard_map/ppermute | solution.py:125
  93.2 132.0 %all-gather.7.cloned.1.call-start = ((), (), s32[]{:S(2)}) async-start(), calls=%async_computation.1 | async-start | bytes 2359296 | tf_op jit(solution)/shard_map/all_gather | solution.py:128
  97.9 0.8 copy-start.10
  100.0 9.4 %collective-permute-start.13 = (f16[1040,128]{1,0:T(8,128)(2,1)S(1)}, f16[1040,128]{1,0:T(8,128)(2,1)S(1)}, u32[]{:S(2)}, u32[]{:S(2)}) collective-permute-start(f16[1040,128]{1,0:T(8,128)(2,1)S(1)} %pad_maximum_fusion.6), channel_id=1, source_target_pairs={{0,4},{4,0},{8,12},{12,8},{16,20},{20,16},{24,28},{28,24},{1,5},{5... | collective-permute-start | bytes 798728 | tf_op jit(solution)/shard_map/ppermute | solution.py:81
  109.5 6.1 %collective-permute-start.14 = (bf16[512,128]{1,0:T(8,128)(2,1)S(1)}, bf16[512,128]{1,0:T(8,128)(2,1)S(1)}, u32[]{:S(2)}, u32[]{:S(2)}) collective-permute-start(bf16[512,128]{1,0:T(8,128)(2,1)S(1)} %get-tuple-element.38), channel_id=1, source_target_pairs={{0,2},{1,3},{2,0},{3,1},{4,6},{5,7},{6,4},{7,5},{8,10},{9,11},{10,... | collective-permute-start | bytes 393224 | tf_op jit(solution)/shard_map/ppermute | solution.py:125
  112.4 37.0 %collective-permute-start.1 = (bf16[128,3072]{1,0:T(8,128)(2,1)}, bf16[128,3072]{1,0:T(8,128)(2,1)}, u32[]{:S(2)}, u32[]{:S(2)}) collective-permute-start(bf16[128,3072]{1,0:T(8,128)(2,1)} %bitcast.6), channel_id=1, source_target_pairs={{0,2},{1,3},{2,0},{3,1},{4,6},{5,7},{6,4},{7,5},{8,10},{9,11},{10,... | collective-permute-start | bytes 2359304 | tf_op jit(solution)/shard_map/ppermute | solution.py:137
  114.0 90.9 %collective-permute-start = (bf16[128,3072]{1,0:T(8,128)(2,1)}, bf16[128,3072]{1,0:T(8,128)(2,1)}, u32[]{:S(2)}, u32[]{:S(2)}) collective-permute-start(bf16[128,3072]{1,0:T(8,128)(2,1)} %bitcast.5), channel_id=1, source_target_pairs={{0,1},{1,0},{2,3},{3,2},{4,5},{5,4},{6,7},{7,6},{8,9},{9,8},{10,11... | collective-permute-start | bytes 2359304 | tf_op jit(solution)/shard_map/ppermute | solution.py:143
  149.4 55.6 %collective-permute-start.2 = (bf16[128,3072]{1,0:T(8,128)(2,1)}, bf16[128,3072]{1,0:T(8,128)(2,1)}, u32[]{:S(2)}, u32[]{:S(2)}) collective-permute-start(bf16[128,3072]{1,0:T(8,128)(2,1)} %collective-permute-done.1), channel_id=1, source_target_pairs={{0,1},{1,0},{2,3},{3,2},{4,5},{5,4},{6,7},{7,6},{8,9},{9,8},{10,11... | collective-permute-start | bytes 2359304 | tf_op jit(solution)/shard_map/ppermute | solution.py:143
  152.7 4.1 %copy-start.8 = (bf16[128,1,4096]{0,2,1:T(8,128)(2,1)S(1)}, bf16[128,1,4096]{0,2,1:T(8,128)(2,1)}, u32[]{:S(2)}) copy-start(bf16[128,1,4096]{0,2,1:T(8,128)(2,1)} %get-tuple-element.22) | copy-start | bytes 3145732
  152.7 5.7 %copy-start.11 = (s32[128,2]{0,1:T(2,128)S(1)}, s32[128,2]{0,1:T(2,128)}, u32[]{:S(2)}) copy-start(s32[128,2]{0,1:T(2,128)} %param.12) | copy-start | bytes 3076
  152.7 5.7 %copy-start.12 = (s32[1,128]{1,0:T(1,128)S(1)}, s32[1,128]{1,0:T(1,128)}, u32[]{:S(2)}) copy-start(s32[1,128]{1,0:T(1,128)} %param.13) | copy-start | bytes 1540
  155.1 57.6 %collective-permute-start.9 = (bf16[128,4096]{1,0:T(8,128)(2,1)}, bf16[128,4096]{1,0:T(8,128)(2,1)}, u32[]{:S(2)}, u32[]{:S(2)}) collective-permute-start(bf16[128,4096]{1,0:T(8,128)(2,1)} %bitcast.24), channel_id=1, source_target_pairs={{0,2},{1,3},{2,0},{3,1},{4,6},{5,7},{6,4},{7,5},{8,10},{9,11},{10,... | collective-permute-start | bytes 3145736 | tf_op jit(solution)/shard_map/ppermute | solution.py:137
  158.2 56.4 %collective-permute-start.16 = (bf16[128,4096]{1,0:T(8,128)(2,1)}, bf16[128,4096]{1,0:T(8,128)(2,1)}, u32[]{:S(2)}, u32[]{:S(2)}) collective-permute-start(bf16[128,4096]{1,0:T(8,128)(2,1)} %bitcast.38), channel_id=1, source_target_pairs={{0,2},{1,3},{2,0},{3,1},{4,6},{5,7},{6,4},{7,5},{8,10},{9,11},{10,... | collective-permute-start | bytes 3145736 | tf_op jit(solution)/shard_map/ppermute | solution.py:137
  208.4 2.9 %copy-start.7 = (bf16[128,1,4096]{0,2,1:T(8,128)(2,1)S(1)}, bf16[128,1,4096]{0,2,1:T(8,128)(2,1)}, u32[]{:S(2)}) copy-start(bf16[128,1,4096]{0,2,1:T(8,128)(2,1)} %get-tuple-element.53) | copy-start | bytes 3145732
  209.5 14.4 %collective-permute-start.7 = (f32[2,512,128]{2,1,0:T(8,128)}, f32[2,512,128]{2,1,0:T(8,128)}, u32[]{:S(2)}, u32[]{:S(2)}) collective-permute-start(f32[2,512,128]{2,1,0:T(8,128)} %pad_maximum_fusion.3), channel_id=1, source_target_pairs={{0,2},{1,3},{2,0},{3,1},{4,6},{5,7},{6,4},{7,5},{8,10},{9,11},{10,... | collective-permute-start | bytes 1572872 | tf_op jit(solution)/shard_map/ppermute | solution.py:171
  212.7 12.5 %collective-permute-start.8 = (bf16[128,4096]{1,0:T(8,128)(2,1)}, bf16[128,4096]{1,0:T(8,128)(2,1)}, u32[]{:S(2)}, u32[]{:S(2)}) collective-permute-start(bf16[128,4096]{1,0:T(8,128)(2,1)} %bitcast.108), channel_id=1, source_target_pairs={{0,1},{1,0},{2,3},{3,2},{4,5},{5,4},{6,7},{7,6},{8,9},{9,8},{10,11... | collective-permute-start | bytes 3145736 | tf_op jit(solution)/shard_map/ppermute | solution.py:143
  212.7 12.5 %collective-permute-start.10 = (bf16[128,4096]{1,0:T(8,128)(2,1)}, bf16[128,4096]{1,0:T(8,128)(2,1)}, u32[]{:S(2)}, u32[]{:S(2)}) collective-permute-start(bf16[128,4096]{1,0:T(8,128)(2,1)} %collective-permute-done.9), channel_id=1, source_target_pairs={{0,1},{1,0},{2,3},{3,2},{4,5},{5,4},{6,7},{7,6},{8,9},{9,8},{10,11... | collective-permute-start | bytes 3145736 | tf_op jit(solution)/shard_map/ppermute | solution.py:143
  214.5 10.8 %copy-start.9 = (bf16[128,1,4096]{2,0,1:T(8,128)(2,1)S(1)}, bf16[128,1,4096]{2,0,1:T(8,128)(2,1)}, u32[]{:S(2)}) copy-start(bf16[128,1,4096]{2,0,1:T(8,128)(2,1)} %copy.32) | copy-start | bytes 3145732
  214.5 16.2 %collective-permute-start.15 = (bf16[128,4096]{1,0:T(8,128)(2,1)}, bf16[128,4096]{1,0:T(8,128)(2,1)}, u32[]{:S(2)}, u32[]{:S(2)}) collective-permute-start(bf16[128,4096]{1,0:T(8,128)(2,1)} %bitcast.37), channel_id=1, source_target_pairs={{0,1},{1,0},{2,3},{3,2},{4,5},{5,4},{6,7},{7,6},{8,9},{9,8},{10,11... | collective-permute-start | bytes 3145736 | tf_op jit(solution)/shard_map/ppermute | solution.py:143
  214.5 16.2 %collective-permute-start.17 = (bf16[128,4096]{1,0:T(8,128)(2,1)}, bf16[128,4096]{1,0:T(8,128)(2,1)}, u32[]{:S(2)}, u32[]{:S(2)}) collective-permute-start(bf16[128,4096]{1,0:T(8,128)(2,1)} %collective-permute-done.16), channel_id=1, source_target_pairs={{0,1},{1,0},{2,3},{3,2},{4,5},{5,4},{6,7},{7,6},{8,9},{9,8},{10,11... | collective-permute-start | bytes 3145736 | tf_op jit(solution)/shard_map/ppermute | solution.py:143
  225.3 5.5 %copy-start.13 = (bf16[4096,256]{1,0:T(8,128)(2,1)S(1)}, bf16[4096,256]{1,0:T(8,128)(2,1)}, u32[]{:S(2)}) copy-start(bf16[4096,256]{1,0:T(8,128)(2,1)} %all-gather.7.cloned.1.call-done) | copy-start | bytes 6291460
  234.5 1.9 collective-permute-start.18
  234.6 3.7 %collective-permute-start.19 = (f32[4,4]{1,0:T(4,128)S(1)}, f32[4,4]{1,0:T(4,128)S(1)}, u32[]{:S(2)}, u32[]{:S(2)}) collective-permute-start(f32[4,4]{1,0:T(4,128)S(1)} %get-tuple-element.43), channel_id=1, source_target_pairs={{0,2},{1,3},{2,0},{3,1},{4,6},{5,7},{6,4},{7,5},{8,10},{9,11},{10,... | collective-permute-start | bytes 200 | tf_op jit(solution)/shard_map/ppermute | solution.py:197
  236.4 3.0 %collective-permute-start.20 = (f32[4,4]{1,0:T(4,128)S(1)}, f32[4,4]{1,0:T(4,128)S(1)}, u32[]{:S(2)}, u32[]{:S(2)}) collective-permute-start(f32[4,4]{1,0:T(4,128)S(1)} %get-tuple-element.42), channel_id=1, source_target_pairs={{0,3},{1,2},{2,1},{3,0},{4,7},{5,6},{6,5},{7,4},{8,11},{9,10},{10,... | collective-permute-start | bytes 200 | tf_op jit(solution)/shard_map/ppermute | solution.py:197
Sparse Core Ops, SparseCore 0:
  93.3 44.7 all-gather.4
  140.3 48.0 all-gather.6

commit v2 on v1

v2 whole, which is shorter than its diff:
```python
import functools

import jax
import jax.numpy as jnp
from jax import lax
from jax.experimental import pallas as pl
from jax.experimental.pallas import tpu as pltpu
from jax.sharding import PartitionSpec as P

RANK = 32
SEG_DEV = 4
CORES = 2
TOP_EXPONENT = 15.0


def bits_of(count):
    return (count - 1).bit_length()


def slot_order(order):
    width = len(order)
    return [
        sum(((slot >> (width - 1 - i)) & 1) << bit for i, bit in enumerate(order))
        for slot in range(1 << width)
    ]


def column_exponent(query):
    peak = jnp.max(jnp.abs(query).astype(jnp.float32), axis=0, keepdims=True)
    bound = jnp.maximum(peak * (0.25 * query.shape[0]), 1e-28)
    return jnp.floor(jnp.log2(bound)) + 1.0


def fold_kernel(steps, width, *refs):
    position_ref, *basis_refs, query_ref, exponent_ref, send_ref, keep_ref = refs
    step = pl.program_id(0)
    rows = basis_refs[0].shape[0]
    scale = jnp.exp2(TOP_EXPONENT - exponent_ref[0:1, :])

    def terms(part):
        return jnp.dot(
            basis_refs[part][...], query_ref[...], preferred_element_type=jnp.float32
        )

    @pl.when(step < steps // 2)
    def _():
        for part in range(width):
            send_ref[pl.ds(part * rows, rows), :] = terms(part) * scale

    @pl.when(step >= steps // 2)
    def _():
        for part in range(width):
            keep_ref[pl.ds(part * rows, rows), :] = terms(part)


def fold_partial(basis, query, exponent, position, order, halves):
    depth, columns = query.shape
    blocks = 1 << len(order)
    count = blocks * halves
    rows = basis.shape[0] // count
    width = min(4, count // 2)
    steps = count // width

    def block(part):
        def index(i, position_ref):
            slot = (i * width + part) // halves ^ (blocks // 2)
            relative = sum(
                ((slot >> (len(order) - 1 - n)) & 1) << bit for n, bit in enumerate(order)
            )
            here = (i * width + part) % halves ^ position_ref[1]
            return here * blocks + (relative ^ position_ref[0]), 0

        return pl.BlockSpec((rows, depth), index)

    out = jax.ShapeDtypeStruct((count // 2 * rows, columns), jnp.float32)
    return pl.pallas_call(
        functools.partial(fold_kernel, steps, width),
        grid_spec=pltpu.PrefetchScalarGridSpec(
            num_scalar_prefetch=1,
            grid=(steps,),
            in_specs=[block(part) for part in range(width)]
            + [
                pl.BlockSpec((depth, columns), lambda i, p: (0, 0)),
                pl.BlockSpec(exponent.shape, lambda i, p: (0, 0)),
            ],
            out_specs=[
                pl.BlockSpec(
                    (width * rows, columns), lambda i, p: (jnp.minimum(i, steps // 2 - 1), 0)
                ),
                pl.BlockSpec(
                    (width * rows, columns), lambda i, p: (jnp.maximum(i - steps // 2, 0), 0)
                ),
            ],
        ),
        out_shape=[out, out],
        compiler_params=pltpu.CompilerParams(vmem_limit_bytes=56 * 1024 * 1024),
        cost_estimate=pl.CostEstimate(
            flops=2 * basis.size * columns,
            bytes_accessed=2 * basis.size + 4 * basis.shape[0] * columns,
            transcendentals=0,
        ),
    )(position, *([basis] * width), query, exponent)


def pack(values, exponent):
    return (values * jnp.exp2(TOP_EXPONENT - exponent)).astype(jnp.float16)


def unpack(packed, exponent):
    return packed.astype(jnp.float32) * jnp.exp2(exponent - TOP_EXPONENT)


def flip(size, mask):
    return [(i, i ^ mask) for i in range(size)]


def tie(*values):
    return lax.optimization_barrier(values)


def start_all(copies, done):
    started = []
    for i, (source, target) in enumerate(copies):
        started.append(pltpu.make_async_copy(source, target, done.at[i]))
        started[i].start()
    return started


def input_kernel(top, fold_ref, mask_ref, *refs):
    *token_refs, out_ref, sent_ref, tokens_ref, held_ref, done = refs
    count = token_refs[0].shape[0]
    copies = [(fold_ref, held_ref)] + [
        (token_ref, tokens_ref.at[pl.ds(i * count, count), :])
        for i, token_ref in enumerate(token_refs)
    ]
    for copy in start_all(copies, done):
        copy.wait()
    terms = jnp.dot(tokens_ref[...], held_ref[...], preferred_element_type=jnp.float32)
    total = tokens_ref.shape[0]
    columns = out_ref.shape[1]
    for k in range(top):
        rows_of = pl.ds(k, total, stride=top)
        out_ref[rows_of, :] = sum(
            terms[:, d * columns : (d + 1) * columns] * mask_ref[d, rows_of, :]
            for d in range(mask_ref.shape[0])
        )
    sent_ref[...] = out_ref[...].astype(sent_ref.dtype)


def input_chosen(pieces, fold, mask, top):
    total = sum(piece.shape[0] for piece in pieces)
    width, across = fold.shape
    columns = mask.shape[2]
    return pl.pallas_call(
        functools.partial(input_kernel, top),
        in_specs=[pl.BlockSpec(memory_space=pl.ANY), pl.BlockSpec(memory_space=pltpu.VMEM)]
        + [pl.BlockSpec(memory_space=pl.ANY)] * len(pieces),
        out_specs=[pl.BlockSpec(memory_space=pltpu.VMEM)] * 2,
        out_shape=[
            jax.ShapeDtypeStruct((total * top, columns), jnp.float32),
            jax.ShapeDtypeStruct((total * top, columns), jnp.bfloat16),
        ],
        scratch_shapes=[
            pltpu.VMEM((total, width), pieces[0].dtype),
            pltpu.VMEM((width, across), fold.dtype),
            pltpu.SemaphoreType.DMA((len(pieces) + 1,)),
        ],
        compiler_params=pltpu.CompilerParams(vmem_limit_bytes=58 * 1024 * 1024),
        cost_estimate=pl.CostEstimate(
            flops=2 * total * width * across,
            bytes_accessed=2 * (total + across) * width,
            transcendentals=0,
        ),
    )(fold, mask, *pieces)


def score_kernel(
    counts, orders, parts, position_ref, mask_ref, member_ref, query_ref, chosen_ref, *refs
):
    *refs, out_ref, tokens_ref, fold_ref, total_ref, folded, done = refs
    token_refs, refs = refs[: len(counts)], refs[len(counts) :]
    held_refs, landed_refs = refs[: 2 * len(orders)], refs[2 * len(orders) :]
    width = fold_ref.shape[0] // parts
    columns = chosen_ref.shape[1]
    copies = []
    for n, order in enumerate(orders):
        slots, rows, _ = held_refs[2 * n].shape
        for slot, relative in enumerate(slot_order(order)):
            start = (relative ^ position_ref[0]) * (rows * len(orders)) + n * rows
            start = pl.multiple_of(start, rows)
            source = held_refs[2 * n + slot // slots].at[slot % slots]
            copies.append((source, fold_ref.at[pl.ds(start, rows), :]))
    fold_copies = start_all(copies, folded)
    started = []
    for part in range(parts):
        across = pl.ds(part * width, width)
        copies = []
        start = 0
        for count, token_ref in zip(counts, token_refs):
            copies.append((token_ref.at[:, across], tokens_ref.at[pl.ds(start, count), across]))
            start += count
        started.append(start_all(copies, done.at[part]))
    for copy in fold_copies:
        copy.wait()
    for part in range(parts):
        for copy in started[part]:
            copy.wait()
        across = pl.ds(part * width, width)
        terms = jnp.dot(
            tokens_ref[:, across], fold_ref[across, :], preferred_element_type=jnp.float32
        )
        total_ref[...] = terms if part == 0 else total_ref[...] + terms
    output = sum(
        total_ref[:, d * columns : (d + 1) * columns] * mask_ref[d]
        for d in range(mask_ref.shape[0])
    )
    halves = len(landed_refs) + 1
    rows = chosen_ref.shape[0] // halves
    summed = jnp.zeros((member_ref.shape[0], columns), jnp.float32)
    for h in range(halves):
        here = pl.ds(h * rows, rows)
        inputs = chosen_ref[here, :]
        for d, landed_ref in enumerate(landed_refs):
            landed = landed_ref[pl.ds((h ^ (d + 1)) * rows, rows), :]
            inputs = inputs + landed.astype(jnp.float32)
        summed = summed + jnp.dot(
            member_ref[:, here],
            inputs * output[h * rows : (h + 1) * rows],
            precision=lax.Precision.HIGHEST,
            preferred_element_type=jnp.float32,
        )
    out_ref[...] = jnp.dot(
        summed,
        query_ref[...],
        precision=lax.Precision.HIGHEST,
        preferred_element_type=jnp.float32,
    )


def partial_scores(
    pieces, held, orders, position, mask, membership, query_sum, chosen, landed
):
    counts = [piece.shape[0] for piece in pieces]
    total = sum(counts)
    width = pieces[0].shape[1]
    across = held[0].shape[2]
    parts = 4
    return pl.pallas_call(
        functools.partial(score_kernel, counts, orders, parts),
        in_specs=[pl.BlockSpec(memory_space=pltpu.SMEM)]
        + [pl.BlockSpec(memory_space=pltpu.VMEM)] * 4
        + [pl.BlockSpec(memory_space=pl.ANY)] * (len(pieces) + len(held))
        + [pl.BlockSpec(memory_space=pltpu.VMEM)] * len(landed),
        out_specs=pl.BlockSpec(memory_space=pltpu.VMEM),
        out_shape=jax.ShapeDtypeStruct((membership.shape[0], query_sum.shape[1]), jnp.float32),
        scratch_shapes=[
            pltpu.VMEM((total, width), pieces[0].dtype),
            pltpu.VMEM((width, across), held[0].dtype),
            pltpu.VMEM((total, across), jnp.float32),
            pltpu.SemaphoreType.DMA((sum(part.shape[0] for part in held),)),
            pltpu.SemaphoreType.DMA((parts, len(pieces))),
        ],
        compiler_params=pltpu.CompilerParams(vmem_limit_bytes=58 * 1024 * 1024),
        cost_estimate=pl.CostEstimate(
            flops=2 * total * width * across,
            bytes_accessed=2 * (total + across) * width,
            transcendentals=0,
        ),
    )(position, mask, membership, query_sum, chosen, *pieces, *held, *landed)


def per_device(
    activations,
    gate_gradient,
    routes,
    sequence_ids,
    input_basis,
    output_basis,
    input_query,
    output_query,
):
    blocks = lax.axis_size("dp")
    group = lax.axis_size("expert")
    halves = group // CORES
    place = lax.axis_index("dp")
    member = lax.axis_index("expert")
    half = member // CORES
    core = member % CORES
    tokens, top = routes.shape
    columns = input_query.shape[2]
    queries = columns // RANK
    count = bits_of(blocks)

    def send(packed, bit):
        return lax.ppermute(packed, "dp", flip(blocks, 1 << bit))

    def own_shard(total):
        shard = total.astype(jnp.bfloat16)
        return shard.reshape(halves, -1, columns)

    def exchange(shard):
        pieces = [shard[0]] + [
            lax.ppermute(shard[d], "expert", flip(group, d * CORES)) for d in range(1, halves)
        ]
        return jnp.concatenate(pieces, axis=1)

    def from_half(part, d):
        return part if d == 0 else lax.ppermute(part, "expert", flip(group, d * CORES))

    def from_core(part):
        return lax.ppermute(part, "expert", flip(group, 1))

    order_first = [(i + 1) % count for i in range(count)]
    order_second = list(range(count))
    position = jnp.stack([place, half]).astype(jnp.int32)
    own = jnp.concatenate([column_exponent(input_query[0]), column_exponent(output_query[0])])

    def joined(keep, landed, exponent):
        total = keep + unpack(landed, exponent)
        middle = total.shape[0] // 2
        return total[:middle], total[middle:]

    send_first, keep_first = fold_partial(
        input_basis[0], input_query[0], own[0:1], position, order_first, halves
    )
    there = [send(own, order_first[0])]
    whole = jnp.maximum(own, there[0])
    there_second = send(own, order_second[0])[1:2]
    send_first, whole = tie(send_first, whole)
    for bit in order_first[1:-1]:
        whole = jnp.maximum(whole, send(whole, bit))
    packed_first = send_first.astype(jnp.float16)
    output_basis, packed_first = tie(output_basis, packed_first)
    landed_first = send(packed_first, order_first[0])

    send_second, keep_second = fold_partial(
        output_basis[0], output_query[0], own[1:2], position, order_second, halves
    )
    send_second, whole = tie(send_second, whole)
    whole = jnp.maximum(whole, send(whole, order_first[-1]))
    packed_second = send_second.astype(jnp.float16)
    activations, routes, packed_second = tie(activations, routes, packed_second)
    landed_second = send(packed_second, order_second[0])

    input_width = activations.shape[1] // halves
    input_parts = [
        lax.dynamic_slice_in_dim(activations, (half ^ d) * input_width, input_width, axis=1)
        for d in range(halves)
    ]
    keep_first, *input_parts = tie(keep_first, *input_parts)
    input_parts = [from_half(part, d) for d, part in enumerate(input_parts)]
    keep_first, send_first = joined(keep_first, landed_first, there[0][0:1])
    packed_first = pack(send_first, whole[0:1] + 1)
    gate_gradient, routes, packed_first = tie(gate_gradient, routes, packed_first)
    landed_first = send(packed_first, order_first[1])

    small = jnp.concatenate([routes.T, sequence_ids], axis=0)
    small = jnp.stack(
        [small] + [lax.ppermute(small, "expert", flip(group, d)) for d in range(1, group)]
    )
    group_routes = small[:, :top].transpose(0, 2, 1).reshape(-1)
    group_sequences = small[:, top]
    gradient = gate_gradient.reshape(tokens * top, -1)
    gradient_width = gradient.shape[1] // halves

    def gradient_part(d, start, size):
        return lax.dynamic_slice(
            gradient, (start, (half ^ d) * gradient_width), (size, gradient_width)
        )

    others = range(1, halves)
    quarter = tokens * top // 4
    early, middle, late = [
        [gradient_part(d, start, size) for d in others]
        for start, size in ((0, quarter), (quarter, quarter), (2 * quarter, 2 * quarter))
    ]
    early = [from_half(part, d) for d, part in zip(others, early)]

    for stage, bit in list(enumerate(order_first))[2:]:
        keep_first, send_first = joined(keep_first, landed_first, whole[0:1] + stage - 1)
        if stage + 1 == count:
            send_first, *input_parts = tie(send_first, *input_parts)
        landed_first = send(pack(send_first, whole[0:1] + stage), bit)
    shard_first = own_shard(keep_first + unpack(landed_first, whole[0:1] + count - 1))
    shard_first, *early = tie(shard_first, *early)
    shard_first, *middle = tie(exchange(shard_first), *middle)
    middle = [from_half(part, d) for d, part in zip(others, middle)]

    keep_second, send_second = joined(keep_second, landed_second, there_second)
    for stage, bit in list(enumerate(order_second))[1:]:
        if stage + 1 == count:
            send_second, shard_first = tie(send_second, shard_first)
        landed_second = send(pack(send_second, whole[1:2] + stage), bit)
        if stage + 1 < count:
            keep_second, send_second = joined(keep_second, landed_second, whole[1:2] + stage)
    shard_second = own_shard(keep_second + unpack(landed_second, whole[1:2] + count - 1))
    shard_second, *middle = tie(shard_second, *middle)
    shard_second, *late = tie(exchange(shard_second), *late)
    late = [from_half(part, d) for d, part in zip(others, late)]

    fold_input = lax.all_gather(shard_first, "dp", axis=0, tiled=True)
    gather_orders = [order_second, order_second[1:] + order_second[:1]]
    held_output = []
    rows = shard_second.shape[0] // len(gather_orders)
    for n, order in enumerate(gather_orders):
        held = shard_second[n * rows : (n + 1) * rows][None]
        for bit in order[:0:-1]:
            held = jnp.concatenate([held, send(held, bit)])
        held_output += [held, send(held, order[0])]

    input_pieces = []
    for part in input_parts:
        input_pieces += [part, from_core(part)]
    own_gradient = gradient_part(0, 0, tokens * top)
    gradient_pieces = [own_gradient, from_core(own_gradient)]
    for pieces in zip(early, middle, late):
        gradient_pieces += pieces
        gradient_pieces += [from_core(piece) for piece in pieces]

    experts = (half ^ jnp.arange(halves, dtype=jnp.int32)) * CORES + core
    mask = (group_routes[None, :, None] == experts[:, None, None]).astype(jnp.float32)
    mask = jnp.broadcast_to(mask, (halves, group_routes.shape[0], columns))
    chosen, sent = input_chosen(input_pieces, fold_input, mask, top)
    landed = [lax.ppermute(sent, "expert", flip(group, d * CORES)) for d in others]

    member_of = jnp.arange(group, dtype=jnp.int32)[:, None] * SEG_DEV
    row_of = jnp.repeat((group_sequences + member_of).reshape(-1), top)
    membership = (
        jnp.arange(group * SEG_DEV, dtype=jnp.int32)[:, None] == row_of[None, :]
    ).astype(jnp.float32)
    column_query = jnp.arange(columns, dtype=jnp.int32) // RANK
    query_sum = (
        column_query[:, None] == jnp.arange(queries, dtype=jnp.int32)[None, :]
    ).astype(jnp.float32)
    partial = partial_scores(
        gradient_pieces,
        held_output,
        gather_orders,
        position,
        mask,
        membership,
        query_sum,
        chosen,
        landed,
    )
    partial = partial.reshape(group, SEG_DEV, queries)
    scores = partial[0]
    for d in range(1, group):
        scores = scores + lax.ppermute(partial[d], "expert", flip(group, d))
    return scores


def solution(mesh):
    return jax.shard_map(
        per_device,
        mesh=mesh,
        in_specs=(
            P(("dp", "expert"), None),
            P(("dp", "expert"), None, None),
            P(("dp", "expert"), None),
            P(("dp", "expert"), None),
            P("expert", None, "dp"),
            P("expert", None, "dp"),
            P("expert", "dp", None),
            P("expert", "dp", None),
        ),
        out_specs=P(("dp", "expert"), None),
        check_vma=False,
    )
```

time: 248 us -> 197 us (0.79)
  local copies, waits for them, and re-layouts: 70 us -> 18.8 us
  blocking collectives: 45.9 us -> 0 us
  Pallas kernels: 14.3 us -> 36.3 us
  starting transfers between devices: 19.4 us -> 35.2 us
  waiting for transfers between devices: 59.8 us -> 72.6 us
  matrix products: 11.9 us -> 0 us
  other arithmetic: 11.6 us -> 19.5 us
    all_gather x1 -> x0, blocking collectives: 45.9 us -> none  [per_device(): small = lax.all_gather(small, 'expert', axis=0)]
    unnamed x31 -> x48, local copies, waits for them, and re-layouts: 40.5 us -> 2.79 us
    pallas_call x4, Pallas kernels: 14.3 us -> 36.3 us  [the longest x2 19.3 us: fold_partial(): pl.pallas_call(functools.partial(fold_kernel, steps, width), grid_spec=pl...]
    ppermute x18 -> x32, starting transfers between devices: 17.4 us -> 33.3 us  [the longest x16 19.9 us: send(): return lax.ppermute(packed, 'dp', flip(blocks, 1 << bit))]
    slice x11 -> x3, local copies, waits for them, and re-layouts: 16.5 us -> 0.82 us  [the longest x1 0.75 us: per_device(): scores = scores + lax.ppermute(partial[d], 'expert', flip(group, d))]
    ppermute x18 -> x32, waiting for transfers between devices: 56.8 us -> 70.8 us  [the longest x16 43.7 us: send(): return lax.ppermute(packed, 'dp', flip(blocks, 1 << bit))]
    dot_general x4 -> x0, matrix products: 11.9 us -> none  [the longest x2 8.43 us: per_device(): jnp.dot(group_gradient[k], fold_output, preferred_element_type=jnp.float32)]
    reshape x1, local copies, waits for them, and re-layouts: 0.09 us -> 7.18 us  [per_device(): gradient = gate_gradient.reshape(tokens * top, -1)]
  transfers between devices with their start and end apart: 23 -> 36, of which waited for: 10 -> 16; matrix products, arithmetic and copies ran while one was open for 26% -> 16% of each run, Pallas kernels for 5% -> 13%
where the time goes in v2:
time: 197 us; the launch traced here: 196 us
  waiting for transfers between devices  72.6 us (37%)
  Pallas kernels  36.3 us (18%)
  starting transfers between devices  35.2 us (18%)
  other arithmetic  19.5 us (10%)
  local copies, waits for them, and re-layouts  18.8 us (10%)
  between operations  13.8 us (7%)
    ppermute x16, waiting for transfers between devices, send(): return lax.ppermute(packed, 'dp', flip(blocks, 1 << bit))  43.7 us
    ppermute x3, waiting for transfers between devices, per_device(): lax.ppermute(small, 'expert', flip(group, d))  22.3 us
    ppermute x16, starting transfers between devices, send(): return lax.ppermute(packed, 'dp', flip(blocks, 1 << bit))  19.9 us
    pallas_call x2, Pallas kernels, fold_partial(): pl.pallas_call(functools.partial(fold_kernel, steps, width), grid_spec=pl...  19.3 us
    pallas_call x1, Pallas kernels, partial_scores(): pl.pallas_call(functools.partial(score_kernel, counts, orders, parts), in...  11.5 us
    reshape x1, local copies, waits for them, and re-layouts, per_device(): gradient = gate_gradient.reshape(tokens * top, -1)  7.18 us
    ppermute x4, starting transfers between devices, from_half(): lax.ppermute(part, 'expert', flip(group, d * CORES))  5.64 us
    pallas_call x1, Pallas kernels, input_chosen(): pl.pallas_call(functools.partial(input_kernel, top), in_specs=[pl.BlockSp...  5.5 us
  transfers between devices with their start and end apart: 36, of which 16 were waited for; matrix products, arithmetic and copies ran while one was open for 16% of the time, Pallas kernels for 13%

profile of v2, /device:TPU:0, one launch (start us, length us, event | category | flops | bytes accessed | tf_op | source)
XLA Modules:
  0.0 196.2 jit_solution(16322379223358581025)
XLA Ops:
  6.5 1.0 abs_reduce_fusion
  8.6 3.1 %collective-permute-start = (f32[2,128]{1,0:T(2,128)S(1)}, f32[2,128]{1,0:T(2,128)S(1)}, u32[]{:S(2)}, u32[]{:S(2)}) collective-permute-start(f32[2,128]{1,0:T(2,128)S(1)} %pad_maximum_fusion.6), channel_id=1, source_target_pairs={{0,8},{4,12},{8,0},{12,4},{16,24},{20,28},{24,16},{28,20},{1,9},{5... | collective-permute-start | bytes 3080 | tf_op jit(solution)/shard_map/ppermute | solution.py:295
  11.7 1.5 collective-permute-start.8
  13.8 8.2 %shard_map.82 = (f32[3072,128]{1,0:T(8,128)}, f32[3072,128]{1,0:T(8,128)}) custom-call(s32[2]{0:T(128)} %pad_add_fusion.3.refs_0_.position_ref, bf16[6144,768]{1,0:T(8,128)(2,1)} %bitcast.61, bf16[6144,768]{1,0:T(8,128)(2,1)} %bitcast.62, bf16[6144,768]{1,0:T(8,128)(2,1)} %bitcast.63, bf16[6144,768]{1,0:T(8,128)(2,1)} %bitcast.64, ...), custom_call_target="tpu_custom_call" | custom-call | flops 1207959552 | bytes 12582912 | tf_op jit(solution)/shard_map/pallas_call | solution.py:76
  23.2 1.5 convert_element_type.58
  24.7 2.7 %collective-permute-start.1 = (f32[2,128]{1,0:T(2,128)S(1)}, f32[2,128]{1,0:T(2,128)S(1)}, u32[]{:S(2)}, u32[]{:S(2)}) collective-permute-start(f32[2,128]{1,0:T(2,128)S(1)} %fusion.9), channel_id=1, source_target_pairs={{0,16},{4,20},{8,24},{12,28},{16,0},{20,4},{24,8},{28,12},{1,17},{... | collective-permute-start | bytes 3080 | tf_op jit(solution)/shard_map/ppermute | solution.py:295
  28.3 11.1 %shard_map.83 = (f32[4096,128]{1,0:T(8,128)}, f32[4096,128]{1,0:T(8,128)}) custom-call(s32[2]{0:T(128)} %pad_add_fusion.3.refs_0_.position_ref, bf16[8192,1024]{1,0:T(8,128)(2,1)} %bitcast.57, bf16[8192,1024]{1,0:T(8,128)(2,1)} %bitcast.58, bf16[8192,1024]{1,0:T(8,128)(2,1)} %bitcast.59, bf16[8192,1024]{1,0:T(8,128)(2,1)} %bitcast.60, ...), custom_call_target="tpu_custom_call" | custom-call | flops 2147483648 | bytes 20971520 | tf_op jit(solution)/shard_map/pallas_call | solution.py:76
  39.5 1.8 convert_element_type.59
  41.9 1.3 constant_dynamic-slice_fusion.2
  43.2 1.5 collective-permute-start.7
  44.7 1.5 collective-permute-start.11
  47.0 1.2 copy-done.2
  49.4 7.2 %reshape.157 = bf16[256,8192]{1,0:T(8,128)(2,1)} reshape(bf16[128,2,8192]{2,1,0:T(2,128)(2,1)} %param.9) | data formatting | bytes 8388608 | tf_op jit(solution)/shard_map/reshape | solution.py:363
  56.6 2.2 %constant_dynamic-slice_fusion.5 = (bf16[64,4096]{1,0:T(8,128)(2,1)}, bf16[64,4096]{1,0:T(8,128)(2,1)S(1)}) fusion(bf16[256,8192]{1,0:T(8,128)(2,1)} %reshape.157, s32[]{:T(128)S(6)} %select_n.39), kind=kLoop, calls=%fused_computation.56 | loop fusion | bytes 2097156 | tf_op jit(solution)/shard_map/dynamic_slice | solution.py:367
  59.3 7.4 %collective-permute-done.7 = f16[4096,128]{1,0:T(8,128)(2,1)S(1)} collective-permute-done((f16[4096,128]{1,0:T(8,128)(2,1)S(1)}, f16[4096,128]{1,0:T(8,128)(2,1)S(1)}, u32[]{:S(2)}, u32[]{:S(2)}) %collective-permute-start.7) | collective-permute-done | bytes 1048608 | tf_op jit(solution)/shard_map/ppermute | solution.py:295
  68.4 1.5 collective-permute-start.12
  70.1 1.6 collective-permute-start.9
  71.7 2.4 %collective-permute-done.12 = f16[768,128]{1,0:T(8,128)(2,1)S(1)} collective-permute-done((f16[768,128]{1,0:T(8,128)(2,1)S(1)}, f16[768,128]{1,0:T(8,128)(2,1)S(1)}, u32[]{:S(2)}, u32[]{:S(2)}) %collective-permute-start.12) | collective-permute-done | bytes 196640 | tf_op jit(solution)/shard_map/ppermute | solution.py:295
  74.3 1.6 collective-permute-start.14
  76.6 2.4 %collective-permute-done.14 = bf16[384,128]{1,0:T(8,128)(2,1)S(1)} collective-permute-done((bf16[384,128]{1,0:T(8,128)(2,1)S(1)}, bf16[384,128]{1,0:T(8,128)(2,1)S(1)}, u32[]{:S(2)}, u32[]{:S(2)}) %collective-permute-start.14) | collective-permute-done | bytes 98336 | tf_op jit(solution)/shard_map/ppermute | solution.py:303
  79.7 2.0 %collective-permute-start.19 = (bf16[64,4096]{1,0:T(8,128)(2,1)}, bf16[64,4096]{1,0:T(8,128)(2,1)}, u32[]{:S(2)}, u32[]{:S(2)}) collective-permute-start(bf16[64,4096]{1,0:T(8,128)(2,1)} %get-tuple-element.67), channel_id=1, source_target_pairs={{0,2},{1,3},{2,0},{3,1},{4,6},{5,7},{6,4},{7,5},{8,10},{9,11},{10,... | collective-permute-start | bytes 1572872 | tf_op jit(solution)/shard_map/ppermute | solution.py:308
  82.5 1.3 slice_add_fusion
  85.3 10.3 %collective-permute-done.18 = f16[1024,128]{1,0:T(8,128)(2,1)S(1)} collective-permute-done((f16[1024,128]{1,0:T(8,128)(2,1)}, f16[1024,128]{1,0:T(8,128)(2,1)S(1)}, u32[]{:S(2)}, u32[]{:S(2)}) %collective-permute-start.18) | collective-permute-done | bytes 262176 | tf_op jit(solution)/shard_map/ppermute | solution.py:295
  95.7 1.6 collective-permute-start.20
  97.3 2.3 %constant_dynamic-slice_fusion.4 = bf16[128,4096]{1,0:T(8,128)(2,1)} fusion(bf16[256,8192]{1,0:T(8,128)(2,1)} %reshape.157, s32[]{:T(128)S(6)} %select_n.39), kind=kLoop, calls=%fused_computation.53 | loop fusion | bytes 2097156 | tf_op jit(solution)/shard_map/dynamic_slice | solution.py:367
  99.7 1.1 collective-permute-done.20
  100.8 1.6 collective-permute-start.21
  103.2 20.8 %collective-permute-done.6 = s32[3,128]{1,0:T(4,128)S(1)} collective-permute-done((s32[3,128]{1,0:T(4,128)S(1)}, s32[3,128]{1,0:T(4,128)S(1)}, u32[]{:S(2)}, u32[]{:S(2)}) %collective-permute-start.6) | collective-permute-done | bytes 1568 | tf_op jit(solution)/shard_map/ppermute | solution.py:359
  124.0 1.3 collective-permute-start.5
  126.1 1.5 collective-permute-done.5
  127.6 1.6 collective-permute-start.28
  129.4 4.5 %collective-permute-done.28 = bf16[1,256,256]{2,1,0:T(8,128)(2,1)S(1)} collective-permute-done((bf16[1,256,256]{2,1,0:T(8,128)(2,1)S(1)}, bf16[1,256,256]{2,1,0:T(8,128)(2,1)S(1)}, u32[]{:S(2)}, u32[]{:S(2)}) %collective-permute-start.28) | collective-permute-done | bytes 131104 | tf_op jit(solution)/shard_map/ppermute | solution.py:295
  135.1 2.1 %collective-permute-done.26 = bf16[2,256,256]{2,1,0:T(8,128)(2,1)S(1)} collective-permute-done((bf16[2,256,256]{2,1,0:T(8,128)(2,1)S(1)}, bf16[2,256,256]{2,1,0:T(8,128)(2,1)S(1)}, u32[]{:S(2)}, u32[]{:S(2)}) %collective-permute-start.26) | collective-permute-done | bytes 262176 | tf_op jit(solution)/shard_map/ppermute | solution.py:295
  137.2 2.2 %collective-permute-start.29 = (bf16[2,256,256]{2,1,0:T(8,128)(2,1)}, bf16[2,256,256]{2,1,0:T(8,128)(2,1)}, u32[]{:S(2)}, u32[]{:S(2)}) collective-permute-start(bf16[2,256,256]{2,1,0:T(8,128)(2,1)} %pad_maximum_fusion.4), channel_id=1, source_target_pairs={{0,16},{4,20},{8,24},{12,28},{16,0},{20,4},{24,8},{28,12},{1,17},{... | collective-permute-start | bytes 786440 | tf_op jit(solution)/shard_map/ppermute | solution.py:295
  139.8 11.4 %collective-permute-done.29 = bf16[2,256,256]{2,1,0:T(8,128)(2,1)} collective-permute-done((bf16[2,256,256]{2,1,0:T(8,128)(2,1)}, bf16[2,256,256]{2,1,0:T(8,128)(2,1)}, u32[]{:S(2)}, u32[]{:S(2)}) %collective-permute-start.29) | collective-permute-done | bytes 262176 | tf_op jit(solution)/shard_map/ppermute | solution.py:295
  151.3 1.1 pad_maximum_fusion.refs_8_
  152.4 2.0 %pad_maximum_fusion.1.refs_10_ = bf16[4,256,256]{2,1,0:T(8,128)(2,1)} fusion(bf16[2,256,256]{2,1,0:T(8,128)(2,1)} %collective-permute-done.29, bf16[1,256,256]{2,1,0:T(8,128)(2,1)} %copy-done.13, bf16[1,256,256]{2,1,0:T(8,128)(2,1)S(1)} %get-tuple-element.77), kind=kLoop, calls=%fused_computation.11 | loop fusion | flops 524288 | bytes 1048576 | tf_op jit(solution)/shard_map/concatenate | solution.py:408
  154.4 2.1 %collective-permute-start.27 = (bf16[4,256,256]{2,1,0:T(8,128)(2,1)S(1)}, bf16[4,256,256]{2,1,0:T(8,128)(2,1)S(1)}, u32[]{:S(2)}, u32[]{:S(2)}) collective-permute-start(bf16[4,256,256]{2,1,0:T(8,128)(2,1)S(1)} %pad_maximum_fusion.refs_8_), channel_id=1, source_target_pairs={{0,4},{4,0},{8,12},{12,8},{16,20},{20,16},{24,28},{28,24},{1,5},{5... | collective-permute-start | bytes 1572872 | tf_op jit(solution)/shard_map/ppermute | solution.py:295
  156.5 1.4 broadcast_in_dim.8.mask_ref
  157.9 5.5 %shard_map.84 = (f32[1024,128]{1,0:T(8,128)}, bf16[1024,128]{1,0:T(8,128)(2,1)}) custom-call(bf16[3072,256]{1,0:T(8,128)(2,1)} %all-gather.2.cloned.1.call-done.fold_ref, f32[2,1024,128]{2,1,0:T(8,128)} %broadcast_in_dim.8.mask_ref, bf16[128,3072]{1,0:T(8,128)(2,1)} %get-tuple-element.62.refs_0_, bf16[128,3072]{1,0:T(8,128)(2,1)} %collective-permute-done.15.refs_1_, ...), custom_call_target="tpu_custom_call" | custom-call | flops 805306368 | bytes 4718592 | tf_op jit(solution)/shard_map/pallas_call | solution.py:154
  163.4 1.3 collective-permute-start.31
  165.7 3.3 %collective-permute-done.27.refs_9_ = bf16[4,256,256]{2,1,0:T(8,128)(2,1)S(1)} collective-permute-done((bf16[4,256,256]{2,1,0:T(8,128)(2,1)S(1)}, bf16[4,256,256]{2,1,0:T(8,128)(2,1)S(1)}, u32[]{:S(2)}, u32[]{:S(2)}) %collective-permute-start.27) | collective-permute-done | bytes 524320 | tf_op jit(solution)/shard_map/ppermute | solution.py:295
  169.1 1.8 collective-permute-done.30.refs_11_
  170.9 1.3 collective-permute-done.31.refs_12_
  172.2 11.5 %shard_map.85 = f32[16,4]{1,0:T(8,128)} custom-call(s32[2]{0:T(128)} %pad_add_fusion.3.refs_0_.position_ref, f32[2,1024,128]{2,1,0:T(8,128)} %broadcast_in_dim.8.mask_ref, f32[16,1024]{1,0:T(8,128)} %fusion.4.member_ref, f32[128,4]{1,0:T(8,128)} %fusion.5.query_ref, f32[1024,128]{1,0:T(8,128)} %get-tuple-element.64.chosen_ref, bf16[256,4096]{1,0:T(8,128)(2,1)} %copy-done.1, ...), custom_call_target="tpu_custom_call" | custom-call | flops 2147483648 | bytes 10485760 | tf_op jit(solution)/shard_map/pallas_call | solution.py:248
  184.5 1.0 collective-permute-start.33
  186.4 1.1 collective-permute-done.34
  188.1 1.3 fusion.7
  (134 shorter events, 19.3 us)
Async XLA Ops:
  6.5 150.0 %all-gather.2.cloned.1.call-start = ((), (), s32[]{:S(2)}) async-start(), calls=%async_computation | async-start | bytes 1769472 | tf_op jit(solution)/shard_map/all_gather | solution.py:401
  8.5 14.0 %copy-start.15 = (f32[1,128]{1,0:T(1,128)}, f32[1,128]{1,0:T(1,128)S(1)}, u32[]{:S(2)}) copy-start(f32[1,128]{1,0:T(1,128)S(1)} %get-tuple-element.96.refs_6_) | copy-start | bytes 1540
  8.6 13.9 %collective-permute-start = (f32[2,128]{1,0:T(2,128)S(1)}, f32[2,128]{1,0:T(2,128)S(1)}, u32[]{:S(2)}, u32[]{:S(2)}) collective-permute-start(f32[2,128]{1,0:T(2,128)S(1)} %pad_maximum_fusion.6), channel_id=1, source_target_pairs={{0,8},{4,12},{8,0},{12,4},{16,24},{20,28},{24,16},{28,20},{1,9},{5... | collective-permute-start | bytes 3080 | tf_op jit(solution)/shard_map/ppermute | solution.py:295
  11.7 16.2 %collective-permute-start.8 = (f32[2,128]{1,0:T(2,128)S(1)}, f32[2,128]{1,0:T(2,128)S(1)}, u32[]{:S(2)}, u32[]{:S(2)}) collective-permute-start(f32[2,128]{1,0:T(2,128)S(1)} %pad_maximum_fusion.6), channel_id=1, source_target_pairs={{0,4},{4,0},{8,12},{12,8},{16,20},{20,16},{24,28},{28,24},{1,5},{5... | collective-permute-start | bytes 3080 | tf_op jit(solution)/shard_map/ppermute | solution.py:295
  24.7 14.8 %collective-permute-start.1 = (f32[2,128]{1,0:T(2,128)S(1)}, f32[2,128]{1,0:T(2,128)S(1)}, u32[]{:S(2)}, u32[]{:S(2)}) collective-permute-start(f32[2,128]{1,0:T(2,128)S(1)} %fusion.9), channel_id=1, source_target_pairs={{0,16},{4,20},{8,24},{12,28},{16,0},{20,4},{24,8},{28,12},{1,17},{... | collective-permute-start | bytes 3080 | tf_op jit(solution)/shard_map/ppermute | solution.py:295
  27.4 19.5 %collective-permute-start.2 = (f16[3072,128]{1,0:T(8,128)(2,1)S(1)}, f16[3072,128]{1,0:T(8,128)(2,1)S(1)}, u32[]{:S(2)}, u32[]{:S(2)}) collective-permute-start(f16[3072,128]{1,0:T(8,128)(2,1)S(1)} %convert_element_type.58), channel_id=1, source_target_pairs={{0,8},{4,12},{8,0},{12,4},{16,24},{20,28},{24,16},{28,20},{1,9},{5... | collective-permute-start | bytes 2359304 | tf_op jit(solution)/shard_map/ppermute | solution.py:295
  41.3 4.9 %collective-permute-start.3 = (f32[2,128]{1,0:T(2,128)S(1)}, f32[2,128]{1,0:T(2,128)S(1)}, u32[]{:S(2)}, u32[]{:S(2)}) collective-permute-start(f32[2,128]{1,0:T(2,128)S(1)} %max.36), channel_id=1, source_target_pairs={{0,4},{4,0},{8,12},{12,8},{16,20},{20,16},{24,28},{28,24},{1,5},{5... | collective-permute-start | bytes 3080 | tf_op jit(solution)/shard_map/ppermute | solution.py:295
  43.2 23.5 %collective-permute-start.7 = (f16[4096,128]{1,0:T(8,128)(2,1)S(1)}, f16[4096,128]{1,0:T(8,128)(2,1)S(1)}, u32[]{:S(2)}, u32[]{:S(2)}) collective-permute-start(f16[4096,128]{1,0:T(8,128)(2,1)S(1)} %convert_element_type.59), channel_id=1, source_target_pairs={{0,4},{4,0},{8,12},{12,8},{16,20},{20,16},{24,28},{28,24},{1,5},{5... | collective-permute-start | bytes 3145736 | tf_op jit(solution)/shard_map/ppermute | solution.py:295
  44.7 23.6 %collective-permute-start.11 = (bf16[128,3072]{1,0:T(8,128)(2,1)}, bf16[128,3072]{1,0:T(8,128)(2,1)}, u32[]{:S(2)}, u32[]{:S(2)}) collective-permute-start(bf16[128,3072]{1,0:T(8,128)(2,1)} %get-tuple-element.56), channel_id=1, source_target_pairs={{0,2},{1,3},{2,0},{3,1},{4,6},{5,7},{6,4},{7,5},{8,10},{9,11},{10,... | collective-permute-start | bytes 2359304 | tf_op jit(solution)/shard_map/ppermute | solution.py:308
  49.1 18.4 %collective-permute-start.10 = (f16[1536,128]{1,0:T(8,128)(2,1)}, f16[1536,128]{1,0:T(8,128)(2,1)S(1)}, u32[]{:S(2)}, u32[]{:S(2)}) collective-permute-start(f16[1536,128]{1,0:T(8,128)(2,1)} %fusion.1), channel_id=1, source_target_pairs={{0,16},{4,20},{8,24},{12,28},{16,0},{20,4},{24,8},{28,12},{1,17},{... | collective-permute-start | bytes 1179656 | tf_op jit(solution)/shard_map/ppermute | solution.py:295
  56.6 10.2 %copy-start.6 = (f32[4096,128]{1,0:T(8,128)S(1)}, f32[4096,128]{1,0:T(8,128)}, u32[]{:S(2)}) copy-start(f32[4096,128]{1,0:T(8,128)} %get-tuple-element.52) | copy-start | bytes 6291460
  56.6 10.2 %copy-start.23 = (f32[128]{0:T(128)S(1)}, f32[128]{0:T(128)}, u32[]{:S(2)}) copy-start(f32[128]{0:T(128)} %exponential_bitcast_fusion.7) | copy-start | bytes 1540
  58.8 15.4 %collective-permute-start.13 = (bf16[64,4096]{1,0:T(8,128)(2,1)S(1)}, bf16[64,4096]{1,0:T(8,128)(2,1)}, u32[]{:S(2)}, u32[]{:S(2)}) collective-permute-start(bf16[64,4096]{1,0:T(8,128)(2,1)S(1)} %get-tuple-element.74), channel_id=1, source_target_pairs={{0,2},{1,3},{2,0},{3,1},{4,6},{5,7},{6,4},{7,5},{8,10},{9,11},{10,... | collective-permute-start | bytes 1572872 | tf_op jit(solution)/shard_map/ppermute | solution.py:308
  68.3 7.5 %copy-start.21 = (s32[128]{0:T(128)S(1)}, s32[128]{0:T(128)}, u32[]{:S(2)}) copy-start(s32[128]{0:T(128)} %and_select_fusion) | copy-start | bytes 1540
  68.4 14.1 %copy-start.19 = (f32[128]{0:T(128)S(1)}, f32[128]{0:T(128)}, u32[]{:S(2)}) copy-start(f32[128]{0:T(128)} %get-tuple-element.92) | copy-start | bytes 1540
  68.4 5.7 %collective-permute-start.12 = (f16[768,128]{1,0:T(8,128)(2,1)S(1)}, f16[768,128]{1,0:T(8,128)(2,1)S(1)}, u32[]{:S(2)}, u32[]{:S(2)}) collective-permute-start(f16[768,128]{1,0:T(8,128)(2,1)S(1)} %multiply_convert_fusion.1), channel_id=1, source_target_pairs={{0,4},{4,0},{8,12},{12,8},{16,20},{20,16},{24,28},{28,24},{1,5},{5... | collective-permute-start | bytes 589832 | tf_op jit(solution)/shard_map/ppermute | solution.py:295
  70.1 11.6 %collective-permute-start.9 = (f16[2048,128]{1,0:T(8,128)(2,1)S(1)}, f16[2048,128]{1,0:T(8,128)(2,1)S(1)}, u32[]{:S(2)}, u32[]{:S(2)}) collective-permute-start(f16[2048,128]{1,0:T(8,128)(2,1)S(1)} %fusion), channel_id=1, source_target_pairs={{0,8},{4,12},{8,0},{12,4},{16,24},{20,28},{24,16},{28,20},{1,9},{5... | collective-permute-start | bytes 1572872 | tf_op jit(solution)/shard_map/ppermute | solution.py:295
  74.3 4.7 %collective-permute-start.14 = (bf16[384,128]{1,0:T(8,128)(2,1)S(1)}, bf16[384,128]{1,0:T(8,128)(2,1)S(1)}, u32[]{:S(2)}, u32[]{:S(2)}) collective-permute-start(bf16[384,128]{1,0:T(8,128)(2,1)S(1)} %get-tuple-element.82), channel_id=1, source_target_pairs={{0,2},{1,3},{2,0},{3,1},{4,6},{5,7},{6,4},{7,5},{8,10},{9,11},{10,... | collective-permute-start | bytes 294920 | tf_op jit(solution)/shard_map/ppermute | solution.py:303
  79.7 16.0 %collective-permute-start.19 = (bf16[64,4096]{1,0:T(8,128)(2,1)}, bf16[64,4096]{1,0:T(8,128)(2,1)}, u32[]{:S(2)}, u32[]{:S(2)}) collective-permute-start(bf16[64,4096]{1,0:T(8,128)(2,1)} %get-tuple-element.67), channel_id=1, source_target_pairs={{0,2},{1,3},{2,0},{3,1},{4,6},{5,7},{6,4},{7,5},{8,10},{9,11},{10,... | collective-permute-start | bytes 1572872 | tf_op jit(solution)/shard_map/ppermute | solution.py:308
  84.6 11.0 %collective-permute-start.18 = (f16[1024,128]{1,0:T(8,128)(2,1)}, f16[1024,128]{1,0:T(8,128)(2,1)S(1)}, u32[]{:S(2)}, u32[]{:S(2)}) collective-permute-start(f16[1024,128]{1,0:T(8,128)(2,1)} %multiply_convert_fusion), channel_id=1, source_target_pairs={{0,16},{4,20},{8,24},{12,28},{16,0},{20,4},{24,8},{28,12},{1,17},{... | collective-permute-start | bytes 786440 | tf_op jit(solution)/shard_map/ppermute | solution.py:295
  85.3 15.5 %copy-start.1 = (bf16[256,4096]{1,0:T(8,128)(2,1)}, bf16[256,4096]{1,0:T(8,128)(2,1)S(1)}, u32[]{:S(2)}) copy-start(bf16[256,4096]{1,0:T(8,128)(2,1)S(1)} %constant_dynamic-slice_fusion.refs_0_) | copy-start | bytes 6291460
  95.7 6.9 %copy-start.20 = (s32[128,2]{0,1:T(2,128)S(1)}, s32[128,2]{0,1:T(2,128)}, u32[]{:S(2)}) copy-start(s32[128,2]{0,1:T(2,128)} %param.10) | copy-start | bytes 3076
  95.7 6.9 %copy-start.22 = (s32[1,128]{1,0:T(1,128)S(1)}, s32[1,128]{1,0:T(1,128)}, u32[]{:S(2)}) copy-start(s32[1,128]{1,0:T(1,128)} %param.11) | copy-start | bytes 1540
  95.7 38.1 %copy-start.4 = (bf16[128,3072]{1,0:T(8,128)(2,1)S(1)}, bf16[128,3072]{1,0:T(8,128)(2,1)}, u32[]{:S(2)}) copy-start(bf16[128,3072]{1,0:T(8,128)(2,1)} %get-tuple-element.62.refs_0_) | copy-start | bytes 2359300
  95.7 5.0 %collective-permute-start.20 = (bf16[512,128]{1,0:T(8,128)(2,1)S(1)}, bf16[512,128]{1,0:T(8,128)(2,1)S(1)}, u32[]{:S(2)}, u32[]{:S(2)}) collective-permute-start(bf16[512,128]{1,0:T(8,128)(2,1)S(1)} %get-tuple-element.80), channel_id=1, source_target_pairs={{0,2},{1,3},{2,0},{3,1},{4,6},{5,7},{6,4},{7,5},{8,10},{9,11},{10,... | collective-permute-start | bytes 393224 | tf_op jit(solution)/shard_map/ppermute | solution.py:303
  99.7 66.1 %collective-permute-start.17 = (bf16[256,4096]{1,0:T(8,128)(2,1)S(1)}, bf16[256,4096]{1,0:T(8,128)(2,1)}, u32[]{:S(2)}, u32[]{:S(2)}) collective-permute-start(bf16[256,4096]{1,0:T(8,128)(2,1)S(1)} %constant_dynamic-slice_fusion.refs_0_), channel_id=1, source_target_pairs={{0,1},{1,0},{2,3},{3,2},{4,5},{5,4},{6,7},{7,6},{8,9},{9,8},{10,11... | collective-permute-start | bytes 6291464 | tf_op jit(solution)/shard_map/ppermute | solution.py:311
  100.8 38.6 %collective-permute-start.21 = (bf16[128,4096]{1,0:T(8,128)(2,1)}, bf16[128,4096]{1,0:T(8,128)(2,1)}, u32[]{:S(2)}, u32[]{:S(2)}) collective-permute-start(bf16[128,4096]{1,0:T(8,128)(2,1)} %constant_dynamic-slice_fusion.4), channel_id=1, source_target_pairs={{0,2},{1,3},{2,0},{3,1},{4,6},{5,7},{6,4},{7,5},{8,10},{9,11},{10,... | collective-permute-start | bytes 3145736 | tf_op jit(solution)/shard_map/ppermute | solution.py:308
  102.4 48.8 %copy-start.9 = (bf16[1,256,256]{2,1,0:T(8,128)(2,1)}, bf16[1,256,256]{2,1,0:T(8,128)(2,1)S(1)}, u32[]{:S(2)}) copy-start(bf16[1,256,256]{2,1,0:T(8,128)(2,1)S(1)} %get-tuple-element.78) | copy-start | bytes 393220
  102.4 22.8 %collective-permute-start.25 = (bf16[1,256,256]{2,1,0:T(8,128)(2,1)S(1)}, bf16[1,256,256]{2,1,0:T(8,128)(2,1)S(1)}, u32[]{:S(2)}, u32[]{:S(2)}) collective-permute-start(bf16[1,256,256]{2,1,0:T(8,128)(2,1)S(1)} %get-tuple-element.78), channel_id=1, source_target_pairs={{0,16},{4,20},{8,24},{12,28},{16,0},{20,4},{24,8},{28,12},{1,17},{... | collective-permute-start | bytes 393224 | tf_op jit(solution)/shard_map/ppermute | solution.py:295
  102.6 21.4 %collective-permute-start.6 = (s32[3,128]{1,0:T(4,128)S(1)}, s32[3,128]{1,0:T(4,128)S(1)}, u32[]{:S(2)}, u32[]{:S(2)}) collective-permute-start(s32[3,128]{1,0:T(4,128)S(1)} %get-tuple-element.87), channel_id=1, source_target_pairs={{0,3},{1,2},{2,1},{3,0},{4,7},{5,6},{6,5},{7,4},{8,11},{9,10},{10,... | collective-permute-start | bytes 4616 | tf_op jit(solution)/shard_map/ppermute | solution.py:359
  102.6 32.2 %collective-permute-start.22 = (bf16[64,4096]{1,0:T(8,128)(2,1)}, bf16[64,4096]{1,0:T(8,128)(2,1)}, u32[]{:S(2)}, u32[]{:S(2)}) collective-permute-start(bf16[64,4096]{1,0:T(8,128)(2,1)} %collective-permute-done.13.refs_2_), channel_id=1, source_target_pairs={{0,1},{1,0},{2,3},{3,2},{4,5},{5,4},{6,7},{7,6},{8,9},{9,8},{10,11... | collective-permute-start | bytes 1572872 | tf_op jit(solution)/shard_map/ppermute | solution.py:311
  124.0 3.6 %collective-permute-start.5 = (s32[3,128]{1,0:T(4,128)S(1)}, s32[3,128]{1,0:T(4,128)S(1)}, u32[]{:S(2)}, u32[]{:S(2)}) collective-permute-start(s32[3,128]{1,0:T(4,128)S(1)} %get-tuple-element.87), channel_id=1, source_target_pairs={{0,2},{1,3},{2,0},{3,1},{4,6},{5,7},{6,4},{7,5},{8,10},{9,11},{10,... | collective-permute-start | bytes 4616 | tf_op jit(solution)/shard_map/ppermute | solution.py:359
  125.2 14.2 %copy-start.12 = (bf16[1,256,256]{2,1,0:T(8,128)(2,1)}, bf16[1,256,256]{2,1,0:T(8,128)(2,1)S(1)}, u32[]{:S(2)}) copy-start(bf16[1,256,256]{2,1,0:T(8,128)(2,1)S(1)} %collective-permute-done.25) | copy-start | bytes 393220
  125.2 3.9 %collective-permute-start.4 = (s32[3,128]{1,0:T(4,128)S(1)}, s32[3,128]{1,0:T(4,128)S(1)}, u32[]{:S(2)}, u32[]{:S(2)}) collective-permute-start(s32[3,128]{1,0:T(4,128)S(1)} %get-tuple-element.87), channel_id=1, source_target_pairs={{0,1},{1,0},{2,3},{3,2},{4,5},{5,4},{6,7},{7,6},{8,9},{9,8},{10,11... | collective-permute-start | bytes 4616 | tf_op jit(solution)/shard_map/ppermute | solution.py:359
  127.6 6.3 %collective-permute-start.28 = (bf16[1,256,256]{2,1,0:T(8,128)(2,1)S(1)}, bf16[1,256,256]{2,1,0:T(8,128)(2,1)S(1)}, u32[]{:S(2)}, u32[]{:S(2)}) collective-permute-start(bf16[1,256,256]{2,1,0:T(8,128)(2,1)S(1)} %get-tuple-element.77), channel_id=1, source_target_pairs={{0,4},{4,0},{8,12},{12,8},{16,20},{20,16},{24,28},{28,24},{1,5},{5... | collective-permute-start | bytes 393224 | tf_op jit(solution)/shard_map/ppermute | solution.py:295
  129.1 8.1 %collective-permute-start.26 = (bf16[2,256,256]{2,1,0:T(8,128)(2,1)S(1)}, bf16[2,256,256]{2,1,0:T(8,128)(2,1)S(1)}, u32[]{:S(2)}, u32[]{:S(2)}) collective-permute-start(bf16[2,256,256]{2,1,0:T(8,128)(2,1)S(1)} %pad_maximum_fusion.3), channel_id=1, source_target_pairs={{0,8},{4,12},{8,0},{12,4},{16,24},{20,28},{24,16},{28,20},{1,9},{5... | collective-permute-start | bytes 786440 | tf_op jit(solution)/shard_map/ppermute | solution.py:295
  133.8 20.6 %collective-permute-start.15 = (bf16[128,3072]{1,0:T(8,128)(2,1)S(1)}, bf16[128,3072]{1,0:T(8,128)(2,1)}, u32[]{:S(2)}, u32[]{:S(2)}) collective-permute-start(bf16[128,3072]{1,0:T(8,128)(2,1)S(1)} %copy-done.4), channel_id=1, source_target_pairs={{0,1},{1,0},{2,3},{3,2},{4,5},{5,4},{6,7},{7,6},{8,9},{9,8},{10,11... | collective-permute-start | bytes 2359304 | tf_op jit(solution)/shard_map/ppermute | solution.py:311
  134.8 21.7 %collective-permute-start.16 = (bf16[128,3072]{1,0:T(8,128)(2,1)}, bf16[128,3072]{1,0:T(8,128)(2,1)}, u32[]{:S(2)}, u32[]{:S(2)}) collective-permute-start(bf16[128,3072]{1,0:T(8,128)(2,1)} %collective-permute-done.11.refs_2_), channel_id=1, source_target_pairs={{0,1},{1,0},{2,3},{3,2},{4,5},{5,4},{6,7},{7,6},{8,9},{9,8},{10,11... | collective-permute-start | bytes 2359304 | tf_op jit(solution)/shard_map/ppermute | solution.py:311
  137.2 14.0 %collective-permute-start.29 = (bf16[2,256,256]{2,1,0:T(8,128)(2,1)}, bf16[2,256,256]{2,1,0:T(8,128)(2,1)}, u32[]{:S(2)}, u32[]{:S(2)}) collective-permute-start(bf16[2,256,256]{2,1,0:T(8,128)(2,1)} %pad_maximum_fusion.4), channel_id=1, source_target_pairs={{0,16},{4,20},{8,24},{12,28},{16,0},{20,4},{24,8},{28,12},{1,17},{... | collective-permute-start | bytes 786440 | tf_op jit(solution)/shard_map/ppermute | solution.py:295
  139.4 31.4 %collective-permute-start.24 = (bf16[128,4096]{1,0:T(8,128)(2,1)}, bf16[128,4096]{1,0:T(8,128)(2,1)}, u32[]{:S(2)}, u32[]{:S(2)}) collective-permute-start(bf16[128,4096]{1,0:T(8,128)(2,1)} %collective-permute-done.21.refs_4_), channel_id=1, source_target_pairs={{0,1},{1,0},{2,3},{3,2},{4,5},{5,4},{6,7},{7,6},{8,9},{9,8},{10,11... | collective-permute-start | bytes 3145736 | tf_op jit(solution)/shard_map/ppermute | solution.py:311
  151.2 12.2 %collective-permute-start.23 = (bf16[64,4096]{1,0:T(8,128)(2,1)}, bf16[64,4096]{1,0:T(8,128)(2,1)}, u32[]{:S(2)}, u32[]{:S(2)}) collective-permute-start(bf16[64,4096]{1,0:T(8,128)(2,1)} %collective-permute-done.19.refs_3_), channel_id=1, source_target_pairs={{0,1},{1,0},{2,3},{3,2},{4,5},{5,4},{6,7},{7,6},{8,9},{9,8},{10,11... | collective-permute-start | bytes 1572872 | tf_op jit(solution)/shard_map/ppermute | solution.py:311
  152.4 11.0 %copy-start.5 = (bf16[4,256,256]{2,1,0:T(8,128)(2,1)}, bf16[4,256,256]{2,1,0:T(8,128)(2,1)S(1)}, u32[]{:S(2)}) copy-start(bf16[4,256,256]{2,1,0:T(8,128)(2,1)S(1)} %pad_maximum_fusion.refs_8_) | copy-start | bytes 1572868
  154.4 14.6 %collective-permute-start.27 = (bf16[4,256,256]{2,1,0:T(8,128)(2,1)S(1)}, bf16[4,256,256]{2,1,0:T(8,128)(2,1)S(1)}, u32[]{:S(2)}, u32[]{:S(2)}) collective-permute-start(bf16[4,256,256]{2,1,0:T(8,128)(2,1)S(1)} %pad_maximum_fusion.refs_8_), channel_id=1, source_target_pairs={{0,4},{4,0},{8,12},{12,8},{16,20},{20,16},{24,28},{28,24},{1,5},{5... | collective-permute-start | bytes 1572872 | tf_op jit(solution)/shard_map/ppermute | solution.py:295
  156.5 14.4 %collective-permute-start.30 = (bf16[4,256,256]{2,1,0:T(8,128)(2,1)}, bf16[4,256,256]{2,1,0:T(8,128)(2,1)}, u32[]{:S(2)}, u32[]{:S(2)}) collective-permute-start(bf16[4,256,256]{2,1,0:T(8,128)(2,1)} %pad_maximum_fusion.1.refs_10_), channel_id=1, source_target_pairs={{0,8},{4,12},{8,0},{12,4},{16,24},{20,28},{24,16},{28,20},{1,9},{5... | collective-permute-start | bytes 1572872 | tf_op jit(solution)/shard_map/ppermute | solution.py:295
  163.4 8.8 %collective-permute-start.31 = (bf16[1024,128]{1,0:T(8,128)(2,1)}, bf16[1024,128]{1,0:T(8,128)(2,1)}, u32[]{:S(2)}, u32[]{:S(2)}) collective-permute-start(bf16[1024,128]{1,0:T(8,128)(2,1)} %get-tuple-element.72), channel_id=1, source_target_pairs={{0,2},{1,3},{2,0},{3,1},{4,6},{5,7},{6,4},{7,5},{8,10},{9,11},{10,... | collective-permute-start | bytes 786440 | tf_op jit(solution)/shard_map/ppermute | solution.py:424
  184.5 3.0 %collective-permute-start.34 = (f32[4,4]{1,0:T(4,128)S(1)}, f32[4,4]{1,0:T(4,128)S(1)}, u32[]{:S(2)}, u32[]{:S(2)}) collective-permute-start(f32[4,4]{1,0:T(4,128)S(1)} %get-tuple-element.84), channel_id=1, source_target_pairs={{0,3},{1,2},{2,1},{3,0},{4,7},{5,6},{6,5},{7,4},{8,11},{9,10},{10,... | collective-permute-start | bytes 200 | tf_op jit(solution)/shard_map/ppermute | solution.py:449
  184.5 3.6 %collective-permute-start.33 = (f32[4,4]{1,0:T(4,128)S(1)}, f32[4,4]{1,0:T(4,128)S(1)}, u32[]{:S(2)}, u32[]{:S(2)}) collective-permute-start(f32[4,4]{1,0:T(4,128)S(1)} %get-tuple-element.85), channel_id=1, source_target_pairs={{0,2},{1,3},{2,0},{3,1},{4,6},{5,7},{6,4},{7,5},{8,10},{9,11},{10,... | collective-permute-start | bytes 200 | tf_op jit(solution)/shard_map/ppermute | solution.py:449
  185.5 2.6 %collective-permute-start.32 = (f32[4,4]{1,0:T(4,128)S(1)}, f32[4,4]{1,0:T(4,128)S(1)}, u32[]{:S(2)}, u32[]{:S(2)}) collective-permute-start(f32[4,4]{1,0:T(4,128)S(1)} %get-tuple-element.83), channel_id=1, source_target_pairs={{0,1},{1,0},{2,3},{3,2},{4,5},{5,4},{6,7},{7,6},{8,9},{9,8},{10,11... | collective-permute-start | bytes 200 | tf_op jit(solution)/shard_map/ppermute | solution.py:449
  (12 other events, 37.6 us)
Sparse Core Ops, SparseCore 0:
  85.4 46.4 all-gather.1

commit v3 on v1

v3 whole, which is shorter than its diff:
```python
import functools

import jax
import jax.numpy as jnp
import numpy as np
from jax import lax
from jax.experimental import pallas as pl
from jax.experimental.pallas import tpu as pltpu
from jax.sharding import PartitionSpec as P

RANK = 32
SEG_DEV = 4
CORES = 2
TOP_EXPONENT = 15.0
TAIL = 16


def bits_of(count):
    return (count - 1).bit_length()


def slot_order(order):
    width = len(order)
    return [
        sum(((slot >> (width - 1 - i)) & 1) << bit for i, bit in enumerate(order))
        for slot in range(1 << width)
    ]


def column_exponent(query):
    peak = jnp.max(jnp.abs(query).astype(jnp.float32), axis=0, keepdims=True)
    bound = jnp.maximum(peak * (0.25 * query.shape[0]), 1e-28)
    return jnp.floor(jnp.log2(bound)) + 1.0


def fold_kernel(width, steps, scaled, *refs):
    basis_refs, refs = refs[1 : 1 + 2 * width], refs[1 + 2 * width :]
    query_refs, out_refs, sum_refs, done = refs[:2], refs[2:4], refs[4:6], refs[6]
    step = pl.program_id(0)
    for chunk in range(2):
        query_ref, out_ref, sum_ref = query_refs[chunk], out_refs[chunk], sum_refs[chunk]
        chunk_refs = basis_refs[chunk * width : (chunk + 1) * width]
        rows = chunk_refs[0].shape[0]

        def piece(index):
            here = pl.ds(index * (width * rows), width * rows)
            return pltpu.make_async_copy(
                sum_ref.at[here, :], out_ref.at[here, :], done.at[chunk, index]
            )

        here = pl.ds(steps * width * rows, TAIL)
        tail = pltpu.make_async_copy(
            sum_ref.at[here, :], out_ref.at[here, :], done.at[chunk, steps]
        )
        for index in range(steps):

            @pl.when(step == chunk * steps + index)
            def _():
                exponent = column_exponent(query_ref[...])
                for part, basis_ref in enumerate(chunk_refs):
                    terms = jnp.dot(
                        basis_ref[...], query_ref[...], preferred_element_type=jnp.float32
                    )
                    if scaled:
                        terms = terms * jnp.exp2(TOP_EXPONENT - exponent)
                    sum_ref[pl.ds((index * width + part) * rows, rows), :] = terms
                piece(index).start()
                if index == 0:
                    sum_ref[here, :] = jnp.broadcast_to(exponent, (TAIL, sum_ref.shape[1]))
                    tail.start()

        @pl.when(step == 2 * steps - 1)
        def _():
            for index in range(steps):
                piece(index).wait()
            tail.wait()


def fold_parts(bases, queries, position, orders, halves, upper):
    columns = queries[0].shape[1]
    blocks = 1 << len(orders[0])
    count = blocks * halves
    width = min(4, count // 2)
    steps = count // 2 // width

    def block(chunk, part):
        order, basis = orders[chunk], bases[chunk]

        def index(i, position_ref):
            i = jnp.clip(i - chunk * steps, 0, steps - 1)
            slot = (i * width + part) // halves + (blocks // 2 if upper else 0)
            relative = sum(
                ((slot >> (len(order) - 1 - n)) & 1) << bit for n, bit in enumerate(order)
            )
            here = (i * width + part) % halves ^ position_ref[1]
            return here * blocks + (relative ^ position_ref[0]), 0

        return pl.BlockSpec((basis.shape[0] // count, basis.shape[1]), index)

    out_shape = [
        jax.ShapeDtypeStruct((basis.shape[0] // 2 + TAIL, columns), jnp.float32)
        for basis in bases
    ]
    return pl.pallas_call(
        functools.partial(fold_kernel, width, steps, upper),
        grid_spec=pltpu.PrefetchScalarGridSpec(
            num_scalar_prefetch=1,
            grid=(2 * steps,),
            in_specs=[block(chunk, part) for chunk in range(2) for part in range(width)]
            + [pl.BlockSpec(query.shape, lambda i, p: (0, 0)) for query in queries],
            out_specs=[pl.BlockSpec(memory_space=pl.ANY)] * 2,
            scratch_shapes=[pltpu.VMEM(out.shape, out.dtype) for out in out_shape]
            + [pltpu.SemaphoreType.DMA((2, steps + 1))],
        ),
        out_shape=out_shape,
        compiler_params=pltpu.CompilerParams(vmem_limit_bytes=56 * 1024 * 1024),
        cost_estimate=pl.CostEstimate(flops=1, bytes_accessed=1, transcendentals=0),
    )(position, *([bases[0]] * width), *([bases[1]] * width), *queries)


def pack(total, exponent):
    half = (total.shape[0] - TAIL) // 2
    scaled = total[half:] * jnp.exp2(TOP_EXPONENT - exponent)
    row = lax.broadcasted_iota(jnp.int32, scaled.shape, 0)
    return jnp.where(row < half, scaled, exponent).astype(jnp.float16)


def unpack(packed):
    tail = packed.shape[0] - TAIL
    exponent = packed[tail : tail + 1].astype(jnp.float32)
    return packed.astype(jnp.float32) * jnp.exp2(exponent - TOP_EXPONENT), exponent


def flip(size, mask):
    return [(i, i ^ mask) for i in range(size)]


def tie(*values):
    return lax.optimization_barrier(values)


def column_kernel(halves, position_ref, source_ref, extra_ref, *out_refs):
    width = source_ref.shape[1]
    for d in range(halves):

        @pl.when(pl.program_id(0) == d)
        def _():
            out_refs[d][:, pl.ds(0, width)] = source_ref[...]
            out_refs[d][:, pl.ds(width, extra_ref.shape[1])] = extra_ref[...]


def column_parts(source, extra, position, halves):
    rows, width = source.shape[0], source.shape[1] // halves
    out_shape = (rows, width + extra.shape[1])
    return pl.pallas_call(
        functools.partial(column_kernel, halves),
        grid_spec=pltpu.PrefetchScalarGridSpec(
            num_scalar_prefetch=1,
            grid=(halves,),
            in_specs=[
                pl.BlockSpec((rows, width), lambda j, p: (0, p[1] ^ j)),
                pl.BlockSpec(extra.shape, lambda j, p: (0, 0)),
            ],
            out_specs=[pl.BlockSpec(out_shape, lambda j, p: (0, 0))] * halves,
        ),
        out_shape=[jax.ShapeDtypeStruct(out_shape, source.dtype)] * halves,
        compiler_params=pltpu.CompilerParams(vmem_limit_bytes=56 * 1024 * 1024),
        cost_estimate=pl.CostEstimate(flops=1, bytes_accessed=1, transcendentals=0),
    )(position, source, extra)


def flatten_kernel(halves, cut, position_ref, source_ref, *out_refs):
    step = pl.program_id(0)
    rows = source_ref.shape[0] * source_ref.shape[1]
    width = source_ref.shape[2] // halves
    for d in range(halves):
        start = pl.multiple_of((position_ref[1] ^ d) * width, width)
        part = source_ref[:, :, pl.ds(start, width)].reshape(rows, width)
        if d == 0:
            out_refs[0][...] = part
            continue

        @pl.when(step < cut)
        def _():
            out_refs[2 * d - 1][...] = part

        @pl.when(step >= cut)
        def _():
            out_refs[2 * d][...] = part


def flattened_parts(source, position, halves, cut):
    tokens, top, width = source.shape
    width = width // halves
    block = 16
    steps, rows = tokens // block, block * top

    def out(index):
        return pl.BlockSpec((rows, width), index)

    specs = [out(lambda i, p: (i, 0))]
    shapes = [(tokens * top, width)]
    for _ in range(1, halves):
        specs += [
            out(lambda i, p: (jnp.minimum(i, cut - 1), 0)),
            out(lambda i, p: (jnp.maximum(i - cut, 0), 0)),
        ]
        shapes += [(cut * rows, width), ((steps - cut) * rows, width)]
    own, *others = pl.pallas_call(
        functools.partial(flatten_kernel, halves, cut),
        grid_spec=pltpu.PrefetchScalarGridSpec(
            num_scalar_prefetch=1,
            grid=(steps,),
            in_specs=[pl.BlockSpec((block, top, width * halves), lambda i, p: (i, 0, 0))],
            out_specs=specs,
        ),
        out_shape=[jax.ShapeDtypeStruct(shape, source.dtype) for shape in shapes],
        compiler_params=pltpu.CompilerParams(vmem_limit_bytes=56 * 1024 * 1024),
        cost_estimate=pl.CostEstimate(
            flops=1, bytes_accessed=4 * source.size, transcendentals=0
        ),
    )(position, source)
    return own, others[0::2], others[1::2]


def start_all(copies, done):
    started = []
    for i, (source, target) in enumerate(copies):
        started.append(pltpu.make_async_copy(source, target, done.at[i]))
        started[i].start()
    return started


def mask_kernel(top, position_ref, *refs):
    *extra_refs, mask_ref, member_ref, rows_ref = refs
    tokens, lanes = extra_refs[0].shape
    lane = lax.broadcasted_iota(jnp.int32, (tokens, lanes), 1).astype(jnp.float32)
    for i, extra_ref in enumerate(extra_refs):
        extra = extra_ref[...].astype(jnp.float32)

        def column(k):
            return jnp.broadcast_to(extra[:, k : k + 1], (tokens, lanes))

        member = jnp.where(column(top) + float(i * SEG_DEV) == lane, 1.0, 0.0)
        for k in range(top):
            rows = pl.ds(i * tokens * top + k, tokens, stride=top)
            rows_ref[rows, :] = member
            for d in range(mask_ref.shape[0]):
                expert = ((position_ref[1] ^ d) * CORES + position_ref[2]).astype(jnp.float32)
                mask_ref[d, rows, :] = jnp.where(column(k) == expert, 1.0, 0.0)
    member_ref[...] = rows_ref[...].astype(member_ref.dtype)


def masks(position, pieces, top, halves, lanes):
    tokens = pieces[0].shape[0]
    rows = len(pieces) * tokens * top
    last = pieces[0].shape[1] // lanes - 1
    return pl.pallas_call(
        functools.partial(mask_kernel, top),
        grid=(1,),
        in_specs=[pl.BlockSpec(memory_space=pltpu.SMEM)]
        + [pl.BlockSpec((tokens, lanes), lambda i: (0, last))] * len(pieces),
        out_specs=[
            pl.BlockSpec((halves, rows, lanes), lambda i: (0, 0, 0)),
            pl.BlockSpec((rows, lanes), lambda i: (0, 0)),
        ],
        out_shape=[
            jax.ShapeDtypeStruct((halves, rows, lanes), jnp.float32),
            jax.ShapeDtypeStruct((rows, lanes), jnp.bfloat16),
        ],
        scratch_shapes=[pltpu.VMEM((rows, lanes), jnp.float32)],
        cost_estimate=pl.CostEstimate(flops=1, bytes_accessed=1, transcendentals=0),
    )(position, *pieces)


def input_kernel(top, layouts, count, position_ref, mask_ref, *refs):
    *refs, out_ref, sent_ref, tokens_ref, held_ref, done = refs
    token_refs, fold_refs = refs[:count], refs[count:]
    rows = token_refs[0].shape[0]
    copies = [
        (token_ref.at[:, pl.ds(0, tokens_ref.shape[1])], tokens_ref.at[pl.ds(i * rows, rows), :])
        for i, token_ref in enumerate(token_refs)
    ]
    for fold_ref, (relatives, offset, block) in zip(fold_refs, layouts):
        rows = fold_ref.shape[1]
        for slot, relative in enumerate(relatives):
            start = pl.multiple_of((relative ^ position_ref[0]) * block + offset, 16)
            copies.append((fold_ref.at[slot], held_ref.at[pl.ds(start, rows), :]))
    for copy in start_all(copies, done):
        copy.wait()
    terms = jnp.dot(tokens_ref[...], held_ref[...], preferred_element_type=jnp.float32)
    total = tokens_ref.shape[0]
    columns = out_ref.shape[1]
    for k in range(top):
        rows_of = pl.ds(k, total, stride=top)
        out_ref[rows_of, :] = sum(
            terms[:, d * columns : (d + 1) * columns] * mask_ref[d, rows_of, :]
            for d in range(mask_ref.shape[0])
        )
    sent_ref[...] = out_ref[...].astype(sent_ref.dtype)


def input_chosen(position, pieces, held, orders, mask, top):
    total = sum(piece.shape[0] for piece in pieces)
    columns = mask.shape[2]
    width, across = pieces[0].shape[1] - columns, held[0].shape[2]
    block = sum(part.shape[1] for part in held[0::2])
    layouts, offset = [], 0
    for first, last, order in zip(held[0::2], held[1::2], orders):
        relatives = slot_order(order)
        middle = first.shape[0]
        layouts += [(relatives[:middle], offset, block), (relatives[middle:], offset, block)]
        offset += first.shape[1]
    slots = sum(part.shape[0] for part in held)
    return pl.pallas_call(
        functools.partial(input_kernel, top, layouts, len(pieces)),
        in_specs=[pl.BlockSpec(memory_space=pltpu.SMEM), pl.BlockSpec(memory_space=pltpu.VMEM)]
        + [pl.BlockSpec(memory_space=pl.ANY)] * (len(pieces) + len(held)),
        out_specs=[pl.BlockSpec(memory_space=pltpu.VMEM)] * 2,
        out_shape=[
            jax.ShapeDtypeStruct((total * top, columns), jnp.float32),
            jax.ShapeDtypeStruct((total * top, columns), jnp.bfloat16),
        ],
        scratch_shapes=[
            pltpu.VMEM((total, width), pieces[0].dtype),
            pltpu.VMEM((width, across), held[0].dtype),
            pltpu.SemaphoreType.DMA((len(pieces) + slots,)),
        ],
        compiler_params=pltpu.CompilerParams(vmem_limit_bytes=58 * 1024 * 1024),
        cost_estimate=pl.CostEstimate(flops=1, bytes_accessed=1, transcendentals=0),
    )(position, mask, *pieces, *held)


def spans(counts):
    starts = [sum(counts[:i]) for i in range(len(counts))]
    return list(zip(starts, counts))


def output_terms(position_ref, layouts, aligned, token_refs, fold_refs, buffers):
    tokens_ref, fold_ref, total_ref, folded, done = buffers
    counts = [token_ref.shape[0] for token_ref in token_refs]
    fold_copies, token_copies, row = [], [], 0
    for held_ref, (relatives, part, size) in zip(fold_refs, layouts):
        rows = held_ref.shape[1]
        for slot, relative in enumerate(relatives):
            block = (relative ^ position_ref[0]) * size + part
            target = row if aligned else pl.multiple_of(block * rows, rows)
            fold_copies.append((held_ref.at[slot], fold_ref.at[pl.ds(target, rows), :]))
            if aligned:
                across = pl.ds(row, rows)
                token_copies.append(
                    [
                        (
                            token_ref.at[:, pl.ds(pl.multiple_of(block * rows, rows), rows)],
                            tokens_ref.at[pl.ds(first, count), across],
                        )
                        for token_ref, (first, count) in zip(token_refs, spans(counts))
                    ]
                )
            row += rows
    if not aligned:
        token_copies = [
            [
                (token_ref, tokens_ref.at[pl.ds(first, count), :])
                for token_ref, (first, count) in zip(token_refs, spans(counts))
            ]
        ]
    fold_copies = start_all(fold_copies, folded)
    token_copies = [start_all(copies, done.at[i]) for i, copies in enumerate(token_copies)]
    for copy in fold_copies:
        copy.wait()
    for copies in token_copies:
        for copy in copies:
            copy.wait()
    total_ref[...] = jnp.dot(
        tokens_ref[...], fold_ref[...], preferred_element_type=jnp.float32
    )


def score_kernel(layouts, aligned, count, landed_count, position_ref, *refs):
    member_ref, query_ref, *refs = refs
    first = landed_count is not None
    if first:
        mask_ref, chosen_ref, *refs = refs
        landed_refs, refs = refs[:landed_count], refs[landed_count:]
    else:
        before_ref, weight_in_ref, *refs = refs
    token_refs, refs = refs[:count], refs[count:]
    *fold_refs, out_ref, weight_ref, tokens_ref, fold_ref, total_ref, folded, done, sent = refs
    if not first:
        weight_copy = pltpu.make_async_copy(weight_in_ref, weight_ref, sent)
        weight_copy.start()
    output_terms(
        position_ref,
        layouts,
        aligned,
        token_refs,
        fold_refs,
        (tokens_ref, fold_ref, total_ref, folded, done),
    )
    halves, total, columns = weight_ref.shape
    if first:
        rows = total // halves
        for h in range(halves):
            here = pl.ds(h * rows, rows)
            inputs = chosen_ref[here, :]
            for d, landed_ref in enumerate(landed_refs):
                landed = landed_ref[pl.ds((h ^ (d + 1)) * rows, rows), :]
                inputs = inputs + landed.astype(jnp.float32)
            for d in range(halves):
                weight_ref[d, here, :] = inputs * mask_ref[d, here, :]
    else:
        weight_copy.wait()
    products = sum(
        total_ref[:, d * columns : (d + 1) * columns] * weight_ref[d] for d in range(halves)
    )
    high = products.astype(jnp.bfloat16)
    low = (products - high.astype(jnp.float32)).astype(jnp.bfloat16)
    summed = sum(
        lax.dot_general(
            member_ref[...],
            part,
            (((0,), (0,)), ((), ())),
            preferred_element_type=jnp.float32,
        )
        for part in (high, low)
    )
    scores = jnp.dot(
        summed,
        query_ref[...],
        precision=lax.Precision.HIGHEST,
        preferred_element_type=jnp.float32,
    )
    scores = scores[: out_ref.shape[0]]
    out_ref[...] = scores if first else scores + before_ref[...]


def score_call(position, membership, query_sum, sequences, values, landed, pieces, folds, layouts, aligned):
    first = landed is not None
    total = sum(piece.shape[0] for piece in pieces)
    across = folds[0].shape[2]
    width = sum(fold.shape[0] * fold.shape[1] for fold in folds)
    slots = sum(fold.shape[0] for fold in folds)
    weights = values[0] if first else values[1]
    scores = jax.ShapeDtypeStruct((sequences, query_sum.shape[1]), jnp.float32)
    vmem, anywhere = pl.BlockSpec(memory_space=pltpu.VMEM), pl.BlockSpec(memory_space=pl.ANY)
    weight_scratch = pltpu.VMEM(weights.shape, jnp.float32)
    out = pl.pallas_call(
        functools.partial(
            score_kernel, layouts, aligned, len(pieces), len(landed) if first else None
        ),
        in_specs=[pl.BlockSpec(memory_space=pltpu.SMEM)]
        + [vmem] * 2
        + ([vmem] * (2 + len(landed)) if first else [vmem, anywhere])
        + [anywhere] * (len(pieces) + len(folds)),
        out_specs=[vmem] * 2 if first else vmem,
        out_shape=[scores, jax.ShapeDtypeStruct(weights.shape, jnp.float32)] if first else scores,
        scratch_shapes=([] if first else [weight_scratch])
        + [
            pltpu.VMEM((total, width), pieces[0].dtype),
            pltpu.VMEM((width, across), folds[0].dtype),
            pltpu.VMEM((total, across), jnp.float32),
            pltpu.SemaphoreType.DMA((slots,)),
            pltpu.SemaphoreType.DMA((slots if aligned else 1, len(pieces))),
            pltpu.SemaphoreType.DMA,
        ],
        compiler_params=pltpu.CompilerParams(vmem_limit_bytes=58 * 1024 * 1024),
        cost_estimate=pl.CostEstimate(flops=1, bytes_accessed=1, transcendentals=0),
    )(position, membership, query_sum, *values, *(landed or []), *pieces, *folds)
    return out


def partial_scores(
    pieces, held, orders, position, mask, membership, query_sum, sequences, chosen, landed
):
    halves_of = [[], []]
    for n, order in enumerate(orders):
        relatives = slot_order(order)
        middle = len(relatives) // 2
        for side in range(2):
            chunk = relatives[side * middle : (side + 1) * middle]
            halves_of[side].append((chunk, n, len(orders)))
    firsts, lasts = held[0::2], held[1::2]
    if held[0].shape[1] % 128 != 0:
        scores, _ = score_call(
            position,
            membership,
            query_sum,
            sequences,
            [mask, chosen],
            landed,
            pieces,
            firsts + lasts,
            halves_of[0] + halves_of[1],
            False,
        )
        return scores
    scores, weights = score_call(
        position,
        membership,
        query_sum,
        sequences,
        [mask, chosen],
        landed,
        pieces,
        firsts,
        halves_of[0],
        True,
    )
    return score_call(
        position,
        membership,
        query_sum,
        sequences,
        [scores, weights],
        None,
        pieces,
        lasts,
        halves_of[1],
        True,
    )


def per_device(
    activations,
    gate_gradient,
    routes,
    sequence_ids,
    input_basis,
    output_basis,
    input_query,
    output_query,
):
    blocks = lax.axis_size("dp")
    group = lax.axis_size("expert")
    halves = group // CORES
    place = lax.axis_index("dp")
    member = lax.axis_index("expert")
    half = member // CORES
    core = member % CORES
    tokens, top = routes.shape
    columns = input_query.shape[2]
    queries = columns // RANK
    count = bits_of(blocks)

    def send(packed, bit):
        return lax.ppermute(packed, "dp", flip(blocks, 1 << bit))

    def joined(keep, landed, exponent):
        values, there = unpack(landed)
        total = keep + values
        exponent = jnp.maximum(exponent, there) + 1
        return total, exponent, total[: (total.shape[0] - TAIL) // 2 + TAIL]

    def own_shard(keep, landed):
        total = (keep + unpack(landed)[0]).astype(jnp.bfloat16)
        return total[: total.shape[0] - TAIL].reshape(halves, -1, columns)

    def exchange(shard):
        pieces = [shard[0]] + [
            lax.ppermute(shard[d], "expert", flip(group, d * CORES)) for d in range(1, halves)
        ]
        return jnp.concatenate(pieces, axis=1)

    def from_half(part, d):
        return part if d == 0 else lax.ppermute(part, "expert", flip(group, d * CORES))

    def from_core(part):
        return lax.ppermute(part, "expert", flip(group, 1))

    order_first = [(i + 1) % count for i in range(count)]
    order_second = list(range(count))
    position = jnp.stack([place, half, core]).astype(jnp.int32)

    def parts(bases, upper):
        queries = (input_query[0], output_query[0])
        return fold_parts(bases, queries, position, (order_first, order_second), halves, upper)

    bases = input_basis[0], output_basis[0]
    packed_first, packed_second = [part.astype(jnp.float16) for part in parts(bases, True)]
    *bases, packed_first, packed_second = tie(*bases, packed_first, packed_second)
    landed_first = send(packed_first, order_first[0])
    landed_second = send(packed_second, order_second[0])
    exponent_first = column_exponent(input_query[0])
    exponent_second = column_exponent(output_query[0])

    others = range(1, halves)
    gather_orders = [order_second, order_second[1:] + order_second[:1]]
    keep_first, keep_second = parts(bases, False)
    activations, keep_first = tie(activations, keep_first)
    extra = jnp.concatenate([routes, sequence_ids.T], axis=1).astype(jnp.bfloat16)
    extra = jnp.pad(extra, ((0, 0), (0, columns - extra.shape[1])))
    input_parts = list(column_parts(activations, extra, position, halves))
    landed_first, *input_parts = tie(landed_first, *input_parts)
    input_parts = [from_half(part, d) for d, part in enumerate(input_parts)]

    total, exponent_first, keep_first = joined(keep_first, landed_first, exponent_first)
    landed_first = send(pack(total, exponent_first), order_first[1])
    total, exponent_second, keep_second = joined(keep_second, landed_second, exponent_second)
    packed_second = pack(total, exponent_second)
    gate_gradient, packed_second = tie(gate_gradient, packed_second)
    landed_second = send(packed_second, order_second[1])
    own_gradient, early, late = flattened_parts(
        gate_gradient, position, halves, tokens // 16 // 4
    )
    landed_first, own_gradient = tie(landed_first, own_gradient)

    for bit in order_first[2:]:
        total, exponent_first, keep_first = joined(keep_first, landed_first, exponent_first)
        landed_first = send(pack(total, exponent_first), bit)
    for bit in order_second[2:]:
        total, exponent_second, keep_second = joined(
            keep_second, landed_second, exponent_second
        )
        packed_second = pack(total, exponent_second)
        packed_second, landed_first = tie(packed_second, landed_first)
        landed_second = send(packed_second, bit)
    own_half, *input_parts = input_parts
    shard_first, *input_parts = tie(own_shard(keep_first, landed_first), *input_parts)
    input_pieces = [own_half, from_core(own_half)]
    for part in input_parts:
        input_pieces += [part, from_core(part)]
    swapped_gradient = from_core(own_gradient)
    mask, membership = masks(position, input_pieces, top, halves, columns)
    query_sum = jnp.asarray(
        np.arange(columns)[:, None] // RANK == np.arange(queries)[None, :], jnp.float32
    )

    def split(shard):
        cut = (shard.shape[0] // len(gather_orders) + 15) // 16 * 16
        return [shard[:cut][None], shard[cut:][None]]

    def stage_of(held, stage):
        return [send(part, bits[stage]) for part, bits in zip(held, gather_orders)]

    def both(held, landed):
        return [jnp.concatenate(pair) for pair in zip(held, landed)]

    shard_first, *early = tie(exchange(shard_first), *early)
    early = [from_half(part, d) for d, part in zip(others, early)]
    held_first = shard_first[None]
    landed_first = send(held_first, order_second[-1])
    landed_second, mask, membership, swapped_gradient = tie(
        landed_second, mask, membership, swapped_gradient
    )
    shard_second = own_shard(keep_second, landed_second)
    shard_second, landed_first, *early = tie(shard_second, landed_first, *early)
    swapped_early = [from_core(part) for part in early]
    shard_second, *late = tie(exchange(shard_second), *late)
    held_first = jnp.concatenate([held_first, landed_first])
    late = [from_half(part, d) for d, part in zip(others, late)]
    held_second = split(shard_second)
    for stage in range(2, count):
        landed_first = send(held_first, order_second[-stage])
        landed = stage_of(held_second, 1 - stage)
        landed_first, *landed = tie(landed_first, *landed, *swapped_early)
        landed, swapped_early = landed[:2], landed[2:]
        held_first = jnp.concatenate([held_first, landed_first])
        held_second = both(held_second, landed)
    last_first = send(held_first, order_second[0])
    last_first, *landed = tie(last_first, *stage_of(held_second, 1 - count))
    held_second = both(held_second, landed)
    last_second = stage_of(held_second, 0)
    held_output = [held_second[0], last_second[0], held_second[1], last_second[1]]

    chosen, sent = input_chosen(
        position, input_pieces, [held_first, last_first], [order_second], mask, top
    )
    sent, *late = tie(sent, *late)
    landed = [lax.ppermute(sent, "expert", flip(group, d * CORES)) for d in others]

    gradient_pieces = [own_gradient, swapped_gradient]
    for first_part, last_part, swapped_part in zip(early, late, swapped_early):
        gradient_pieces += [first_part, last_part, swapped_part, from_core(last_part)]

    partial = partial_scores(
        gradient_pieces,
        held_output,
        gather_orders,
        position,
        mask,
        membership,
        query_sum,
        group * SEG_DEV,
        chosen,
        landed,
    )
    partial = partial.reshape(group, SEG_DEV, queries)
    scores = partial[0]
    for d in range(1, group):
        scores = scores + lax.ppermute(partial[d], "expert", flip(group, d))
    return scores


def solution(mesh):
    return jax.shard_map(
        per_device,
        mesh=mesh,
        in_specs=(
            P(("dp", "expert"), None),
            P(("dp", "expert"), None, None),
            P(("dp", "expert"), None),
            P(("dp", "expert"), None),
            P("expert", None, "dp"),
            P("expert", None, "dp"),
            P("expert", "dp", None),
            P("expert", "dp", None),
        ),
        out_specs=P(("dp", "expert"), None),
        check_vma=False,
    )
```

time: 248 us -> 177 us (0.71)
  local copies, waits for them, and re-layouts: 70 us -> 5.19 us
  blocking collectives: 45.9 us -> 0 us
  Pallas kernels: 14.3 us -> 54.1 us
  between operations: 13.9 us -> 0.43 us
  starting transfers between devices: 19.4 us -> 31.3 us
  matrix products: 11.9 us -> 0 us
  other arithmetic: 11.6 us -> 19.3 us
  waiting for transfers between devices: 59.8 us -> 65.8 us
    all_gather x1 -> x0, blocking collectives: 45.9 us -> none  [per_device(): small = lax.all_gather(small, 'expert', axis=0)]
    pallas_call x4 -> x8, Pallas kernels: 14.3 us -> 54.1 us  [the longest x2 21.1 us: fold_parts(): pl.pallas_call(functools.partial(fold_kernel, width, steps, upper), grid_...]
    unnamed x31 -> x42, local copies, waits for them, and re-layouts: 40.5 us -> 3.61 us
    slice x11 -> x1, local copies, waits for them, and re-layouts: 16.5 us -> 0.76 us  [per_device(): scores = scores + lax.ppermute(partial[d], 'expert', flip(group, d))]
    dynamic_slice x8 -> x0, local copies, waits for them, and re-layouts: 12.1 us -> none  [gathered(): lax.dynamic_index_in_dim(parts, half ^ d, axis=1, keepdims=False)]
    dot_general x4 -> x0, matrix products: 11.9 us -> none  [the longest x2 8.43 us: per_device(): jnp.dot(group_gradient[k], fold_output, preferred_element_type=jnp.float32)]
    ppermute x18 -> x26, starting transfers between devices: 17.4 us -> 29.1 us  [the longest x15 23.3 us: send(): return lax.ppermute(packed, 'dp', flip(blocks, 1 << bit))]
    ppermute x18 -> x26, waiting for transfers between devices: 56.8 us -> 62.9 us  [the longest x15 47.2 us: send(): return lax.ppermute(packed, 'dp', flip(blocks, 1 << bit))]
  transfers between devices with their start and end apart: 23 -> 29, of which waited for: 10 -> 15; matrix products, arithmetic and copies ran while one was open for 26% -> 9% of each run, Pallas kernels for 5% -> 21%
where the time goes in v3:
time: 177 us; the launch traced here: 176 us
  waiting for transfers between devices  65.8 us (37%)
  Pallas kernels  54.1 us (31%)
  starting transfers between devices  31.3 us (18%)
  other arithmetic  19.3 us (11%)
  local copies, waits for them, and re-layouts  5.19 us (3%)
    ppermute x15, waiting for transfers between devices, send(): return lax.ppermute(packed, 'dp', flip(blocks, 1 << bit))  47.2 us
    ppermute x15, starting transfers between devices, send(): return lax.ppermute(packed, 'dp', flip(blocks, 1 << bit))  23.3 us
    pallas_call x2, Pallas kernels, fold_parts(): pl.pallas_call(functools.partial(fold_kernel, width, steps, upper), grid_...  21.1 us
    pallas_call x2, Pallas kernels, score_call(): pl.pallas_call(functools.partial(score_kernel, layouts, aligned, len(piec...  14.4 us
    ppermute x2, waiting for transfers between devices, exchange(): lax.ppermute(shard[d], 'expert', flip(group, d * CORES))  8.92 us
    pallas_call x1, Pallas kernels, flattened_parts(): pl.pallas_call(functools.partial(flatten_kernel, halves, cut), grid_spec=...  7.52 us
    ppermute x1, waiting for transfers between devices, per_device(): lax.ppermute(sent, 'expert', flip(group, d * CORES))  6.71 us
    pallas_call x1, Pallas kernels, input_chosen(): pl.pallas_call(functools.partial(input_kernel, top, layouts, len(pieces))...  5.54 us
  transfers between devices with their start and end apart: 29, of which 15 were waited for; matrix products, arithmetic and copies ran while one was open for 9% of the time, Pallas kernels for 21%

profile of v3, /device:TPU:0, one launch (start us, length us, event | category | flops | bytes accessed | tf_op | source)
XLA Modules:
  0.0 176.2 jit_solution(3839900567257074521)
XLA Ops:
  0.6 10.6 %shard_map.91 = (f32[3088,128]{1,0:T(8,128)}, f32[4112,128]{1,0:T(8,128)}) custom-call(s32[3]{0:T(128)} %pad_add_fusion.refs_0_.position_ref, bf16[6144,768]{1,0:T(8,128)(2,1)} %bitcast.70, bf16[6144,768]{1,0:T(8,128)(2,1)} %bitcast.71, bf16[6144,768]{1,0:T(8,128)(2,1)} %bitcast.72, bf16[6144,768]{1,0:T(8,128)(2,1)} %bitcast.73, ...), custom_call_target="tpu_custom_call" | custom-call | flops 1 | bytes 1 | tf_op jit(solution)/shard_map/pallas_call | solution.py:104
  11.2 1.7 convert_element_type.65
  13.3 1.2 convert_element_type.66
  14.4 3.0 %collective-permute-start.2 = (f16[3088,128]{1,0:T(8,128)(2,1)S(1)}, f16[3088,128]{1,0:T(8,128)(2,1)}, u32[]{:S(2)}, u32[]{:S(2)}) collective-permute-start(f16[3088,128]{1,0:T(8,128)(2,1)S(1)} %convert_element_type.65), channel_id=1, source_target_pairs={{0,8},{4,12},{8,0},{12,4},{16,24},{20,28},{24,16},{28,20},{1,9},{5... | collective-permute-start | bytes 2371592 | tf_op jit(solution)/shard_map/ppermute | solution.py:547
  17.5 1.5 collective-permute-start
  19.0 10.6 %shard_map.92 = (f32[3088,128]{1,0:T(8,128)}, f32[4112,128]{1,0:T(8,128)}) custom-call(s32[3]{0:T(128)} %pad_add_fusion.refs_0_.position_ref, bf16[6144,768]{1,0:T(8,128)(2,1)} %bitcast.74, bf16[6144,768]{1,0:T(8,128)(2,1)} %bitcast.75, bf16[6144,768]{1,0:T(8,128)(2,1)} %bitcast.76, bf16[6144,768]{1,0:T(8,128)(2,1)} %bitcast.77, ...), custom_call_target="tpu_custom_call" | custom-call | flops 1 | bytes 1 | tf_op jit(solution)/shard_map/pallas_call | solution.py:104
  30.4 3.3 %shard_map.93 = (bf16[128,3200]{1,0:T(8,128)(2,1)}, bf16[128,3200]{1,0:T(8,128)(2,1)}) custom-call(s32[3]{0:T(128)} %pad_add_fusion.refs_0_.position_ref, bf16[128,6144]{1,0:T(8,128)(2,1)} %source_ref, bf16[128,128]{1,0:T(8,128)(2,1)} %pad.4.extra_ref), custom_call_target="tpu_custom_call" | custom-call | flops 1 | bytes 1 | tf_op jit(solution)/shard_map/pallas_call | solution.py:155
  33.8 1.4 collective-permute-done.2
  35.9 1.4 multiply_add_fusion.1
  37.4 1.0 fusion.3
  38.4 2.8 %collective-permute-start.3 = (f16[1552,128]{1,0:T(8,128)(2,1)}, f16[1552,128]{1,0:T(8,128)(2,1)}, u32[]{:S(2)}, u32[]{:S(2)}) collective-permute-start(f16[1552,128]{1,0:T(8,128)(2,1)} %fusion.3), channel_id=1, source_target_pairs={{0,16},{4,20},{8,24},{12,28},{16,0},{20,4},{24,8},{28,12},{1,17},{... | collective-permute-start | bytes 1191944 | tf_op jit(solution)/shard_map/ppermute | solution.py:547
  41.2 1.5 collective-permute-start.7
  43.4 1.4 multiply_add_fusion
  44.8 1.2 fusion.1
  46.0 1.6 collective-permute-start.1
  47.6 7.5 %shard_map.94 = (bf16[256,4096]{1,0:T(8,128)(2,1)}, bf16[64,4096]{1,0:T(8,128)(2,1)}, bf16[192,4096]{1,0:T(8,128)(2,1)}) custom-call(s32[3]{0:T(128)} %pad_add_fusion.refs_0_.position_ref, bf16[128,2,8192]{2,1,0:T(2,128)(2,1)} %source_ref.1), custom_call_target="tpu_custom_call" | custom-call | flops 1 | bytes 8388608 | tf_op jit(solution)/shard_map/pallas_call | solution.py:209
  55.1 3.5 %collective-permute-done.3 = f16[1552,128]{1,0:T(8,128)(2,1)} collective-permute-done((f16[1552,128]{1,0:T(8,128)(2,1)}, f16[1552,128]{1,0:T(8,128)(2,1)}, u32[]{:S(2)}, u32[]{:S(2)}) %collective-permute-start.3) | collective-permute-done | bytes 397344 | tf_op jit(solution)/shard_map/ppermute | solution.py:547
  59.3 1.3 slice_add_fusion.1
  60.7 1.4 collective-permute-start.4
  62.1 6.0 %collective-permute-done.1 = f16[2064,128]{1,0:T(8,128)(2,1)S(1)} collective-permute-done((f16[2064,128]{1,0:T(8,128)(2,1)}, f16[2064,128]{1,0:T(8,128)(2,1)S(1)}, u32[]{:S(2)}, u32[]{:S(2)}) %collective-permute-start.1) | collective-permute-done | bytes 528416 | tf_op jit(solution)/shard_map/ppermute | solution.py:547
  70.5 4.3 %collective-permute-done.10 = bf16[384,128]{1,0:T(8,128)(2,1)S(1)} collective-permute-done((bf16[384,128]{1,0:T(8,128)(2,1)S(1)}, bf16[384,128]{1,0:T(8,128)(2,1)S(1)}, u32[]{:S(2)}, u32[]{:S(2)}) %collective-permute-start.10) | collective-permute-done | bytes 98336 | tf_op jit(solution)/shard_map/ppermute | solution.py:561
  76.1 2.3 %collective-permute-start.11 = (bf16[1,384,256]{2,1,0:T(8,128)(2,1)}, bf16[1,384,256]{2,1,0:T(8,128)(2,1)S(1)}, u32[]{:S(2)}, u32[]{:S(2)}) collective-permute-start(bf16[1,384,256]{2,1,0:T(8,128)(2,1)} %bitcast.26), channel_id=1, source_target_pairs={{0,16},{4,20},{8,24},{12,28},{16,0},{20,4},{24,8},{28,12},{1,17},{... | collective-permute-start | bytes 589832 | tf_op jit(solution)/shard_map/ppermute | solution.py:547
  78.4 2.2 %shard_map.95 = (f32[2,1024,128]{2,1,0:T(8,128)}, bf16[1024,128]{1,0:T(8,128)(2,1)}) custom-call(s32[3]{0:T(128)} %pad_add_fusion.refs_0_.position_ref, bf16[128,3200]{1,0:T(8,128)(2,1)} %get-tuple-element.75.refs_0_, bf16[128,3200]{1,0:T(8,128)(2,1)} %collective-permute-done.6.refs_1_, bf16[128,3200]{1,0:T(8,128)(2,1)} %copy-done.4, ...), custom_call_target="tpu_custom_call" | custom-call | flops 1 | bytes 1 | tf_op jit(solution)/shard_map/pallas_call | solution.py:258
  80.7 8.3 %collective-permute-done.5 = f16[1040,128]{1,0:T(8,128)(2,1)} collective-permute-done((f16[1040,128]{1,0:T(8,128)(2,1)}, f16[1040,128]{1,0:T(8,128)(2,1)}, u32[]{:S(2)}, u32[]{:S(2)}) %collective-permute-start.5) | collective-permute-done | bytes 266272 | tf_op jit(solution)/shard_map/ppermute | solution.py:547
  89.6 1.0 fusion.6
  90.7 2.3 %collective-permute-done.11 = bf16[1,384,256]{2,1,0:T(8,128)(2,1)S(1)} collective-permute-done((bf16[1,384,256]{2,1,0:T(8,128)(2,1)}, bf16[1,384,256]{2,1,0:T(8,128)(2,1)S(1)}, u32[]{:S(2)}, u32[]{:S(2)}) %collective-permute-start.11) | collective-permute-done | bytes 196640 | tf_op jit(solution)/shard_map/ppermute | solution.py:547
  93.9 4.7 %collective-permute-done.14 = bf16[512,128]{1,0:T(8,128)(2,1)S(1)} collective-permute-done((bf16[512,128]{1,0:T(8,128)(2,1)S(1)}, bf16[512,128]{1,0:T(8,128)(2,1)S(1)}, u32[]{:S(2)}, u32[]{:S(2)}) %collective-permute-start.14) | collective-permute-done | bytes 131104 | tf_op jit(solution)/shard_map/ppermute | solution.py:561
  99.2 1.0 pad_maximum_fusion.3
  100.3 1.5 collective-permute-start.16
  101.8 2.4 %collective-permute-start.15 = (bf16[1,256,256]{2,1,0:T(8,128)(2,1)S(1)}, bf16[1,256,256]{2,1,0:T(8,128)(2,1)S(1)}, u32[]{:S(2)}, u32[]{:S(2)}) collective-permute-start(bf16[1,256,256]{2,1,0:T(8,128)(2,1)S(1)} %get-tuple-element.126), channel_id=1, source_target_pairs={{0,16},{4,20},{8,24},{12,28},{16,0},{20,4},{24,8},{28,12},{1,17},{... | collective-permute-start | bytes 393224 | tf_op jit(solution)/shard_map/ppermute | solution.py:547
  104.2 2.1 %collective-permute-done.16 = bf16[1,256,256]{2,1,0:T(8,128)(2,1)S(1)} collective-permute-done((bf16[1,256,256]{2,1,0:T(8,128)(2,1)S(1)}, bf16[1,256,256]{2,1,0:T(8,128)(2,1)S(1)}, u32[]{:S(2)}, u32[]{:S(2)}) %collective-permute-start.16) | collective-permute-done | bytes 131104 | tf_op jit(solution)/shard_map/ppermute | solution.py:547
  106.3 6.1 %collective-permute-done.15 = bf16[1,256,256]{2,1,0:T(8,128)(2,1)S(1)} collective-permute-done((bf16[1,256,256]{2,1,0:T(8,128)(2,1)S(1)}, bf16[1,256,256]{2,1,0:T(8,128)(2,1)S(1)}, u32[]{:S(2)}, u32[]{:S(2)}) %collective-permute-start.15) | collective-permute-done | bytes 131104 | tf_op jit(solution)/shard_map/ppermute | solution.py:547
  112.4 2.2 %collective-permute-done.13 = bf16[2,384,256]{2,1,0:T(8,128)(2,1)S(1)} collective-permute-done((bf16[2,384,256]{2,1,0:T(8,128)(2,1)S(1)}, bf16[2,384,256]{2,1,0:T(8,128)(2,1)S(1)}, u32[]{:S(2)}, u32[]{:S(2)}) %collective-permute-start.13) | collective-permute-done | bytes 393248 | tf_op jit(solution)/shard_map/ppermute | solution.py:547
  114.6 1.2 pad_maximum_fusion.refs_4_
  115.8 1.5 collective-permute-start.18
  117.4 1.3 collective-permute-start.20
  118.7 1.2 collective-permute-start.19
  119.8 11.8 %collective-permute-done.20 = bf16[2,256,256]{2,1,0:T(8,128)(2,1)S(1)} collective-permute-done((bf16[2,256,256]{2,1,0:T(8,128)(2,1)S(1)}, bf16[2,256,256]{2,1,0:T(8,128)(2,1)S(1)}, u32[]{:S(2)}, u32[]{:S(2)}) %collective-permute-start.20) | collective-permute-done | bytes 262176 | tf_op jit(solution)/shard_map/ppermute | solution.py:547
  131.6 3.4 %collective-permute-done.18.refs_5_ = bf16[4,384,256]{2,1,0:T(8,128)(2,1)S(1)} collective-permute-done((bf16[4,384,256]{2,1,0:T(8,128)(2,1)S(1)}, bf16[4,384,256]{2,1,0:T(8,128)(2,1)S(1)}, u32[]{:S(2)}, u32[]{:S(2)}) %collective-permute-start.18) | collective-permute-done | bytes 786464 | tf_op jit(solution)/shard_map/ppermute | solution.py:547
  136.0 5.5 %shard_map.96 = (f32[1024,128]{1,0:T(8,128)}, bf16[1024,128]{1,0:T(8,128)(2,1)}) custom-call(s32[3]{0:T(128)} %pad_add_fusion.refs_0_.position_ref, f32[2,1024,128]{2,1,0:T(8,128)} %get-tuple-element.83.mask_ref.refs_2_, bf16[128,3200]{1,0:T(8,128)(2,1)} %get-tuple-element.75.refs_0_, bf16[128,3200]{1,0:T(8,128)(2,1)} %collective-permute-done.6.refs_1_, ...), custom_call_target="tpu_custom_call" | custom-call | flops 1 | bytes 1 | tf_op jit(solution)/shard_map/pallas_call | solution.py:315
  142.7 1.5 collective-permute-start.24
  144.2 1.4 collective-permute-start.22
  145.6 6.7 %collective-permute-done.22.refs_4_ = bf16[1024,128]{1,0:T(8,128)(2,1)S(1)} collective-permute-done((bf16[1024,128]{1,0:T(8,128)(2,1)S(1)}, bf16[1024,128]{1,0:T(8,128)(2,1)S(1)}, u32[]{:S(2)}, u32[]{:S(2)}) %collective-permute-start.22) | collective-permute-done | bytes 262176 | tf_op jit(solution)/shard_map/ppermute | solution.py:670
  153.5 7.2 %shard_map.97 = (f32[16,4]{1,0:T(8,128)}, f32[2,1024,128]{2,1,0:T(8,128)}) custom-call(s32[3]{0:T(128)} %pad_add_fusion.refs_0_.position_ref, bf16[1024,128]{1,0:T(8,128)(2,1)} %get-tuple-element.82.refs_0_, f32[128,4]{1,0:T(8,128)} %constant.71.clone.refs_1_, f32[2,1024,128]{2,1,0:T(8,128)} %get-tuple-element.83.mask_ref.refs_2_, ...), custom_call_target="tpu_custom_call" | custom-call | flops 1 | bytes 1 | tf_op jit(solution)/shard_map/pallas_call | solution.py:448
  161.9 7.1 %shard_map.98 = f32[16,4]{1,0:T(8,128)} custom-call(s32[3]{0:T(128)} %pad_add_fusion.refs_0_.position_ref, bf16[1024,128]{1,0:T(8,128)(2,1)} %get-tuple-element.82.refs_0_, f32[128,4]{1,0:T(8,128)} %constant.71.clone.refs_1_, f32[16,4]{1,0:T(8,128)} %get-tuple-element.107.refs_2_, f32[2,1024,128]{2,1,0:T(8,128)} %get-tuple-element.108.refs_3_, ...), custom_call_target="tpu_custom_call" | custom-call | flops 1 | bytes 1 | tf_op jit(solution)/shard_map/pallas_call | solution.py:448
  169.8 1.5 collective-permute-start.28
  172.8 2.1 %collective-permute-done.27 = f32[4,4]{1,0:T(4,128)S(1)} collective-permute-done((f32[4,4]{1,0:T(4,128)S(1)}, f32[4,4]{1,0:T(4,128)S(1)}, u32[]{:S(2)}, u32[]{:S(2)}) %collective-permute-start.27) | collective-permute-done | bytes 96 | tf_op jit(solution)/shard_map/ppermute | solution.py:691
  174.9 1.2 fusion.11
  (103 shorter events, 16.7 us)
Async XLA Ops:
  11.2 2.1 %copy-start.8 = (f32[4112,128]{1,0:T(8,128)S(1)}, f32[4112,128]{1,0:T(8,128)}, u32[]{:S(2)}) copy-start(f32[4112,128]{1,0:T(8,128)} %get-tuple-element.58) | copy-start | bytes 6316036
  12.9 6.1 %copy-start.19 = (s32[128,2]{0,1:T(2,128)S(1)}, s32[128,2]{0,1:T(2,128)}, u32[]{:S(2)}) copy-start(s32[128,2]{0,1:T(2,128)} %param.11) | copy-start | bytes 3076
  12.9 6.1 %copy-start.20 = (s32[1,128]{1,0:T(1,128)S(1)}, s32[1,128]{1,0:T(1,128)}, u32[]{:S(2)}) copy-start(s32[1,128]{1,0:T(1,128)} %param.12) | copy-start | bytes 1540
  14.4 20.8 %collective-permute-start.2 = (f16[3088,128]{1,0:T(8,128)(2,1)S(1)}, f16[3088,128]{1,0:T(8,128)(2,1)}, u32[]{:S(2)}, u32[]{:S(2)}) collective-permute-start(f16[3088,128]{1,0:T(8,128)(2,1)S(1)} %convert_element_type.65), channel_id=1, source_target_pairs={{0,8},{4,12},{8,0},{12,4},{16,24},{20,28},{24,16},{28,20},{1,9},{5... | collective-permute-start | bytes 2371592 | tf_op jit(solution)/shard_map/ppermute | solution.py:547
  17.5 25.2 %collective-permute-start = (f16[4112,128]{1,0:T(8,128)(2,1)}, f16[4112,128]{1,0:T(8,128)(2,1)}, u32[]{:S(2)}, u32[]{:S(2)}) collective-permute-start(f16[4112,128]{1,0:T(8,128)(2,1)} %convert_element_type.66), channel_id=1, source_target_pairs={{0,4},{4,0},{8,12},{12,8},{16,20},{20,16},{24,28},{28,24},{1,5},{5... | collective-permute-start | bytes 3158024 | tf_op jit(solution)/shard_map/ppermute | solution.py:547
  29.6 4.1 %copy-start.12 = (bf16[1,768,128]{2,1,0:T(8,128)(2,1)S(1)}, bf16[1,768,128]{2,1,0:T(8,128)(2,1)}, u32[]{:S(2)}) copy-start(bf16[1,768,128]{2,1,0:T(8,128)(2,1)} %param.15) | copy-start | bytes 589828
  29.6 4.2 %copy-start.6 = (bf16[1,1024,128]{2,1,0:T(8,128)(2,1)S(1)}, bf16[1,1024,128]{2,1,0:T(8,128)(2,1)}, u32[]{:S(2)}) copy-start(bf16[1,1024,128]{2,1,0:T(8,128)(2,1)} %param.16) | copy-start | bytes 786436
  29.7 6.2 %copy-start.13 = (f32[3088,128]{1,0:T(8,128)S(1)}, f32[3088,128]{1,0:T(8,128)}, u32[]{:S(2)}) copy-start(f32[3088,128]{1,0:T(8,128)} %get-tuple-element.65) | copy-start | bytes 4743172
  35.9 6.8 %copy-start.3 = (bf16[128,3200]{1,0:T(8,128)(2,1)S(1)}, bf16[128,3200]{1,0:T(8,128)(2,1)}, u32[]{:S(2)}) copy-start(bf16[128,3200]{1,0:T(8,128)(2,1)} %get-tuple-element.75.refs_0_) | copy-start | bytes 2457604
  35.9 7.5 %copy-start.7 = (f32[4112,128]{1,0:T(8,128)S(1)}, f32[4112,128]{1,0:T(8,128)}, u32[]{:S(2)}) copy-start(f32[4112,128]{1,0:T(8,128)} %get-tuple-element.61) | copy-start | bytes 6316036
  38.4 20.2 %collective-permute-start.3 = (f16[1552,128]{1,0:T(8,128)(2,1)}, f16[1552,128]{1,0:T(8,128)(2,1)}, u32[]{:S(2)}, u32[]{:S(2)}) collective-permute-start(f16[1552,128]{1,0:T(8,128)(2,1)} %fusion.3), channel_id=1, source_target_pairs={{0,16},{4,20},{8,24},{12,28},{16,0},{20,4},{24,8},{28,12},{1,17},{... | collective-permute-start | bytes 1191944 | tf_op jit(solution)/shard_map/ppermute | solution.py:547
  41.2 28.1 %collective-permute-start.7 = (bf16[128,3200]{1,0:T(8,128)(2,1)}, bf16[128,3200]{1,0:T(8,128)(2,1)S(1)}, u32[]{:S(2)}, u32[]{:S(2)}) collective-permute-start(bf16[128,3200]{1,0:T(8,128)(2,1)} %get-tuple-element.77), channel_id=1, source_target_pairs={{0,2},{1,3},{2,0},{3,1},{4,6},{5,7},{6,4},{7,5},{8,10},{9,11},{10,... | collective-permute-start | bytes 2457608 | tf_op jit(solution)/shard_map/ppermute | solution.py:566
  42.7 33.4 %collective-permute-start.6 = (bf16[128,3200]{1,0:T(8,128)(2,1)S(1)}, bf16[128,3200]{1,0:T(8,128)(2,1)}, u32[]{:S(2)}, u32[]{:S(2)}) collective-permute-start(bf16[128,3200]{1,0:T(8,128)(2,1)S(1)} %copy-done.3), channel_id=1, source_target_pairs={{0,1},{1,0},{2,3},{3,2},{4,5},{5,4},{6,7},{7,6},{8,9},{9,8},{10,11... | collective-permute-start | bytes 2457608 | tf_op jit(solution)/shard_map/ppermute | solution.py:569
  46.0 22.2 %collective-permute-start.1 = (f16[2064,128]{1,0:T(8,128)(2,1)}, f16[2064,128]{1,0:T(8,128)(2,1)S(1)}, u32[]{:S(2)}, u32[]{:S(2)}) collective-permute-start(f16[2064,128]{1,0:T(8,128)(2,1)} %fusion.1), channel_id=1, source_target_pairs={{0,8},{4,12},{8,0},{12,4},{16,24},{20,28},{24,16},{28,20},{1,9},{5... | collective-permute-start | bytes 1585160 | tf_op jit(solution)/shard_map/ppermute | solution.py:547
  59.3 2.9 %copy-start = (bf16[256,4096]{1,0:T(8,128)(2,1)S(1)}, bf16[256,4096]{1,0:T(8,128)(2,1)}, u32[]{:S(2)}) copy-start(bf16[256,4096]{1,0:T(8,128)(2,1)} %get-tuple-element.81.refs_5_.refs_4_) | copy-start | bytes 6291460
  60.7 8.5 %collective-permute-start.4 = (f16[784,128]{1,0:T(8,128)(2,1)S(1)}, f16[784,128]{1,0:T(8,128)(2,1)S(1)}, u32[]{:S(2)}, u32[]{:S(2)}) collective-permute-start(f16[784,128]{1,0:T(8,128)(2,1)S(1)} %get-tuple-element.117), channel_id=1, source_target_pairs={{0,4},{4,0},{8,12},{12,8},{16,20},{20,16},{24,28},{28,24},{1,5},{5... | collective-permute-start | bytes 602120 | tf_op jit(solution)/shard_map/ppermute | solution.py:547
  62.1 26.8 %collective-permute-start.9 = (bf16[256,4096]{1,0:T(8,128)(2,1)S(1)}, bf16[256,4096]{1,0:T(8,128)(2,1)}, u32[]{:S(2)}, u32[]{:S(2)}) collective-permute-start(bf16[256,4096]{1,0:T(8,128)(2,1)S(1)} %copy-done), channel_id=1, source_target_pairs={{0,1},{1,0},{2,3},{3,2},{4,5},{5,4},{6,7},{7,6},{8,9},{9,8},{10,11... | collective-permute-start | bytes 6291464 | tf_op jit(solution)/shard_map/ppermute | solution.py:569
  69.3 6.8 %copy-start.4 = (bf16[128,3200]{1,0:T(8,128)(2,1)}, bf16[128,3200]{1,0:T(8,128)(2,1)S(1)}, u32[]{:S(2)}) copy-start(bf16[128,3200]{1,0:T(8,128)(2,1)S(1)} %collective-permute-done.7.refs_2_) | copy-start | bytes 2457604
  69.3 9.1 %collective-permute-start.8 = (bf16[128,3200]{1,0:T(8,128)(2,1)S(1)}, bf16[128,3200]{1,0:T(8,128)(2,1)}, u32[]{:S(2)}, u32[]{:S(2)}) collective-permute-start(bf16[128,3200]{1,0:T(8,128)(2,1)S(1)} %collective-permute-done.7.refs_2_), channel_id=1, source_target_pairs={{0,1},{1,0},{2,3},{3,2},{4,5},{5,4},{6,7},{7,6},{8,9},{9,8},{10,11... | collective-permute-start | bytes 2457608 | tf_op jit(solution)/shard_map/ppermute | solution.py:569
  69.4 19.5 %collective-permute-start.5 = (f16[1040,128]{1,0:T(8,128)(2,1)}, f16[1040,128]{1,0:T(8,128)(2,1)}, u32[]{:S(2)}, u32[]{:S(2)}) collective-permute-start(f16[1040,128]{1,0:T(8,128)(2,1)} %get-tuple-element.74), channel_id=1, source_target_pairs={{0,16},{4,20},{8,24},{12,28},{16,0},{20,4},{24,8},{28,12},{1,17},{... | collective-permute-start | bytes 798728 | tf_op jit(solution)/shard_map/ppermute | solution.py:547
  69.9 4.9 %collective-permute-start.10 = (bf16[384,128]{1,0:T(8,128)(2,1)S(1)}, bf16[384,128]{1,0:T(8,128)(2,1)S(1)}, u32[]{:S(2)}, u32[]{:S(2)}) collective-permute-start(bf16[384,128]{1,0:T(8,128)(2,1)S(1)} %get-tuple-element.130), channel_id=1, source_target_pairs={{0,2},{1,3},{2,0},{3,1},{4,6},{5,7},{6,4},{7,5},{8,10},{9,11},{10,... | collective-permute-start | bytes 294920 | tf_op jit(solution)/shard_map/ppermute | solution.py:561
  75.5 17.5 %collective-permute-start.12 = (bf16[64,4096]{1,0:T(8,128)(2,1)}, bf16[64,4096]{1,0:T(8,128)(2,1)}, u32[]{:S(2)}, u32[]{:S(2)}) collective-permute-start(bf16[64,4096]{1,0:T(8,128)(2,1)} %get-tuple-element.88), channel_id=1, source_target_pairs={{0,2},{1,3},{2,0},{3,1},{4,6},{5,7},{6,4},{7,5},{8,10},{9,11},{10,... | collective-permute-start | bytes 1572872 | tf_op jit(solution)/shard_map/ppermute | solution.py:566
  76.1 16.9 %collective-permute-start.11 = (bf16[1,384,256]{2,1,0:T(8,128)(2,1)}, bf16[1,384,256]{2,1,0:T(8,128)(2,1)S(1)}, u32[]{:S(2)}, u32[]{:S(2)}) collective-permute-start(bf16[1,384,256]{2,1,0:T(8,128)(2,1)} %bitcast.26), channel_id=1, source_target_pairs={{0,16},{4,20},{8,24},{12,28},{16,0},{20,4},{24,8},{28,12},{1,17},{... | collective-permute-start | bytes 589832 | tf_op jit(solution)/shard_map/ppermute | solution.py:547
  93.0 5.5 %collective-permute-start.14 = (bf16[512,128]{1,0:T(8,128)(2,1)S(1)}, bf16[512,128]{1,0:T(8,128)(2,1)S(1)}, u32[]{:S(2)}, u32[]{:S(2)}) collective-permute-start(bf16[512,128]{1,0:T(8,128)(2,1)S(1)} %get-tuple-element.128), channel_id=1, source_target_pairs={{0,2},{1,3},{2,0},{3,1},{4,6},{5,7},{6,4},{7,5},{8,10},{9,11},{10,... | collective-permute-start | bytes 393224 | tf_op jit(solution)/shard_map/ppermute | solution.py:561
  98.6 43.0 %collective-permute-start.21 = (bf16[192,4096]{1,0:T(8,128)(2,1)}, bf16[192,4096]{1,0:T(8,128)(2,1)S(1)}, u32[]{:S(2)}, u32[]{:S(2)}) collective-permute-start(bf16[192,4096]{1,0:T(8,128)(2,1)} %get-tuple-element.100), channel_id=1, source_target_pairs={{0,2},{1,3},{2,0},{3,1},{4,6},{5,7},{6,4},{7,5},{8,10},{9,11},{10,... | collective-permute-start | bytes 4718600 | tf_op jit(solution)/shard_map/ppermute | solution.py:566
  99.2 15.4 %collective-permute-start.17 = (bf16[64,4096]{1,0:T(8,128)(2,1)}, bf16[64,4096]{1,0:T(8,128)(2,1)S(1)}, u32[]{:S(2)}, u32[]{:S(2)}) collective-permute-start(bf16[64,4096]{1,0:T(8,128)(2,1)} %collective-permute-done.12.refs_7_.refs_6_), channel_id=1, source_target_pairs={{0,1},{1,0},{2,3},{3,2},{4,5},{5,4},{6,7},{7,6},{8,9},{9,8},{10,11... | collective-permute-start | bytes 1572872 | tf_op jit(solution)/shard_map/ppermute | solution.py:569
  100.2 14.4 %collective-permute-start.13 = (bf16[2,384,256]{2,1,0:T(8,128)(2,1)S(1)}, bf16[2,384,256]{2,1,0:T(8,128)(2,1)S(1)}, u32[]{:S(2)}, u32[]{:S(2)}) collective-permute-start(bf16[2,384,256]{2,1,0:T(8,128)(2,1)S(1)} %pad_maximum_fusion.3), channel_id=1, source_target_pairs={{0,8},{4,12},{8,0},{12,4},{16,24},{20,28},{24,16},{28,20},{1,9},{5... | collective-permute-start | bytes 1179656 | tf_op jit(solution)/shard_map/ppermute | solution.py:547
  100.3 6.0 %collective-permute-start.16 = (bf16[1,256,256]{2,1,0:T(8,128)(2,1)S(1)}, bf16[1,256,256]{2,1,0:T(8,128)(2,1)S(1)}, u32[]{:S(2)}, u32[]{:S(2)}) collective-permute-start(bf16[1,256,256]{2,1,0:T(8,128)(2,1)S(1)} %get-tuple-element.125), channel_id=1, source_target_pairs={{0,4},{4,0},{8,12},{12,8},{16,20},{20,16},{24,28},{28,24},{1,5},{5... | collective-permute-start | bytes 393224 | tf_op jit(solution)/shard_map/ppermute | solution.py:547
  101.8 10.6 %collective-permute-start.15 = (bf16[1,256,256]{2,1,0:T(8,128)(2,1)S(1)}, bf16[1,256,256]{2,1,0:T(8,128)(2,1)S(1)}, u32[]{:S(2)}, u32[]{:S(2)}) collective-permute-start(bf16[1,256,256]{2,1,0:T(8,128)(2,1)S(1)} %get-tuple-element.126), channel_id=1, source_target_pairs={{0,16},{4,20},{8,24},{12,28},{16,0},{20,4},{24,8},{28,12},{1,17},{... | collective-permute-start | bytes 393224 | tf_op jit(solution)/shard_map/ppermute | solution.py:547
  114.6 26.9 %copy-start.9 = (bf16[64,4096]{1,0:T(8,128)(2,1)}, bf16[64,4096]{1,0:T(8,128)(2,1)S(1)}, u32[]{:S(2)}) copy-start(bf16[64,4096]{1,0:T(8,128)(2,1)S(1)} %collective-permute-done.17.refs_9_.refs_8_) | copy-start | bytes 1572868
  115.8 19.2 %copy-start.5 = (bf16[4,384,256]{2,1,0:T(8,128)(2,1)}, bf16[4,384,256]{2,1,0:T(8,128)(2,1)S(1)}, u32[]{:S(2)}) copy-start(bf16[4,384,256]{2,1,0:T(8,128)(2,1)S(1)} %pad_maximum_fusion.refs_4_) | copy-start | bytes 2359300
  115.8 19.2 %collective-permute-start.18 = (bf16[4,384,256]{2,1,0:T(8,128)(2,1)S(1)}, bf16[4,384,256]{2,1,0:T(8,128)(2,1)S(1)}, u32[]{:S(2)}, u32[]{:S(2)}) collective-permute-start(bf16[4,384,256]{2,1,0:T(8,128)(2,1)S(1)} %pad_maximum_fusion.refs_4_), channel_id=1, source_target_pairs={{0,4},{4,0},{8,12},{12,8},{16,20},{20,16},{24,28},{28,24},{1,5},{5... | collective-permute-start | bytes 2359304 | tf_op jit(solution)/shard_map/ppermute | solution.py:547
  117.4 14.2 %collective-permute-start.20 = (bf16[2,256,256]{2,1,0:T(8,128)(2,1)S(1)}, bf16[2,256,256]{2,1,0:T(8,128)(2,1)S(1)}, u32[]{:S(2)}, u32[]{:S(2)}) collective-permute-start(bf16[2,256,256]{2,1,0:T(8,128)(2,1)S(1)} %pad_maximum_fusion.6), channel_id=1, source_target_pairs={{0,16},{4,20},{8,24},{12,28},{16,0},{20,4},{24,8},{28,12},{1,17},{... | collective-permute-start | bytes 786440 | tf_op jit(solution)/shard_map/ppermute | solution.py:547
  118.7 13.0 %collective-permute-start.19 = (bf16[2,256,256]{2,1,0:T(8,128)(2,1)S(1)}, bf16[2,256,256]{2,1,0:T(8,128)(2,1)S(1)}, u32[]{:S(2)}, u32[]{:S(2)}) collective-permute-start(bf16[2,256,256]{2,1,0:T(8,128)(2,1)S(1)} %pad_maximum_fusion.5), channel_id=1, source_target_pairs={{0,8},{4,12},{8,0},{12,4},{16,24},{20,28},{24,16},{28,20},{1,9},{5... | collective-permute-start | bytes 786440 | tf_op jit(solution)/shard_map/ppermute | solution.py:547
  135.1 0.9 copy-start.14
  141.5 2.6 %copy-start.18 = (bf16[1024,128]{1,0:T(8,128)(2,1)S(1)}, bf16[1024,128]{1,0:T(8,128)(2,1)}, u32[]{:S(2)}) copy-start(bf16[1024,128]{1,0:T(8,128)(2,1)} %get-tuple-element.101) | copy-start | bytes 786436
  141.6 10.8 %copy-start.1 = (bf16[192,4096]{1,0:T(8,128)(2,1)}, bf16[192,4096]{1,0:T(8,128)(2,1)S(1)}, u32[]{:S(2)}) copy-start(bf16[192,4096]{1,0:T(8,128)(2,1)S(1)} %collective-permute-done.21.refs_8_.refs_7_) | copy-start | bytes 4718596
  141.6 10.7 %collective-permute-start.23 = (bf16[192,4096]{1,0:T(8,128)(2,1)S(1)}, bf16[192,4096]{1,0:T(8,128)(2,1)S(1)}, u32[]{:S(2)}, u32[]{:S(2)}) collective-permute-start(bf16[192,4096]{1,0:T(8,128)(2,1)S(1)} %collective-permute-done.21.refs_8_.refs_7_), channel_id=1, source_target_pairs={{0,1},{1,0},{2,3},{3,2},{4,5},{5,4},{6,7},{7,6},{8,9},{9,8},{10,11... | collective-permute-start | bytes 4718600 | tf_op jit(solution)/shard_map/ppermute | solution.py:569
  141.7 10.6 %copy-start.10 = (bf16[4,256,256]{2,1,0:T(8,128)(2,1)}, bf16[4,256,256]{2,1,0:T(8,128)(2,1)S(1)}, u32[]{:S(2)}) copy-start(bf16[4,256,256]{2,1,0:T(8,128)(2,1)S(1)} %pad_maximum_fusion.1.refs_11_) | copy-start | bytes 1572868
  141.8 10.5 %copy-start.11 = (bf16[4,256,256]{2,1,0:T(8,128)(2,1)}, bf16[4,256,256]{2,1,0:T(8,128)(2,1)S(1)}, u32[]{:S(2)}) copy-start(bf16[4,256,256]{2,1,0:T(8,128)(2,1)S(1)} %pad_maximum_fusion.2.refs_12_) | copy-start | bytes 1572868
  141.8 19.0 %collective-permute-start.25 = (bf16[4,256,256]{2,1,0:T(8,128)(2,1)S(1)}, bf16[4,256,256]{2,1,0:T(8,128)(2,1)S(1)}, u32[]{:S(2)}, u32[]{:S(2)}) collective-permute-start(bf16[4,256,256]{2,1,0:T(8,128)(2,1)S(1)} %pad_maximum_fusion.2.refs_12_), channel_id=1, source_target_pairs={{0,8},{4,12},{8,0},{12,4},{16,24},{20,28},{24,16},{28,20},{1,9},{5... | collective-permute-start | bytes 1572872 | tf_op jit(solution)/shard_map/ppermute | solution.py:547
  142.7 18.1 %collective-permute-start.24 = (bf16[4,256,256]{2,1,0:T(8,128)(2,1)S(1)}, bf16[4,256,256]{2,1,0:T(8,128)(2,1)S(1)}, u32[]{:S(2)}, u32[]{:S(2)}) collective-permute-start(bf16[4,256,256]{2,1,0:T(8,128)(2,1)S(1)} %pad_maximum_fusion.1.refs_11_), channel_id=1, source_target_pairs={{0,4},{4,0},{8,12},{12,8},{16,20},{20,16},{24,28},{28,24},{1,5},{5... | collective-permute-start | bytes 1572872 | tf_op jit(solution)/shard_map/ppermute | solution.py:547
  144.2 8.1 %collective-permute-start.22 = (bf16[1024,128]{1,0:T(8,128)(2,1)S(1)}, bf16[1024,128]{1,0:T(8,128)(2,1)S(1)}, u32[]{:S(2)}, u32[]{:S(2)}) collective-permute-start(bf16[1024,128]{1,0:T(8,128)(2,1)S(1)} %copy-done.18), channel_id=1, source_target_pairs={{0,2},{1,3},{2,0},{3,1},{4,6},{5,7},{6,4},{7,5},{8,10},{9,11},{10,... | collective-permute-start | bytes 786440 | tf_op jit(solution)/shard_map/ppermute | solution.py:670
  152.3 1.2 copy-start.2
  160.8 1.0 copy-start.16
  169.8 2.1 %collective-permute-start.26 = (f32[4,4]{1,0:T(4,128)S(1)}, f32[4,4]{1,0:T(4,128)S(1)}, u32[]{:S(2)}, u32[]{:S(2)}) collective-permute-start(f32[4,4]{1,0:T(4,128)S(1)} %get-tuple-element.131), channel_id=1, source_target_pairs={{0,1},{1,0},{2,3},{3,2},{4,5},{5,4},{6,7},{7,6},{8,9},{9,8},{10,11... | collective-permute-start | bytes 200 | tf_op jit(solution)/shard_map/ppermute | solution.py:691
  169.8 3.0 %collective-permute-start.28 = (f32[4,4]{1,0:T(4,128)S(1)}, f32[4,4]{1,0:T(4,128)S(1)}, u32[]{:S(2)}, u32[]{:S(2)}) collective-permute-start(f32[4,4]{1,0:T(4,128)S(1)} %get-tuple-element.132), channel_id=1, source_target_pairs={{0,3},{1,2},{2,1},{3,0},{4,7},{5,6},{6,5},{7,4},{8,11},{9,10},{10,... | collective-permute-start | bytes 200 | tf_op jit(solution)/shard_map/ppermute | solution.py:691
  171.3 3.6 %collective-permute-start.27 = (f32[4,4]{1,0:T(4,128)S(1)}, f32[4,4]{1,0:T(4,128)S(1)}, u32[]{:S(2)}, u32[]{:S(2)}) collective-permute-start(f32[4,4]{1,0:T(4,128)S(1)} %get-tuple-element.133), channel_id=1, source_target_pairs={{0,2},{1,3},{2,0},{3,1},{4,6},{5,7},{6,4},{7,5},{8,10},{9,11},{10,... | collective-permute-start | bytes 200 | tf_op jit(solution)/shard_map/ppermute | solution.py:691
  (2 other events, 1.6 us)

commit v4 on v3

--- a/solution.py
+++ b/solution.py
@@ -118,17 +118,12 @@
     )(position, *([bases[0]] * width), *([bases[1]] * width), *queries)
 
 
-def pack(total, exponent):
-    half = (total.shape[0] - TAIL) // 2
-    scaled = total[half:] * jnp.exp2(TOP_EXPONENT - exponent)
+def pack(keep, landed, there, exponent):
+    half = (keep.shape[0] - TAIL) // 2
+    values = landed[half:].astype(jnp.float32) * jnp.exp2(there - TOP_EXPONENT)
+    scaled = (keep[half:] + values) * jnp.exp2(TOP_EXPONENT - exponent)
     row = lax.broadcasted_iota(jnp.int32, scaled.shape, 0)
     return jnp.where(row < half, scaled, exponent).astype(jnp.float16)
-
-
-def unpack(packed):
-    tail = packed.shape[0] - TAIL
-    exponent = packed[tail : tail + 1].astype(jnp.float32)
-    return packed.astype(jnp.float32) * jnp.exp2(exponent - TOP_EXPONENT), exponent
 
 
 def flip(size, mask):
@@ -169,7 +164,7 @@
     )(position, source, extra)
 
 
-def flatten_kernel(halves, cut, position_ref, source_ref, *out_refs):
+def flatten_kernel(halves, cuts, position_ref, source_ref, *out_refs):
     step = pl.program_id(0)
     rows = source_ref.shape[0] * source_ref.shape[1]
     width = source_ref.shape[2] // halves
@@ -179,35 +174,29 @@
         if d == 0:
             out_refs[0][...] = part
             continue
-
-        @pl.when(step < cut)
-        def _():
-            out_refs[2 * d - 1][...] = part
-
-        @pl.when(step >= cut)
-        def _():
-            out_refs[2 * d][...] = part
-
-
-def flattened_parts(source, position, halves, cut):
+        for n in range(len(cuts) - 1):
+
+            @pl.when((step >= cuts[n]) & (step < cuts[n + 1]))
+            def _():
+                out_refs[1 + n * (halves - 1) + d - 1][...] = part
+
+
+def flattened_parts(source, position, halves, sizes):
     tokens, top, width = source.shape
     width = width // halves
     block = 16
     steps, rows = tokens // block, block * top
-
-    def out(index):
-        return pl.BlockSpec((rows, width), index)
-
-    specs = [out(lambda i, p: (i, 0))]
-    shapes = [(tokens * top, width)]
-    for _ in range(1, halves):
-        specs += [
-            out(lambda i, p: (jnp.minimum(i, cut - 1), 0)),
-            out(lambda i, p: (jnp.maximum(i - cut, 0), 0)),
-        ]
-        shapes += [(cut * rows, width), ((steps - cut) * rows, width)]
-    own, *others = pl.pallas_call(
-        functools.partial(flatten_kernel, halves, cut),
+    cuts = [sum(sizes[:n]) for n in range(len(sizes) + 1)] + [steps]
+
+    def out(first, last):
+        return pl.BlockSpec((rows, width), lambda i, p: (jnp.clip(i, first, last - 1) - first, 0))
+
+    specs, shapes = [out(0, steps)], [(tokens * top, width)]
+    for first, last in zip(cuts, cuts[1:]):
+        specs += [out(first, last)] * (halves - 1)
+        shapes += [((last - first) * rows, width)] * (halves - 1)
+    own, *away = pl.pallas_call(
+        functools.partial(flatten_kernel, halves, cuts),
         grid_spec=pltpu.PrefetchScalarGridSpec(
             num_scalar_prefetch=1,
             grid=(steps,),
@@ -220,7 +209,7 @@
             flops=1, bytes_accessed=4 * source.size, transcendentals=0
         ),
     )(position, source)
-    return own, others[0::2], others[1::2]
+    return own, *[away[n : n + halves - 1] for n in range(0, len(away), halves - 1)]
 
 
 def start_all(copies, done):
@@ -232,7 +221,7 @@
 
 
 def mask_kernel(top, position_ref, *refs):
-    *extra_refs, mask_ref, member_ref, rows_ref = refs
+    *extra_refs, mask_ref, small_mask_ref, member_ref, rows_ref = refs
     tokens, lanes = extra_refs[0].shape
     lane = lax.broadcasted_iota(jnp.int32, (tokens, lanes), 1).astype(jnp.float32)
     for i, extra_ref in enumerate(extra_refs):
@@ -249,6 +238,7 @@
                 expert = ((position_ref[1] ^ d) * CORES + position_ref[2]).astype(jnp.float32)
                 mask_ref[d, rows, :] = jnp.where(column(k) == expert, 1.0, 0.0)
     member_ref[...] = rows_ref[...].astype(member_ref.dtype)
+    small_mask_ref[...] = mask_ref[...].astype(small_mask_ref.dtype)
 
 
 def masks(position, pieces, top, halves, lanes):
@@ -262,10 +252,12 @@
         + [pl.BlockSpec((tokens, lanes), lambda i: (0, last))] * len(pieces),
         out_specs=[
             pl.BlockSpec((halves, rows, lanes), lambda i: (0, 0, 0)),
+            pl.BlockSpec((halves, rows, lanes), lambda i: (0, 0, 0)),
             pl.BlockSpec((rows, lanes), lambda i: (0, 0)),
         ],
         out_shape=[
             jax.ShapeDtypeStruct((halves, rows, lanes), jnp.float32),
+            jax.ShapeDtypeStruct((halves, rows, lanes), jnp.bfloat16),
             jax.ShapeDtypeStruct((rows, lanes), jnp.bfloat16),
         ],
         scratch_shapes=[pltpu.VMEM((rows, lanes), jnp.float32)],
@@ -377,148 +369,119 @@
     )
 
 
-def score_kernel(layouts, aligned, count, landed_count, position_ref, *refs):
-    member_ref, query_ref, *refs = refs
-    first = landed_count is not None
-    if first:
-        mask_ref, chosen_ref, *refs = refs
-        landed_refs, refs = refs[:landed_count], refs[landed_count:]
-    else:
-        before_ref, weight_in_ref, *refs = refs
+def first_kernel(layouts, count, position_ref, *refs):
     token_refs, refs = refs[:count], refs[count:]
-    *fold_refs, out_ref, weight_ref, tokens_ref, fold_ref, total_ref, folded, done, sent = refs
-    if not first:
-        weight_copy = pltpu.make_async_copy(weight_in_ref, weight_ref, sent)
-        weight_copy.start()
-    output_terms(
-        position_ref,
-        layouts,
-        aligned,
-        token_refs,
-        fold_refs,
-        (tokens_ref, fold_ref, total_ref, folded, done),
-    )
-    halves, total, columns = weight_ref.shape
-    if first:
-        rows = total // halves
-        for h in range(halves):
-            here = pl.ds(h * rows, rows)
-            inputs = chosen_ref[here, :]
-            for d, landed_ref in enumerate(landed_refs):
-                landed = landed_ref[pl.ds((h ^ (d + 1)) * rows, rows), :]
-                inputs = inputs + landed.astype(jnp.float32)
-            for d in range(halves):
-                weight_ref[d, here, :] = inputs * mask_ref[d, here, :]
-    else:
-        weight_copy.wait()
-    products = sum(
-        total_ref[:, d * columns : (d + 1) * columns] * weight_ref[d] for d in range(halves)
-    )
-    high = products.astype(jnp.bfloat16)
-    low = (products - high.astype(jnp.float32)).astype(jnp.bfloat16)
-    summed = sum(
-        lax.dot_general(
-            member_ref[...],
-            part,
-            (((0,), (0,)), ((), ())),
-            preferred_element_type=jnp.float32,
+    *fold_refs, total_ref, tokens_ref, fold_ref, folded, done = refs
+    buffers = tokens_ref, fold_ref, total_ref, folded, done
+    output_terms(position_ref, layouts, True, token_refs, fold_refs, buffers)
+
+
+def last_kernel(layouts, aligned, count, extra_count, group, position_ref, *refs):
+    query_ref, *refs = refs
+    extra_refs, refs = refs[:extra_count], refs[extra_count:]
+    token_refs, refs = refs[:count], refs[count:]
+    held_refs, refs = refs[-extra_count:], refs[:-extra_count]
+    fold_refs, refs = refs[: len(layouts)], refs[len(layouts) :]
+    out_refs, (tokens_ref, fold_ref, total_ref, folded, done, extra_done) = refs[:group], refs[group:]
+    extra_copies = start_all(list(zip(extra_refs, held_refs)), extra_done)
+    buffers = tokens_ref, fold_ref, total_ref, folded, done
+    output_terms(position_ref, layouts, aligned, token_refs, fold_refs, buffers)
+    for copy in extra_copies:
+        copy.wait()
+    mask_ref, member_ref, chosen_ref, *refs = held_refs
+    halves = mask_ref.shape[0]
+    landed_refs, before_refs = refs[: halves - 1], refs[halves - 1 :]
+    columns = chosen_ref.shape[1]
+    rows = chosen_ref.shape[0] // halves
+    summed = 0.0
+    for h in range(halves):
+        here = pl.ds(h * rows, rows)
+        inputs = chosen_ref[here, :]
+        for d, landed_ref in enumerate(landed_refs):
+            landed = landed_ref[pl.ds((h ^ (d + 1)) * rows, rows), :]
+            inputs = inputs + landed.astype(jnp.float32)
+        total = total_ref[here, :]
+        for before_ref in before_refs:
+            total = total + before_ref[here, :]
+        products = inputs * sum(
+            total[:, d * columns : (d + 1) * columns] * mask_ref[d, here, :].astype(jnp.float32)
+            for d in range(halves)
         )
-        for part in (high, low)
-    )
+        high = products.astype(jnp.bfloat16)
+        low = (products - high.astype(jnp.float32)).astype(jnp.bfloat16)
+        for part in (high, low):
+            summed = summed + lax.dot_general(
+                member_ref[here, :],
+                part,
+                (((0,), (0,)), ((), ())),
+                preferred_element_type=jnp.float32,
+            )
     scores = jnp.dot(
         summed,
         query_ref[...],
         precision=lax.Precision.HIGHEST,
         preferred_element_type=jnp.float32,
     )
-    scores = scores[: out_ref.shape[0]]
-    out_ref[...] = scores if first else scores + before_ref[...]
-
-
-def score_call(position, membership, query_sum, sequences, values, landed, pieces, folds, layouts, aligned):
-    first = landed is not None
+    for i, out_ref in enumerate(out_refs):
+        out_ref[...] = scores[i * SEG_DEV : (i + 1) * SEG_DEV]
+
+
+def score_call(position, query_sum, extras, group, pieces, folds, layouts, aligned):
     total = sum(piece.shape[0] for piece in pieces)
     across = folds[0].shape[2]
     width = sum(fold.shape[0] * fold.shape[1] for fold in folds)
     slots = sum(fold.shape[0] for fold in folds)
-    weights = values[0] if first else values[1]
-    scores = jax.ShapeDtypeStruct((sequences, query_sum.shape[1]), jnp.float32)
     vmem, anywhere = pl.BlockSpec(memory_space=pltpu.VMEM), pl.BlockSpec(memory_space=pl.ANY)
-    weight_scratch = pltpu.VMEM(weights.shape, jnp.float32)
-    out = pl.pallas_call(
-        functools.partial(
-            score_kernel, layouts, aligned, len(pieces), len(landed) if first else None
+    smem = pl.BlockSpec(memory_space=pltpu.SMEM)
+    totals = jax.ShapeDtypeStruct((total, across), jnp.float32)
+    semaphores = [
+        pltpu.SemaphoreType.DMA((slots,)),
+        pltpu.SemaphoreType.DMA((slots if aligned else 1, len(pieces))),
+    ]
+    buffers = [
+        pltpu.VMEM((total, width), pieces[0].dtype),
+        pltpu.VMEM((width, across), folds[0].dtype),
+    ]
+    options = dict(
+        compiler_params=pltpu.CompilerParams(vmem_limit_bytes=58 * 1024 * 1024),
+        cost_estimate=pl.CostEstimate(
+            flops=1,
+            bytes_accessed=1 if extras else 2 * (total + across) * width,
+            transcendentals=0,
         ),
-        in_specs=[pl.BlockSpec(memory_space=pltpu.SMEM)]
-        + [vmem] * 2
-        + ([vmem] * (2 + len(landed)) if first else [vmem, anywhere])
-        + [anywhere] * (len(pieces) + len(folds)),
-        out_specs=[vmem] * 2 if first else vmem,
-        out_shape=[scores, jax.ShapeDtypeStruct(weights.shape, jnp.float32)] if first else scores,
-        scratch_shapes=([] if first else [weight_scratch])
-        + [
-            pltpu.VMEM((total, width), pieces[0].dtype),
-            pltpu.VMEM((width, across), folds[0].dtype),
-            pltpu.VMEM((total, across), jnp.float32),
-            pltpu.SemaphoreType.DMA((slots,)),
-            pltpu.SemaphoreType.DMA((slots if aligned else 1, len(pieces))),
-            pltpu.SemaphoreType.DMA,
-        ],
-        compiler_params=pltpu.CompilerParams(vmem_limit_bytes=58 * 1024 * 1024),
-        cost_estimate=pl.CostEstimate(flops=1, bytes_accessed=1, transcendentals=0),
-    )(position, membership, query_sum, *values, *(landed or []), *pieces, *folds)
-    return out
-
-
-def partial_scores(
-    pieces, held, orders, position, mask, membership, query_sum, sequences, chosen, landed
-):
-    halves_of = [[], []]
+    )
+    if not extras:
+        return pl.pallas_call(
+            functools.partial(first_kernel, layouts, len(pieces)),
+            in_specs=[smem] + [anywhere] * (len(pieces) + len(folds)),
+            out_specs=vmem,
+            out_shape=totals,
+            scratch_shapes=buffers + semaphores,
+            **options,
+        )(position, *pieces, *folds)
+    scores = jax.ShapeDtypeStruct((SEG_DEV, query_sum.shape[1]), jnp.float32)
+    return pl.pallas_call(
+        functools.partial(last_kernel, layouts, aligned, len(pieces), len(extras), group),
+        in_specs=[smem, vmem] + [anywhere] * (len(extras) + len(pieces) + len(folds)),
+        out_specs=[vmem] * group,
+        out_shape=[scores] * group,
+        scratch_shapes=buffers
+        + [pltpu.VMEM(totals.shape, jnp.float32)]
+        + semaphores
+        + [pltpu.SemaphoreType.DMA((len(extras),))]
+        + [pltpu.VMEM(extra.shape, extra.dtype) for extra in extras],
+        **options,
+    )(position, query_sum, *extras, *pieces, *folds)
+
+
+def output_layouts(orders):
+    sides = [[], []]
     for n, order in enumerate(orders):
         relatives = slot_order(order)
         middle = len(relatives) // 2
-        for side in range(2):
-            chunk = relatives[side * middle : (side + 1) * middle]
-            halves_of[side].append((chunk, n, len(orders)))
-    firsts, lasts = held[0::2], held[1::2]
-    if held[0].shape[1] % 128 != 0:
-        scores, _ = score_call(
-            position,
-            membership,
-            query_sum,
-            sequences,
-            [mask, chosen],
-            landed,
-            pieces,
-            firsts + lasts,
-            halves_of[0] + halves_of[1],
-            False,
-        )
-        return scores
-    scores, weights = score_call(
-        position,
-        membership,
-        query_sum,
-        sequences,
-        [mask, chosen],
-        landed,
-        pieces,
-        firsts,
-        halves_of[0],
-        True,
-    )
-    return score_call(
-        position,
-        membership,
-        query_sum,
-        sequences,
-        [scores, weights],
-        None,
-        pieces,
-        lasts,
-        halves_of[1],
-        True,
-    )
+        sides[0].append((relatives[:middle], n, len(orders)))
+        sides[1].append((relatives[middle:], n, len(orders)))
+    return sides
 
 
 def per_device(
@@ -547,14 +510,19 @@
         return lax.ppermute(packed, "dp", flip(blocks, 1 << bit))
 
     def joined(keep, landed, exponent):
-        values, there = unpack(landed)
-        total = keep + values
+        half = (keep.shape[0] - TAIL) // 2
+        there = landed[2 * half : 2 * half + 1].astype(jnp.float32)
         exponent = jnp.maximum(exponent, there) + 1
-        return total, exponent, total[: (total.shape[0] - TAIL) // 2 + TAIL]
+        packed = pack(keep, landed, there, exponent)
+        here = slice(0, half + TAIL)
+        values = landed[here].astype(jnp.float32) * jnp.exp2(there - TOP_EXPONENT)
+        return packed, exponent, keep[here] + values
 
     def own_shard(keep, landed):
-        total = (keep + unpack(landed)[0]).astype(jnp.bfloat16)
-        return total[: total.shape[0] - TAIL].reshape(halves, -1, columns)
+        rows = keep.shape[0] - TAIL
+        there = landed[rows : rows + 1].astype(jnp.float32)
+        values = landed[:rows].astype(jnp.float32) * jnp.exp2(there - TOP_EXPONENT)
+        return (keep[:rows] + values).astype(jnp.bfloat16).reshape(halves, -1, columns)
 
     def exchange(shard):
         pieces = [shard[0]] + [
@@ -594,25 +562,25 @@
     landed_first, *input_parts = tie(landed_first, *input_parts)
     input_parts = [from_half(part, d) for d, part in enumerate(input_parts)]
 
-    total, exponent_first, keep_first = joined(keep_first, landed_first, exponent_first)
-    landed_first = send(pack(total, exponent_first), order_first[1])
-    total, exponent_second, keep_second = joined(keep_second, landed_second, exponent_second)
-    packed_second = pack(total, exponent_second)
+    packed_first, exponent_first, keep_first = joined(keep_first, landed_first, exponent_first)
+    landed_first = send(packed_first, order_first[1])
+    packed_second, exponent_second, keep_second = joined(
+        keep_second, landed_second, exponent_second
+    )
     gate_gradient, packed_second = tie(gate_gradient, packed_second)
     landed_second = send(packed_second, order_second[1])
-    own_gradient, early, late = flattened_parts(
-        gate_gradient, position, halves, tokens // 16 // 4
-    )
+    own_gradient, *away = flattened_parts(gate_gradient, position, halves, (2,))
     landed_first, own_gradient = tie(landed_first, own_gradient)
 
     for bit in order_first[2:]:
-        total, exponent_first, keep_first = joined(keep_first, landed_first, exponent_first)
-        landed_first = send(pack(total, exponent_first), bit)
+        packed_first, exponent_first, keep_first = joined(
+            keep_first, landed_first, exponent_first
+        )
+        landed_first = send(packed_first, bit)
     for bit in order_second[2:]:
-        total, exponent_second, keep_second = joined(
+        packed_second, exponent_second, keep_second = joined(
             keep_second, landed_second, exponent_second
         )
-        packed_second = pack(total, exponent_second)
         packed_second, landed_first = tie(packed_second, landed_first)
         landed_second = send(packed_second, bit)
     own_half, *input_parts = input_parts
@@ -621,7 +589,7 @@
     for part in input_parts:
         input_pieces += [part, from_core(part)]
     swapped_gradient = from_core(own_gradient)
-    mask, membership = masks(position, input_pieces, top, halves, columns)
+    mask, small_mask, membership = masks(position, input_pieces, top, halves, columns)
     query_sum = jnp.asarray(
         np.arange(columns)[:, None] // RANK == np.arange(queries)[None, :], jnp.float32
     )
@@ -636,56 +604,64 @@
     def both(held, landed):
         return [jnp.concatenate(pair) for pair in zip(held, landed)]
 
-    shard_first, *early = tie(exchange(shard_first), *early)
-    early = [from_half(part, d) for d, part in zip(others, early)]
+    shard_first, *away[0] = tie(exchange(shard_first), *away[0])
+    away[0] = [from_half(part, d) for d, part in zip(others, away[0])]
     held_first = shard_first[None]
     landed_first = send(held_first, order_second[-1])
-    landed_second, mask, membership, swapped_gradient = tie(
-        landed_second, mask, membership, swapped_gradient
+    landed_second, mask, small_mask, membership, swapped_gradient = tie(
+        landed_second, mask, small_mask, membership, swapped_gradient
     )
     shard_second = own_shard(keep_second, landed_second)
-    shard_second, landed_first, *early = tie(shard_second, landed_first, *early)
-    swapped_early = [from_core(part) for part in early]
-    shard_second, *late = tie(exchange(shard_second), *late)
+    shard_second, landed_first, *away[0] = tie(shard_second, landed_first, *away[0])
+    swapped = [[from_core(part) for part in away[0]]]
+    shard_second, *away[1] = tie(exchange(shard_second), *away[1])
     held_first = jnp.concatenate([held_first, landed_first])
-    late = [from_half(part, d) for d, part in zip(others, late)]
+    away[1] = [from_half(part, d) for d, part in zip(others, away[1])]
     held_second = split(shard_second)
     for stage in range(2, count):
         landed_first = send(held_first, order_second[-stage])
         landed = stage_of(held_second, 1 - stage)
-        landed_first, *landed = tie(landed_first, *landed, *swapped_early)
-        landed, swapped_early = landed[:2], landed[2:]
+        landed_first, *landed = tie(landed_first, *landed, *swapped[0])
+        landed, swapped[0] = landed[:2], landed[2:]
         held_first = jnp.concatenate([held_first, landed_first])
         held_second = both(held_second, landed)
     last_first = send(held_first, order_second[0])
     last_first, *landed = tie(last_first, *stage_of(held_second, 1 - count))
     held_second = both(held_second, landed)
     last_second = stage_of(held_second, 0)
-    held_output = [held_second[0], last_second[0], held_second[1], last_second[1]]
-
+    last_first, *away[1] = tie(last_first, *away[1])
+    swapped.append([from_core(part) for part in away[1]])
+
+    pieces = [own_gradient, swapped_gradient]
+    for d in range(halves - 1):
+        pieces += [part[d] for part in away] + [part[d] for part in swapped]
+    layouts = output_layouts(gather_orders)
+    aligned = held_second[0].shape[1] % 128 == 0
     chosen, sent = input_chosen(
         position, input_pieces, [held_first, last_first], [order_second], mask, top
     )
-    sent, *late = tie(sent, *late)
+    before = []
+    if aligned:
+        sent, *held_second = tie(sent, *held_second)
+        before = [
+            score_call(
+                position, query_sum, [], group, pieces, held_second, layouts[0], aligned
+            )
+        ]
+        held_second, layouts = last_second, layouts[1]
+    else:
+        held_second, layouts = held_second + last_second, layouts[0] + layouts[1]
     landed = [lax.ppermute(sent, "expert", flip(group, d * CORES)) for d in others]
-
-    gradient_pieces = [own_gradient, swapped_gradient]
-    for first_part, last_part, swapped_part in zip(early, late, swapped_early):
-        gradient_pieces += [first_part, last_part, swapped_part, from_core(last_part)]
-
-    partial = partial_scores(
-        gradient_pieces,
-        held_output,
-        gather_orders,
+    partial = score_call(
         position,
-        mask,
-        membership,
         query_sum,
-        group * SEG_DEV,
-        chosen,
-        landed,
-    )
-    partial = partial.reshape(group, SEG_DEV, queries)
+        [small_mask, membership, chosen, *landed, *before],
+        group,
+        pieces,
+        held_second,
+        layouts,
+        aligned,
+    )
     scores = partial[0]
     for d in range(1, group):
         scores = scores + lax.ppermute(partial[d], "expert", flip(group, d))

time: 177 us -> 164 us (0.927)
  waiting for transfers between devices: 65.8 us -> 56 us
  other arithmetic: 19.3 us -> 16 us
  starting transfers between devices: 31.3 us -> 34.3 us
    ppermute x1, waiting for transfers between devices: 6.71 us -> 0.54 us  [per_device(): lax.ppermute(sent, 'expert', flip(group, d * CORES))]
    add x4 -> x0, other arithmetic: 4.26 us -> none  [joined(): total = keep + values]
    convert_element_type x2, other arithmetic: 2.2 us -> 4.18 us  [pack(): return jnp.where(row < half, scaled, exponent).astype(jnp.float16)]
    ppermute x2, waiting for transfers between devices: 8.92 us -> 7.04 us  [exchange(): lax.ppermute(shard[d], 'expert', flip(group, d * CORES))]
    unnamed x42 -> x46, local copies, waits for them, and re-layouts: 3.61 us -> 3.02 us
  transfers between devices with their start and end apart: 29 -> 29, of which waited for: 15 -> 16; matrix products, arithmetic and copies ran while one was open for 9% -> 7% of each run, Pallas kernels for 21% -> 22%
where the time goes in v4:
time: 164 us
  waiting for transfers between devices  56 us (34%)
  Pallas kernels  53.2 us (32%)
  starting transfers between devices  34.3 us (21%)
  other arithmetic  16 us (10%)
  local copies, waits for them, and re-layouts  3.84 us (2%)
    ppermute x15, waiting for transfers between devices, send(): return lax.ppermute(packed, 'dp', flip(blocks, 1 << bit))  45.8 us
    ppermute x15, starting transfers between devices, send(): return lax.ppermute(packed, 'dp', flip(blocks, 1 << bit))  24.2 us
    pallas_call x2, Pallas kernels, fold_parts(): pl.pallas_call(functools.partial(fold_kernel, width, steps, upper), grid_...  21.1 us
    pallas_call x1, Pallas kernels, flattened_parts(): pl.pallas_call(functools.partial(flatten_kernel, halves, cuts), grid_spec...  7.49 us
    pallas_call x1, Pallas kernels, score_call(): pl.pallas_call(functools.partial(last_kernel, layouts, aligned, len(piece...  7.23 us
    ppermute x2, waiting for transfers between devices, exchange(): lax.ppermute(shard[d], 'expert', flip(group, d * CORES))  7.04 us
    pallas_call x1, Pallas kernels, score_call(): pl.pallas_call(functools.partial(first_kernel, layouts, len(pieces)), in_...  6.11 us
    pallas_call x1, Pallas kernels, input_chosen(): pl.pallas_call(functools.partial(input_kernel, top, layouts, len(pieces))...  5.54 us
  transfers between devices with their start and end apart: 29, of which 16 were waited for; matrix products, arithmetic and copies ran while one was open for 7% of the time, Pallas kernels for 22%

profile of v4, /device:TPU:0, one launch (start us, length us, event | category | flops | bytes accessed | tf_op | source)
XLA Modules:
  0.0 163.7 jit_solution(1763424785674741883)
XLA Ops:
  0.7 10.6 %shard_map.91 = (f32[3088,128]{1,0:T(8,128)}, f32[4112,128]{1,0:T(8,128)}) custom-call(s32[3]{0:T(128)} %pad_add_fusion.refs_0_.position_ref, bf16[6144,768]{1,0:T(8,128)(2,1)} %bitcast.70, bf16[6144,768]{1,0:T(8,128)(2,1)} %bitcast.71, bf16[6144,768]{1,0:T(8,128)(2,1)} %bitcast.72, bf16[6144,768]{1,0:T(8,128)(2,1)} %bitcast.73, ...), custom_call_target="tpu_custom_call" | custom-call | flops 1 | bytes 1 | tf_op jit(solution)/shard_map/pallas_call | solution.py:104
  11.2 1.9 %convert_element_type.78 = f16[4112,128]{1,0:T(8,128)(2,1)S(1)} convert(f32[4112,128]{1,0:T(8,128)} %get-tuple-element.65) | non-fusion elementwise | flops 526336 | bytes 3158016 | tf_op jit(solution)/shard_map/convert_element_type | solution.py:548
  13.3 1.0 convert_element_type.77
  14.3 3.0 %collective-permute-start.2 = (f16[3088,128]{1,0:T(8,128)(2,1)}, f16[3088,128]{1,0:T(8,128)(2,1)}, u32[]{:S(2)}, u32[]{:S(2)}) collective-permute-start(f16[3088,128]{1,0:T(8,128)(2,1)} %convert_element_type.77), channel_id=1, source_target_pairs={{0,8},{4,12},{8,0},{12,4},{16,24},{20,28},{24,16},{28,20},{1,9},{5... | collective-permute-start | bytes 2371592 | tf_op jit(solution)/shard_map/ppermute | solution.py:510
  17.3 1.5 collective-permute-start
  18.9 10.6 %shard_map.92 = (f32[3088,128]{1,0:T(8,128)}, f32[4112,128]{1,0:T(8,128)}) custom-call(s32[3]{0:T(128)} %pad_add_fusion.refs_0_.position_ref, bf16[6144,768]{1,0:T(8,128)(2,1)} %bitcast.74, bf16[6144,768]{1,0:T(8,128)(2,1)} %bitcast.75, bf16[6144,768]{1,0:T(8,128)(2,1)} %bitcast.76, bf16[6144,768]{1,0:T(8,128)(2,1)} %bitcast.77, ...), custom_call_target="tpu_custom_call" | custom-call | flops 1 | bytes 1 | tf_op jit(solution)/shard_map/pallas_call | solution.py:104
  30.2 3.3 %shard_map.93 = (bf16[128,3200]{1,0:T(8,128)(2,1)}, bf16[128,3200]{1,0:T(8,128)(2,1)}) custom-call(s32[3]{0:T(128)} %pad_add_fusion.refs_0_.position_ref, bf16[128,6144]{1,0:T(8,128)(2,1)} %source_ref, bf16[128,128]{1,0:T(8,128)(2,1)} %pad.4.extra_ref), custom_call_target="tpu_custom_call" | custom-call | flops 1 | bytes 1 | tf_op jit(solution)/shard_map/pallas_call | solution.py:150
  33.6 1.6 collective-permute-done.2
  35.9 2.3 %select_convert_fusion.1 = (f16[1552,128]{1,0:T(8,128)(2,1)}, f32[1552,128]{1,0:T(8,128)S(1)}) fusion(f32[3088,128]{1,0:T(8,128)S(1)} %copy-done.13, f32[128]{0:T(128)S(1)} %bitcast.85, f32[128]{0:T(128)S(1)} %get-tuple-element.123, f16[3088,128]{1,0:T(8,128)(2,1)} %collective-permute-done.2, f32[128]{0:T(128)S(1)} %get-tuple-element.136, ...), kind=kLoop, calls=%fused_computation.2 | loop fusion | flops 1787904 | bytes 3578896 | tf_op jit(solution)/shard_map/convert_element_type | solution.py:126
  38.3 2.8 %collective-permute-start.3 = (f16[1552,128]{1,0:T(8,128)(2,1)}, f16[1552,128]{1,0:T(8,128)(2,1)S(1)}, u32[]{:S(2)}, u32[]{:S(2)}) collective-permute-start(f16[1552,128]{1,0:T(8,128)(2,1)} %get-tuple-element.129), channel_id=1, source_target_pairs={{0,16},{4,20},{8,24},{12,28},{16,0},{20,4},{24,8},{28,12},{1,17},{... | collective-permute-start | bytes 1191944 | tf_op jit(solution)/shard_map/ppermute | solution.py:510
  41.0 1.0 collective-permute-done
  42.0 1.9 %select_convert_fusion = (f16[2064,128]{1,0:T(8,128)(2,1)}, f32[2064,128]{1,0:T(8,128)S(1)}) fusion(f32[4112,128]{1,0:T(8,128)S(1)} %copy-done.8, f16[4112,128]{1,0:T(8,128)(2,1)S(1)} %collective-permute-done, f32[128]{0:T(128)S(1)} %bitcast.84, f32[128]{0:T(128)S(1)} %get-tuple-element.125, f32[128]{0:T(128)S(1)} %get-tuple-element.133, ...), kind=kLoop, calls=%fused_computation | loop fusion | flops 2377728 | bytes 4759056 | tf_op jit(solution)/shard_map/convert_element_type | solution.py:126
  44.5 1.5 collective-permute-start.7
  46.0 7.5 %shard_map.94 = (bf16[256,4096]{1,0:T(8,128)(2,1)}, bf16[64,4096]{1,0:T(8,128)(2,1)}, bf16[192,4096]{1,0:T(8,128)(2,1)}) custom-call(s32[3]{0:T(128)} %pad_add_fusion.refs_0_.position_ref, bf16[128,2,8192]{2,1,0:T(2,128)(2,1)} %source_ref.1), custom_call_target="tpu_custom_call" | custom-call | flops 1 | bytes 8388608 | tf_op jit(solution)/shard_map/pallas_call | solution.py:198
  53.5 4.9 %collective-permute-done.3 = f16[1552,128]{1,0:T(8,128)(2,1)S(1)} collective-permute-done((f16[1552,128]{1,0:T(8,128)(2,1)}, f16[1552,128]{1,0:T(8,128)(2,1)S(1)}, u32[]{:S(2)}, u32[]{:S(2)}) %collective-permute-start.3) | collective-permute-done | bytes 397344 | tf_op jit(solution)/shard_map/ppermute | solution.py:510
  58.6 1.4 collective-permute-start.4
  60.0 4.3 %collective-permute-done.1 = f16[2064,128]{1,0:T(8,128)(2,1)S(1)} collective-permute-done((f16[2064,128]{1,0:T(8,128)(2,1)}, f16[2064,128]{1,0:T(8,128)(2,1)S(1)}, u32[]{:S(2)}, u32[]{:S(2)}) %collective-permute-start.1) | collective-permute-done | bytes 528416 | tf_op jit(solution)/shard_map/ppermute | solution.py:510
  66.3 1.0 collective-permute-start.5
  67.3 1.6 collective-permute-start.10
  68.9 3.3 %collective-permute-done.10 = bf16[384,128]{1,0:T(8,128)(2,1)S(1)} collective-permute-done((bf16[384,128]{1,0:T(8,128)(2,1)S(1)}, bf16[384,128]{1,0:T(8,128)(2,1)S(1)}, u32[]{:S(2)}, u32[]{:S(2)}) %collective-permute-start.10) | collective-permute-done | bytes 98336 | tf_op jit(solution)/shard_map/ppermute | solution.py:529
  72.9 1.5 collective-permute-start.12
  75.4 1.9 %collective-permute-start.11 = (bf16[1,384,256]{2,1,0:T(8,128)(2,1)}, bf16[1,384,256]{2,1,0:T(8,128)(2,1)S(1)}, u32[]{:S(2)}, u32[]{:S(2)}) collective-permute-start(bf16[1,384,256]{2,1,0:T(8,128)(2,1)} %bitcast.26), channel_id=1, source_target_pairs={{0,16},{4,20},{8,24},{12,28},{16,0},{20,4},{24,8},{28,12},{1,17},{... | collective-permute-start | bytes 589832 | tf_op jit(solution)/shard_map/ppermute | solution.py:510
  77.2 2.4 %shard_map.95 = (f32[2,1024,128]{2,1,0:T(8,128)}, bf16[2,1024,128]{2,1,0:T(8,128)(2,1)}, bf16[1024,128]{1,0:T(8,128)(2,1)}) custom-call(s32[3]{0:T(128)} %pad_add_fusion.refs_0_.position_ref, bf16[128,3200]{1,0:T(8,128)(2,1)} %get-tuple-element.82.refs_0_, bf16[128,3200]{1,0:T(8,128)(2,1)} %copy-done.5, bf16[128,3200]{1,0:T(8,128)(2,1)} %copy-done.4, ...), custom_call_target="tpu_custom_call" | custom-call | flops 1 | bytes 1 | tf_op jit(solution)/shard_map/pallas_call | solution.py:248
  79.6 7.1 %collective-permute-done.5 = f16[1040,128]{1,0:T(8,128)(2,1)} collective-permute-done((f16[1040,128]{1,0:T(8,128)(2,1)}, f16[1040,128]{1,0:T(8,128)(2,1)}, u32[]{:S(2)}, u32[]{:S(2)}) %collective-permute-start.5) | collective-permute-done | bytes 266272 | tf_op jit(solution)/shard_map/ppermute | solution.py:510
  87.4 1.2 fusion.4
  88.6 1.8 %collective-permute-done.11 = bf16[1,384,256]{2,1,0:T(8,128)(2,1)S(1)} collective-permute-done((bf16[1,384,256]{2,1,0:T(8,128)(2,1)}, bf16[1,384,256]{2,1,0:T(8,128)(2,1)S(1)}, u32[]{:S(2)}, u32[]{:S(2)}) %collective-permute-start.11) | collective-permute-done | bytes 196640 | tf_op jit(solution)/shard_map/ppermute | solution.py:510
  90.4 1.4 collective-permute-start.14
  91.8 3.7 %collective-permute-done.14 = bf16[512,128]{1,0:T(8,128)(2,1)S(1)} collective-permute-done((bf16[512,128]{1,0:T(8,128)(2,1)S(1)}, bf16[512,128]{1,0:T(8,128)(2,1)S(1)}, u32[]{:S(2)}, u32[]{:S(2)}) %collective-permute-start.14) | collective-permute-done | bytes 131104 | tf_op jit(solution)/shard_map/ppermute | solution.py:529
  95.5 1.4 collective-permute-start.21
  98.0 3.0 %collective-permute-start.15 = (bf16[1,256,256]{2,1,0:T(8,128)(2,1)S(1)}, bf16[1,256,256]{2,1,0:T(8,128)(2,1)S(1)}, u32[]{:S(2)}, u32[]{:S(2)}) collective-permute-start(bf16[1,256,256]{2,1,0:T(8,128)(2,1)S(1)} %get-tuple-element.144), channel_id=1, source_target_pairs={{0,16},{4,20},{8,24},{12,28},{16,0},{20,4},{24,8},{28,12},{1,17},{... | collective-permute-start | bytes 393224 | tf_op jit(solution)/shard_map/ppermute | solution.py:510
  101.0 1.5 collective-permute-start.16
  102.5 7.6 %collective-permute-done.15 = bf16[1,256,256]{2,1,0:T(8,128)(2,1)S(1)} collective-permute-done((bf16[1,256,256]{2,1,0:T(8,128)(2,1)S(1)}, bf16[1,256,256]{2,1,0:T(8,128)(2,1)S(1)}, u32[]{:S(2)}, u32[]{:S(2)}) %collective-permute-start.15) | collective-permute-done | bytes 131104 | tf_op jit(solution)/shard_map/ppermute | solution.py:510
  110.1 2.2 %collective-permute-done.13 = bf16[2,384,256]{2,1,0:T(8,128)(2,1)S(1)} collective-permute-done((bf16[2,384,256]{2,1,0:T(8,128)(2,1)S(1)}, bf16[2,384,256]{2,1,0:T(8,128)(2,1)S(1)}, u32[]{:S(2)}, u32[]{:S(2)}) %collective-permute-start.13) | collective-permute-done | bytes 393248 | tf_op jit(solution)/shard_map/ppermute | solution.py:510
  112.3 1.2 pad_maximum_fusion.refs_4_
  113.6 1.6 collective-permute-start.18
  115.1 1.3 collective-permute-start.20
  116.5 1.8 %collective-permute-start.19 = (bf16[2,256,256]{2,1,0:T(8,128)(2,1)S(1)}, bf16[2,256,256]{2,1,0:T(8,128)(2,1)S(1)}, u32[]{:S(2)}, u32[]{:S(2)}) collective-permute-start(bf16[2,256,256]{2,1,0:T(8,128)(2,1)S(1)} %pad_maximum_fusion.5), channel_id=1, source_target_pairs={{0,8},{4,12},{8,0},{12,4},{16,24},{20,28},{24,16},{28,20},{1,9},{5... | collective-permute-start | bytes 786440 | tf_op jit(solution)/shard_map/ppermute | solution.py:510
  118.2 11.1 %collective-permute-done.20 = bf16[2,256,256]{2,1,0:T(8,128)(2,1)S(1)} collective-permute-done((bf16[2,256,256]{2,1,0:T(8,128)(2,1)S(1)}, bf16[2,256,256]{2,1,0:T(8,128)(2,1)S(1)}, u32[]{:S(2)}, u32[]{:S(2)}) %collective-permute-start.20) | collective-permute-done | bytes 262176 | tf_op jit(solution)/shard_map/ppermute | solution.py:510
  129.4 3.4 %collective-permute-done.18.refs_5_ = bf16[4,384,256]{2,1,0:T(8,128)(2,1)S(1)} collective-permute-done((bf16[4,384,256]{2,1,0:T(8,128)(2,1)S(1)}, bf16[4,384,256]{2,1,0:T(8,128)(2,1)S(1)}, u32[]{:S(2)}, u32[]{:S(2)}) %collective-permute-start.18) | collective-permute-done | bytes 786464 | tf_op jit(solution)/shard_map/ppermute | solution.py:510
  133.0 1.5 collective-permute-start.25
  134.5 1.5 collective-permute-start.24
  136.0 5.5 %shard_map.96 = (f32[1024,128]{1,0:T(8,128)}, bf16[1024,128]{1,0:T(8,128)(2,1)}) custom-call(s32[3]{0:T(128)} %pad_add_fusion.refs_0_.position_ref, f32[2,1024,128]{2,1,0:T(8,128)} %get-tuple-element.92.mask_ref, bf16[128,3200]{1,0:T(8,128)(2,1)} %get-tuple-element.82.refs_0_, bf16[128,3200]{1,0:T(8,128)(2,1)} %copy-done.5, bf16[128,3200]{1,0:T(8,128)(2,1)} %copy-done.4, ...), custom_call_target="tpu_custom_call" | custom-call | flops 1 | bytes 1 | tf_op jit(solution)/shard_map/pallas_call | solution.py:307
  142.2 1.1 copy-done.2
  143.3 6.1 %shard_map.97.refs_5_ = f32[1024,256]{1,0:T(8,128)} custom-call(s32[3]{0:T(128)} %pad_add_fusion.refs_0_.position_ref, bf16[256,4096]{1,0:T(8,128)(2,1)} %get-tuple-element.89.refs_0_.refs_6_, bf16[256,4096]{1,0:T(8,128)(2,1)} %copy-done, bf16[64,4096]{1,0:T(8,128)(2,1)} %collective-permute-done.12.refs_2_.refs_8_, bf16[192,4096]{1,0:T(8,128)(2,1)} %copy-done.1, ...), custom_call_target="tpu_custom_call" | custom-call | flops 1 | bytes 5242880 | tf_op jit(solution)/shard_map/pallas_call | solution.py:454
  150.7 7.2 %shard_map.98 = (f32[4,4]{1,0:T(4,128)}, f32[4,4]{1,0:T(4,128)}, f32[4,4]{1,0:T(4,128)}, f32[4,4]{1,0:T(4,128)}) custom-call(s32[3]{0:T(128)} %pad_add_fusion.refs_0_.position_ref, f32[128,4]{1,0:T(8,128)} %constant.71.clone.refs_0_, bf16[2,1024,128]{2,1,0:T(8,128)(2,1)} %get-tuple-element.90.refs_1_, bf16[1024,128]{1,0:T(8,128)(2,1)} %get-tuple-element.91.refs_2_, ...), custom_call_target="tpu_custom_call" | custom-call | flops 1 | bytes 1 | tf_op jit(solution)/shard_map/pallas_call | solution.py:463
  158.0 1.2 collective-permute-start.27
  159.9 1.8 %collective-permute-done.27 = f32[4,4]{1,0:T(4,128)S(1)} collective-permute-done((f32[4,4]{1,0:T(4,128)}, f32[4,4]{1,0:T(4,128)S(1)}, u32[]{:S(2)}, u32[]{:S(2)}) %collective-permute-start.27) | collective-permute-done | bytes 96 | tf_op jit(solution)/shard_map/ppermute | solution.py:667
  162.5 1.3 add_add_fusion
  (106 shorter events, 12.2 us)
Async XLA Ops:
  13.3 5.5 %copy-start.21 = (s32[128,2]{0,1:T(2,128)S(1)}, s32[128,2]{0,1:T(2,128)}, u32[]{:S(2)}) copy-start(s32[128,2]{0,1:T(2,128)} %param.11) | copy-start | bytes 3076
  13.3 5.6 %copy-start.22 = (s32[1,128]{1,0:T(1,128)S(1)}, s32[1,128]{1,0:T(1,128)}, u32[]{:S(2)}) copy-start(s32[1,128]{1,0:T(1,128)} %param.12) | copy-start | bytes 1540
  14.3 21.0 %collective-permute-start.2 = (f16[3088,128]{1,0:T(8,128)(2,1)}, f16[3088,128]{1,0:T(8,128)(2,1)}, u32[]{:S(2)}, u32[]{:S(2)}) collective-permute-start(f16[3088,128]{1,0:T(8,128)(2,1)} %convert_element_type.77), channel_id=1, source_target_pairs={{0,8},{4,12},{8,0},{12,4},{16,24},{20,28},{24,16},{28,20},{1,9},{5... | collective-permute-start | bytes 2371592 | tf_op jit(solution)/shard_map/ppermute | solution.py:510
  17.3 24.7 %collective-permute-start = (f16[4112,128]{1,0:T(8,128)(2,1)S(1)}, f16[4112,128]{1,0:T(8,128)(2,1)S(1)}, u32[]{:S(2)}, u32[]{:S(2)}) collective-permute-start(f16[4112,128]{1,0:T(8,128)(2,1)S(1)} %convert_element_type.78), channel_id=1, source_target_pairs={{0,4},{4,0},{8,12},{12,8},{16,20},{20,16},{24,28},{28,24},{1,5},{5... | collective-permute-start | bytes 3158024 | tf_op jit(solution)/shard_map/ppermute | solution.py:510
  29.4 4.1 %copy-start.12 = (bf16[1,768,128]{2,1,0:T(8,128)(2,1)S(1)}, bf16[1,768,128]{2,1,0:T(8,128)(2,1)}, u32[]{:S(2)}) copy-start(bf16[1,768,128]{2,1,0:T(8,128)(2,1)} %param.15) | copy-start | bytes 589828
  29.5 4.1 %copy-start.7 = (bf16[1,1024,128]{2,1,0:T(8,128)(2,1)S(1)}, bf16[1,1024,128]{2,1,0:T(8,128)(2,1)}, u32[]{:S(2)}) copy-start(bf16[1,1024,128]{2,1,0:T(8,128)(2,1)} %param.16) | copy-start | bytes 786436
  29.6 6.3 %copy-start.13 = (f32[3088,128]{1,0:T(8,128)S(1)}, f32[3088,128]{1,0:T(8,128)}, u32[]{:S(2)}) copy-start(f32[3088,128]{1,0:T(8,128)} %get-tuple-element.72) | copy-start | bytes 4743172
  35.9 6.1 %copy-start.8 = (f32[4112,128]{1,0:T(8,128)S(1)}, f32[4112,128]{1,0:T(8,128)}, u32[]{:S(2)}) copy-start(f32[4112,128]{1,0:T(8,128)} %get-tuple-element.68) | copy-start | bytes 6316036
  38.3 20.1 %collective-permute-start.3 = (f16[1552,128]{1,0:T(8,128)(2,1)}, f16[1552,128]{1,0:T(8,128)(2,1)S(1)}, u32[]{:S(2)}, u32[]{:S(2)}) collective-permute-start(f16[1552,128]{1,0:T(8,128)(2,1)} %get-tuple-element.129), channel_id=1, source_target_pairs={{0,16},{4,20},{8,24},{12,28},{16,0},{20,4},{24,8},{28,12},{1,17},{... | collective-permute-start | bytes 1191944 | tf_op jit(solution)/shard_map/ppermute | solution.py:510
  42.0 4.0 %copy-start.3 = (bf16[128,3200]{1,0:T(8,128)(2,1)S(1)}, bf16[128,3200]{1,0:T(8,128)(2,1)}, u32[]{:S(2)}) copy-start(bf16[128,3200]{1,0:T(8,128)(2,1)} %get-tuple-element.82.refs_0_) | copy-start | bytes 2457604
  43.9 20.3 %collective-permute-start.1 = (f16[2064,128]{1,0:T(8,128)(2,1)}, f16[2064,128]{1,0:T(8,128)(2,1)S(1)}, u32[]{:S(2)}, u32[]{:S(2)}) collective-permute-start(f16[2064,128]{1,0:T(8,128)(2,1)} %get-tuple-element.70), channel_id=1, source_target_pairs={{0,8},{4,12},{8,0},{12,4},{16,24},{20,28},{24,16},{28,20},{1,9},{5... | collective-permute-start | bytes 1585160 | tf_op jit(solution)/shard_map/ppermute | solution.py:510
  44.5 21.7 %collective-permute-start.7 = (bf16[128,3200]{1,0:T(8,128)(2,1)}, bf16[128,3200]{1,0:T(8,128)(2,1)S(1)}, u32[]{:S(2)}, u32[]{:S(2)}) collective-permute-start(bf16[128,3200]{1,0:T(8,128)(2,1)} %get-tuple-element.84), channel_id=1, source_target_pairs={{0,2},{1,3},{2,0},{3,1},{4,6},{5,7},{6,4},{7,5},{8,10},{9,11},{10,... | collective-permute-start | bytes 2457608 | tf_op jit(solution)/shard_map/ppermute | solution.py:534
  46.0 28.4 %collective-permute-start.6 = (bf16[128,3200]{1,0:T(8,128)(2,1)S(1)}, bf16[128,3200]{1,0:T(8,128)(2,1)S(1)}, u32[]{:S(2)}, u32[]{:S(2)}) collective-permute-start(bf16[128,3200]{1,0:T(8,128)(2,1)S(1)} %copy-done.3), channel_id=1, source_target_pairs={{0,1},{1,0},{2,3},{3,2},{4,5},{5,4},{6,7},{7,6},{8,9},{9,8},{10,11... | collective-permute-start | bytes 2457608 | tf_op jit(solution)/shard_map/ppermute | solution.py:537
  58.4 5.9 %copy-start.16 = (f16[1552,128]{1,0:T(8,128)(2,1)}, f16[1552,128]{1,0:T(8,128)(2,1)S(1)}, u32[]{:S(2)}) copy-start(f16[1552,128]{1,0:T(8,128)(2,1)S(1)} %collective-permute-done.3) | copy-start | bytes 1191940
  58.4 28.3 %collective-permute-start.9 = (bf16[256,4096]{1,0:T(8,128)(2,1)}, bf16[256,4096]{1,0:T(8,128)(2,1)S(1)}, u32[]{:S(2)}, u32[]{:S(2)}) collective-permute-start(bf16[256,4096]{1,0:T(8,128)(2,1)} %get-tuple-element.89.refs_0_.refs_6_), channel_id=1, source_target_pairs={{0,1},{1,0},{2,3},{3,2},{4,5},{5,4},{6,7},{7,6},{8,9},{9,8},{10,11... | collective-permute-start | bytes 6291464 | tf_op jit(solution)/shard_map/ppermute | solution.py:537
  58.6 7.5 %collective-permute-start.4 = (f16[784,128]{1,0:T(8,128)(2,1)S(1)}, f16[784,128]{1,0:T(8,128)(2,1)S(1)}, u32[]{:S(2)}, u32[]{:S(2)}) collective-permute-start(f16[784,128]{1,0:T(8,128)(2,1)S(1)} %get-tuple-element.135), channel_id=1, source_target_pairs={{0,4},{4,0},{8,12},{12,8},{16,20},{20,16},{24,28},{28,24},{1,5},{5... | collective-permute-start | bytes 602120 | tf_op jit(solution)/shard_map/ppermute | solution.py:510
  64.2 10.2 %copy-start.15 = (f16[2064,128]{1,0:T(8,128)(2,1)}, f16[2064,128]{1,0:T(8,128)(2,1)S(1)}, u32[]{:S(2)}) copy-start(f16[2064,128]{1,0:T(8,128)(2,1)S(1)} %collective-permute-done.1) | copy-start | bytes 1585156
  66.2 8.3 %copy-start.4 = (bf16[128,3200]{1,0:T(8,128)(2,1)}, bf16[128,3200]{1,0:T(8,128)(2,1)S(1)}, u32[]{:S(2)}) copy-start(bf16[128,3200]{1,0:T(8,128)(2,1)S(1)} %collective-permute-done.7.refs_2_) | copy-start | bytes 2457604
  66.2 11.0 %collective-permute-start.8 = (bf16[128,3200]{1,0:T(8,128)(2,1)S(1)}, bf16[128,3200]{1,0:T(8,128)(2,1)}, u32[]{:S(2)}, u32[]{:S(2)}) collective-permute-start(bf16[128,3200]{1,0:T(8,128)(2,1)S(1)} %collective-permute-done.7.refs_2_), channel_id=1, source_target_pairs={{0,1},{1,0},{2,3},{3,2},{4,5},{5,4},{6,7},{7,6},{8,9},{9,8},{10,11... | collective-permute-start | bytes 2457608 | tf_op jit(solution)/shard_map/ppermute | solution.py:537
  66.3 20.4 %collective-permute-start.5 = (f16[1040,128]{1,0:T(8,128)(2,1)}, f16[1040,128]{1,0:T(8,128)(2,1)}, u32[]{:S(2)}, u32[]{:S(2)}) collective-permute-start(f16[1040,128]{1,0:T(8,128)(2,1)} %get-tuple-element.81), channel_id=1, source_target_pairs={{0,16},{4,20},{8,24},{12,28},{16,0},{20,4},{24,8},{28,12},{1,17},{... | collective-permute-start | bytes 798728 | tf_op jit(solution)/shard_map/ppermute | solution.py:510
  67.3 4.9 %collective-permute-start.10 = (bf16[384,128]{1,0:T(8,128)(2,1)S(1)}, bf16[384,128]{1,0:T(8,128)(2,1)S(1)}, u32[]{:S(2)}, u32[]{:S(2)}) collective-permute-start(bf16[384,128]{1,0:T(8,128)(2,1)S(1)} %get-tuple-element.148), channel_id=1, source_target_pairs={{0,2},{1,3},{2,0},{3,1},{4,6},{5,7},{6,4},{7,5},{8,10},{9,11},{10,... | collective-permute-start | bytes 294920 | tf_op jit(solution)/shard_map/ppermute | solution.py:529
  72.9 17.4 %collective-permute-start.12 = (bf16[64,4096]{1,0:T(8,128)(2,1)}, bf16[64,4096]{1,0:T(8,128)(2,1)}, u32[]{:S(2)}, u32[]{:S(2)}) collective-permute-start(bf16[64,4096]{1,0:T(8,128)(2,1)} %get-tuple-element.97), channel_id=1, source_target_pairs={{0,2},{1,3},{2,0},{3,1},{4,6},{5,7},{6,4},{7,5},{8,10},{9,11},{10,... | collective-permute-start | bytes 1572872 | tf_op jit(solution)/shard_map/ppermute | solution.py:534
  75.4 12.0 %slice-start = ((f16[2064,128]{1,0:T(8,128)(2,1)}), f16[1040,128]{1,0:T(8,128)(2,1)S(1)}, s32[]{:S(2)}) async-start(f16[2064,128]{1,0:T(8,128)(2,1)} %copy-done.15), calls=%async_computation | async-start | bytes 532480 | tf_op jit(solution)/shard_map/slice | solution.py:518
  75.4 15.0 %collective-permute-start.11 = (bf16[1,384,256]{2,1,0:T(8,128)(2,1)}, bf16[1,384,256]{2,1,0:T(8,128)(2,1)S(1)}, u32[]{:S(2)}, u32[]{:S(2)}) collective-permute-start(bf16[1,384,256]{2,1,0:T(8,128)(2,1)} %bitcast.26), channel_id=1, source_target_pairs={{0,16},{4,20},{8,24},{12,28},{16,0},{20,4},{24,8},{28,12},{1,17},{... | collective-permute-start | bytes 589832 | tf_op jit(solution)/shard_map/ppermute | solution.py:510
  86.7 8.8 %copy-start = (bf16[256,4096]{1,0:T(8,128)(2,1)}, bf16[256,4096]{1,0:T(8,128)(2,1)S(1)}, u32[]{:S(2)}) copy-start(bf16[256,4096]{1,0:T(8,128)(2,1)S(1)} %collective-permute-done.9.refs_1_.refs_7_) | copy-start | bytes 6291460
  87.4 8.2 %copy-start.20 = (bf16[192,4096]{1,0:T(8,128)(2,1)S(1)}, bf16[192,4096]{1,0:T(8,128)(2,1)}, u32[]{:S(2)}) copy-start(bf16[192,4096]{1,0:T(8,128)(2,1)} %get-tuple-element.107) | copy-start | bytes 4718596
  90.4 5.1 %collective-permute-start.14 = (bf16[512,128]{1,0:T(8,128)(2,1)S(1)}, bf16[512,128]{1,0:T(8,128)(2,1)S(1)}, u32[]{:S(2)}, u32[]{:S(2)}) collective-permute-start(bf16[512,128]{1,0:T(8,128)(2,1)S(1)} %get-tuple-element.146), channel_id=1, source_target_pairs={{0,2},{1,3},{2,0},{3,1},{4,6},{5,7},{6,4},{7,5},{8,10},{9,11},{10,... | collective-permute-start | bytes 393224 | tf_op jit(solution)/shard_map/ppermute | solution.py:529
  95.5 37.3 %collective-permute-start.21 = (bf16[192,4096]{1,0:T(8,128)(2,1)S(1)}, bf16[192,4096]{1,0:T(8,128)(2,1)S(1)}, u32[]{:S(2)}, u32[]{:S(2)}) collective-permute-start(bf16[192,4096]{1,0:T(8,128)(2,1)S(1)} %copy-done.20), channel_id=1, source_target_pairs={{0,2},{1,3},{2,0},{3,1},{4,6},{5,7},{6,4},{7,5},{8,10},{9,11},{10,... | collective-permute-start | bytes 4718600 | tf_op jit(solution)/shard_map/ppermute | solution.py:534
  97.0 15.4 %collective-permute-start.17 = (bf16[64,4096]{1,0:T(8,128)(2,1)}, bf16[64,4096]{1,0:T(8,128)(2,1)S(1)}, u32[]{:S(2)}, u32[]{:S(2)}) collective-permute-start(bf16[64,4096]{1,0:T(8,128)(2,1)} %collective-permute-done.12.refs_2_.refs_8_), channel_id=1, source_target_pairs={{0,1},{1,0},{2,3},{3,2},{4,5},{5,4},{6,7},{7,6},{8,9},{9,8},{10,11... | collective-permute-start | bytes 1572872 | tf_op jit(solution)/shard_map/ppermute | solution.py:537
  97.9 14.4 %collective-permute-start.13 = (bf16[2,384,256]{2,1,0:T(8,128)(2,1)S(1)}, bf16[2,384,256]{2,1,0:T(8,128)(2,1)S(1)}, u32[]{:S(2)}, u32[]{:S(2)}) collective-permute-start(bf16[2,384,256]{2,1,0:T(8,128)(2,1)S(1)} %pad_maximum_fusion.3), channel_id=1, source_target_pairs={{0,8},{4,12},{8,0},{12,4},{16,24},{20,28},{24,16},{28,20},{1,9},{5... | collective-permute-start | bytes 1179656 | tf_op jit(solution)/shard_map/ppermute | solution.py:510
  98.0 12.1 %collective-permute-start.15 = (bf16[1,256,256]{2,1,0:T(8,128)(2,1)S(1)}, bf16[1,256,256]{2,1,0:T(8,128)(2,1)S(1)}, u32[]{:S(2)}, u32[]{:S(2)}) collective-permute-start(bf16[1,256,256]{2,1,0:T(8,128)(2,1)S(1)} %get-tuple-element.144), channel_id=1, source_target_pairs={{0,16},{4,20},{8,24},{12,28},{16,0},{20,4},{24,8},{28,12},{1,17},{... | collective-permute-start | bytes 393224 | tf_op jit(solution)/shard_map/ppermute | solution.py:510
  101.0 9.1 %collective-permute-start.16 = (bf16[1,256,256]{2,1,0:T(8,128)(2,1)S(1)}, bf16[1,256,256]{2,1,0:T(8,128)(2,1)S(1)}, u32[]{:S(2)}, u32[]{:S(2)}) collective-permute-start(bf16[1,256,256]{2,1,0:T(8,128)(2,1)S(1)} %get-tuple-element.143), channel_id=1, source_target_pairs={{0,4},{4,0},{8,12},{12,8},{16,20},{20,16},{24,28},{28,24},{1,5},{5... | collective-permute-start | bytes 393224 | tf_op jit(solution)/shard_map/ppermute | solution.py:510
  112.3 4.1 %copy-start.9 = (bf16[64,4096]{1,0:T(8,128)(2,1)}, bf16[64,4096]{1,0:T(8,128)(2,1)S(1)}, u32[]{:S(2)}) copy-start(bf16[64,4096]{1,0:T(8,128)(2,1)S(1)} %collective-permute-done.17.refs_4_.refs_10_) | copy-start | bytes 1572868
  113.5 19.5 %copy-start.6 = (bf16[4,384,256]{2,1,0:T(8,128)(2,1)}, bf16[4,384,256]{2,1,0:T(8,128)(2,1)S(1)}, u32[]{:S(2)}) copy-start(bf16[4,384,256]{2,1,0:T(8,128)(2,1)S(1)} %pad_maximum_fusion.refs_4_) | copy-start | bytes 2359300
  113.6 19.2 %collective-permute-start.18 = (bf16[4,384,256]{2,1,0:T(8,128)(2,1)S(1)}, bf16[4,384,256]{2,1,0:T(8,128)(2,1)S(1)}, u32[]{:S(2)}, u32[]{:S(2)}) collective-permute-start(bf16[4,384,256]{2,1,0:T(8,128)(2,1)S(1)} %pad_maximum_fusion.refs_4_), channel_id=1, source_target_pairs={{0,4},{4,0},{8,12},{12,8},{16,20},{20,16},{24,28},{28,24},{1,5},{5... | collective-permute-start | bytes 2359304 | tf_op jit(solution)/shard_map/ppermute | solution.py:510
  115.1 14.2 %collective-permute-start.20 = (bf16[2,256,256]{2,1,0:T(8,128)(2,1)S(1)}, bf16[2,256,256]{2,1,0:T(8,128)(2,1)S(1)}, u32[]{:S(2)}, u32[]{:S(2)}) collective-permute-start(bf16[2,256,256]{2,1,0:T(8,128)(2,1)S(1)} %pad_maximum_fusion.6), channel_id=1, source_target_pairs={{0,16},{4,20},{8,24},{12,28},{16,0},{20,4},{24,8},{28,12},{1,17},{... | collective-permute-start | bytes 786440 | tf_op jit(solution)/shard_map/ppermute | solution.py:510
  116.5 12.9 %collective-permute-start.19 = (bf16[2,256,256]{2,1,0:T(8,128)(2,1)S(1)}, bf16[2,256,256]{2,1,0:T(8,128)(2,1)S(1)}, u32[]{:S(2)}, u32[]{:S(2)}) collective-permute-start(bf16[2,256,256]{2,1,0:T(8,128)(2,1)S(1)} %pad_maximum_fusion.5), channel_id=1, source_target_pairs={{0,8},{4,12},{8,0},{12,4},{16,24},{20,28},{24,16},{28,20},{1,9},{5... | collective-permute-start | bytes 786440 | tf_op jit(solution)/shard_map/ppermute | solution.py:510
  132.8 3.2 %copy-start.17 = (bf16[4,384,256]{2,1,0:T(8,128)(2,1)}, bf16[4,384,256]{2,1,0:T(8,128)(2,1)S(1)}, u32[]{:S(2)}) copy-start(bf16[4,384,256]{2,1,0:T(8,128)(2,1)S(1)} %collective-permute-done.18.refs_5_) | copy-start | bytes 2359300
  132.8 8.8 %copy-start.1 = (bf16[192,4096]{1,0:T(8,128)(2,1)}, bf16[192,4096]{1,0:T(8,128)(2,1)S(1)}, u32[]{:S(2)}) copy-start(bf16[192,4096]{1,0:T(8,128)(2,1)S(1)} %collective-permute-done.21.refs_3_.refs_9_) | copy-start | bytes 4718596
  132.8 9.4 %collective-permute-start.23 = (bf16[192,4096]{1,0:T(8,128)(2,1)S(1)}, bf16[192,4096]{1,0:T(8,128)(2,1)S(1)}, u32[]{:S(2)}, u32[]{:S(2)}) collective-permute-start(bf16[192,4096]{1,0:T(8,128)(2,1)S(1)} %collective-permute-done.21.refs_3_.refs_9_), channel_id=1, source_target_pairs={{0,1},{1,0},{2,3},{3,2},{4,5},{5,4},{6,7},{7,6},{8,9},{9,8},{10,11... | collective-permute-start | bytes 4718600 | tf_op jit(solution)/shard_map/ppermute | solution.py:537
  132.9 8.6 %copy-start.10 = (bf16[4,256,256]{2,1,0:T(8,128)(2,1)}, bf16[4,256,256]{2,1,0:T(8,128)(2,1)S(1)}, u32[]{:S(2)}) copy-start(bf16[4,256,256]{2,1,0:T(8,128)(2,1)S(1)} %pad_maximum_fusion.2.refs_7_) | copy-start | bytes 1572868
  133.0 8.6 %copy-start.11 = (bf16[4,256,256]{2,1,0:T(8,128)(2,1)}, bf16[4,256,256]{2,1,0:T(8,128)(2,1)S(1)}, u32[]{:S(2)}) copy-start(bf16[4,256,256]{2,1,0:T(8,128)(2,1)S(1)} %pad_maximum_fusion.1.refs_6_) | copy-start | bytes 1572868
  133.0 16.4 %collective-permute-start.25 = (bf16[4,256,256]{2,1,0:T(8,128)(2,1)S(1)}, bf16[4,256,256]{2,1,0:T(8,128)(2,1)}, u32[]{:S(2)}, u32[]{:S(2)}) collective-permute-start(bf16[4,256,256]{2,1,0:T(8,128)(2,1)S(1)} %pad_maximum_fusion.2.refs_7_), channel_id=1, source_target_pairs={{0,8},{4,12},{8,0},{12,4},{16,24},{20,28},{24,16},{28,20},{1,9},{5... | collective-permute-start | bytes 1572872 | tf_op jit(solution)/shard_map/ppermute | solution.py:510
  134.5 14.9 %collective-permute-start.24 = (bf16[4,256,256]{2,1,0:T(8,128)(2,1)S(1)}, bf16[4,256,256]{2,1,0:T(8,128)(2,1)S(1)}, u32[]{:S(2)}, u32[]{:S(2)}) collective-permute-start(bf16[4,256,256]{2,1,0:T(8,128)(2,1)S(1)} %pad_maximum_fusion.1.refs_6_), channel_id=1, source_target_pairs={{0,4},{4,0},{8,12},{12,8},{16,20},{20,16},{24,28},{28,24},{1,5},{5... | collective-permute-start | bytes 1572872 | tf_op jit(solution)/shard_map/ppermute | solution.py:510
  141.6 8.4 %collective-permute-start.22 = (bf16[1024,128]{1,0:T(8,128)(2,1)}, bf16[1024,128]{1,0:T(8,128)(2,1)S(1)}, u32[]{:S(2)}, u32[]{:S(2)}) collective-permute-start(bf16[1024,128]{1,0:T(8,128)(2,1)} %get-tuple-element.113), channel_id=1, source_target_pairs={{0,2},{1,3},{2,0},{3,1},{4,6},{5,7},{6,4},{7,5},{8,10},{9,11},{10,... | collective-permute-start | bytes 786440 | tf_op jit(solution)/shard_map/ppermute | solution.py:654
  157.9 1.9 %collective-permute-start.26 = (f32[4,4]{1,0:T(4,128)}, f32[4,4]{1,0:T(4,128)S(1)}, u32[]{:S(2)}, u32[]{:S(2)}) collective-permute-start(f32[4,4]{1,0:T(4,128)} %get-tuple-element.120), channel_id=1, source_target_pairs={{0,1},{1,0},{2,3},{3,2},{4,5},{5,4},{6,7},{7,6},{8,9},{9,8},{10,11... | collective-permute-start | bytes 200 | tf_op jit(solution)/shard_map/ppermute | solution.py:667
  158.0 3.7 %collective-permute-start.27 = (f32[4,4]{1,0:T(4,128)}, f32[4,4]{1,0:T(4,128)S(1)}, u32[]{:S(2)}, u32[]{:S(2)}) collective-permute-start(f32[4,4]{1,0:T(4,128)} %get-tuple-element.121), channel_id=1, source_target_pairs={{0,2},{1,3},{2,0},{3,1},{4,6},{5,7},{6,4},{7,5},{8,10},{9,11},{10,... | collective-permute-start | bytes 200 | tf_op jit(solution)/shard_map/ppermute | solution.py:667
  159.2 3.2 %collective-permute-start.28 = (f32[4,4]{1,0:T(4,128)}, f32[4,4]{1,0:T(4,128)S(1)}, u32[]{:S(2)}, u32[]{:S(2)}) collective-permute-start(f32[4,4]{1,0:T(4,128)} %get-tuple-element.122), channel_id=1, source_target_pairs={{0,3},{1,2},{2,1},{3,0},{4,7},{5,6},{6,5},{7,4},{8,11},{9,10},{10,... | collective-permute-start | bytes 200 | tf_op jit(solution)/shard_map/ppermute | solution.py:667
  (6 other events, 7.4 us)

commit v5 on v4

--- a/solution.py
+++ b/solution.py
@@ -164,52 +164,32 @@
     )(position, source, extra)
 
 
-def flatten_kernel(halves, cuts, position_ref, source_ref, *out_refs):
-    step = pl.program_id(0)
-    rows = source_ref.shape[0] * source_ref.shape[1]
-    width = source_ref.shape[2] // halves
-    for d in range(halves):
+def flatten_kernel(position_ref, source_ref, *out_refs):
+    rows, width = out_refs[0].shape
+    for d, out_ref in enumerate(out_refs):
         start = pl.multiple_of((position_ref[1] ^ d) * width, width)
-        part = source_ref[:, :, pl.ds(start, width)].reshape(rows, width)
-        if d == 0:
-            out_refs[0][...] = part
-            continue
-        for n in range(len(cuts) - 1):
-
-            @pl.when((step >= cuts[n]) & (step < cuts[n + 1]))
-            def _():
-                out_refs[1 + n * (halves - 1) + d - 1][...] = part
-
-
-def flattened_parts(source, position, halves, sizes):
+        out_ref[...] = source_ref[:, :, pl.ds(start, width)].reshape(rows, width)
+
+
+def flattened_parts(source, position, halves):
     tokens, top, width = source.shape
-    width = width // halves
-    block = 16
-    steps, rows = tokens // block, block * top
-    cuts = [sum(sizes[:n]) for n in range(len(sizes) + 1)] + [steps]
-
-    def out(first, last):
-        return pl.BlockSpec((rows, width), lambda i, p: (jnp.clip(i, first, last - 1) - first, 0))
-
-    specs, shapes = [out(0, steps)], [(tokens * top, width)]
-    for first, last in zip(cuts, cuts[1:]):
-        specs += [out(first, last)] * (halves - 1)
-        shapes += [((last - first) * rows, width)] * (halves - 1)
+    block = 32
+    out = (tokens * top, width // halves)
     own, *away = pl.pallas_call(
-        functools.partial(flatten_kernel, halves, cuts),
+        flatten_kernel,
         grid_spec=pltpu.PrefetchScalarGridSpec(
             num_scalar_prefetch=1,
-            grid=(steps,),
-            in_specs=[pl.BlockSpec((block, top, width * halves), lambda i, p: (i, 0, 0))],
-            out_specs=specs,
+            grid=(tokens // block,),
+            in_specs=[pl.BlockSpec((block, top, width), lambda i, p: (i, 0, 0))],
+            out_specs=[pl.BlockSpec((block * top, out[1]), lambda i, p: (i, 0))] * halves,
         ),
-        out_shape=[jax.ShapeDtypeStruct(shape, source.dtype) for shape in shapes],
+        out_shape=[jax.ShapeDtypeStruct(out, source.dtype)] * halves,
         compiler_params=pltpu.CompilerParams(vmem_limit_bytes=56 * 1024 * 1024),
         cost_estimate=pl.CostEstimate(
             flops=1, bytes_accessed=4 * source.size, transcendentals=0
         ),
     )(position, source)
-    return own, *[away[n : n + halves - 1] for n in range(0, len(away), halves - 1)]
+    return own, away
 
 
 def start_all(copies, done):
@@ -265,8 +245,8 @@
     )(position, *pieces)
 
 
-def input_kernel(top, layouts, count, position_ref, mask_ref, *refs):
-    *refs, out_ref, sent_ref, tokens_ref, held_ref, done = refs
+def input_kernel(top, layouts, count, position_ref, mask_in_ref, *refs):
+    *refs, out_ref, sent_ref, tokens_ref, held_ref, mask_ref, done = refs
     token_refs, fold_refs = refs[:count], refs[count:]
     rows = token_refs[0].shape[0]
     copies = [
@@ -278,9 +258,11 @@
         for slot, relative in enumerate(relatives):
             start = pl.multiple_of((relative ^ position_ref[0]) * block + offset, 16)
             copies.append((fold_ref.at[slot], held_ref.at[pl.ds(start, rows), :]))
-    for copy in start_all(copies, done):
+    *copies, mask_copy = start_all(copies + [(mask_in_ref, mask_ref)], done)
+    for copy in copies:
         copy.wait()
     terms = jnp.dot(tokens_ref[...], held_ref[...], preferred_element_type=jnp.float32)
+    mask_copy.wait()
     total = tokens_ref.shape[0]
     columns = out_ref.shape[1]
     for k in range(top):
@@ -306,8 +288,8 @@
     slots = sum(part.shape[0] for part in held)
     return pl.pallas_call(
         functools.partial(input_kernel, top, layouts, len(pieces)),
-        in_specs=[pl.BlockSpec(memory_space=pltpu.SMEM), pl.BlockSpec(memory_space=pltpu.VMEM)]
-        + [pl.BlockSpec(memory_space=pl.ANY)] * (len(pieces) + len(held)),
+        in_specs=[pl.BlockSpec(memory_space=pltpu.SMEM)]
+        + [pl.BlockSpec(memory_space=pl.ANY)] * (1 + len(pieces) + len(held)),
         out_specs=[pl.BlockSpec(memory_space=pltpu.VMEM)] * 2,
         out_shape=[
             jax.ShapeDtypeStruct((total * top, columns), jnp.float32),
@@ -316,7 +298,8 @@
         scratch_shapes=[
             pltpu.VMEM((total, width), pieces[0].dtype),
             pltpu.VMEM((width, across), held[0].dtype),
-            pltpu.SemaphoreType.DMA((len(pieces) + slots,)),
+            pltpu.VMEM(mask.shape, mask.dtype),
+            pltpu.SemaphoreType.DMA((len(pieces) + slots + 1,)),
         ],
         compiler_params=pltpu.CompilerParams(vmem_limit_bytes=58 * 1024 * 1024),
         cost_estimate=pl.CostEstimate(flops=1, bytes_accessed=1, transcendentals=0),
@@ -536,8 +519,8 @@
     def from_core(part):
         return lax.ppermute(part, "expert", flip(group, 1))
 
-    order_first = [(i + 1) % count for i in range(count)]
     order_second = list(range(count))
+    order_first = order_second[1::-1] + order_second[2:]
     position = jnp.stack([place, half, core]).astype(jnp.int32)
 
     def parts(bases, upper):
@@ -569,7 +552,7 @@
     )
     gate_gradient, packed_second = tie(gate_gradient, packed_second)
     landed_second = send(packed_second, order_second[1])
-    own_gradient, *away = flattened_parts(gate_gradient, position, halves, (2,))
+    own_gradient, away = flattened_parts(gate_gradient, position, halves)
     landed_first, own_gradient = tie(landed_first, own_gradient)
 
     for bit in order_first[2:]:
@@ -581,7 +564,7 @@
         packed_second, exponent_second, keep_second = joined(
             keep_second, landed_second, exponent_second
         )
-        packed_second, landed_first = tie(packed_second, landed_first)
+        keep_second, landed_first = tie(keep_second, landed_first)
         landed_second = send(packed_second, bit)
     own_half, *input_parts = input_parts
     shard_first, *input_parts = tie(own_shard(keep_first, landed_first), *input_parts)
@@ -604,42 +587,38 @@
     def both(held, landed):
         return [jnp.concatenate(pair) for pair in zip(held, landed)]
 
-    shard_first, *away[0] = tie(exchange(shard_first), *away[0])
-    away[0] = [from_half(part, d) for d, part in zip(others, away[0])]
+    shard_first = exchange(shard_first)
+    shard_first, landed_second = tie(shard_first, landed_second)
     held_first = shard_first[None]
     landed_first = send(held_first, order_second[-1])
-    landed_second, mask, small_mask, membership, swapped_gradient = tie(
-        landed_second, mask, small_mask, membership, swapped_gradient
-    )
-    shard_second = own_shard(keep_second, landed_second)
-    shard_second, landed_first, *away[0] = tie(shard_second, landed_first, *away[0])
-    swapped = [[from_core(part) for part in away[0]]]
-    shard_second, *away[1] = tie(exchange(shard_second), *away[1])
+    shard_second = exchange(own_shard(keep_second, landed_second))
+    shard_second, *away = tie(shard_second, *away)
+    landed_first, mask, small_mask, membership, swapped_gradient = tie(
+        landed_first, mask, small_mask, membership, swapped_gradient
+    )
     held_first = jnp.concatenate([held_first, landed_first])
-    away[1] = [from_half(part, d) for d, part in zip(others, away[1])]
+    away = [from_half(part, d) for d, part in zip(others, away)]
     held_second = split(shard_second)
     for stage in range(2, count):
         landed_first = send(held_first, order_second[-stage])
         landed = stage_of(held_second, 1 - stage)
-        landed_first, *landed = tie(landed_first, *landed, *swapped[0])
-        landed, swapped[0] = landed[:2], landed[2:]
+        held_second = both(held_second, landed)
+        landed_first, *held_second = tie(landed_first, *held_second)
         held_first = jnp.concatenate([held_first, landed_first])
-        held_second = both(held_second, landed)
     last_first = send(held_first, order_second[0])
-    last_first, *landed = tie(last_first, *stage_of(held_second, 1 - count))
-    held_second = both(held_second, landed)
+    held_second = both(held_second, stage_of(held_second, 1 - count))
     last_second = stage_of(held_second, 0)
-    last_first, *away[1] = tie(last_first, *away[1])
-    swapped.append([from_core(part) for part in away[1]])
-
+    last_first, *held_second = tie(last_first, *held_second)
+
+    chosen, sent = input_chosen(
+        position, input_pieces, [held_first, last_first], [order_second], mask, top
+    )
+    sent, *away = tie(sent, *away)
     pieces = [own_gradient, swapped_gradient]
-    for d in range(halves - 1):
-        pieces += [part[d] for part in away] + [part[d] for part in swapped]
+    for part in away:
+        pieces += [part, from_core(part)]
     layouts = output_layouts(gather_orders)
     aligned = held_second[0].shape[1] % 128 == 0
-    chosen, sent = input_chosen(
-        position, input_pieces, [held_first, last_first], [order_second], mask, top
-    )
     before = []
     if aligned:
         sent, *held_second = tie(sent, *held_second)

time: 164 us -> 157 us (0.957)
  other arithmetic: 16 us -> 9.33 us
  waiting for transfers between devices: 56 us -> 61.8 us
  starting transfers between devices: 34.3 us -> 29.1 us
  Pallas kernels: 53.2 us -> 50.2 us
    convert_element_type x2 -> x3, other arithmetic: 4.18 us -> 0.78 us  [pack(): return jnp.where(row < half, scaled, exponent).astype(jnp.float16)]
    ppermute x2, waiting for transfers between devices: 7.04 us -> 10.4 us  [exchange(): lax.ppermute(shard[d], 'expert', flip(group, d * CORES))]
    ppermute x3 -> x2, starting transfers between devices: 4.47 us -> 1.59 us  [from_half(): lax.ppermute(part, 'expert', flip(group, d * CORES))]
    ppermute x2, starting transfers between devices: 3.01 us -> 0.21 us  [exchange(): lax.ppermute(shard[d], 'expert', flip(group, d * CORES))]
    pallas_call x1, Pallas kernels: 7.49 us -> 5.45 us  [flattened_parts(): pl.pallas_call(flatten_kernel, grid_spec=pltpu.PrefetchScalarGridSpec(num...]
    ppermute x15, waiting for transfers between devices: 45.8 us -> 47.5 us  [send(): return lax.ppermute(packed, 'dp', flip(blocks, 1 << bit))]
    unnamed x46 -> x40, local copies, waits for them, and re-layouts: 3.02 us -> 4.58 us
  transfers between devices with their start and end apart: 29 -> 27, of which waited for: 16 -> 17; matrix products, arithmetic and copies ran while one was open for 7% -> 4% of each run, Pallas kernels for 22% -> 21%
where the time goes in v5:
time: 157 us; the launch traced here: 156 us
  waiting for transfers between devices  61.8 us (39%)
  Pallas kernels  50.2 us (32%)
  starting transfers between devices  29.1 us (19%)
  other arithmetic  9.33 us (6%)
  local copies, waits for them, and re-layouts  5.47 us (3%)
    ppermute x15, waiting for transfers between devices, send(): return lax.ppermute(packed, 'dp', flip(blocks, 1 << bit))  47.5 us
    ppermute x15, starting transfers between devices, send(): return lax.ppermute(packed, 'dp', flip(blocks, 1 << bit))  22.6 us
    pallas_call x2, Pallas kernels, fold_parts(): pl.pallas_call(functools.partial(fold_kernel, width, steps, upper), grid_...  21.1 us
    ppermute x2, waiting for transfers between devices, exchange(): lax.ppermute(shard[d], 'expert', flip(group, d * CORES))  10.4 us
    pallas_call x1, Pallas kernels, score_call(): pl.pallas_call(functools.partial(last_kernel, layouts, aligned, len(piece...  7.05 us
    pallas_call x1, Pallas kernels, score_call(): pl.pallas_call(functools.partial(first_kernel, layouts, len(pieces)), in_...  5.85 us
    pallas_call x1, Pallas kernels, flattened_parts(): pl.pallas_call(flatten_kernel, grid_spec=pltpu.PrefetchScalarGridSpec(num...  5.45 us
    pallas_call x1, Pallas kernels, input_chosen(): pl.pallas_call(functools.partial(input_kernel, top, layouts, len(pieces))...  5.07 us
  transfers between devices with their start and end apart: 27, of which 17 were waited for; matrix products, arithmetic and copies ran while one was open for 4% of the time, Pallas kernels for 21%

profile of v5, /device:TPU:0, one launch (start us, length us, event | category | flops | bytes accessed | tf_op | source)
XLA Modules:
  0.0 156.4 jit_solution(1473249945857760583)
XLA Ops:
  0.0 0.6 pad_add_fusion.refs_0_.position_ref
  0.6 10.5 %shard_map.91 = (f32[3088,128]{1,0:T(8,128)}, f32[4112,128]{1,0:T(8,128)}) custom-call(s32[3]{0:T(128)} %pad_add_fusion.refs_0_.position_ref, bf16[6144,768]{1,0:T(8,128)(2,1)} %bitcast.65, bf16[6144,768]{1,0:T(8,128)(2,1)} %bitcast.66, bf16[6144,768]{1,0:T(8,128)(2,1)} %bitcast.67, bf16[6144,768]{1,0:T(8,128)(2,1)} %bitcast.68, ...), custom_call_target="tpu_custom_call" | custom-call | flops 1 | bytes 1 | tf_op jit(solution)/shard_map/pallas_call | solution.py:104
  11.2 1.9 %convert_element_type.78 = f16[4112,128]{1,0:T(8,128)(2,1)S(1)} convert(f32[4112,128]{1,0:T(8,128)} %get-tuple-element.60) | non-fusion elementwise | flops 526336 | bytes 3158016 | tf_op jit(solution)/shard_map/convert_element_type | solution.py:531
  13.2 1.0 convert_element_type.77
  14.2 2.9 %collective-permute-start.2 = (f16[4112,128]{1,0:T(8,128)(2,1)S(1)}, f16[4112,128]{1,0:T(8,128)(2,1)S(1)}, u32[]{:S(2)}, u32[]{:S(2)}) collective-permute-start(f16[4112,128]{1,0:T(8,128)(2,1)S(1)} %convert_element_type.78), channel_id=1, source_target_pairs={{0,4},{4,0},{8,12},{12,8},{16,20},{20,16},{24,28},{28,24},{1,5},{5... | collective-permute-start | bytes 3158024 | tf_op jit(solution)/shard_map/ppermute | solution.py:493
  17.1 1.6 %collective-permute-start = (f16[3088,128]{1,0:T(8,128)(2,1)}, f16[3088,128]{1,0:T(8,128)(2,1)S(1)}, u32[]{:S(2)}, u32[]{:S(2)}) collective-permute-start(f16[3088,128]{1,0:T(8,128)(2,1)} %convert_element_type.77), channel_id=1, source_target_pairs={{0,8},{4,12},{8,0},{12,4},{16,24},{20,28},{24,16},{28,20},{1,9},{5... | collective-permute-start | bytes 2371592 | tf_op jit(solution)/shard_map/ppermute | solution.py:493
  18.8 10.5 %shard_map.92 = (f32[3088,128]{1,0:T(8,128)}, f32[4112,128]{1,0:T(8,128)}) custom-call(s32[3]{0:T(128)} %pad_add_fusion.refs_0_.position_ref, bf16[6144,768]{1,0:T(8,128)(2,1)} %bitcast.69, bf16[6144,768]{1,0:T(8,128)(2,1)} %bitcast.70, bf16[6144,768]{1,0:T(8,128)(2,1)} %bitcast.71, bf16[6144,768]{1,0:T(8,128)(2,1)} %bitcast.72, ...), custom_call_target="tpu_custom_call" | custom-call | flops 1 | bytes 1 | tf_op jit(solution)/shard_map/pallas_call | solution.py:104
  29.5 0.6 pad.4.extra_ref
  30.1 3.3 %shard_map.93 = (bf16[128,3200]{1,0:T(8,128)(2,1)}, bf16[128,3200]{1,0:T(8,128)(2,1)}) custom-call(s32[3]{0:T(128)} %pad_add_fusion.refs_0_.position_ref, bf16[128,6144]{1,0:T(8,128)(2,1)} %source_ref, bf16[128,128]{1,0:T(8,128)(2,1)} %pad.4.extra_ref), custom_call_target="tpu_custom_call" | custom-call | flops 1 | bytes 1 | tf_op jit(solution)/shard_map/pallas_call | solution.py:150
  33.5 2.9 %collective-permute-done = f16[3088,128]{1,0:T(8,128)(2,1)S(1)} collective-permute-done((f16[3088,128]{1,0:T(8,128)(2,1)}, f16[3088,128]{1,0:T(8,128)(2,1)S(1)}, u32[]{:S(2)}, u32[]{:S(2)}) %collective-permute-start) | collective-permute-done | bytes 790560 | tf_op jit(solution)/shard_map/ppermute | solution.py:493
  37.3 3.9 %collective-permute-done.2 = f16[4112,128]{1,0:T(8,128)(2,1)S(1)} collective-permute-done((f16[4112,128]{1,0:T(8,128)(2,1)S(1)}, f16[4112,128]{1,0:T(8,128)(2,1)S(1)}, u32[]{:S(2)}, u32[]{:S(2)}) %collective-permute-start.2) | collective-permute-done | bytes 1052704 | tf_op jit(solution)/shard_map/ppermute | solution.py:493
  41.2 1.2 multiply_add_fusion
  42.4 2.2 %collective-permute-start.3 = (f16[2064,128]{1,0:T(8,128)(2,1)S(1)}, f16[2064,128]{1,0:T(8,128)(2,1)S(1)}, u32[]{:S(2)}, u32[]{:S(2)}) collective-permute-start(f16[2064,128]{1,0:T(8,128)(2,1)S(1)} %get-tuple-element.75), channel_id=1, source_target_pairs={{0,8},{4,12},{8,0},{12,4},{16,24},{20,28},{24,16},{28,20},{1,9},{5... | collective-permute-start | bytes 1585160 | tf_op jit(solution)/shard_map/ppermute | solution.py:493
  44.6 1.5 collective-permute-start.5
  46.2 5.4 %shard_map.94 = (bf16[256,4096]{1,0:T(8,128)(2,1)}, bf16[256,4096]{1,0:T(8,128)(2,1)}) custom-call(s32[3]{0:T(128)} %pad_add_fusion.refs_0_.position_ref, bf16[128,2,8192]{2,1,0:T(2,128)(2,1)} %source_ref.1), custom_call_target="tpu_custom_call" | custom-call | flops 1 | bytes 8388608 | tf_op jit(solution)/shard_map/pallas_call | solution.py:178
  51.9 2.6 %collective-permute-start.4 = (f16[784,128]{1,0:T(8,128)(2,1)S(1)}, f16[784,128]{1,0:T(8,128)(2,1)S(1)}, u32[]{:S(2)}, u32[]{:S(2)}) collective-permute-start(f16[784,128]{1,0:T(8,128)(2,1)S(1)} %get-tuple-element.124), channel_id=1, source_target_pairs={{0,16},{4,20},{8,24},{12,28},{16,0},{20,4},{24,8},{28,12},{1,17},{... | collective-permute-start | bytes 602120 | tf_op jit(solution)/shard_map/ppermute | solution.py:493
  54.5 3.1 %collective-permute-done.3 = f16[2064,128]{1,0:T(8,128)(2,1)S(1)} collective-permute-done((f16[2064,128]{1,0:T(8,128)(2,1)S(1)}, f16[2064,128]{1,0:T(8,128)(2,1)S(1)}, u32[]{:S(2)}, u32[]{:S(2)}) %collective-permute-start.3) | collective-permute-done | bytes 528416 | tf_op jit(solution)/shard_map/ppermute | solution.py:493
  57.9 6.6 %collective-permute-done.4 = f16[784,128]{1,0:T(8,128)(2,1)S(1)} collective-permute-done((f16[784,128]{1,0:T(8,128)(2,1)S(1)}, f16[784,128]{1,0:T(8,128)(2,1)S(1)}, u32[]{:S(2)}, u32[]{:S(2)}) %collective-permute-start.4) | collective-permute-done | bytes 200736 | tf_op jit(solution)/shard_map/ppermute | solution.py:493
  65.3 4.0 %collective-permute-done.6 = bf16[384,128]{1,0:T(8,128)(2,1)S(1)} collective-permute-done((bf16[384,128]{1,0:T(8,128)(2,1)S(1)}, bf16[384,128]{1,0:T(8,128)(2,1)S(1)}, u32[]{:S(2)}, u32[]{:S(2)}) %collective-permute-start.6) | collective-permute-done | bytes 98336 | tf_op jit(solution)/shard_map/ppermute | solution.py:512
  69.4 5.3 %collective-permute-done.7 = f16[1040,128]{1,0:T(8,128)(2,1)S(1)} collective-permute-done((f16[1040,128]{1,0:T(8,128)(2,1)S(1)}, f16[1040,128]{1,0:T(8,128)(2,1)S(1)}, u32[]{:S(2)}, u32[]{:S(2)}) %collective-permute-start.7) | collective-permute-done | bytes 266272 | tf_op jit(solution)/shard_map/ppermute | solution.py:493
  74.9 6.4 %collective-permute-done.13 = bf16[512,128]{1,0:T(8,128)(2,1)S(1)} collective-permute-done((bf16[512,128]{1,0:T(8,128)(2,1)S(1)}, bf16[512,128]{1,0:T(8,128)(2,1)S(1)}, u32[]{:S(2)}, u32[]{:S(2)}) %collective-permute-start.13) | collective-permute-done | bytes 131104 | tf_op jit(solution)/shard_map/ppermute | solution.py:512
  81.5 1.0 copy-done.4
  82.5 2.4 %shard_map.95 = (f32[2,1024,128]{2,1,0:T(8,128)}, bf16[2,1024,128]{2,1,0:T(8,128)(2,1)}, bf16[1024,128]{1,0:T(8,128)(2,1)}) custom-call(s32[3]{0:T(128)} %pad_add_fusion.refs_0_.position_ref, bf16[128,3200]{1,0:T(8,128)(2,1)} %get-tuple-element.80.refs_0_, bf16[128,3200]{1,0:T(8,128)(2,1)} %copy-done.4, bf16[128,3200]{1,0:T(8,128)(2,1)} %copy-done.3, ...), custom_call_target="tpu_custom_call" | custom-call | flops 1 | bytes 1 | tf_op jit(solution)/shard_map/pallas_call | solution.py:228
  84.9 3.4 %collective-permute-done.8 = bf16[1,384,256]{2,1,0:T(8,128)(2,1)} collective-permute-done((bf16[1,384,256]{2,1,0:T(8,128)(2,1)S(1)}, bf16[1,384,256]{2,1,0:T(8,128)(2,1)}, u32[]{:S(2)}, u32[]{:S(2)}) %collective-permute-start.8) | collective-permute-done | bytes 196640 | tf_op jit(solution)/shard_map/ppermute | solution.py:493
  88.2 1.2 pad_maximum_fusion.1
  89.4 5.6 %collective-permute-start.12 = (bf16[2,384,256]{2,1,0:T(8,128)(2,1)S(1)}, bf16[2,384,256]{2,1,0:T(8,128)(2,1)S(1)}, u32[]{:S(2)}, u32[]{:S(2)}) collective-permute-start(bf16[2,384,256]{2,1,0:T(8,128)(2,1)S(1)} %pad_maximum_fusion.1), channel_id=1, source_target_pairs={{0,8},{4,12},{8,0},{12,4},{16,24},{20,28},{24,16},{28,20},{1,9},{5... | collective-permute-start | bytes 1179656 | tf_op jit(solution)/shard_map/ppermute | solution.py:493
  95.0 1.5 collective-permute-start.15
  96.5 5.0 %collective-permute-done.15 = bf16[1,256,256]{2,1,0:T(8,128)(2,1)S(1)} collective-permute-done((bf16[1,256,256]{2,1,0:T(8,128)(2,1)S(1)}, bf16[1,256,256]{2,1,0:T(8,128)(2,1)S(1)}, u32[]{:S(2)}, u32[]{:S(2)}) %collective-permute-start.15) | collective-permute-done | bytes 131104 | tf_op jit(solution)/shard_map/ppermute | solution.py:493
  101.4 5.7 %collective-permute-done.14 = bf16[1,256,256]{2,1,0:T(8,128)(2,1)S(1)} collective-permute-done((bf16[1,256,256]{2,1,0:T(8,128)(2,1)S(1)}, bf16[1,256,256]{2,1,0:T(8,128)(2,1)S(1)}, u32[]{:S(2)}, u32[]{:S(2)}) %collective-permute-start.14) | collective-permute-done | bytes 131104 | tf_op jit(solution)/shard_map/ppermute | solution.py:493
  107.2 1.0 pad_maximum_fusion.refs_4_
  108.2 1.9 %collective-permute-start.16 = (bf16[4,384,256]{2,1,0:T(8,128)(2,1)S(1)}, bf16[4,384,256]{2,1,0:T(8,128)(2,1)S(1)}, u32[]{:S(2)}, u32[]{:S(2)}) collective-permute-start(bf16[4,384,256]{2,1,0:T(8,128)(2,1)S(1)} %pad_maximum_fusion.refs_4_), channel_id=1, source_target_pairs={{0,4},{4,0},{8,12},{12,8},{16,20},{20,16},{24,28},{28,24},{1,5},{5... | collective-permute-start | bytes 2359304 | tf_op jit(solution)/shard_map/ppermute | solution.py:493
  110.1 2.8 %collective-permute-start.18 = (bf16[2,256,256]{2,1,0:T(8,128)(2,1)S(1)}, bf16[2,256,256]{2,1,0:T(8,128)(2,1)S(1)}, u32[]{:S(2)}, u32[]{:S(2)}) collective-permute-start(bf16[2,256,256]{2,1,0:T(8,128)(2,1)S(1)} %pad_maximum_fusion.4), channel_id=1, source_target_pairs={{0,16},{4,20},{8,24},{12,28},{16,0},{20,4},{24,8},{28,12},{1,17},{... | collective-permute-start | bytes 786440 | tf_op jit(solution)/shard_map/ppermute | solution.py:493
  112.9 6.2 %collective-permute-done.18 = bf16[2,256,256]{2,1,0:T(8,128)(2,1)S(1)} collective-permute-done((bf16[2,256,256]{2,1,0:T(8,128)(2,1)S(1)}, bf16[2,256,256]{2,1,0:T(8,128)(2,1)S(1)}, u32[]{:S(2)}, u32[]{:S(2)}) %collective-permute-start.18) | collective-permute-done | bytes 262176 | tf_op jit(solution)/shard_map/ppermute | solution.py:493
  119.1 2.7 %collective-permute-done.17 = bf16[2,256,256]{2,1,0:T(8,128)(2,1)S(1)} collective-permute-done((bf16[2,256,256]{2,1,0:T(8,128)(2,1)S(1)}, bf16[2,256,256]{2,1,0:T(8,128)(2,1)S(1)}, u32[]{:S(2)}, u32[]{:S(2)}) %collective-permute-start.17) | collective-permute-done | bytes 262176 | tf_op jit(solution)/shard_map/ppermute | solution.py:493
  121.9 0.9 copy-done.13
  122.8 5.1 %shard_map.96 = (f32[1024,128]{1,0:T(8,128)}, bf16[1024,128]{1,0:T(8,128)(2,1)}) custom-call(s32[3]{0:T(128)} %pad_add_fusion.refs_0_.position_ref, f32[2,1024,128]{2,1,0:T(8,128)} %get-tuple-element.88.mask_in_ref, bf16[128,3200]{1,0:T(8,128)(2,1)} %get-tuple-element.80.refs_0_, bf16[128,3200]{1,0:T(8,128)(2,1)} %copy-done.4, bf16[128,3200]{1,0:T(8,128)(2,1)} %copy-done.3, ...), custom_call_target="tpu_custom_call" | custom-call | flops 1 | bytes 1 | tf_op jit(solution)/shard_map/pallas_call | solution.py:289
  128.3 0.7 collective-permute-start.22
  129.0 2.2 %collective-permute-start.20 = (bf16[1024,128]{1,0:T(8,128)(2,1)}, bf16[1024,128]{1,0:T(8,128)(2,1)S(1)}, u32[]{:S(2)}, u32[]{:S(2)}) collective-permute-start(bf16[1024,128]{1,0:T(8,128)(2,1)} %get-tuple-element.104), channel_id=1, source_target_pairs={{0,2},{1,3},{2,0},{3,1},{4,6},{5,7},{6,4},{7,5},{8,10},{9,11},{10,... | collective-permute-start | bytes 786440 | tf_op jit(solution)/shard_map/ppermute | solution.py:633
  131.2 1.2 collective-permute-done.21.refs_3_.refs_9_
  132.3 1.4 copy-done.1
  133.7 5.9 %shard_map.97.refs_5_ = f32[1024,256]{1,0:T(8,128)} custom-call(s32[3]{0:T(128)} %pad_add_fusion.refs_0_.position_ref, bf16[256,4096]{1,0:T(8,128)(2,1)} %get-tuple-element.85.refs_0_.refs_6_, bf16[256,4096]{1,0:T(8,128)(2,1)} %copy-done, bf16[256,4096]{1,0:T(8,128)(2,1)} %collective-permute-done.19.refs_2_.refs_8_, bf16[256,4096]{1,0:T(8,128)(2,1)} %copy-done.1, ...), custom_call_target="tpu_custom_call" | custom-call | flops 1 | bytes 5242880 | tf_op jit(solution)/shard_map/pallas_call | solution.py:437
  139.6 2.8 %collective-permute-done.23.refs_11_ = bf16[4,256,256]{2,1,0:T(8,128)(2,1)S(1)} collective-permute-done((bf16[4,256,256]{2,1,0:T(8,128)(2,1)S(1)}, bf16[4,256,256]{2,1,0:T(8,128)(2,1)S(1)}, u32[]{:S(2)}, u32[]{:S(2)}) %collective-permute-start.23) | collective-permute-done | bytes 524320 | tf_op jit(solution)/shard_map/ppermute | solution.py:493
  142.4 0.8 copy-done.14
  143.4 7.1 %shard_map.98 = (f32[4,4]{1,0:T(4,128)}, f32[4,4]{1,0:T(4,128)}, f32[4,4]{1,0:T(4,128)}, f32[4,4]{1,0:T(4,128)}) custom-call(s32[3]{0:T(128)} %pad_add_fusion.refs_0_.position_ref, f32[128,4]{1,0:T(8,128)} %constant.71.clone.refs_0_, bf16[2,1024,128]{2,1,0:T(8,128)(2,1)} %get-tuple-element.86.refs_1_, bf16[1024,128]{1,0:T(8,128)(2,1)} %get-tuple-element.87.refs_2_, ...), custom_call_target="tpu_custom_call" | custom-call | flops 1 | bytes 1 | tf_op jit(solution)/shard_map/pallas_call | solution.py:446
  150.5 1.3 collective-permute-start.25
  152.4 1.8 %collective-permute-done.25 = f32[4,4]{1,0:T(4,128)S(1)} collective-permute-done((f32[4,4]{1,0:T(4,128)}, f32[4,4]{1,0:T(4,128)S(1)}, u32[]{:S(2)}, u32[]{:S(2)}) %collective-permute-start.25) | collective-permute-done | bytes 96 | tf_op jit(solution)/shard_map/ppermute | solution.py:646
  154.3 0.9 collective-permute-done.26
  155.1 1.3 add_add_fusion
  (93 shorter events, 4.5 us)
Async XLA Ops:
  11.2 2.0 %copy-start.10 = (f32[3088,128]{1,0:T(8,128)S(1)}, f32[3088,128]{1,0:T(8,128)}, u32[]{:S(2)}) copy-start(f32[3088,128]{1,0:T(8,128)} %get-tuple-element.59) | copy-start | bytes 4743172
  13.2 5.5 %copy-start.17 = (s32[128,2]{0,1:T(2,128)S(1)}, s32[128,2]{0,1:T(2,128)}, u32[]{:S(2)}) copy-start(s32[128,2]{0,1:T(2,128)} %param.11) | copy-start | bytes 3076
  13.2 5.6 %copy-start.18 = (s32[1,128]{1,0:T(1,128)S(1)}, s32[1,128]{1,0:T(1,128)}, u32[]{:S(2)}) copy-start(s32[1,128]{1,0:T(1,128)} %param.12) | copy-start | bytes 1540
  14.2 27.0 %collective-permute-start.2 = (f16[4112,128]{1,0:T(8,128)(2,1)S(1)}, f16[4112,128]{1,0:T(8,128)(2,1)S(1)}, u32[]{:S(2)}, u32[]{:S(2)}) collective-permute-start(f16[4112,128]{1,0:T(8,128)(2,1)S(1)} %convert_element_type.78), channel_id=1, source_target_pairs={{0,4},{4,0},{8,12},{12,8},{16,20},{20,16},{24,28},{28,24},{1,5},{5... | collective-permute-start | bytes 3158024 | tf_op jit(solution)/shard_map/ppermute | solution.py:493
  17.1 19.3 %collective-permute-start = (f16[3088,128]{1,0:T(8,128)(2,1)}, f16[3088,128]{1,0:T(8,128)(2,1)S(1)}, u32[]{:S(2)}, u32[]{:S(2)}) collective-permute-start(f16[3088,128]{1,0:T(8,128)(2,1)} %convert_element_type.77), channel_id=1, source_target_pairs={{0,8},{4,12},{8,0},{12,4},{16,24},{20,28},{24,16},{28,20},{1,9},{5... | collective-permute-start | bytes 2371592 | tf_op jit(solution)/shard_map/ppermute | solution.py:493
  29.4 4.1 %copy-start.8 = (bf16[1,768,128]{2,1,0:T(8,128)(2,1)S(1)}, bf16[1,768,128]{2,1,0:T(8,128)(2,1)}, u32[]{:S(2)}) copy-start(bf16[1,768,128]{2,1,0:T(8,128)(2,1)} %param.15) | copy-start | bytes 589828
  29.4 4.1 %copy-start.6 = (bf16[1,1024,128]{2,1,0:T(8,128)(2,1)S(1)}, bf16[1,1024,128]{2,1,0:T(8,128)(2,1)}, u32[]{:S(2)}) copy-start(bf16[1,1024,128]{2,1,0:T(8,128)(2,1)} %param.16) | copy-start | bytes 786436
  29.5 7.0 %copy-start.9 = (f32[3088,128]{1,0:T(8,128)S(1)}, f32[3088,128]{1,0:T(8,128)}, u32[]{:S(2)}) copy-start(f32[3088,128]{1,0:T(8,128)} %get-tuple-element.64) | copy-start | bytes 4743172
  36.5 4.8 %copy-start.7 = (f32[4112,128]{1,0:T(8,128)S(1)}, f32[4112,128]{1,0:T(8,128)}, u32[]{:S(2)}) copy-start(f32[4112,128]{1,0:T(8,128)} %get-tuple-element.70) | copy-start | bytes 6316036
  36.8 14.8 %collective-permute-start.1 = (f16[1552,128]{1,0:T(8,128)(2,1)S(1)}, f16[1552,128]{1,0:T(8,128)(2,1)S(1)}, u32[]{:S(2)}, u32[]{:S(2)}) collective-permute-start(f16[1552,128]{1,0:T(8,128)(2,1)S(1)} %get-tuple-element.119), channel_id=1, source_target_pairs={{0,4},{4,0},{8,12},{12,8},{16,20},{20,16},{24,28},{28,24},{1,5},{5... | collective-permute-start | bytes 1191944 | tf_op jit(solution)/shard_map/ppermute | solution.py:493
  42.4 15.2 %collective-permute-start.3 = (f16[2064,128]{1,0:T(8,128)(2,1)S(1)}, f16[2064,128]{1,0:T(8,128)(2,1)S(1)}, u32[]{:S(2)}, u32[]{:S(2)}) collective-permute-start(f16[2064,128]{1,0:T(8,128)(2,1)S(1)} %get-tuple-element.75), channel_id=1, source_target_pairs={{0,8},{4,12},{8,0},{12,4},{16,24},{20,28},{24,16},{28,20},{1,9},{5... | collective-permute-start | bytes 1585160 | tf_op jit(solution)/shard_map/ppermute | solution.py:493
  44.6 20.0 %collective-permute-start.5 = (bf16[128,3200]{1,0:T(8,128)(2,1)}, bf16[128,3200]{1,0:T(8,128)(2,1)S(1)}, u32[]{:S(2)}, u32[]{:S(2)}) collective-permute-start(bf16[128,3200]{1,0:T(8,128)(2,1)} %get-tuple-element.77), channel_id=1, source_target_pairs={{0,2},{1,3},{2,0},{3,1},{4,6},{5,7},{6,4},{7,5},{8,10},{9,11},{10,... | collective-permute-start | bytes 2457608 | tf_op jit(solution)/shard_map/ppermute | solution.py:517
  51.9 12.6 %collective-permute-start.4 = (f16[784,128]{1,0:T(8,128)(2,1)S(1)}, f16[784,128]{1,0:T(8,128)(2,1)S(1)}, u32[]{:S(2)}, u32[]{:S(2)}) collective-permute-start(f16[784,128]{1,0:T(8,128)(2,1)S(1)} %get-tuple-element.124), channel_id=1, source_target_pairs={{0,16},{4,20},{8,24},{12,28},{16,0},{20,4},{24,8},{28,12},{1,17},{... | collective-permute-start | bytes 602120 | tf_op jit(solution)/shard_map/ppermute | solution.py:493
  54.5 33.7 %collective-permute-start.11 = (bf16[256,4096]{1,0:T(8,128)(2,1)}, bf16[256,4096]{1,0:T(8,128)(2,1)S(1)}, u32[]{:S(2)}, u32[]{:S(2)}) collective-permute-start(bf16[256,4096]{1,0:T(8,128)(2,1)} %get-tuple-element.85.refs_0_.refs_6_), channel_id=1, source_target_pairs={{0,1},{1,0},{2,3},{3,2},{4,5},{5,4},{6,7},{7,6},{8,9},{9,8},{10,11... | collective-permute-start | bytes 6291464 | tf_op jit(solution)/shard_map/ppermute | solution.py:520
  57.9 6.9 %copy-start.2 = (bf16[128,3200]{1,0:T(8,128)(2,1)S(1)}, bf16[128,3200]{1,0:T(8,128)(2,1)}, u32[]{:S(2)}) copy-start(bf16[128,3200]{1,0:T(8,128)(2,1)} %get-tuple-element.80.refs_0_) | copy-start | bytes 2457604
  64.5 10.2 %collective-permute-start.7 = (f16[1040,128]{1,0:T(8,128)(2,1)S(1)}, f16[1040,128]{1,0:T(8,128)(2,1)S(1)}, u32[]{:S(2)}, u32[]{:S(2)}) collective-permute-start(f16[1040,128]{1,0:T(8,128)(2,1)S(1)} %get-tuple-element.121), channel_id=1, source_target_pairs={{0,16},{4,20},{8,24},{12,28},{16,0},{20,4},{24,8},{28,12},{1,17},{... | collective-permute-start | bytes 798728 | tf_op jit(solution)/shard_map/ppermute | solution.py:493
  64.6 10.2 %copy-start.3 = (bf16[128,3200]{1,0:T(8,128)(2,1)}, bf16[128,3200]{1,0:T(8,128)(2,1)S(1)}, u32[]{:S(2)}) copy-start(bf16[128,3200]{1,0:T(8,128)(2,1)S(1)} %collective-permute-done.5.refs_2_) | copy-start | bytes 2457604
  64.6 4.7 %collective-permute-start.6 = (bf16[384,128]{1,0:T(8,128)(2,1)S(1)}, bf16[384,128]{1,0:T(8,128)(2,1)S(1)}, u32[]{:S(2)}, u32[]{:S(2)}) collective-permute-start(bf16[384,128]{1,0:T(8,128)(2,1)S(1)} %get-tuple-element.138), channel_id=1, source_target_pairs={{0,2},{1,3},{2,0},{3,1},{4,6},{5,7},{6,4},{7,5},{8,10},{9,11},{10,... | collective-permute-start | bytes 294920 | tf_op jit(solution)/shard_map/ppermute | solution.py:512
  64.8 16.7 %collective-permute-start.9 = (bf16[128,3200]{1,0:T(8,128)(2,1)S(1)}, bf16[128,3200]{1,0:T(8,128)(2,1)S(1)}, u32[]{:S(2)}, u32[]{:S(2)}) collective-permute-start(bf16[128,3200]{1,0:T(8,128)(2,1)S(1)} %copy-done.2), channel_id=1, source_target_pairs={{0,1},{1,0},{2,3},{3,2},{4,5},{5,4},{6,7},{7,6},{8,9},{9,8},{10,11... | collective-permute-start | bytes 2457608 | tf_op jit(solution)/shard_map/ppermute | solution.py:520
  64.8 17.6 %collective-permute-start.10 = (bf16[128,3200]{1,0:T(8,128)(2,1)S(1)}, bf16[128,3200]{1,0:T(8,128)(2,1)}, u32[]{:S(2)}, u32[]{:S(2)}) collective-permute-start(bf16[128,3200]{1,0:T(8,128)(2,1)S(1)} %collective-permute-done.5.refs_2_), channel_id=1, source_target_pairs={{0,1},{1,0},{2,3},{3,2},{4,5},{5,4},{6,7},{7,6},{8,9},{9,8},{10,11... | collective-permute-start | bytes 2457608 | tf_op jit(solution)/shard_map/ppermute | solution.py:520
  74.8 6.5 %collective-permute-start.13 = (bf16[512,128]{1,0:T(8,128)(2,1)S(1)}, bf16[512,128]{1,0:T(8,128)(2,1)S(1)}, u32[]{:S(2)}, u32[]{:S(2)}) collective-permute-start(bf16[512,128]{1,0:T(8,128)(2,1)S(1)} %get-tuple-element.136), channel_id=1, source_target_pairs={{0,2},{1,3},{2,0},{3,1},{4,6},{5,7},{6,4},{7,5},{8,10},{9,11},{10,... | collective-permute-start | bytes 393224 | tf_op jit(solution)/shard_map/ppermute | solution.py:512
  81.3 46.6 %collective-permute-start.19 = (bf16[256,4096]{1,0:T(8,128)(2,1)}, bf16[256,4096]{1,0:T(8,128)(2,1)}, u32[]{:S(2)}, u32[]{:S(2)}) collective-permute-start(bf16[256,4096]{1,0:T(8,128)(2,1)} %get-tuple-element.100), channel_id=1, source_target_pairs={{0,2},{1,3},{2,0},{3,1},{4,6},{5,7},{6,4},{7,5},{8,10},{9,11},{10,... | collective-permute-start | bytes 6291464 | tf_op jit(solution)/shard_map/ppermute | solution.py:517
  81.4 6.8 %collective-permute-start.8 = (bf16[1,384,256]{2,1,0:T(8,128)(2,1)S(1)}, bf16[1,384,256]{2,1,0:T(8,128)(2,1)}, u32[]{:S(2)}, u32[]{:S(2)}) collective-permute-start(bf16[1,384,256]{2,1,0:T(8,128)(2,1)S(1)} %bitcast.77), channel_id=1, source_target_pairs={{0,16},{4,20},{8,24},{12,28},{16,0},{20,4},{24,8},{28,12},{1,17},{... | collective-permute-start | bytes 589832 | tf_op jit(solution)/shard_map/ppermute | solution.py:493
  81.5 1.0 copy-start.4
  88.2 18.9 %copy-start = (bf16[256,4096]{1,0:T(8,128)(2,1)}, bf16[256,4096]{1,0:T(8,128)(2,1)S(1)}, u32[]{:S(2)}) copy-start(bf16[256,4096]{1,0:T(8,128)(2,1)S(1)} %collective-permute-done.11.refs_1_.refs_7_) | copy-start | bytes 6291460
  89.4 17.8 %collective-permute-start.12 = (bf16[2,384,256]{2,1,0:T(8,128)(2,1)S(1)}, bf16[2,384,256]{2,1,0:T(8,128)(2,1)S(1)}, u32[]{:S(2)}, u32[]{:S(2)}) collective-permute-start(bf16[2,384,256]{2,1,0:T(8,128)(2,1)S(1)} %pad_maximum_fusion.1), channel_id=1, source_target_pairs={{0,8},{4,12},{8,0},{12,4},{16,24},{20,28},{24,16},{28,20},{1,9},{5... | collective-permute-start | bytes 1179656 | tf_op jit(solution)/shard_map/ppermute | solution.py:493
  95.0 6.4 %collective-permute-start.15 = (bf16[1,256,256]{2,1,0:T(8,128)(2,1)S(1)}, bf16[1,256,256]{2,1,0:T(8,128)(2,1)S(1)}, u32[]{:S(2)}, u32[]{:S(2)}) collective-permute-start(bf16[1,256,256]{2,1,0:T(8,128)(2,1)S(1)} %get-tuple-element.133), channel_id=1, source_target_pairs={{0,4},{4,0},{8,12},{12,8},{16,20},{20,16},{24,28},{28,24},{1,5},{5... | collective-permute-start | bytes 393224 | tf_op jit(solution)/shard_map/ppermute | solution.py:493
  96.5 10.7 %collective-permute-start.14 = (bf16[1,256,256]{2,1,0:T(8,128)(2,1)S(1)}, bf16[1,256,256]{2,1,0:T(8,128)(2,1)S(1)}, u32[]{:S(2)}, u32[]{:S(2)}) collective-permute-start(bf16[1,256,256]{2,1,0:T(8,128)(2,1)S(1)} %get-tuple-element.134), channel_id=1, source_target_pairs={{0,16},{4,20},{8,24},{12,28},{16,0},{20,4},{24,8},{28,12},{1,17},{... | collective-permute-start | bytes 393224 | tf_op jit(solution)/shard_map/ppermute | solution.py:493
  108.2 13.6 %copy-start.5 = (bf16[4,384,256]{2,1,0:T(8,128)(2,1)}, bf16[4,384,256]{2,1,0:T(8,128)(2,1)S(1)}, u32[]{:S(2)}) copy-start(bf16[4,384,256]{2,1,0:T(8,128)(2,1)S(1)} %pad_maximum_fusion.refs_4_) | copy-start | bytes 2359300
  108.2 13.6 %collective-permute-start.16 = (bf16[4,384,256]{2,1,0:T(8,128)(2,1)S(1)}, bf16[4,384,256]{2,1,0:T(8,128)(2,1)S(1)}, u32[]{:S(2)}, u32[]{:S(2)}) collective-permute-start(bf16[4,384,256]{2,1,0:T(8,128)(2,1)S(1)} %pad_maximum_fusion.refs_4_), channel_id=1, source_target_pairs={{0,4},{4,0},{8,12},{12,8},{16,20},{20,16},{24,28},{28,24},{1,5},{5... | collective-permute-start | bytes 2359304 | tf_op jit(solution)/shard_map/ppermute | solution.py:493
  110.1 9.0 %collective-permute-start.18 = (bf16[2,256,256]{2,1,0:T(8,128)(2,1)S(1)}, bf16[2,256,256]{2,1,0:T(8,128)(2,1)S(1)}, u32[]{:S(2)}, u32[]{:S(2)}) collective-permute-start(bf16[2,256,256]{2,1,0:T(8,128)(2,1)S(1)} %pad_maximum_fusion.4), channel_id=1, source_target_pairs={{0,16},{4,20},{8,24},{12,28},{16,0},{20,4},{24,8},{28,12},{1,17},{... | collective-permute-start | bytes 786440 | tf_op jit(solution)/shard_map/ppermute | solution.py:493
  112.9 8.9 %collective-permute-start.17 = (bf16[2,256,256]{2,1,0:T(8,128)(2,1)S(1)}, bf16[2,256,256]{2,1,0:T(8,128)(2,1)S(1)}, u32[]{:S(2)}, u32[]{:S(2)}) collective-permute-start(bf16[2,256,256]{2,1,0:T(8,128)(2,1)S(1)} %pad_maximum_fusion.3), channel_id=1, source_target_pairs={{0,8},{4,12},{8,0},{12,4},{16,24},{20,28},{24,16},{28,20},{1,9},{5... | collective-permute-start | bytes 786440 | tf_op jit(solution)/shard_map/ppermute | solution.py:493
  119.1 8.9 %copy-start.12 = (bf16[4,256,256]{2,1,0:T(8,128)(2,1)}, bf16[4,256,256]{2,1,0:T(8,128)(2,1)S(1)}, u32[]{:S(2)}) copy-start(bf16[4,256,256]{2,1,0:T(8,128)(2,1)S(1)} %constant_dynamic-update-slice_fusion.2.refs_5_) | copy-start | bytes 1572868
  121.8 6.5 %copy-start.11 = (bf16[4,256,256]{2,1,0:T(8,128)(2,1)}, bf16[4,256,256]{2,1,0:T(8,128)(2,1)S(1)}, u32[]{:S(2)}) copy-start(bf16[4,256,256]{2,1,0:T(8,128)(2,1)S(1)} %constant_dynamic-update-slice_fusion.refs_4_) | copy-start | bytes 1572868
  121.8 0.9 copy-start.13
  127.9 4.4 %collective-permute-start.21 = (bf16[256,4096]{1,0:T(8,128)(2,1)}, bf16[256,4096]{1,0:T(8,128)(2,1)S(1)}, u32[]{:S(2)}, u32[]{:S(2)}) collective-permute-start(bf16[256,4096]{1,0:T(8,128)(2,1)} %collective-permute-done.19.refs_2_.refs_8_), channel_id=1, source_target_pairs={{0,1},{1,0},{2,3},{3,2},{4,5},{5,4},{6,7},{7,6},{8,9},{9,8},{10,11... | collective-permute-start | bytes 6291464 | tf_op jit(solution)/shard_map/ppermute | solution.py:520
  128.0 14.3 %collective-permute-start.23 = (bf16[4,256,256]{2,1,0:T(8,128)(2,1)S(1)}, bf16[4,256,256]{2,1,0:T(8,128)(2,1)S(1)}, u32[]{:S(2)}, u32[]{:S(2)}) collective-permute-start(bf16[4,256,256]{2,1,0:T(8,128)(2,1)S(1)} %constant_dynamic-update-slice_fusion.2.refs_5_), channel_id=1, source_target_pairs={{0,8},{4,12},{8,0},{12,4},{16,24},{20,28},{24,16},{28,20},{1,9},{5... | collective-permute-start | bytes 1572872 | tf_op jit(solution)/shard_map/ppermute | solution.py:493
  128.3 14.1 %collective-permute-start.22 = (bf16[4,256,256]{2,1,0:T(8,128)(2,1)S(1)}, bf16[4,256,256]{2,1,0:T(8,128)(2,1)S(1)}, u32[]{:S(2)}, u32[]{:S(2)}) collective-permute-start(bf16[4,256,256]{2,1,0:T(8,128)(2,1)S(1)} %constant_dynamic-update-slice_fusion.refs_4_), channel_id=1, source_target_pairs={{0,4},{4,0},{8,12},{12,8},{16,20},{20,16},{24,28},{28,24},{1,5},{5... | collective-permute-start | bytes 1572872 | tf_op jit(solution)/shard_map/ppermute | solution.py:493
  129.0 13.4 %collective-permute-start.20 = (bf16[1024,128]{1,0:T(8,128)(2,1)}, bf16[1024,128]{1,0:T(8,128)(2,1)S(1)}, u32[]{:S(2)}, u32[]{:S(2)}) collective-permute-start(bf16[1024,128]{1,0:T(8,128)(2,1)} %get-tuple-element.104), channel_id=1, source_target_pairs={{0,2},{1,3},{2,0},{3,1},{4,6},{5,7},{6,4},{7,5},{8,10},{9,11},{10,... | collective-permute-start | bytes 786440 | tf_op jit(solution)/shard_map/ppermute | solution.py:633
  132.3 1.4 copy-start.1
  142.3 0.8 copy-start.14
  142.4 0.9 copy-start.15
  142.4 1.0 copy-start.16
  150.5 1.9 %collective-permute-start.24 = (f32[4,4]{1,0:T(4,128)}, f32[4,4]{1,0:T(4,128)S(1)}, u32[]{:S(2)}, u32[]{:S(2)}) collective-permute-start(f32[4,4]{1,0:T(4,128)} %get-tuple-element.110), channel_id=1, source_target_pairs={{0,1},{1,0},{2,3},{3,2},{4,5},{5,4},{6,7},{7,6},{8,9},{9,8},{10,11... | collective-permute-start | bytes 200 | tf_op jit(solution)/shard_map/ppermute | solution.py:646
  150.5 3.7 %collective-permute-start.25 = (f32[4,4]{1,0:T(4,128)}, f32[4,4]{1,0:T(4,128)S(1)}, u32[]{:S(2)}, u32[]{:S(2)}) collective-permute-start(f32[4,4]{1,0:T(4,128)} %get-tuple-element.111), channel_id=1, source_target_pairs={{0,2},{1,3},{2,0},{3,1},{4,6},{5,7},{6,4},{7,5},{8,10},{9,11},{10,... | collective-permute-start | bytes 200 | tf_op jit(solution)/shard_map/ppermute | solution.py:646
  151.9 3.2 %collective-permute-start.26 = (f32[4,4]{1,0:T(4,128)}, f32[4,4]{1,0:T(4,128)S(1)}, u32[]{:S(2)}, u32[]{:S(2)}) collective-permute-start(f32[4,4]{1,0:T(4,128)} %get-tuple-element.112), channel_id=1, source_target_pairs={{0,3},{1,2},{2,1},{3,0},{4,7},{5,6},{6,5},{7,4},{8,11},{9,10},{10,... | collective-permute-start | bytes 200 | tf_op jit(solution)/shard_map/ppermute | solution.py:646

commit v6 on v5

--- a/solution.py
+++ b/solution.py
@@ -164,32 +164,50 @@
     )(position, source, extra)
 
 
-def flatten_kernel(position_ref, source_ref, *out_refs):
+def flatten_kernel(halves, position_ref, source_ref, *out_refs):
+    step = pl.program_id(0)
     rows, width = out_refs[0].shape
-    for d, out_ref in enumerate(out_refs):
+    for d in range(halves):
         start = pl.multiple_of((position_ref[1] ^ d) * width, width)
-        out_ref[...] = source_ref[:, :, pl.ds(start, width)].reshape(rows, width)
+        part = source_ref[:, :, pl.ds(start, width)].reshape(rows, width)
+        if d == 0:
+            out_refs[0][...] = part
+            continue
+
+        @pl.when(step == 0)
+        def _():
+            out_refs[2 * d - 1][...] = part
+
+        @pl.when(step > 0)
+        def _():
+            out_refs[2 * d][...] = part
 
 
 def flattened_parts(source, position, halves):
     tokens, top, width = source.shape
     block = 32
-    out = (tokens * top, width // halves)
+    rows, width = block * top, width // halves
+    shapes = [tokens * top] + [rows, tokens * top - rows] * (halves - 1)
+    specs = [
+        pl.BlockSpec((rows, width), lambda i, p: (i, 0)),
+        pl.BlockSpec((rows, width), lambda i, p: (0, 0)),
+        pl.BlockSpec((rows, width), lambda i, p: (jnp.maximum(i - 1, 0), 0)),
+    ]
     own, *away = pl.pallas_call(
-        flatten_kernel,
+        functools.partial(flatten_kernel, halves),
         grid_spec=pltpu.PrefetchScalarGridSpec(
             num_scalar_prefetch=1,
             grid=(tokens // block,),
-            in_specs=[pl.BlockSpec((block, top, width), lambda i, p: (i, 0, 0))],
-            out_specs=[pl.BlockSpec((block * top, out[1]), lambda i, p: (i, 0))] * halves,
+            in_specs=[pl.BlockSpec((block,) + source.shape[1:], lambda i, p: (i, 0, 0))],
+            out_specs=specs[:1] + specs[1:] * (halves - 1),
         ),
-        out_shape=[jax.ShapeDtypeStruct(out, source.dtype)] * halves,
+        out_shape=[jax.ShapeDtypeStruct((count, width), source.dtype) for count in shapes],
         compiler_params=pltpu.CompilerParams(vmem_limit_bytes=56 * 1024 * 1024),
         cost_estimate=pl.CostEstimate(
             flops=1, bytes_accessed=4 * source.size, transcendentals=0
         ),
     )(position, source)
-    return own, away
+    return own, away[0::2], away[1::2]
 
 
 def start_all(copies, done):
@@ -427,11 +445,7 @@
     ]
     options = dict(
         compiler_params=pltpu.CompilerParams(vmem_limit_bytes=58 * 1024 * 1024),
-        cost_estimate=pl.CostEstimate(
-            flops=1,
-            bytes_accessed=1 if extras else 2 * (total + across) * width,
-            transcendentals=0,
-        ),
+        cost_estimate=pl.CostEstimate(flops=1, bytes_accessed=1, transcendentals=0),
     )
     if not extras:
         return pl.pallas_call(
@@ -529,7 +543,9 @@
 
     bases = input_basis[0], output_basis[0]
     packed_first, packed_second = [part.astype(jnp.float16) for part in parts(bases, True)]
-    *bases, packed_first, packed_second = tie(*bases, packed_first, packed_second)
+    *bases, activations, packed_first, packed_second = tie(
+        *bases, activations, packed_first, packed_second
+    )
     landed_first = send(packed_first, order_first[0])
     landed_second = send(packed_second, order_second[0])
     exponent_first = column_exponent(input_query[0])
@@ -537,12 +553,11 @@
 
     others = range(1, halves)
     gather_orders = [order_second, order_second[1:] + order_second[:1]]
-    keep_first, keep_second = parts(bases, False)
-    activations, keep_first = tie(activations, keep_first)
     extra = jnp.concatenate([routes, sequence_ids.T], axis=1).astype(jnp.bfloat16)
     extra = jnp.pad(extra, ((0, 0), (0, columns - extra.shape[1])))
     input_parts = list(column_parts(activations, extra, position, halves))
-    landed_first, *input_parts = tie(landed_first, *input_parts)
+    *bases, input_parts[0] = tie(*bases, input_parts[0])
+    keep_first, keep_second = parts(bases, False)
     input_parts = [from_half(part, d) for d, part in enumerate(input_parts)]
 
     packed_first, exponent_first, keep_first = joined(keep_first, landed_first, exponent_first)
@@ -552,7 +567,8 @@
     )
     gate_gradient, packed_second = tie(gate_gradient, packed_second)
     landed_second = send(packed_second, order_second[1])
-    own_gradient, away = flattened_parts(gate_gradient, position, halves)
+    own_gradient, early, late = flattened_parts(gate_gradient, position, halves)
+    early = [from_half(part, d) for d, part in zip(others, early)]
     landed_first, own_gradient = tie(landed_first, own_gradient)
 
     for bit in order_first[2:]:
@@ -587,17 +603,19 @@
     def both(held, landed):
         return [jnp.concatenate(pair) for pair in zip(held, landed)]
 
+    shard_first, *early = tie(shard_first, *early)
+    swapped_early = [from_core(part) for part in early]
     shard_first = exchange(shard_first)
     shard_first, landed_second = tie(shard_first, landed_second)
     held_first = shard_first[None]
     landed_first = send(held_first, order_second[-1])
     shard_second = exchange(own_shard(keep_second, landed_second))
-    shard_second, *away = tie(shard_second, *away)
-    landed_first, mask, small_mask, membership, swapped_gradient = tie(
-        landed_first, mask, small_mask, membership, swapped_gradient
+    shard_second, *late = tie(shard_second, *late)
+    landed_first, mask, small_mask, membership, swapped_gradient, *swapped_early = tie(
+        landed_first, mask, small_mask, membership, swapped_gradient, *swapped_early
     )
     held_first = jnp.concatenate([held_first, landed_first])
-    away = [from_half(part, d) for d, part in zip(others, away)]
+    late = [from_half(part, d) for d, part in zip(others, late)]
     held_second = split(shard_second)
     for stage in range(2, count):
         landed_first = send(held_first, order_second[-stage])
@@ -609,14 +627,14 @@
     held_second = both(held_second, stage_of(held_second, 1 - count))
     last_second = stage_of(held_second, 0)
     last_first, *held_second = tie(last_first, *held_second)
+    last_first, *late = tie(last_first, *late)
 
     chosen, sent = input_chosen(
         position, input_pieces, [held_first, last_first], [order_second], mask, top
     )
-    sent, *away = tie(sent, *away)
     pieces = [own_gradient, swapped_gradient]
-    for part in away:
-        pieces += [part, from_core(part)]
+    for first_part, last_part, swapped_part in zip(early, late, swapped_early):
+        pieces += [first_part, last_part, swapped_part, from_core(last_part)]
     layouts = output_layouts(gather_orders)
     aligned = held_second[0].shape[1] % 128 == 0
     before = []

time: 157 us -> 151 us (0.962)
  waiting for transfers between devices: 61.8 us -> 45 us
  starting transfers between devices: 29.1 us -> 37 us
  other arithmetic: 9.33 us -> 12.6 us
    ppermute x15, waiting for transfers between devices: 47.5 us -> 36 us  [send(): return lax.ppermute(packed, 'dp', flip(blocks, 1 << bit))]
    ppermute x2, waiting for transfers between devices: 10.4 us -> 5.54 us  [exchange(): lax.ppermute(shard[d], 'expert', flip(group, d * CORES))]
    ppermute x2, starting transfers between devices: 0.21 us -> 3.88 us  [exchange(): lax.ppermute(shard[d], 'expert', flip(group, d * CORES))]
    ppermute x2 -> x3, starting transfers between devices: 1.59 us -> 4.96 us  [from_half(): lax.ppermute(part, 'expert', flip(group, d * CORES))]
    unnamed x40 -> x42, local copies, waits for them, and re-layouts: 4.58 us -> 3.18 us
  transfers between devices with their start and end apart: 27 -> 29, of which waited for: 17 -> 13; matrix products, arithmetic and copies ran while one was open for 4% -> 6% of each run, Pallas kernels for 21% -> 22%
where the time goes in v6:
time: 151 us; the launch traced here: 150 us
  Pallas kernels  51 us (34%)
  waiting for transfers between devices  45 us (30%)
  starting transfers between devices  37 us (25%)
  other arithmetic  12.6 us (8%)
  local copies, waits for them, and re-layouts  4.06 us (3%)
    ppermute x15, waiting for transfers between devices, send(): return lax.ppermute(packed, 'dp', flip(blocks, 1 << bit))  36 us
    ppermute x15, starting transfers between devices, send(): return lax.ppermute(packed, 'dp', flip(blocks, 1 << bit))  23.8 us
    pallas_call x2, Pallas kernels, fold_parts(): pl.pallas_call(functools.partial(fold_kernel, width, steps, upper), grid_...  21.3 us
    pallas_call x1, Pallas kernels, score_call(): pl.pallas_call(functools.partial(last_kernel, layouts, aligned, len(piece...  7.24 us
    pallas_call x1, Pallas kernels, score_call(): pl.pallas_call(functools.partial(first_kernel, layouts, len(pieces)), in_...  6.14 us
    pallas_call x1, Pallas kernels, flattened_parts(): pl.pallas_call(functools.partial(flatten_kernel, halves), grid_spec=pltpu...  5.56 us
    ppermute x2, waiting for transfers between devices, exchange(): lax.ppermute(shard[d], 'expert', flip(group, d * CORES))  5.54 us
    pallas_call x1, Pallas kernels, input_chosen(): pl.pallas_call(functools.partial(input_kernel, top, layouts, len(pieces))...  5.08 us
  transfers between devices with their start and end apart: 29, of which 13 were waited for; matrix products, arithmetic and copies ran while one was open for 6% of the time, Pallas kernels for 22%

profile of v6, /device:TPU:0, one launch (start us, length us, event | category | flops | bytes accessed | tf_op | source)
XLA Modules:
  0.0 150.1 jit_solution(17534829460295303987)
XLA Ops:
  0.6 10.6 %shard_map.91 = (f32[3088,128]{1,0:T(8,128)}, f32[4112,128]{1,0:T(8,128)}) custom-call(s32[3]{0:T(128)} %pad_add_fusion.refs_0_.position_ref, bf16[6144,768]{1,0:T(8,128)(2,1)} %bitcast.65, bf16[6144,768]{1,0:T(8,128)(2,1)} %bitcast.66, bf16[6144,768]{1,0:T(8,128)(2,1)} %bitcast.67, bf16[6144,768]{1,0:T(8,128)(2,1)} %bitcast.68, ...), custom_call_target="tpu_custom_call" | custom-call | flops 1 | bytes 1 | tf_op jit(solution)/shard_map/pallas_call | solution.py:104
  11.2 2.6 %convert_element_type.77 = f16[3088,128]{1,0:T(8,128)(2,1)} convert(f32[3088,128]{1,0:T(8,128)} %get-tuple-element.62) | non-fusion elementwise | flops 395264 | bytes 2371584 | tf_op jit(solution)/shard_map/convert_element_type | solution.py:545
  13.9 3.1 %collective-permute-start = (f16[3088,128]{1,0:T(8,128)(2,1)}, f16[3088,128]{1,0:T(8,128)(2,1)S(1)}, u32[]{:S(2)}, u32[]{:S(2)}) collective-permute-start(f16[3088,128]{1,0:T(8,128)(2,1)} %convert_element_type.77), channel_id=1, source_target_pairs={{0,8},{4,12},{8,0},{12,4},{16,24},{20,28},{24,16},{28,20},{1,9},{5... | collective-permute-start | bytes 2371592 | tf_op jit(solution)/shard_map/ppermute | solution.py:507
  17.0 1.5 collective-permute-start.2
  19.3 3.4 %shard_map.92 = (bf16[128,3200]{1,0:T(8,128)(2,1)}, bf16[128,3200]{1,0:T(8,128)(2,1)}) custom-call(s32[3]{0:T(128)} %pad_add_fusion.refs_0_.position_ref, bf16[128,6144]{1,0:T(8,128)(2,1)} %source_ref, bf16[128,128]{1,0:T(8,128)(2,1)} %pad.4.extra_ref), custom_call_target="tpu_custom_call" | custom-call | flops 1 | bytes 1 | tf_op jit(solution)/shard_map/pallas_call | solution.py:150
  22.6 1.5 %collective-permute-start.5 = (bf16[128,3200]{1,0:T(8,128)(2,1)}, bf16[128,3200]{1,0:T(8,128)(2,1)S(1)}, u32[]{:S(2)}, u32[]{:S(2)}) collective-permute-start(bf16[128,3200]{1,0:T(8,128)(2,1)} %get-tuple-element.79), channel_id=1, source_target_pairs={{0,2},{1,3},{2,0},{3,1},{4,6},{5,7},{6,4},{7,5},{8,10},{9,11},{10,... | collective-permute-start | bytes 2457608 | tf_op jit(solution)/shard_map/ppermute | solution.py:531
  24.2 10.7 %shard_map.93 = (f32[3088,128]{1,0:T(8,128)}, f32[4112,128]{1,0:T(8,128)}) custom-call(s32[3]{0:T(128)} %pad_add_fusion.refs_0_.position_ref, bf16[6144,768]{1,0:T(8,128)(2,1)} %bitcast.69, bf16[6144,768]{1,0:T(8,128)(2,1)} %bitcast.70, bf16[6144,768]{1,0:T(8,128)(2,1)} %bitcast.71, bf16[6144,768]{1,0:T(8,128)(2,1)} %bitcast.72, ...), custom_call_target="tpu_custom_call" | custom-call | flops 1 | bytes 1 | tf_op jit(solution)/shard_map/pallas_call | solution.py:104
  35.1 1.9 %select_convert_fusion.1 = (f16[1552,128]{1,0:T(8,128)(2,1)S(1)}, f32[1552,128]{1,0:T(8,128)S(1)}) fusion(f32[3088,128]{1,0:T(8,128)} %get-tuple-element.70, f16[3088,128]{1,0:T(8,128)(2,1)S(1)} %collective-permute-done, f32[128]{0:T(128)S(1)} %bitcast.79, f32[128]{0:T(128)S(1)} %get-tuple-element.121, f32[128]{0:T(128)S(1)} %get-tuple-element.132, ...), kind=kLoop, calls=%fused_computation.2 | loop fusion | flops 1787904 | bytes 3578896 | tf_op jit(solution)/shard_map/convert_element_type | solution.py:126
  36.9 1.5 %collective-permute-start.1 = (f16[1552,128]{1,0:T(8,128)(2,1)S(1)}, f16[1552,128]{1,0:T(8,128)(2,1)S(1)}, u32[]{:S(2)}, u32[]{:S(2)}) collective-permute-start(f16[1552,128]{1,0:T(8,128)(2,1)S(1)} %get-tuple-element.125), channel_id=1, source_target_pairs={{0,4},{4,0},{8,12},{12,8},{16,20},{20,16},{24,28},{28,24},{1,5},{5... | collective-permute-start | bytes 1191944 | tf_op jit(solution)/shard_map/ppermute | solution.py:507
  38.5 4.7 %collective-permute-done.2 = f16[4112,128]{1,0:T(8,128)(2,1)S(1)} collective-permute-done((f16[4112,128]{1,0:T(8,128)(2,1)S(1)}, f16[4112,128]{1,0:T(8,128)(2,1)S(1)}, u32[]{:S(2)}, u32[]{:S(2)}) %collective-permute-start.2) | collective-permute-done | bytes 1052704 | tf_op jit(solution)/shard_map/ppermute | solution.py:507
  43.2 1.2 multiply_add_fusion
  44.5 5.6 %shard_map.94 = (bf16[256,4096]{1,0:T(8,128)(2,1)}, bf16[64,4096]{1,0:T(8,128)(2,1)}, bf16[192,4096]{1,0:T(8,128)(2,1)}) custom-call(s32[3]{0:T(128)} %pad_add_fusion.refs_0_.position_ref, bf16[128,2,8192]{2,1,0:T(2,128)(2,1)} %source_ref.1), custom_call_target="tpu_custom_call" | custom-call | flops 1 | bytes 8388608 | tf_op jit(solution)/shard_map/pallas_call | solution.py:196
  50.1 1.9 %collective-permute-start.6 = (bf16[64,4096]{1,0:T(8,128)(2,1)}, bf16[64,4096]{1,0:T(8,128)(2,1)S(1)}, u32[]{:S(2)}, u32[]{:S(2)}) collective-permute-start(bf16[64,4096]{1,0:T(8,128)(2,1)} %get-tuple-element.81), channel_id=1, source_target_pairs={{0,2},{1,3},{2,0},{3,1},{4,6},{5,7},{6,4},{7,5},{8,10},{9,11},{10,... | collective-permute-start | bytes 1572872 | tf_op jit(solution)/shard_map/ppermute | solution.py:531
  52.2 2.7 %collective-permute-start.4 = (f16[784,128]{1,0:T(8,128)(2,1)S(1)}, f16[784,128]{1,0:T(8,128)(2,1)S(1)}, u32[]{:S(2)}, u32[]{:S(2)}) collective-permute-start(f16[784,128]{1,0:T(8,128)(2,1)S(1)} %get-tuple-element.130), channel_id=1, source_target_pairs={{0,16},{4,20},{8,24},{12,28},{16,0},{20,4},{24,8},{28,12},{1,17},{... | collective-permute-start | bytes 602120 | tf_op jit(solution)/shard_map/ppermute | solution.py:507
  54.9 4.9 %collective-permute-done.3 = f16[2064,128]{1,0:T(8,128)(2,1)S(1)} collective-permute-done((f16[2064,128]{1,0:T(8,128)(2,1)S(1)}, f16[2064,128]{1,0:T(8,128)(2,1)S(1)}, u32[]{:S(2)}, u32[]{:S(2)}) %collective-permute-start.3) | collective-permute-done | bytes 528416 | tf_op jit(solution)/shard_map/ppermute | solution.py:507
  60.3 1.4 collective-permute-done.6.refs_2_.refs_8_
  61.6 2.7 %collective-permute-start.8 = (f16[1040,128]{1,0:T(8,128)(2,1)S(1)}, f16[1040,128]{1,0:T(8,128)(2,1)S(1)}, u32[]{:S(2)}, u32[]{:S(2)}) collective-permute-start(f16[1040,128]{1,0:T(8,128)(2,1)S(1)} %get-tuple-element.127), channel_id=1, source_target_pairs={{0,16},{4,20},{8,24},{12,28},{16,0},{20,4},{24,8},{28,12},{1,17},{... | collective-permute-start | bytes 798728 | tf_op jit(solution)/shard_map/ppermute | solution.py:507
  64.4 2.3 %collective-permute-start.7 = (bf16[384,128]{1,0:T(8,128)(2,1)S(1)}, bf16[384,128]{1,0:T(8,128)(2,1)S(1)}, u32[]{:S(2)}, u32[]{:S(2)}) collective-permute-start(bf16[384,128]{1,0:T(8,128)(2,1)S(1)} %get-tuple-element.144), channel_id=1, source_target_pairs={{0,2},{1,3},{2,0},{3,1},{4,6},{5,7},{6,4},{7,5},{8,10},{9,11},{10,... | collective-permute-start | bytes 294920 | tf_op jit(solution)/shard_map/ppermute | solution.py:526
  67.2 2.1 %collective-permute-done.7 = bf16[384,128]{1,0:T(8,128)(2,1)S(1)} collective-permute-done((bf16[384,128]{1,0:T(8,128)(2,1)S(1)}, bf16[384,128]{1,0:T(8,128)(2,1)S(1)}, u32[]{:S(2)}, u32[]{:S(2)}) %collective-permute-start.7) | collective-permute-done | bytes 98336 | tf_op jit(solution)/shard_map/ppermute | solution.py:526
  70.0 3.3 %collective-permute-done.8 = f16[1040,128]{1,0:T(8,128)(2,1)S(1)} collective-permute-done((f16[1040,128]{1,0:T(8,128)(2,1)S(1)}, f16[1040,128]{1,0:T(8,128)(2,1)S(1)}, u32[]{:S(2)}, u32[]{:S(2)}) %collective-permute-start.8) | collective-permute-done | bytes 266272 | tf_op jit(solution)/shard_map/ppermute | solution.py:507
  73.4 1.6 %collective-permute-start.15 = (bf16[512,128]{1,0:T(8,128)(2,1)S(1)}, bf16[512,128]{1,0:T(8,128)(2,1)S(1)}, u32[]{:S(2)}, u32[]{:S(2)}) collective-permute-start(bf16[512,128]{1,0:T(8,128)(2,1)S(1)} %get-tuple-element.142), channel_id=1, source_target_pairs={{0,2},{1,3},{2,0},{3,1},{4,6},{5,7},{6,4},{7,5},{8,10},{9,11},{10,... | collective-permute-start | bytes 393224 | tf_op jit(solution)/shard_map/ppermute | solution.py:526
  75.0 3.5 %collective-permute-done.15 = bf16[512,128]{1,0:T(8,128)(2,1)S(1)} collective-permute-done((bf16[512,128]{1,0:T(8,128)(2,1)S(1)}, bf16[512,128]{1,0:T(8,128)(2,1)S(1)}, u32[]{:S(2)}, u32[]{:S(2)}) %collective-permute-start.15) | collective-permute-done | bytes 131104 | tf_op jit(solution)/shard_map/ppermute | solution.py:526
  78.5 0.7 pad_maximum_fusion.2
  79.2 0.9 copy-done.4
  80.1 1.5 %collective-permute-start.21 = (bf16[192,4096]{1,0:T(8,128)(2,1)}, bf16[192,4096]{1,0:T(8,128)(2,1)}, u32[]{:S(2)}, u32[]{:S(2)}) collective-permute-start(bf16[192,4096]{1,0:T(8,128)(2,1)} %get-tuple-element.103), channel_id=1, source_target_pairs={{0,2},{1,3},{2,0},{3,1},{4,6},{5,7},{6,4},{7,5},{8,10},{9,11},{10,... | collective-permute-start | bytes 4718600 | tf_op jit(solution)/shard_map/ppermute | solution.py:531
  81.7 2.4 %shard_map.95 = (f32[2,1024,128]{2,1,0:T(8,128)}, bf16[2,1024,128]{2,1,0:T(8,128)(2,1)}, bf16[1024,128]{1,0:T(8,128)(2,1)}) custom-call(s32[3]{0:T(128)} %pad_add_fusion.refs_0_.position_ref, bf16[128,3200]{1,0:T(8,128)(2,1)} %get-tuple-element.84.refs_0_, bf16[128,3200]{1,0:T(8,128)(2,1)} %copy-done.4, bf16[128,3200]{1,0:T(8,128)(2,1)} %copy-done.3, ...), custom_call_target="tpu_custom_call" | custom-call | flops 1 | bytes 1 | tf_op jit(solution)/shard_map/pallas_call | solution.py:246
  84.0 5.2 %collective-permute-done.9 = bf16[1,384,256]{2,1,0:T(8,128)(2,1)} collective-permute-done((bf16[1,384,256]{2,1,0:T(8,128)(2,1)}, bf16[1,384,256]{2,1,0:T(8,128)(2,1)}, u32[]{:S(2)}, u32[]{:S(2)}) %collective-permute-start.9) | collective-permute-done | bytes 196640 | tf_op jit(solution)/shard_map/ppermute | solution.py:507
  89.2 1.5 pad_maximum_fusion.1
  90.9 0.9 collective-permute-start.16
  91.7 1.5 collective-permute-start.17
  93.2 6.3 %collective-permute-done.16 = bf16[1,256,256]{2,1,0:T(8,128)(2,1)S(1)} collective-permute-done((bf16[1,256,256]{2,1,0:T(8,128)(2,1)S(1)}, bf16[1,256,256]{2,1,0:T(8,128)(2,1)S(1)}, u32[]{:S(2)}, u32[]{:S(2)}) %collective-permute-start.16) | collective-permute-done | bytes 131104 | tf_op jit(solution)/shard_map/ppermute | solution.py:507
  99.6 0.8 collective-permute-done.14
  100.4 1.1 pad_maximum_fusion.refs_4_
  101.5 1.6 %collective-permute-start.18 = (bf16[4,384,256]{2,1,0:T(8,128)(2,1)S(1)}, bf16[4,384,256]{2,1,0:T(8,128)(2,1)S(1)}, u32[]{:S(2)}, u32[]{:S(2)}) collective-permute-start(bf16[4,384,256]{2,1,0:T(8,128)(2,1)S(1)} %pad_maximum_fusion.refs_4_), channel_id=1, source_target_pairs={{0,4},{4,0},{8,12},{12,8},{16,20},{20,16},{24,28},{28,24},{1,5},{5... | collective-permute-start | bytes 2359304 | tf_op jit(solution)/shard_map/ppermute | solution.py:507
  103.0 2.4 %collective-permute-start.19 = (bf16[2,256,256]{2,1,0:T(8,128)(2,1)S(1)}, bf16[2,256,256]{2,1,0:T(8,128)(2,1)S(1)}, u32[]{:S(2)}, u32[]{:S(2)}) collective-permute-start(bf16[2,256,256]{2,1,0:T(8,128)(2,1)S(1)} %pad_maximum_fusion.3), channel_id=1, source_target_pairs={{0,8},{4,12},{8,0},{12,4},{16,24},{20,28},{24,16},{28,20},{1,9},{5... | collective-permute-start | bytes 786440 | tf_op jit(solution)/shard_map/ppermute | solution.py:507
  105.5 1.6 %collective-permute-start.20 = (bf16[2,256,256]{2,1,0:T(8,128)(2,1)S(1)}, bf16[2,256,256]{2,1,0:T(8,128)(2,1)S(1)}, u32[]{:S(2)}, u32[]{:S(2)}) collective-permute-start(bf16[2,256,256]{2,1,0:T(8,128)(2,1)S(1)} %pad_maximum_fusion.4), channel_id=1, source_target_pairs={{0,16},{4,20},{8,24},{12,28},{16,0},{20,4},{24,8},{28,12},{1,17},{... | collective-permute-start | bytes 786440 | tf_op jit(solution)/shard_map/ppermute | solution.py:507
  107.2 7.0 %collective-permute-done.19 = bf16[2,256,256]{2,1,0:T(8,128)(2,1)S(1)} collective-permute-done((bf16[2,256,256]{2,1,0:T(8,128)(2,1)S(1)}, bf16[2,256,256]{2,1,0:T(8,128)(2,1)S(1)}, u32[]{:S(2)}, u32[]{:S(2)}) %collective-permute-start.19) | collective-permute-done | bytes 262176 | tf_op jit(solution)/shard_map/ppermute | solution.py:507
  114.2 3.8 %collective-permute-done.20 = bf16[2,256,256]{2,1,0:T(8,128)(2,1)S(1)} collective-permute-done((bf16[2,256,256]{2,1,0:T(8,128)(2,1)S(1)}, bf16[2,256,256]{2,1,0:T(8,128)(2,1)S(1)}, u32[]{:S(2)}, u32[]{:S(2)}) %collective-permute-start.20) | collective-permute-done | bytes 262176 | tf_op jit(solution)/shard_map/ppermute | solution.py:507
  118.8 3.5 %collective-permute-start.25 = (bf16[4,256,256]{2,1,0:T(8,128)(2,1)S(1)}, bf16[4,256,256]{2,1,0:T(8,128)(2,1)S(1)}, u32[]{:S(2)}, u32[]{:S(2)}) collective-permute-start(bf16[4,256,256]{2,1,0:T(8,128)(2,1)S(1)} %constant_dynamic-update-slice_fusion.2.refs_7_), channel_id=1, source_target_pairs={{0,8},{4,12},{8,0},{12,4},{16,24},{20,28},{24,16},{28,20},{1,9},{5... | collective-permute-start | bytes 1572872 | tf_op jit(solution)/shard_map/ppermute | solution.py:507
  122.3 5.1 %shard_map.96 = (f32[1024,128]{1,0:T(8,128)}, bf16[1024,128]{1,0:T(8,128)(2,1)}) custom-call(s32[3]{0:T(128)} %pad_add_fusion.refs_0_.position_ref, f32[2,1024,128]{2,1,0:T(8,128)} %get-tuple-element.93.mask_in_ref, bf16[128,3200]{1,0:T(8,128)(2,1)} %get-tuple-element.84.refs_0_, bf16[128,3200]{1,0:T(8,128)(2,1)} %copy-done.4, bf16[128,3200]{1,0:T(8,128)(2,1)} %copy-done.3, ...), custom_call_target="tpu_custom_call" | custom-call | flops 1 | bytes 1 | tf_op jit(solution)/shard_map/pallas_call | solution.py:307
  127.4 1.8 %collective-permute-start.22 = (bf16[1024,128]{1,0:T(8,128)(2,1)}, bf16[1024,128]{1,0:T(8,128)(2,1)S(1)}, u32[]{:S(2)}, u32[]{:S(2)}) collective-permute-start(bf16[1024,128]{1,0:T(8,128)(2,1)} %get-tuple-element.109), channel_id=1, source_target_pairs={{0,2},{1,3},{2,0},{3,1},{4,6},{5,7},{6,4},{7,5},{8,10},{9,11},{10,... | collective-permute-start | bytes 786440 | tf_op jit(solution)/shard_map/ppermute | solution.py:651
  129.2 1.2 copy-done.1
  130.4 6.1 %shard_map.97.refs_5_ = f32[1024,256]{1,0:T(8,128)} custom-call(s32[3]{0:T(128)} %pad_add_fusion.refs_0_.position_ref, bf16[256,4096]{1,0:T(8,128)(2,1)} %get-tuple-element.89.refs_0_.refs_6_, bf16[256,4096]{1,0:T(8,128)(2,1)} %copy-done, bf16[64,4096]{1,0:T(8,128)(2,1)} %copy-done.9, bf16[192,4096]{1,0:T(8,128)(2,1)} %collective-permute-done.21.refs_3_.refs_9_, ...), custom_call_target="tpu_custom_call" | custom-call | flops 1 | bytes 1 | tf_op jit(solution)/shard_map/pallas_call | solution.py:451
  136.6 0.7 copy-done.15
  137.6 7.2 %shard_map.98 = (f32[4,4]{1,0:T(4,128)}, f32[4,4]{1,0:T(4,128)}, f32[4,4]{1,0:T(4,128)}, f32[4,4]{1,0:T(4,128)}) custom-call(s32[3]{0:T(128)} %pad_add_fusion.refs_0_.position_ref, f32[128,4]{1,0:T(8,128)} %constant.71.clone.refs_0_, bf16[2,1024,128]{2,1,0:T(8,128)(2,1)} %get-tuple-element.91.refs_1_, bf16[1024,128]{1,0:T(8,128)(2,1)} %get-tuple-element.92.refs_2_, ...), custom_call_target="tpu_custom_call" | custom-call | flops 1 | bytes 1 | tf_op jit(solution)/shard_map/pallas_call | solution.py:460
  145.1 1.3 collective-permute-start.27
  146.8 1.4 collective-permute-done.28
  148.8 1.3 add_add_fusion
  (99 shorter events, 6.3 us)
Async XLA Ops:
  11.2 2.6 %copy-start.8 = (f32[4112,128]{1,0:T(8,128)S(1)}, f32[4112,128]{1,0:T(8,128)}, u32[]{:S(2)}) copy-start(f32[4112,128]{1,0:T(8,128)} %get-tuple-element.63) | copy-start | bytes 6316036
  13.8 4.7 %copy-start.19 = (s32[1,128]{1,0:T(1,128)S(1)}, s32[1,128]{1,0:T(1,128)}, u32[]{:S(2)}) copy-start(s32[1,128]{1,0:T(1,128)} %param.12) | copy-start | bytes 1540
  13.8 4.7 %copy-start.18 = (s32[128,2]{0,1:T(2,128)S(1)}, s32[128,2]{0,1:T(2,128)}, u32[]{:S(2)}) copy-start(s32[128,2]{0,1:T(2,128)} %param.11) | copy-start | bytes 3076
  13.9 21.1 %collective-permute-start = (f16[3088,128]{1,0:T(8,128)(2,1)}, f16[3088,128]{1,0:T(8,128)(2,1)S(1)}, u32[]{:S(2)}, u32[]{:S(2)}) collective-permute-start(f16[3088,128]{1,0:T(8,128)(2,1)} %convert_element_type.77), channel_id=1, source_target_pairs={{0,8},{4,12},{8,0},{12,4},{16,24},{20,28},{24,16},{28,20},{1,9},{5... | collective-permute-start | bytes 2371592 | tf_op jit(solution)/shard_map/ppermute | solution.py:507
  17.0 26.2 %collective-permute-start.2 = (f16[4112,128]{1,0:T(8,128)(2,1)S(1)}, f16[4112,128]{1,0:T(8,128)(2,1)S(1)}, u32[]{:S(2)}, u32[]{:S(2)}) collective-permute-start(f16[4112,128]{1,0:T(8,128)(2,1)S(1)} %convert_element_type.78), channel_id=1, source_target_pairs={{0,4},{4,0},{8,12},{12,8},{16,20},{20,16},{24,28},{28,24},{1,5},{5... | collective-permute-start | bytes 3158024 | tf_op jit(solution)/shard_map/ppermute | solution.py:507
  22.6 37.6 %collective-permute-start.5 = (bf16[128,3200]{1,0:T(8,128)(2,1)}, bf16[128,3200]{1,0:T(8,128)(2,1)S(1)}, u32[]{:S(2)}, u32[]{:S(2)}) collective-permute-start(bf16[128,3200]{1,0:T(8,128)(2,1)} %get-tuple-element.79), channel_id=1, source_target_pairs={{0,2},{1,3},{2,0},{3,1},{4,6},{5,7},{6,4},{7,5},{8,10},{9,11},{10,... | collective-permute-start | bytes 2457608 | tf_op jit(solution)/shard_map/ppermute | solution.py:531
  24.2 10.7 %copy-start.10 = (bf16[1,768,128]{2,1,0:T(8,128)(2,1)S(1)}, bf16[1,768,128]{2,1,0:T(8,128)(2,1)}, u32[]{:S(2)}) copy-start(bf16[1,768,128]{2,1,0:T(8,128)(2,1)} %param.15) | copy-start | bytes 589828
  24.2 10.8 %copy-start.6 = (bf16[1,1024,128]{2,1,0:T(8,128)(2,1)S(1)}, bf16[1,1024,128]{2,1,0:T(8,128)(2,1)}, u32[]{:S(2)}) copy-start(bf16[1,1024,128]{2,1,0:T(8,128)(2,1)} %param.16) | copy-start | bytes 786436
  35.1 8.1 %copy-start.7 = (f32[4112,128]{1,0:T(8,128)S(1)}, f32[4112,128]{1,0:T(8,128)}, u32[]{:S(2)}) copy-start(f32[4112,128]{1,0:T(8,128)} %get-tuple-element.72) | copy-start | bytes 6316036
  36.9 15.0 %collective-permute-start.1 = (f16[1552,128]{1,0:T(8,128)(2,1)S(1)}, f16[1552,128]{1,0:T(8,128)(2,1)S(1)}, u32[]{:S(2)}, u32[]{:S(2)}) collective-permute-start(f16[1552,128]{1,0:T(8,128)(2,1)S(1)} %get-tuple-element.125), channel_id=1, source_target_pairs={{0,4},{4,0},{8,12},{12,8},{16,20},{20,16},{24,28},{28,24},{1,5},{5... | collective-permute-start | bytes 1191944 | tf_op jit(solution)/shard_map/ppermute | solution.py:507
  44.4 15.5 %collective-permute-start.3 = (f16[2064,128]{1,0:T(8,128)(2,1)S(1)}, f16[2064,128]{1,0:T(8,128)(2,1)S(1)}, u32[]{:S(2)}, u32[]{:S(2)}) collective-permute-start(f16[2064,128]{1,0:T(8,128)(2,1)S(1)} %get-tuple-element.77), channel_id=1, source_target_pairs={{0,8},{4,12},{8,0},{12,4},{16,24},{20,28},{24,16},{28,20},{1,9},{5... | collective-permute-start | bytes 1585160 | tf_op jit(solution)/shard_map/ppermute | solution.py:507
  50.1 11.6 %collective-permute-start.6 = (bf16[64,4096]{1,0:T(8,128)(2,1)}, bf16[64,4096]{1,0:T(8,128)(2,1)S(1)}, u32[]{:S(2)}, u32[]{:S(2)}) collective-permute-start(bf16[64,4096]{1,0:T(8,128)(2,1)} %get-tuple-element.81), channel_id=1, source_target_pairs={{0,2},{1,3},{2,0},{3,1},{4,6},{5,7},{6,4},{7,5},{8,10},{9,11},{10,... | collective-permute-start | bytes 1572872 | tf_op jit(solution)/shard_map/ppermute | solution.py:531
  52.2 7.9 %collective-permute-start.4 = (f16[784,128]{1,0:T(8,128)(2,1)S(1)}, f16[784,128]{1,0:T(8,128)(2,1)S(1)}, u32[]{:S(2)}, u32[]{:S(2)}) collective-permute-start(f16[784,128]{1,0:T(8,128)(2,1)S(1)} %get-tuple-element.130), channel_id=1, source_target_pairs={{0,16},{4,20},{8,24},{12,28},{16,0},{20,4},{24,8},{28,12},{1,17},{... | collective-permute-start | bytes 602120 | tf_op jit(solution)/shard_map/ppermute | solution.py:507
  54.9 34.3 %collective-permute-start.12 = (bf16[256,4096]{1,0:T(8,128)(2,1)}, bf16[256,4096]{1,0:T(8,128)(2,1)S(1)}, u32[]{:S(2)}, u32[]{:S(2)}) collective-permute-start(bf16[256,4096]{1,0:T(8,128)(2,1)} %get-tuple-element.89.refs_0_.refs_6_), channel_id=1, source_target_pairs={{0,1},{1,0},{2,3},{3,2},{4,5},{5,4},{6,7},{7,6},{8,9},{9,8},{10,11... | collective-permute-start | bytes 6291464 | tf_op jit(solution)/shard_map/ppermute | solution.py:534
  60.1 6.6 %copy-start.2 = (bf16[128,3200]{1,0:T(8,128)(2,1)S(1)}, bf16[128,3200]{1,0:T(8,128)(2,1)}, u32[]{:S(2)}) copy-start(bf16[128,3200]{1,0:T(8,128)(2,1)} %get-tuple-element.84.refs_0_) | copy-start | bytes 2457604
  60.3 13.2 %copy-start.3 = (bf16[128,3200]{1,0:T(8,128)(2,1)}, bf16[128,3200]{1,0:T(8,128)(2,1)S(1)}, u32[]{:S(2)}) copy-start(bf16[128,3200]{1,0:T(8,128)(2,1)S(1)} %collective-permute-done.5.refs_2_) | copy-start | bytes 2457604
  61.6 11.8 %copy-start.9 = (bf16[64,4096]{1,0:T(8,128)(2,1)}, bf16[64,4096]{1,0:T(8,128)(2,1)S(1)}, u32[]{:S(2)}) copy-start(bf16[64,4096]{1,0:T(8,128)(2,1)S(1)} %collective-permute-done.6.refs_2_.refs_8_) | copy-start | bytes 1572868
  61.6 11.6 %collective-permute-start.8 = (f16[1040,128]{1,0:T(8,128)(2,1)S(1)}, f16[1040,128]{1,0:T(8,128)(2,1)S(1)}, u32[]{:S(2)}, u32[]{:S(2)}) collective-permute-start(f16[1040,128]{1,0:T(8,128)(2,1)S(1)} %get-tuple-element.127), channel_id=1, source_target_pairs={{0,16},{4,20},{8,24},{12,28},{16,0},{20,4},{24,8},{28,12},{1,17},{... | collective-permute-start | bytes 798728 | tf_op jit(solution)/shard_map/ppermute | solution.py:507
  64.4 4.9 %collective-permute-start.7 = (bf16[384,128]{1,0:T(8,128)(2,1)S(1)}, bf16[384,128]{1,0:T(8,128)(2,1)S(1)}, u32[]{:S(2)}, u32[]{:S(2)}) collective-permute-start(bf16[384,128]{1,0:T(8,128)(2,1)S(1)} %get-tuple-element.144), channel_id=1, source_target_pairs={{0,2},{1,3},{2,0},{3,1},{4,6},{5,7},{6,4},{7,5},{8,10},{9,11},{10,... | collective-permute-start | bytes 294920 | tf_op jit(solution)/shard_map/ppermute | solution.py:526
  66.7 12.6 %collective-permute-start.10 = (bf16[128,3200]{1,0:T(8,128)(2,1)S(1)}, bf16[128,3200]{1,0:T(8,128)(2,1)S(1)}, u32[]{:S(2)}, u32[]{:S(2)}) collective-permute-start(bf16[128,3200]{1,0:T(8,128)(2,1)S(1)} %copy-done.2), channel_id=1, source_target_pairs={{0,1},{1,0},{2,3},{3,2},{4,5},{5,4},{6,7},{7,6},{8,9},{9,8},{10,11... | collective-permute-start | bytes 2457608 | tf_op jit(solution)/shard_map/ppermute | solution.py:534
  66.7 15.0 %collective-permute-start.11 = (bf16[128,3200]{1,0:T(8,128)(2,1)S(1)}, bf16[128,3200]{1,0:T(8,128)(2,1)}, u32[]{:S(2)}, u32[]{:S(2)}) collective-permute-start(bf16[128,3200]{1,0:T(8,128)(2,1)S(1)} %collective-permute-done.5.refs_2_), channel_id=1, source_target_pairs={{0,1},{1,0},{2,3},{3,2},{4,5},{5,4},{6,7},{7,6},{8,9},{9,8},{10,11... | collective-permute-start | bytes 2457608 | tf_op jit(solution)/shard_map/ppermute | solution.py:534
  69.3 20.0 %collective-permute-start.13 = (bf16[64,4096]{1,0:T(8,128)(2,1)S(1)}, bf16[64,4096]{1,0:T(8,128)(2,1)}, u32[]{:S(2)}, u32[]{:S(2)}) collective-permute-start(bf16[64,4096]{1,0:T(8,128)(2,1)S(1)} %collective-permute-done.6.refs_2_.refs_8_), channel_id=1, source_target_pairs={{0,1},{1,0},{2,3},{3,2},{4,5},{5,4},{6,7},{7,6},{8,9},{9,8},{10,11... | collective-permute-start | bytes 1572872 | tf_op jit(solution)/shard_map/ppermute | solution.py:534
  73.4 5.0 %collective-permute-start.15 = (bf16[512,128]{1,0:T(8,128)(2,1)S(1)}, bf16[512,128]{1,0:T(8,128)(2,1)S(1)}, u32[]{:S(2)}, u32[]{:S(2)}) collective-permute-start(bf16[512,128]{1,0:T(8,128)(2,1)S(1)} %get-tuple-element.142), channel_id=1, source_target_pairs={{0,2},{1,3},{2,0},{3,1},{4,6},{5,7},{6,4},{7,5},{8,10},{9,11},{10,... | collective-permute-start | bytes 393224 | tf_op jit(solution)/shard_map/ppermute | solution.py:526
  78.5 10.8 %collective-permute-start.9 = (bf16[1,384,256]{2,1,0:T(8,128)(2,1)}, bf16[1,384,256]{2,1,0:T(8,128)(2,1)}, u32[]{:S(2)}, u32[]{:S(2)}) collective-permute-start(bf16[1,384,256]{2,1,0:T(8,128)(2,1)} %bitcast.26), channel_id=1, source_target_pairs={{0,16},{4,20},{8,24},{12,28},{16,0},{20,4},{24,8},{28,12},{1,17},{... | collective-permute-start | bytes 589832 | tf_op jit(solution)/shard_map/ppermute | solution.py:507
  79.2 0.9 copy-start.4
  80.1 10.7 %copy-start.13 = (bf16[512,256]{1,0:T(8,128)(2,1)S(1)}, bf16[512,256]{1,0:T(8,128)(2,1)}, u32[]{:S(2)}) copy-start(bf16[512,256]{1,0:T(8,128)(2,1)} %pad_maximum_fusion.2) | copy-start | bytes 786436
  80.1 37.9 %collective-permute-start.21 = (bf16[192,4096]{1,0:T(8,128)(2,1)}, bf16[192,4096]{1,0:T(8,128)(2,1)}, u32[]{:S(2)}, u32[]{:S(2)}) collective-permute-start(bf16[192,4096]{1,0:T(8,128)(2,1)} %get-tuple-element.103), channel_id=1, source_target_pairs={{0,2},{1,3},{2,0},{3,1},{4,6},{5,7},{6,4},{7,5},{8,10},{9,11},{10,... | collective-permute-start | bytes 4718600 | tf_op jit(solution)/shard_map/ppermute | solution.py:531
  89.2 10.3 %copy-start = (bf16[256,4096]{1,0:T(8,128)(2,1)}, bf16[256,4096]{1,0:T(8,128)(2,1)S(1)}, u32[]{:S(2)}) copy-start(bf16[256,4096]{1,0:T(8,128)(2,1)S(1)} %collective-permute-done.12.refs_1_.refs_7_) | copy-start | bytes 6291460
  90.7 9.6 %collective-permute-start.14 = (bf16[2,384,256]{2,1,0:T(8,128)(2,1)S(1)}, bf16[2,384,256]{2,1,0:T(8,128)(2,1)S(1)}, u32[]{:S(2)}, u32[]{:S(2)}) collective-permute-start(bf16[2,384,256]{2,1,0:T(8,128)(2,1)S(1)} %pad_maximum_fusion.1), channel_id=1, source_target_pairs={{0,8},{4,12},{8,0},{12,4},{16,24},{20,28},{24,16},{28,20},{1,9},{5... | collective-permute-start | bytes 1179656 | tf_op jit(solution)/shard_map/ppermute | solution.py:507
  90.9 8.6 %collective-permute-start.16 = (bf16[1,256,256]{2,1,0:T(8,128)(2,1)S(1)}, bf16[1,256,256]{2,1,0:T(8,128)(2,1)S(1)}, u32[]{:S(2)}, u32[]{:S(2)}) collective-permute-start(bf16[1,256,256]{2,1,0:T(8,128)(2,1)S(1)} %get-tuple-element.140), channel_id=1, source_target_pairs={{0,16},{4,20},{8,24},{12,28},{16,0},{20,4},{24,8},{28,12},{1,17},{... | collective-permute-start | bytes 393224 | tf_op jit(solution)/shard_map/ppermute | solution.py:507
  91.7 7.8 %collective-permute-start.17 = (bf16[1,256,256]{2,1,0:T(8,128)(2,1)S(1)}, bf16[1,256,256]{2,1,0:T(8,128)(2,1)S(1)}, u32[]{:S(2)}, u32[]{:S(2)}) collective-permute-start(bf16[1,256,256]{2,1,0:T(8,128)(2,1)S(1)} %get-tuple-element.139), channel_id=1, source_target_pairs={{0,4},{4,0},{8,12},{12,8},{16,20},{20,16},{24,28},{28,24},{1,5},{5... | collective-permute-start | bytes 393224 | tf_op jit(solution)/shard_map/ppermute | solution.py:507
  101.5 20.9 %copy-start.5 = (bf16[4,384,256]{2,1,0:T(8,128)(2,1)}, bf16[4,384,256]{2,1,0:T(8,128)(2,1)S(1)}, u32[]{:S(2)}) copy-start(bf16[4,384,256]{2,1,0:T(8,128)(2,1)S(1)} %pad_maximum_fusion.refs_4_) | copy-start | bytes 2359300
  101.5 16.6 %collective-permute-start.18 = (bf16[4,384,256]{2,1,0:T(8,128)(2,1)S(1)}, bf16[4,384,256]{2,1,0:T(8,128)(2,1)S(1)}, u32[]{:S(2)}, u32[]{:S(2)}) collective-permute-start(bf16[4,384,256]{2,1,0:T(8,128)(2,1)S(1)} %pad_maximum_fusion.refs_4_), channel_id=1, source_target_pairs={{0,4},{4,0},{8,12},{12,8},{16,20},{20,16},{24,28},{28,24},{1,5},{5... | collective-permute-start | bytes 2359304 | tf_op jit(solution)/shard_map/ppermute | solution.py:507
  103.0 11.1 %collective-permute-start.19 = (bf16[2,256,256]{2,1,0:T(8,128)(2,1)S(1)}, bf16[2,256,256]{2,1,0:T(8,128)(2,1)S(1)}, u32[]{:S(2)}, u32[]{:S(2)}) collective-permute-start(bf16[2,256,256]{2,1,0:T(8,128)(2,1)S(1)} %pad_maximum_fusion.3), channel_id=1, source_target_pairs={{0,8},{4,12},{8,0},{12,4},{16,24},{20,28},{24,16},{28,20},{1,9},{5... | collective-permute-start | bytes 786440 | tf_op jit(solution)/shard_map/ppermute | solution.py:507
  105.5 12.5 %collective-permute-start.20 = (bf16[2,256,256]{2,1,0:T(8,128)(2,1)S(1)}, bf16[2,256,256]{2,1,0:T(8,128)(2,1)S(1)}, u32[]{:S(2)}, u32[]{:S(2)}) collective-permute-start(bf16[2,256,256]{2,1,0:T(8,128)(2,1)S(1)} %pad_maximum_fusion.4), channel_id=1, source_target_pairs={{0,16},{4,20},{8,24},{12,28},{16,0},{20,4},{24,8},{28,12},{1,17},{... | collective-permute-start | bytes 786440 | tf_op jit(solution)/shard_map/ppermute | solution.py:507
  114.2 13.2 %copy-start.12 = (bf16[4,256,256]{2,1,0:T(8,128)(2,1)}, bf16[4,256,256]{2,1,0:T(8,128)(2,1)S(1)}, u32[]{:S(2)}) copy-start(bf16[4,256,256]{2,1,0:T(8,128)(2,1)S(1)} %constant_dynamic-update-slice_fusion.refs_6_) | copy-start | bytes 1572868
  118.0 9.4 %copy-start.11 = (bf16[4,256,256]{2,1,0:T(8,128)(2,1)}, bf16[4,256,256]{2,1,0:T(8,128)(2,1)S(1)}, u32[]{:S(2)}) copy-start(bf16[4,256,256]{2,1,0:T(8,128)(2,1)S(1)} %constant_dynamic-update-slice_fusion.2.refs_7_) | copy-start | bytes 1572868
  118.0 4.3 %copy-start.14 = (bf16[4,384,256]{2,1,0:T(8,128)(2,1)}, bf16[4,384,256]{2,1,0:T(8,128)(2,1)S(1)}, u32[]{:S(2)}) copy-start(bf16[4,384,256]{2,1,0:T(8,128)(2,1)S(1)} %collective-permute-done.18.refs_5_) | copy-start | bytes 2359300
  118.1 11.2 %collective-permute-start.23 = (bf16[192,4096]{1,0:T(8,128)(2,1)}, bf16[192,4096]{1,0:T(8,128)(2,1)S(1)}, u32[]{:S(2)}, u32[]{:S(2)}) collective-permute-start(bf16[192,4096]{1,0:T(8,128)(2,1)} %collective-permute-done.21.refs_3_.refs_9_), channel_id=1, source_target_pairs={{0,1},{1,0},{2,3},{3,2},{4,5},{5,4},{6,7},{7,6},{8,9},{9,8},{10,11... | collective-permute-start | bytes 4718600 | tf_op jit(solution)/shard_map/ppermute | solution.py:534
  118.1 18.4 %collective-permute-start.24 = (bf16[4,256,256]{2,1,0:T(8,128)(2,1)S(1)}, bf16[4,256,256]{2,1,0:T(8,128)(2,1)S(1)}, u32[]{:S(2)}, u32[]{:S(2)}) collective-permute-start(bf16[4,256,256]{2,1,0:T(8,128)(2,1)S(1)} %constant_dynamic-update-slice_fusion.refs_6_), channel_id=1, source_target_pairs={{0,4},{4,0},{8,12},{12,8},{16,20},{20,16},{24,28},{28,24},{1,5},{5... | collective-permute-start | bytes 1572872 | tf_op jit(solution)/shard_map/ppermute | solution.py:507
  118.8 17.8 %collective-permute-start.25 = (bf16[4,256,256]{2,1,0:T(8,128)(2,1)S(1)}, bf16[4,256,256]{2,1,0:T(8,128)(2,1)S(1)}, u32[]{:S(2)}, u32[]{:S(2)}) collective-permute-start(bf16[4,256,256]{2,1,0:T(8,128)(2,1)S(1)} %constant_dynamic-update-slice_fusion.2.refs_7_), channel_id=1, source_target_pairs={{0,8},{4,12},{8,0},{12,4},{16,24},{20,28},{24,16},{28,20},{1,9},{5... | collective-permute-start | bytes 1572872 | tf_op jit(solution)/shard_map/ppermute | solution.py:507
  127.4 9.2 %collective-permute-start.22 = (bf16[1024,128]{1,0:T(8,128)(2,1)}, bf16[1024,128]{1,0:T(8,128)(2,1)S(1)}, u32[]{:S(2)}, u32[]{:S(2)}) collective-permute-start(bf16[1024,128]{1,0:T(8,128)(2,1)} %get-tuple-element.109), channel_id=1, source_target_pairs={{0,2},{1,3},{2,0},{3,1},{4,6},{5,7},{6,4},{7,5},{8,10},{9,11},{10,... | collective-permute-start | bytes 786440 | tf_op jit(solution)/shard_map/ppermute | solution.py:651
  129.2 1.2 copy-start.1
  136.6 0.9 copy-start.16
  136.6 1.0 copy-start.17
  144.8 3.3 %collective-permute-start.28 = (f32[4,4]{1,0:T(4,128)}, f32[4,4]{1,0:T(4,128)S(1)}, u32[]{:S(2)}, u32[]{:S(2)}) collective-permute-start(f32[4,4]{1,0:T(4,128)} %get-tuple-element.118), channel_id=1, source_target_pairs={{0,3},{1,2},{2,1},{3,0},{4,7},{5,6},{6,5},{7,4},{8,11},{9,10},{10,... | collective-permute-start | bytes 200 | tf_op jit(solution)/shard_map/ppermute | solution.py:664
  145.1 3.6 %collective-permute-start.27 = (f32[4,4]{1,0:T(4,128)}, f32[4,4]{1,0:T(4,128)S(1)}, u32[]{:S(2)}, u32[]{:S(2)}) collective-permute-start(f32[4,4]{1,0:T(4,128)} %get-tuple-element.117), channel_id=1, source_target_pairs={{0,2},{1,3},{2,0},{3,1},{4,6},{5,7},{6,4},{7,5},{8,10},{9,11},{10,... | collective-permute-start | bytes 200 | tf_op jit(solution)/shard_map/ppermute | solution.py:664
  146.4 2.4 %collective-permute-start.26 = (f32[4,4]{1,0:T(4,128)}, f32[4,4]{1,0:T(4,128)S(1)}, u32[]{:S(2)}, u32[]{:S(2)}) collective-permute-start(f32[4,4]{1,0:T(4,128)} %get-tuple-element.116), channel_id=1, source_target_pairs={{0,1},{1,0},{2,3},{3,2},{4,5},{5,4},{6,7},{7,6},{8,9},{9,8},{10,11... | collective-permute-start | bytes 200 | tf_op jit(solution)/shard_map/ppermute | solution.py:664
  (1 other events, 0.8 us)

commit v7 on v6

--- a/solution.py
+++ b/solution.py
@@ -259,7 +259,7 @@
             jax.ShapeDtypeStruct((rows, lanes), jnp.bfloat16),
         ],
         scratch_shapes=[pltpu.VMEM((rows, lanes), jnp.float32)],
-        cost_estimate=pl.CostEstimate(flops=1, bytes_accessed=1, transcendentals=0),
+        cost_estimate=pl.CostEstimate(flops=1, bytes_accessed=60000000, transcendentals=0),
     )(position, *pieces)
 
 
@@ -444,7 +444,7 @@
         pltpu.VMEM((width, across), folds[0].dtype),
     ]
     options = dict(
-        compiler_params=pltpu.CompilerParams(vmem_limit_bytes=58 * 1024 * 1024),
+        compiler_params=pltpu.CompilerParams(vmem_limit_bytes=32 * 1024 * 1024),
         cost_estimate=pl.CostEstimate(flops=1, bytes_accessed=1, transcendentals=0),
     )
     if not extras:
@@ -588,7 +588,6 @@
     for part in input_parts:
         input_pieces += [part, from_core(part)]
     swapped_gradient = from_core(own_gradient)
-    mask, small_mask, membership = masks(position, input_pieces, top, halves, columns)
     query_sum = jnp.asarray(
         np.arange(columns)[:, None] // RANK == np.arange(queries)[None, :], jnp.float32
     )
@@ -610,9 +609,10 @@
     held_first = shard_first[None]
     landed_first = send(held_first, order_second[-1])
     shard_second = exchange(own_shard(keep_second, landed_second))
-    shard_second, *late = tie(shard_second, *late)
-    landed_first, mask, small_mask, membership, swapped_gradient, *swapped_early = tie(
-        landed_first, mask, small_mask, membership, swapped_gradient, *swapped_early
+    shard_second, *rest = tie(shard_second, *late, *input_pieces)
+    late, input_pieces = rest[: halves - 1], rest[halves - 1 :]
+    landed_first, swapped_gradient, *swapped_early = tie(
+        landed_first, swapped_gradient, *swapped_early
     )
     held_first = jnp.concatenate([held_first, landed_first])
     late = [from_half(part, d) for d, part in zip(others, late)]
@@ -621,10 +621,15 @@
         landed_first = send(held_first, order_second[-stage])
         landed = stage_of(held_second, 1 - stage)
         held_second = both(held_second, landed)
-        landed_first, *held_second = tie(landed_first, *held_second)
+        if stage + 1 == count:
+            input_pieces[0], *rest = tie(input_pieces[0], *held_second)
+            mask, small_mask, membership = masks(position, input_pieces, top, halves, columns)
+            landed_first, mask, small_mask, membership, *rest = tie(
+                landed_first, mask, small_mask, membership, *rest
+            )
         held_first = jnp.concatenate([held_first, landed_first])
     last_first = send(held_first, order_second[0])
-    held_second = both(held_second, stage_of(held_second, 1 - count))
+    held_second = both(rest, stage_of(held_second, 1 - count))
     last_second = stage_of(held_second, 0)
     last_first, *held_second = tie(last_first, *held_second)
     last_first, *late = tie(last_first, *late)

time: 151 us -> 147 us (0.974)
  Pallas kernels: 51 us -> 47.5 us
  waiting for transfers between devices: 45 us -> 48.4 us
  local copies, waits for them, and re-layouts: 4.06 us -> 2.38 us
    ppermute x1, starting transfers between devices: 1.81 us -> 5.72 us  [per_device(): lax.ppermute(sent, 'expert', flip(group, d * CORES))]
    ppermute x15, starting transfers between devices: 23.8 us -> 20.3 us  [send(): return lax.ppermute(packed, 'dp', flip(blocks, 1 << bit))]
    unnamed x42, local copies, waits for them, and re-layouts: 3.18 us -> 0.81 us
    ppermute x1, waiting for transfers between devices: 0.01 us -> 2.06 us  [per_device(): lax.ppermute(sent, 'expert', flip(group, d * CORES))]
    pallas_call x1, Pallas kernels: 7.24 us -> 5.28 us  [score_call(): pl.pallas_call(functools.partial(last_kernel, layouts, aligned, len(piece...]
    pallas_call x1, Pallas kernels: 6.14 us -> 4.47 us  [score_call(): pl.pallas_call(functools.partial(first_kernel, layouts, len(pieces)), in_...]
  transfers between devices with their start and end apart: 29 -> 29, of which waited for: 13 -> 13; matrix products, arithmetic and copies ran while one was open for 6% -> 7% of each run, Pallas kernels for 22% -> 22%
where the time goes in v7:
time: 147 us
  waiting for transfers between devices  48.4 us (33%)
  Pallas kernels  47.5 us (32%)
  starting transfers between devices  37.1 us (25%)
  other arithmetic  11.2 us (8%)
  local copies, waits for them, and re-layouts  2.38 us (2%)
    ppermute x15, waiting for transfers between devices, send(): return lax.ppermute(packed, 'dp', flip(blocks, 1 << bit))  37 us
    pallas_call x2, Pallas kernels, fold_parts(): pl.pallas_call(functools.partial(fold_kernel, width, steps, upper), grid_...  21.3 us
    ppermute x15, starting transfers between devices, send(): return lax.ppermute(packed, 'dp', flip(blocks, 1 << bit))  20.3 us
    ppermute x2, waiting for transfers between devices, exchange(): lax.ppermute(shard[d], 'expert', flip(group, d * CORES))  5.78 us
    ppermute x1, starting transfers between devices, per_device(): lax.ppermute(sent, 'expert', flip(group, d * CORES))  5.72 us
    pallas_call x1, Pallas kernels, flattened_parts(): pl.pallas_call(functools.partial(flatten_kernel, halves), grid_spec=pltpu...  5.61 us
    pallas_call x1, Pallas kernels, score_call(): pl.pallas_call(functools.partial(last_kernel, layouts, aligned, len(piece...  5.28 us
    pallas_call x1, Pallas kernels, input_chosen(): pl.pallas_call(functools.partial(input_kernel, top, layouts, len(pieces))...  5.23 us
  transfers between devices with their start and end apart: 29, of which 13 were waited for; matrix products, arithmetic and copies ran while one was open for 7% of the time, Pallas kernels for 22%

profile of v7, /device:TPU:0, one launch (start us, length us, event | category | flops | bytes accessed | tf_op | source)
XLA Modules:
  0.0 146.9 jit_solution(12655346108286711709)
XLA Ops:
  0.6 10.6 %shard_map.91 = (f32[3088,128]{1,0:T(8,128)}, f32[4112,128]{1,0:T(8,128)}) custom-call(s32[3]{0:T(128)} %pad_add_fusion.refs_0_.position_ref, bf16[6144,768]{1,0:T(8,128)(2,1)} %bitcast.65, bf16[6144,768]{1,0:T(8,128)(2,1)} %bitcast.66, bf16[6144,768]{1,0:T(8,128)(2,1)} %bitcast.67, bf16[6144,768]{1,0:T(8,128)(2,1)} %bitcast.68, ...), custom_call_target="tpu_custom_call" | custom-call | flops 1 | bytes 1 | tf_op jit(solution)/shard_map/pallas_call | solution.py:104
  11.2 2.6 %convert_element_type.77 = f16[3088,128]{1,0:T(8,128)(2,1)} convert(f32[3088,128]{1,0:T(8,128)} %get-tuple-element.69) | non-fusion elementwise | flops 395264 | bytes 2371584 | tf_op jit(solution)/shard_map/convert_element_type | solution.py:545
  13.9 3.1 %collective-permute-start = (f16[3088,128]{1,0:T(8,128)(2,1)}, f16[3088,128]{1,0:T(8,128)(2,1)S(1)}, u32[]{:S(2)}, u32[]{:S(2)}) collective-permute-start(f16[3088,128]{1,0:T(8,128)(2,1)} %convert_element_type.77), channel_id=1, source_target_pairs={{0,8},{4,12},{8,0},{12,4},{16,24},{20,28},{24,16},{28,20},{1,9},{5... | collective-permute-start | bytes 2371592 | tf_op jit(solution)/shard_map/ppermute | solution.py:507
  17.0 1.5 %collective-permute-start.2 = (f16[4112,128]{1,0:T(8,128)(2,1)S(1)}, f16[4112,128]{1,0:T(8,128)(2,1)S(1)}, u32[]{:S(2)}, u32[]{:S(2)}) collective-permute-start(f16[4112,128]{1,0:T(8,128)(2,1)S(1)} %convert_element_type.78), channel_id=1, source_target_pairs={{0,4},{4,0},{8,12},{12,8},{16,20},{20,16},{24,28},{28,24},{1,5},{5... | collective-permute-start | bytes 3158024 | tf_op jit(solution)/shard_map/ppermute | solution.py:507
  18.7 0.6 pad.4.extra_ref
  19.3 3.3 %shard_map.92 = (bf16[128,3200]{1,0:T(8,128)(2,1)}, bf16[128,3200]{1,0:T(8,128)(2,1)}) custom-call(s32[3]{0:T(128)} %pad_add_fusion.refs_0_.position_ref, bf16[128,6144]{1,0:T(8,128)(2,1)} %source_ref, bf16[128,128]{1,0:T(8,128)(2,1)} %pad.4.extra_ref), custom_call_target="tpu_custom_call" | custom-call | flops 1 | bytes 1 | tf_op jit(solution)/shard_map/pallas_call | solution.py:150
  22.5 1.5 %collective-permute-start.5 = (bf16[128,3200]{1,0:T(8,128)(2,1)}, bf16[128,3200]{1,0:T(8,128)(2,1)S(1)}, u32[]{:S(2)}, u32[]{:S(2)}) collective-permute-start(bf16[128,3200]{1,0:T(8,128)(2,1)} %get-tuple-element.86), channel_id=1, source_target_pairs={{0,2},{1,3},{2,0},{3,1},{4,6},{5,7},{6,4},{7,5},{8,10},{9,11},{10,... | collective-permute-start | bytes 2457608 | tf_op jit(solution)/shard_map/ppermute | solution.py:531
  24.1 10.7 %shard_map.93 = (f32[3088,128]{1,0:T(8,128)}, f32[4112,128]{1,0:T(8,128)}) custom-call(s32[3]{0:T(128)} %pad_add_fusion.refs_0_.position_ref, bf16[6144,768]{1,0:T(8,128)(2,1)} %bitcast.69, bf16[6144,768]{1,0:T(8,128)(2,1)} %bitcast.70, bf16[6144,768]{1,0:T(8,128)(2,1)} %bitcast.71, bf16[6144,768]{1,0:T(8,128)(2,1)} %bitcast.72, ...), custom_call_target="tpu_custom_call" | custom-call | flops 1 | bytes 1 | tf_op jit(solution)/shard_map/pallas_call | solution.py:104
  35.0 1.9 %select_convert_fusion.1 = (f16[1552,128]{1,0:T(8,128)(2,1)S(1)}, f32[1552,128]{1,0:T(8,128)S(1)}) fusion(f32[3088,128]{1,0:T(8,128)} %get-tuple-element.77, f16[3088,128]{1,0:T(8,128)(2,1)S(1)} %collective-permute-done, f32[128]{0:T(128)S(1)} %bitcast.82, f32[128]{0:T(128)S(1)} %get-tuple-element.135, f32[128]{0:T(128)S(1)} %get-tuple-element.146, ...), kind=kLoop, calls=%fused_computation.2 | loop fusion | flops 1787904 | bytes 3578896 | tf_op jit(solution)/shard_map/convert_element_type | solution.py:126
  36.8 1.6 %collective-permute-start.1 = (f16[1552,128]{1,0:T(8,128)(2,1)S(1)}, f16[1552,128]{1,0:T(8,128)(2,1)S(1)}, u32[]{:S(2)}, u32[]{:S(2)}) collective-permute-start(f16[1552,128]{1,0:T(8,128)(2,1)S(1)} %get-tuple-element.139), channel_id=1, source_target_pairs={{0,4},{4,0},{8,12},{12,8},{16,20},{20,16},{24,28},{28,24},{1,5},{5... | collective-permute-start | bytes 1191944 | tf_op jit(solution)/shard_map/ppermute | solution.py:507
  38.5 4.7 %collective-permute-done.2 = f16[4112,128]{1,0:T(8,128)(2,1)S(1)} collective-permute-done((f16[4112,128]{1,0:T(8,128)(2,1)S(1)}, f16[4112,128]{1,0:T(8,128)(2,1)S(1)}, u32[]{:S(2)}, u32[]{:S(2)}) %collective-permute-start.2) | collective-permute-done | bytes 1052704 | tf_op jit(solution)/shard_map/ppermute | solution.py:507
  43.2 1.2 multiply_add_fusion
  44.5 5.6 %shard_map.94 = (bf16[256,4096]{1,0:T(8,128)(2,1)}, bf16[64,4096]{1,0:T(8,128)(2,1)}, bf16[192,4096]{1,0:T(8,128)(2,1)}) custom-call(s32[3]{0:T(128)} %pad_add_fusion.refs_0_.position_ref, bf16[128,2,8192]{2,1,0:T(2,128)(2,1)} %source_ref.1), custom_call_target="tpu_custom_call" | custom-call | flops 1 | bytes 8388608 | tf_op jit(solution)/shard_map/pallas_call | solution.py:196
  50.1 1.9 %collective-permute-start.6 = (bf16[64,4096]{1,0:T(8,128)(2,1)}, bf16[64,4096]{1,0:T(8,128)(2,1)S(1)}, u32[]{:S(2)}, u32[]{:S(2)}) collective-permute-start(bf16[64,4096]{1,0:T(8,128)(2,1)} %get-tuple-element.88), channel_id=1, source_target_pairs={{0,2},{1,3},{2,0},{3,1},{4,6},{5,7},{6,4},{7,5},{8,10},{9,11},{10,... | collective-permute-start | bytes 1572872 | tf_op jit(solution)/shard_map/ppermute | solution.py:531
  52.3 2.7 %collective-permute-start.4 = (f16[784,128]{1,0:T(8,128)(2,1)S(1)}, f16[784,128]{1,0:T(8,128)(2,1)S(1)}, u32[]{:S(2)}, u32[]{:S(2)}) collective-permute-start(f16[784,128]{1,0:T(8,128)(2,1)S(1)} %get-tuple-element.144), channel_id=1, source_target_pairs={{0,16},{4,20},{8,24},{12,28},{16,0},{20,4},{24,8},{28,12},{1,17},{... | collective-permute-start | bytes 602120 | tf_op jit(solution)/shard_map/ppermute | solution.py:507
  54.9 4.9 %collective-permute-done.3 = f16[2064,128]{1,0:T(8,128)(2,1)S(1)} collective-permute-done((f16[2064,128]{1,0:T(8,128)(2,1)S(1)}, f16[2064,128]{1,0:T(8,128)(2,1)S(1)}, u32[]{:S(2)}, u32[]{:S(2)}) %collective-permute-start.3) | collective-permute-done | bytes 528416 | tf_op jit(solution)/shard_map/ppermute | solution.py:507
  60.2 1.4 collective-permute-done.6.refs_2_.refs_8_
  61.7 2.7 %collective-permute-start.8 = (f16[1040,128]{1,0:T(8,128)(2,1)S(1)}, f16[1040,128]{1,0:T(8,128)(2,1)S(1)}, u32[]{:S(2)}, u32[]{:S(2)}) collective-permute-start(f16[1040,128]{1,0:T(8,128)(2,1)S(1)} %get-tuple-element.141), channel_id=1, source_target_pairs={{0,16},{4,20},{8,24},{12,28},{16,0},{20,4},{24,8},{28,12},{1,17},{... | collective-permute-start | bytes 798728 | tf_op jit(solution)/shard_map/ppermute | solution.py:507
  64.4 2.3 %collective-permute-start.7 = (bf16[384,128]{1,0:T(8,128)(2,1)S(1)}, bf16[384,128]{1,0:T(8,128)(2,1)S(1)}, u32[]{:S(2)}, u32[]{:S(2)}) collective-permute-start(bf16[384,128]{1,0:T(8,128)(2,1)S(1)} %get-tuple-element.158), channel_id=1, source_target_pairs={{0,2},{1,3},{2,0},{3,1},{4,6},{5,7},{6,4},{7,5},{8,10},{9,11},{10,... | collective-permute-start | bytes 294920 | tf_op jit(solution)/shard_map/ppermute | solution.py:526
  67.2 2.1 %collective-permute-done.7 = bf16[384,128]{1,0:T(8,128)(2,1)S(1)} collective-permute-done((bf16[384,128]{1,0:T(8,128)(2,1)S(1)}, bf16[384,128]{1,0:T(8,128)(2,1)S(1)}, u32[]{:S(2)}, u32[]{:S(2)}) %collective-permute-start.7) | collective-permute-done | bytes 98336 | tf_op jit(solution)/shard_map/ppermute | solution.py:526
  69.3 4.0 %collective-permute-done.8 = f16[1040,128]{1,0:T(8,128)(2,1)S(1)} collective-permute-done((f16[1040,128]{1,0:T(8,128)(2,1)S(1)}, f16[1040,128]{1,0:T(8,128)(2,1)S(1)}, u32[]{:S(2)}, u32[]{:S(2)}) %collective-permute-start.8) | collective-permute-done | bytes 266272 | tf_op jit(solution)/shard_map/ppermute | solution.py:507
  73.4 1.6 %collective-permute-start.13 = (bf16[512,128]{1,0:T(8,128)(2,1)S(1)}, bf16[512,128]{1,0:T(8,128)(2,1)S(1)}, u32[]{:S(2)}, u32[]{:S(2)}) collective-permute-start(bf16[512,128]{1,0:T(8,128)(2,1)S(1)} %get-tuple-element.156), channel_id=1, source_target_pairs={{0,2},{1,3},{2,0},{3,1},{4,6},{5,7},{6,4},{7,5},{8,10},{9,11},{10,... | collective-permute-start | bytes 393224 | tf_op jit(solution)/shard_map/ppermute | solution.py:526
  75.0 3.7 %collective-permute-done.13 = bf16[512,128]{1,0:T(8,128)(2,1)S(1)} collective-permute-done((bf16[512,128]{1,0:T(8,128)(2,1)S(1)}, bf16[512,128]{1,0:T(8,128)(2,1)S(1)}, u32[]{:S(2)}, u32[]{:S(2)}) %collective-permute-start.13) | collective-permute-done | bytes 131104 | tf_op jit(solution)/shard_map/ppermute | solution.py:526
  78.8 1.3 collective-permute-start.21
  80.1 8.0 %collective-permute-done.9 = bf16[1,384,256]{2,1,0:T(8,128)(2,1)S(1)} collective-permute-done((bf16[1,384,256]{2,1,0:T(8,128)(2,1)S(1)}, bf16[1,384,256]{2,1,0:T(8,128)(2,1)S(1)}, u32[]{:S(2)}, u32[]{:S(2)}) %collective-permute-start.9) | collective-permute-done | bytes 196640 | tf_op jit(solution)/shard_map/ppermute | solution.py:507
  88.2 0.8 pad_maximum_fusion.1
  89.0 0.9 collective-permute-start.16
  89.9 1.5 %collective-permute-start.17 = (bf16[1,256,256]{2,1,0:T(8,128)(2,1)S(1)}, bf16[1,256,256]{2,1,0:T(8,128)(2,1)S(1)}, u32[]{:S(2)}, u32[]{:S(2)}) collective-permute-start(bf16[1,256,256]{2,1,0:T(8,128)(2,1)S(1)} %get-tuple-element.153), channel_id=1, source_target_pairs={{0,4},{4,0},{8,12},{12,8},{16,20},{20,16},{24,28},{28,24},{1,5},{5... | collective-permute-start | bytes 393224 | tf_op jit(solution)/shard_map/ppermute | solution.py:507
  91.3 6.2 %collective-permute-done.16 = bf16[1,256,256]{2,1,0:T(8,128)(2,1)S(1)} collective-permute-done((bf16[1,256,256]{2,1,0:T(8,128)(2,1)S(1)}, bf16[1,256,256]{2,1,0:T(8,128)(2,1)S(1)}, u32[]{:S(2)}, u32[]{:S(2)}) %collective-permute-start.16) | collective-permute-done | bytes 131104 | tf_op jit(solution)/shard_map/ppermute | solution.py:507
  97.5 0.7 pad_maximum_fusion.3
  98.3 0.7 pad_maximum_fusion.4
  99.0 2.4 %shard_map.95 = (f32[2,1024,128]{2,1,0:T(8,128)}, bf16[2,1024,128]{2,1,0:T(8,128)(2,1)}, bf16[1024,128]{1,0:T(8,128)(2,1)}) custom-call(s32[3]{0:T(128)} %pad_add_fusion.refs_0_.position_ref, bf16[128,3200]{1,0:T(8,128)(2,1)} %get-tuple-element.101.refs_0_, bf16[128,3200]{1,0:T(8,128)(2,1)} %copy-done.8, bf16[128,3200]{1,0:T(8,128)(2,1)} %copy-done.7, ...), custom_call_target="tpu_custom_call" | custom-call | flops 1 | bytes 60000000 | tf_op jit(solution)/shard_map/pallas_call | solution.py:246
  101.4 1.1 pad_maximum_fusion.refs_4_
  102.5 1.4 collective-permute-start.18
  104.3 3.1 %collective-permute-start.20 = (bf16[2,256,256]{2,1,0:T(8,128)(2,1)S(1)}, bf16[2,256,256]{2,1,0:T(8,128)(2,1)S(1)}, u32[]{:S(2)}, u32[]{:S(2)}) collective-permute-start(bf16[2,256,256]{2,1,0:T(8,128)(2,1)S(1)} %copy-done.15), channel_id=1, source_target_pairs={{0,16},{4,20},{8,24},{12,28},{16,0},{20,4},{24,8},{28,12},{1,17},{... | collective-permute-start | bytes 786440 | tf_op jit(solution)/shard_map/ppermute | solution.py:507
  107.4 0.7 constant_dynamic-update-slice_fusion.1
  108.1 5.4 %collective-permute-done.19 = bf16[2,256,256]{2,1,0:T(8,128)(2,1)S(1)} collective-permute-done((bf16[2,256,256]{2,1,0:T(8,128)(2,1)S(1)}, bf16[2,256,256]{2,1,0:T(8,128)(2,1)S(1)}, u32[]{:S(2)}, u32[]{:S(2)}) %collective-permute-start.19) | collective-permute-done | bytes 262176 | tf_op jit(solution)/shard_map/ppermute | solution.py:507
  113.5 0.7 constant_dynamic-update-slice_fusion.refs_6_
  114.2 3.9 %collective-permute-done.18.refs_5_ = bf16[4,384,256]{2,1,0:T(8,128)(2,1)S(1)} collective-permute-done((bf16[4,384,256]{2,1,0:T(8,128)(2,1)S(1)}, bf16[4,384,256]{2,1,0:T(8,128)(2,1)S(1)}, u32[]{:S(2)}, u32[]{:S(2)}) %collective-permute-start.18) | collective-permute-done | bytes 786464 | tf_op jit(solution)/shard_map/ppermute | solution.py:507
  118.1 1.4 collective-permute-start.24
  119.5 5.2 %shard_map.96 = (f32[1024,128]{1,0:T(8,128)}, bf16[1024,128]{1,0:T(8,128)(2,1)}) custom-call(s32[3]{0:T(128)} %pad_add_fusion.refs_0_.position_ref, f32[2,1024,128]{2,1,0:T(8,128)} %get-tuple-element.112.mask_in_ref, bf16[128,3200]{1,0:T(8,128)(2,1)} %get-tuple-element.101.refs_0_, bf16[128,3200]{1,0:T(8,128)(2,1)} %copy-done.8, ...), custom_call_target="tpu_custom_call" | custom-call | flops 1 | bytes 1 | tf_op jit(solution)/shard_map/pallas_call | solution.py:307
  124.8 5.7 %collective-permute-start.22 = (bf16[1024,128]{1,0:T(8,128)(2,1)}, bf16[1024,128]{1,0:T(8,128)(2,1)S(1)}, u32[]{:S(2)}, u32[]{:S(2)}) collective-permute-start(bf16[1024,128]{1,0:T(8,128)(2,1)} %get-tuple-element.123), channel_id=1, source_target_pairs={{0,2},{1,3},{2,0},{3,1},{4,6},{5,7},{6,4},{7,5},{8,10},{9,11},{10,... | collective-permute-start | bytes 786440 | tf_op jit(solution)/shard_map/ppermute | solution.py:656
  130.5 4.5 %shard_map.97.refs_5_ = f32[1024,256]{1,0:T(8,128)S(1)} custom-call(s32[3]{0:T(128)S(1)} %copy-done.5, bf16[256,4096]{1,0:T(8,128)(2,1)S(1)} %copy-done, bf16[256,4096]{1,0:T(8,128)(2,1)S(1)} %collective-permute-done.10.refs_1_.refs_7_, bf16[64,4096]{1,0:T(8,128)(2,1)S(1)} %collective-permute-done.6.refs_2_.refs_8_, ...), custom_call_target="tpu_custom_call" | custom-call | flops 1 | bytes 1 | tf_op jit(solution)/shard_map/pallas_call | solution.py:451
  135.0 2.1 %collective-permute-done.22.refs_4_ = bf16[1024,128]{1,0:T(8,128)(2,1)S(1)} collective-permute-done((bf16[1024,128]{1,0:T(8,128)(2,1)}, bf16[1024,128]{1,0:T(8,128)(2,1)S(1)}, u32[]{:S(2)}, u32[]{:S(2)}) %collective-permute-start.22) | collective-permute-done | bytes 262176 | tf_op jit(solution)/shard_map/ppermute | solution.py:656
  137.1 5.3 %shard_map.98 = (f32[4,4]{1,0:T(4,128)S(1)}, f32[4,4]{1,0:T(4,128)S(1)}, f32[4,4]{1,0:T(4,128)S(1)}, f32[4,4]{1,0:T(4,128)S(1)}) custom-call(s32[3]{0:T(128)S(1)} %copy-done.5, f32[128,4]{1,0:T(8,128)S(1)} %copy-done.4, bf16[2,1024,128]{2,1,0:T(8,128)(2,1)S(1)} %copy-done.1, bf16[1024,128]{1,0:T(8,128)(2,1)S(1)} %copy-done.3, f32[1024,128]{1,0:T(8,128)S(1)} %copy-done.2, ...), custom_call_target="tpu_custom_call" | custom-call | flops 1 | bytes 1 | tf_op jit(solution)/shard_map/pallas_call | solution.py:460
  142.8 1.5 collective-permute-start.27
  144.3 1.1 collective-permute-done.28
  145.4 0.9 collective-permute-done.27
  (99 shorter events, 4.1 us)
Async XLA Ops:
  11.2 2.6 %copy-start.13 = (f32[4112,128]{1,0:T(8,128)S(1)}, f32[4112,128]{1,0:T(8,128)}, u32[]{:S(2)}) copy-start(f32[4112,128]{1,0:T(8,128)} %get-tuple-element.70) | copy-start | bytes 6316036
  13.8 4.7 %copy-start.19 = (s32[1,128]{1,0:T(1,128)S(1)}, s32[1,128]{1,0:T(1,128)}, u32[]{:S(2)}) copy-start(s32[1,128]{1,0:T(1,128)} %param.12) | copy-start | bytes 1540
  13.8 4.7 %copy-start.18 = (s32[128,2]{0,1:T(2,128)S(1)}, s32[128,2]{0,1:T(2,128)}, u32[]{:S(2)}) copy-start(s32[128,2]{0,1:T(2,128)} %param.11) | copy-start | bytes 3076
  13.9 21.0 %collective-permute-start = (f16[3088,128]{1,0:T(8,128)(2,1)}, f16[3088,128]{1,0:T(8,128)(2,1)S(1)}, u32[]{:S(2)}, u32[]{:S(2)}) collective-permute-start(f16[3088,128]{1,0:T(8,128)(2,1)} %convert_element_type.77), channel_id=1, source_target_pairs={{0,8},{4,12},{8,0},{12,4},{16,24},{20,28},{24,16},{28,20},{1,9},{5... | collective-permute-start | bytes 2371592 | tf_op jit(solution)/shard_map/ppermute | solution.py:507
  17.0 26.2 %collective-permute-start.2 = (f16[4112,128]{1,0:T(8,128)(2,1)S(1)}, f16[4112,128]{1,0:T(8,128)(2,1)S(1)}, u32[]{:S(2)}, u32[]{:S(2)}) collective-permute-start(f16[4112,128]{1,0:T(8,128)(2,1)S(1)} %convert_element_type.78), channel_id=1, source_target_pairs={{0,4},{4,0},{8,12},{12,8},{16,20},{20,16},{24,28},{28,24},{1,5},{5... | collective-permute-start | bytes 3158024 | tf_op jit(solution)/shard_map/ppermute | solution.py:507
  22.5 37.7 %collective-permute-start.5 = (bf16[128,3200]{1,0:T(8,128)(2,1)}, bf16[128,3200]{1,0:T(8,128)(2,1)S(1)}, u32[]{:S(2)}, u32[]{:S(2)}) collective-permute-start(bf16[128,3200]{1,0:T(8,128)(2,1)} %get-tuple-element.86), channel_id=1, source_target_pairs={{0,2},{1,3},{2,0},{3,1},{4,6},{5,7},{6,4},{7,5},{8,10},{9,11},{10,... | collective-permute-start | bytes 2457608 | tf_op jit(solution)/shard_map/ppermute | solution.py:531
  24.1 10.7 %copy-start.14 = (bf16[1,768,128]{2,1,0:T(8,128)(2,1)S(1)}, bf16[1,768,128]{2,1,0:T(8,128)(2,1)}, u32[]{:S(2)}) copy-start(bf16[1,768,128]{2,1,0:T(8,128)(2,1)} %param.15) | copy-start | bytes 589828
  24.1 10.8 %copy-start.11 = (bf16[1,1024,128]{2,1,0:T(8,128)(2,1)S(1)}, bf16[1,1024,128]{2,1,0:T(8,128)(2,1)}, u32[]{:S(2)}) copy-start(bf16[1,1024,128]{2,1,0:T(8,128)(2,1)} %param.16) | copy-start | bytes 786436
  35.0 8.2 %copy-start.12 = (f32[4112,128]{1,0:T(8,128)S(1)}, f32[4112,128]{1,0:T(8,128)}, u32[]{:S(2)}) copy-start(f32[4112,128]{1,0:T(8,128)} %get-tuple-element.79) | copy-start | bytes 6316036
  36.8 15.2 %collective-permute-start.1 = (f16[1552,128]{1,0:T(8,128)(2,1)S(1)}, f16[1552,128]{1,0:T(8,128)(2,1)S(1)}, u32[]{:S(2)}, u32[]{:S(2)}) collective-permute-start(f16[1552,128]{1,0:T(8,128)(2,1)S(1)} %get-tuple-element.139), channel_id=1, source_target_pairs={{0,4},{4,0},{8,12},{12,8},{16,20},{20,16},{24,28},{28,24},{1,5},{5... | collective-permute-start | bytes 1191944 | tf_op jit(solution)/shard_map/ppermute | solution.py:507
  44.4 15.5 %collective-permute-start.3 = (f16[2064,128]{1,0:T(8,128)(2,1)S(1)}, f16[2064,128]{1,0:T(8,128)(2,1)S(1)}, u32[]{:S(2)}, u32[]{:S(2)}) collective-permute-start(f16[2064,128]{1,0:T(8,128)(2,1)S(1)} %get-tuple-element.84), channel_id=1, source_target_pairs={{0,8},{4,12},{8,0},{12,4},{16,24},{20,28},{24,16},{28,20},{1,9},{5... | collective-permute-start | bytes 1585160 | tf_op jit(solution)/shard_map/ppermute | solution.py:507
  50.1 11.6 %collective-permute-start.6 = (bf16[64,4096]{1,0:T(8,128)(2,1)}, bf16[64,4096]{1,0:T(8,128)(2,1)S(1)}, u32[]{:S(2)}, u32[]{:S(2)}) collective-permute-start(bf16[64,4096]{1,0:T(8,128)(2,1)} %get-tuple-element.88), channel_id=1, source_target_pairs={{0,2},{1,3},{2,0},{3,1},{4,6},{5,7},{6,4},{7,5},{8,10},{9,11},{10,... | collective-permute-start | bytes 1572872 | tf_op jit(solution)/shard_map/ppermute | solution.py:531
  52.3 7.8 %collective-permute-start.4 = (f16[784,128]{1,0:T(8,128)(2,1)S(1)}, f16[784,128]{1,0:T(8,128)(2,1)S(1)}, u32[]{:S(2)}, u32[]{:S(2)}) collective-permute-start(f16[784,128]{1,0:T(8,128)(2,1)S(1)} %get-tuple-element.144), channel_id=1, source_target_pairs={{0,16},{4,20},{8,24},{12,28},{16,0},{20,4},{24,8},{28,12},{1,17},{... | collective-permute-start | bytes 602120 | tf_op jit(solution)/shard_map/ppermute | solution.py:507
  54.9 33.2 %collective-permute-start.10 = (bf16[256,4096]{1,0:T(8,128)(2,1)}, bf16[256,4096]{1,0:T(8,128)(2,1)S(1)}, u32[]{:S(2)}, u32[]{:S(2)}) collective-permute-start(bf16[256,4096]{1,0:T(8,128)(2,1)} %get-tuple-element.91.refs_0_.refs_6_), channel_id=1, source_target_pairs={{0,1},{1,0},{2,3},{3,2},{4,5},{5,4},{6,7},{7,6},{8,9},{9,8},{10,11... | collective-permute-start | bytes 6291464 | tf_op jit(solution)/shard_map/ppermute | solution.py:534
  60.1 6.6 %copy-start.6 = (bf16[128,3200]{1,0:T(8,128)(2,1)S(1)}, bf16[128,3200]{1,0:T(8,128)(2,1)}, u32[]{:S(2)}) copy-start(bf16[128,3200]{1,0:T(8,128)(2,1)} %get-tuple-element.101.refs_0_) | copy-start | bytes 2457604
  60.2 13.2 %copy-start.7 = (bf16[128,3200]{1,0:T(8,128)(2,1)}, bf16[128,3200]{1,0:T(8,128)(2,1)S(1)}, u32[]{:S(2)}) copy-start(bf16[128,3200]{1,0:T(8,128)(2,1)S(1)} %collective-permute-done.5.refs_2_) | copy-start | bytes 2457604
  61.7 11.6 %collective-permute-start.8 = (f16[1040,128]{1,0:T(8,128)(2,1)S(1)}, f16[1040,128]{1,0:T(8,128)(2,1)S(1)}, u32[]{:S(2)}, u32[]{:S(2)}) collective-permute-start(f16[1040,128]{1,0:T(8,128)(2,1)S(1)} %get-tuple-element.141), channel_id=1, source_target_pairs={{0,16},{4,20},{8,24},{12,28},{16,0},{20,4},{24,8},{28,12},{1,17},{... | collective-permute-start | bytes 798728 | tf_op jit(solution)/shard_map/ppermute | solution.py:507
  64.4 4.9 %collective-permute-start.7 = (bf16[384,128]{1,0:T(8,128)(2,1)S(1)}, bf16[384,128]{1,0:T(8,128)(2,1)S(1)}, u32[]{:S(2)}, u32[]{:S(2)}) collective-permute-start(bf16[384,128]{1,0:T(8,128)(2,1)S(1)} %get-tuple-element.158), channel_id=1, source_target_pairs={{0,2},{1,3},{2,0},{3,1},{4,6},{5,7},{6,4},{7,5},{8,10},{9,11},{10,... | collective-permute-start | bytes 294920 | tf_op jit(solution)/shard_map/ppermute | solution.py:526
  66.7 12.1 %collective-permute-start.14 = (bf16[128,3200]{1,0:T(8,128)(2,1)S(1)}, bf16[128,3200]{1,0:T(8,128)(2,1)S(1)}, u32[]{:S(2)}, u32[]{:S(2)}) collective-permute-start(bf16[128,3200]{1,0:T(8,128)(2,1)S(1)} %copy-done.6), channel_id=1, source_target_pairs={{0,1},{1,0},{2,3},{3,2},{4,5},{5,4},{6,7},{7,6},{8,9},{9,8},{10,11... | collective-permute-start | bytes 2457608 | tf_op jit(solution)/shard_map/ppermute | solution.py:534
  66.7 21.5 %collective-permute-start.11 = (bf16[64,4096]{1,0:T(8,128)(2,1)S(1)}, bf16[64,4096]{1,0:T(8,128)(2,1)S(1)}, u32[]{:S(2)}, u32[]{:S(2)}) collective-permute-start(bf16[64,4096]{1,0:T(8,128)(2,1)S(1)} %collective-permute-done.6.refs_2_.refs_8_), channel_id=1, source_target_pairs={{0,1},{1,0},{2,3},{3,2},{4,5},{5,4},{6,7},{7,6},{8,9},{9,8},{10,11... | collective-permute-start | bytes 1572872 | tf_op jit(solution)/shard_map/ppermute | solution.py:534
  69.3 9.5 %collective-permute-start.15 = (bf16[128,3200]{1,0:T(8,128)(2,1)S(1)}, bf16[128,3200]{1,0:T(8,128)(2,1)S(1)}, u32[]{:S(2)}, u32[]{:S(2)}) collective-permute-start(bf16[128,3200]{1,0:T(8,128)(2,1)S(1)} %collective-permute-done.5.refs_2_), channel_id=1, source_target_pairs={{0,1},{1,0},{2,3},{3,2},{4,5},{5,4},{6,7},{7,6},{8,9},{9,8},{10,11... | collective-permute-start | bytes 2457608 | tf_op jit(solution)/shard_map/ppermute | solution.py:534
  73.4 5.3 %collective-permute-start.13 = (bf16[512,128]{1,0:T(8,128)(2,1)S(1)}, bf16[512,128]{1,0:T(8,128)(2,1)S(1)}, u32[]{:S(2)}, u32[]{:S(2)}) collective-permute-start(bf16[512,128]{1,0:T(8,128)(2,1)S(1)} %get-tuple-element.156), channel_id=1, source_target_pairs={{0,2},{1,3},{2,0},{3,1},{4,6},{5,7},{6,4},{7,5},{8,10},{9,11},{10,... | collective-permute-start | bytes 393224 | tf_op jit(solution)/shard_map/ppermute | solution.py:526
  78.7 9.5 %collective-permute-start.9 = (bf16[1,384,256]{2,1,0:T(8,128)(2,1)S(1)}, bf16[1,384,256]{2,1,0:T(8,128)(2,1)S(1)}, u32[]{:S(2)}, u32[]{:S(2)}) collective-permute-start(bf16[1,384,256]{2,1,0:T(8,128)(2,1)S(1)} %bitcast.77), channel_id=1, source_target_pairs={{0,16},{4,20},{8,24},{12,28},{16,0},{20,4},{24,8},{28,12},{1,17},{... | collective-permute-start | bytes 589832 | tf_op jit(solution)/shard_map/ppermute | solution.py:507
  78.8 9.4 %copy-start.8 = (bf16[128,3200]{1,0:T(8,128)(2,1)}, bf16[128,3200]{1,0:T(8,128)(2,1)S(1)}, u32[]{:S(2)}) copy-start(bf16[128,3200]{1,0:T(8,128)(2,1)S(1)} %collective-permute-done.14.refs_1_) | copy-start | bytes 2457604
  78.8 10.2 %copy-start.9 = (bf16[128,3200]{1,0:T(8,128)(2,1)}, bf16[128,3200]{1,0:T(8,128)(2,1)S(1)}, u32[]{:S(2)}) copy-start(bf16[128,3200]{1,0:T(8,128)(2,1)S(1)} %collective-permute-done.15.refs_3_) | copy-start | bytes 2457604
  78.8 39.3 %collective-permute-start.21 = (bf16[192,4096]{1,0:T(8,128)(2,1)}, bf16[192,4096]{1,0:T(8,128)(2,1)}, u32[]{:S(2)}, u32[]{:S(2)}) collective-permute-start(bf16[192,4096]{1,0:T(8,128)(2,1)} %get-tuple-element.117), channel_id=1, source_target_pairs={{0,2},{1,3},{2,0},{3,1},{4,6},{5,7},{6,4},{7,5},{8,10},{9,11},{10,... | collective-permute-start | bytes 4718600 | tf_op jit(solution)/shard_map/ppermute | solution.py:531
  89.0 12.4 %collective-permute-start.12 = (bf16[2,384,256]{2,1,0:T(8,128)(2,1)}, bf16[2,384,256]{2,1,0:T(8,128)(2,1)}, u32[]{:S(2)}, u32[]{:S(2)}) collective-permute-start(bf16[2,384,256]{2,1,0:T(8,128)(2,1)} %pad_maximum_fusion.1), channel_id=1, source_target_pairs={{0,8},{4,12},{8,0},{12,4},{16,24},{20,28},{24,16},{28,20},{1,9},{5... | collective-permute-start | bytes 1179656 | tf_op jit(solution)/shard_map/ppermute | solution.py:507
  89.0 8.5 %collective-permute-start.16 = (bf16[1,256,256]{2,1,0:T(8,128)(2,1)S(1)}, bf16[1,256,256]{2,1,0:T(8,128)(2,1)S(1)}, u32[]{:S(2)}, u32[]{:S(2)}) collective-permute-start(bf16[1,256,256]{2,1,0:T(8,128)(2,1)S(1)} %get-tuple-element.154), channel_id=1, source_target_pairs={{0,16},{4,20},{8,24},{12,28},{16,0},{20,4},{24,8},{28,12},{1,17},{... | collective-permute-start | bytes 393224 | tf_op jit(solution)/shard_map/ppermute | solution.py:507
  89.9 8.4 %collective-permute-start.17 = (bf16[1,256,256]{2,1,0:T(8,128)(2,1)S(1)}, bf16[1,256,256]{2,1,0:T(8,128)(2,1)S(1)}, u32[]{:S(2)}, u32[]{:S(2)}) collective-permute-start(bf16[1,256,256]{2,1,0:T(8,128)(2,1)S(1)} %get-tuple-element.153), channel_id=1, source_target_pairs={{0,4},{4,0},{8,12},{12,8},{16,20},{20,16},{24,28},{28,24},{1,5},{5... | collective-permute-start | bytes 393224 | tf_op jit(solution)/shard_map/ppermute | solution.py:507
  101.3 2.6 %copy-start.16 = (bf16[2,256,256]{2,1,0:T(8,128)(2,1)S(1)}, bf16[2,256,256]{2,1,0:T(8,128)(2,1)}, u32[]{:S(2)}) copy-start(bf16[2,256,256]{2,1,0:T(8,128)(2,1)} %pad_maximum_fusion.3) | copy-start | bytes 786436
  101.3 3.0 %copy-start.15 = (bf16[2,256,256]{2,1,0:T(8,128)(2,1)S(1)}, bf16[2,256,256]{2,1,0:T(8,128)(2,1)}, u32[]{:S(2)}) copy-start(bf16[2,256,256]{2,1,0:T(8,128)(2,1)} %pad_maximum_fusion.4) | copy-start | bytes 786436
  102.5 17.0 %copy-start.10 = (bf16[4,384,256]{2,1,0:T(8,128)(2,1)}, bf16[4,384,256]{2,1,0:T(8,128)(2,1)S(1)}, u32[]{:S(2)}) copy-start(bf16[4,384,256]{2,1,0:T(8,128)(2,1)S(1)} %pad_maximum_fusion.refs_4_) | copy-start | bytes 2359300
  102.5 15.6 %collective-permute-start.18 = (bf16[4,384,256]{2,1,0:T(8,128)(2,1)S(1)}, bf16[4,384,256]{2,1,0:T(8,128)(2,1)S(1)}, u32[]{:S(2)}, u32[]{:S(2)}) collective-permute-start(bf16[4,384,256]{2,1,0:T(8,128)(2,1)S(1)} %pad_maximum_fusion.refs_4_), channel_id=1, source_target_pairs={{0,4},{4,0},{8,12},{12,8},{16,20},{20,16},{24,28},{28,24},{1,5},{5... | collective-permute-start | bytes 2359304 | tf_op jit(solution)/shard_map/ppermute | solution.py:507
  103.9 9.6 %collective-permute-start.19 = (bf16[2,256,256]{2,1,0:T(8,128)(2,1)S(1)}, bf16[2,256,256]{2,1,0:T(8,128)(2,1)S(1)}, u32[]{:S(2)}, u32[]{:S(2)}) collective-permute-start(bf16[2,256,256]{2,1,0:T(8,128)(2,1)S(1)} %copy-done.16), channel_id=1, source_target_pairs={{0,8},{4,12},{8,0},{12,4},{16,24},{20,28},{24,16},{28,20},{1,9},{5... | collective-permute-start | bytes 786440 | tf_op jit(solution)/shard_map/ppermute | solution.py:507
  104.3 9.9 %collective-permute-start.20 = (bf16[2,256,256]{2,1,0:T(8,128)(2,1)S(1)}, bf16[2,256,256]{2,1,0:T(8,128)(2,1)S(1)}, u32[]{:S(2)}, u32[]{:S(2)}) collective-permute-start(bf16[2,256,256]{2,1,0:T(8,128)(2,1)S(1)} %copy-done.15), channel_id=1, source_target_pairs={{0,16},{4,20},{8,24},{12,28},{16,0},{20,4},{24,8},{28,12},{1,17},{... | collective-permute-start | bytes 786440 | tf_op jit(solution)/shard_map/ppermute | solution.py:507
  114.2 16.3 %copy-start.5 = (s32[3]{0:T(128)S(1)}, s32[3]{0:T(128)}, u32[]{:S(2)}) copy-start(s32[3]{0:T(128)} %pad_add_fusion.refs_0_.position_ref) | copy-start | bytes 40
  118.1 12.4 %collective-permute-start.23 = (bf16[192,4096]{1,0:T(8,128)(2,1)}, bf16[192,4096]{1,0:T(8,128)(2,1)}, u32[]{:S(2)}, u32[]{:S(2)}) collective-permute-start(bf16[192,4096]{1,0:T(8,128)(2,1)} %collective-permute-done.21.refs_3_.refs_9_), channel_id=1, source_target_pairs={{0,1},{1,0},{2,3},{3,2},{4,5},{5,4},{6,7},{7,6},{8,9},{9,8},{10,11... | collective-permute-start | bytes 4718600 | tf_op jit(solution)/shard_map/ppermute | solution.py:534
  118.1 16.9 %collective-permute-start.24 = (bf16[4,256,256]{2,1,0:T(8,128)(2,1)}, bf16[4,256,256]{2,1,0:T(8,128)(2,1)}, u32[]{:S(2)}, u32[]{:S(2)}) collective-permute-start(bf16[4,256,256]{2,1,0:T(8,128)(2,1)} %constant_dynamic-update-slice_fusion.refs_6_), channel_id=1, source_target_pairs={{0,4},{4,0},{8,12},{12,8},{16,20},{20,16},{24,28},{28,24},{1,5},{5... | collective-permute-start | bytes 1572872 | tf_op jit(solution)/shard_map/ppermute | solution.py:507
  119.5 15.5 %collective-permute-start.25 = (bf16[4,256,256]{2,1,0:T(8,128)(2,1)S(1)}, bf16[4,256,256]{2,1,0:T(8,128)(2,1)}, u32[]{:S(2)}, u32[]{:S(2)}) collective-permute-start(bf16[4,256,256]{2,1,0:T(8,128)(2,1)S(1)} %constant_dynamic-update-slice_fusion.2.refs_7_), channel_id=1, source_target_pairs={{0,8},{4,12},{8,0},{12,4},{16,24},{20,28},{24,16},{28,20},{1,9},{5... | collective-permute-start | bytes 1572872 | tf_op jit(solution)/shard_map/ppermute | solution.py:507
  119.5 11.0 %copy-start = (bf16[256,4096]{1,0:T(8,128)(2,1)S(1)}, bf16[256,4096]{1,0:T(8,128)(2,1)}, u32[]{:S(2)}) copy-start(bf16[256,4096]{1,0:T(8,128)(2,1)} %get-tuple-element.91.refs_0_.refs_6_) | copy-start | bytes 6291460
  124.7 12.3 %copy-start.1 = (bf16[2,1024,128]{2,1,0:T(8,128)(2,1)S(1)}, bf16[2,1024,128]{2,1,0:T(8,128)(2,1)}, u32[]{:S(2)}) copy-start(bf16[2,1024,128]{2,1,0:T(8,128)(2,1)} %get-tuple-element.110.refs_1_) | copy-start | bytes 1572868
  124.7 12.3 %copy-start.2 = (f32[1024,128]{1,0:T(8,128)S(1)}, f32[1024,128]{1,0:T(8,128)}, u32[]{:S(2)}) copy-start(f32[1024,128]{1,0:T(8,128)} %get-tuple-element.119.refs_3_) | copy-start | bytes 1572868
  124.7 12.3 %copy-start.3 = (bf16[1024,128]{1,0:T(8,128)(2,1)S(1)}, bf16[1024,128]{1,0:T(8,128)(2,1)}, u32[]{:S(2)}) copy-start(bf16[1024,128]{1,0:T(8,128)(2,1)} %get-tuple-element.111.refs_2_) | copy-start | bytes 786436
  124.7 12.3 %copy-start.4 = (f32[128,4]{1,0:T(8,128)S(1)}, f32[128,4]{1,0:T(8,128)}, u32[]{:S(2)}) copy-start(f32[128,4]{1,0:T(8,128)} %constant.71.clone.refs_0_) | copy-start | bytes 6148
  124.8 12.3 %collective-permute-start.22 = (bf16[1024,128]{1,0:T(8,128)(2,1)}, bf16[1024,128]{1,0:T(8,128)(2,1)S(1)}, u32[]{:S(2)}, u32[]{:S(2)}) collective-permute-start(bf16[1024,128]{1,0:T(8,128)(2,1)} %get-tuple-element.123), channel_id=1, source_target_pairs={{0,2},{1,3},{2,0},{3,1},{4,6},{5,7},{6,4},{7,5},{8,10},{9,11},{10,... | collective-permute-start | bytes 786440 | tf_op jit(solution)/shard_map/ppermute | solution.py:656
  142.3 3.1 %collective-permute-start.28 = (f32[4,4]{1,0:T(4,128)S(1)}, f32[4,4]{1,0:T(4,128)S(1)}, u32[]{:S(2)}, u32[]{:S(2)}) collective-permute-start(f32[4,4]{1,0:T(4,128)S(1)} %get-tuple-element.132), channel_id=1, source_target_pairs={{0,3},{1,2},{2,1},{3,0},{4,7},{5,6},{6,5},{7,4},{8,11},{9,10},{10,... | collective-permute-start | bytes 200 | tf_op jit(solution)/shard_map/ppermute | solution.py:669
  142.8 3.6 %collective-permute-start.27 = (f32[4,4]{1,0:T(4,128)S(1)}, f32[4,4]{1,0:T(4,128)S(1)}, u32[]{:S(2)}, u32[]{:S(2)}) collective-permute-start(f32[4,4]{1,0:T(4,128)S(1)} %get-tuple-element.131), channel_id=1, source_target_pairs={{0,2},{1,3},{2,0},{3,1},{4,6},{5,7},{6,4},{7,5},{8,10},{9,11},{10,... | collective-permute-start | bytes 200 | tf_op jit(solution)/shard_map/ppermute | solution.py:669
  144.2 2.1 %collective-permute-start.26 = (f32[4,4]{1,0:T(4,128)S(1)}, f32[4,4]{1,0:T(4,128)S(1)}, u32[]{:S(2)}, u32[]{:S(2)}) collective-permute-start(f32[4,4]{1,0:T(4,128)S(1)} %get-tuple-element.130), channel_id=1, source_target_pairs={{0,1},{1,0},{2,3},{3,2},{4,5},{5,4},{6,7},{7,6},{8,9},{9,8},{10,11... | collective-permute-start | bytes 200 | tf_op jit(solution)/shard_map/ppermute | solution.py:669
  (1 other events, 1.4 us)
